TPU v7x, 32 devices: a whole 2x2x4 slice. The times are simulated.
32 devices in a mesh: dp: 4 (over y, x), seq: 4 (over z), tensor: 2 (over core).
Axes of the slice: x: 2, y: 2, z: 4, core: 2. Of those that a mesh axis runs over, the one named last changes fastest.
Arguments:
- inputs: bfloat16 [2048, 3584], P(('dp', 'seq'), 'tensor'), parts along dimension 0, may hold values from -6 to 6
- cotangent: bfloat16 [2048, 3584], P(('dp', 'seq'), 'tensor'), parts along dimension 0, may hold values from -6 to 6
- norm_gain: float32 [2, 3584], replicated, may hold values from 0.25 to 1.75
- head_gain: float32 [2, 2, 128], replicated, may hold values from 0.5 to 2.5
- query_weight: bfloat16 [2, 3584, 2048], P(None, None, 'tensor'), may hold values from -0.09375 to 0.09375
- key_weight: bfloat16 [2, 3584, 1024], P(None, None, 'tensor'), may hold values from -0.09375 to 0.09375
- output_weight: bfloat16 [2, 2048, 3584], P(None, 'tensor'), may hold values from -0.375 to 0.375
- modality: int32 [2048], P(('dp', 'seq')), parts along dimension 0, may hold values 0 or 1
- segments: int32 [2048], P('dp'), parts along dimension 0, may hold values from 0 to 63, never falling along the last dimension, each value on 1 to 256 neighbouring positions
- block_order: int32 [16], P('dp'), parts along dimension 0, may hold values from 0 to 3, each once
Outputs:
- attention_out: bfloat16 [2048, 3584], P(('dp', 'seq'), 'tensor'), parts along dimension 0
- grad_input: bfloat16 [2048, 3584], P(('dp', 'seq'), 'tensor'), parts along dimension 0
There are 4 independent parts, one for each index of `dp`. A program takes and returns all parts, laid end to end along the dimension named above; an argument that names none is the same for every part. Nothing has to cross between parts.
Inputs may be any that keep to these rules, and one draw needn't show every extreme that they name: `modality`: 1 marks an image token, 0 a text token. `segments`: never falls along the sequence; each segment covers 1 to 256 positions and one covers exactly 256. `block_order`: each block appears once.
All inputs are finite; a program needn't handle non-finite values. No bound on the sum of `modality` on one device may be relied on, other than what follows from the above.
Results may differ from a plain program's by a relative error of at most 0.022.
Values may be sent and summed in bfloat16 or wider, within the bound.
No kernel may reach another device: no remote copies, remote signals or barrier semaphores. Data moves between devices by JAX's collectives and lax.ppermute only.
A program may use at most 128 MiB of HBM per device.

v0:
```python
import math

import jax
import jax.numpy as jnp
from jax import lax
from jax.sharding import PartitionSpec as P

D = 3584
KV_HEADS = 4
HEAD_DIM = 128


epsilon = 1e-06


def partner_2(value, axis, bit):
    mask = 2**bit
    pairs = [(source, source ^ mask) for source in range(lax.axis_size(axis))]
    return lax.ppermute(value, axis, pairs)


def row_norm(values, scaling):
    factor = lax.rsqrt(jnp.mean(values * values, axis=-1, keepdims=True) + epsilon)
    return (values * factor * scaling, factor)


def norm_back(values, factor, scaling, upstream):
    unit_rows = values * factor
    inner_mean = jnp.mean(scaling * upstream * unit_rows, axis=-1, keepdims=True)
    return factor * (scaling * upstream - unit_rows * inner_mean)


def modality_plan(modality):
    row_count = modality.shape[0]
    ordering = jnp.argsort(modality, stable=True)
    inverse = (
        jnp.zeros((row_count,), jnp.int32).at[ordering].set(jnp.arange(row_count, dtype=jnp.int32))
    )
    image_count = jnp.sum(modality)
    counts = jnp.stack([row_count - image_count, image_count])
    return (ordering, inverse, counts)


def expert_pick(plan, weights, operand):
    ordering, inverse, counts = plan
    result = lax.ragged_dot(operand[ordering], weights, counts, preferred_element_type=jnp.float32)
    return result[inverse]


def expert_back(plan, weights, operand):
    return expert_pick(plan, jnp.swapaxes(weights, 1, 2), operand)


def local(
    inputs,
    cotangent,
    norm_gain,
    head_gain,
    query_weight,
    key_weight,
    output_weight,
    modality,
    segments,
    block_order,
):
    tensor_rank = lax.axis_index("tensor")
    block_rank = lax.axis_index("seq")
    tensor_count = lax.axis_size("tensor")
    block_count = lax.axis_size("seq")
    local_rows = inputs.shape[0]
    local_width = inputs.shape[1]
    all_rows = local_rows * block_count
    score_scale = 1.0 / math.sqrt(HEAD_DIM)
    whole_rows, whole_cotangent = (
        lax.all_gather(inputs, "tensor", axis=1, tiled=True),
        lax.all_gather(cotangent, "tensor", axis=1, tiled=True),
    )
    plan = modality_plan(modality)
    is_image = (modality == 1)[:, None]
    head_image = is_image[:, :, None]
    rows_float = whole_rows.astype(jnp.float32)
    row_scaling = jnp.where(is_image, norm_gain[1][None, :], norm_gain[0][None, :])
    normed, row_factor = row_norm(rows_float, row_scaling)
    normed = normed.astype(jnp.bfloat16)
    query_heads = query_weight.shape[2] // HEAD_DIM
    query_raw = expert_pick(plan, query_weight, normed).reshape(local_rows, query_heads, HEAD_DIM)
    query_scaling = jnp.where(head_image, head_gain[1, 0], head_gain[0, 0])
    query_normed, query_factor = row_norm(query_raw, query_scaling)
    query_normed = query_normed.astype(jnp.bfloat16)
    slice_blocks = key_weight.shape[2] // HEAD_DIM
    key_raw = expert_pick(plan, key_weight, normed).reshape(local_rows, slice_blocks, HEAD_DIM)
    block_index = tensor_rank * slice_blocks + jnp.arange(slice_blocks, dtype=jnp.int32)
    is_key = (block_index % 2 == 0)[None, :, None]
    key_scaling = jnp.where(head_image, head_gain[1, 1], head_gain[0, 1])
    key_normed, key_factor = row_norm(key_raw, key_scaling)
    slice_out = jnp.where(is_key, key_normed, key_raw).astype(jnp.bfloat16)
    is_even = tensor_rank % 2 == 0
    if tensor_count > KV_HEADS:
        partner = partner_2(slice_out, "tensor", 0)
        memory = jnp.where(
            is_even,
            jnp.concatenate([slice_out, partner], 1),
            jnp.concatenate([partner, slice_out], 1),
        )
    else:
        memory = slice_out
    pair_count = memory.shape[1] // 2
    per_group = query_heads // pair_count
    query_group = query_normed.reshape(local_rows, pair_count, per_group, HEAD_DIM)

    def segment_of(first_row, row_count):
        positions = first_row + jnp.arange(row_count, dtype=jnp.int32)
        anchor = block_order[positions // local_rows] * local_rows + positions % local_rows
        return segments[anchor]

    query_segments = segment_of(block_rank * local_rows, local_rows)

    def score_weights(shard_rows, first_row):
        key_rows = shard_rows[:, 0::2]
        value_rows = shard_rows[:, 1::2]
        scores = (
            jnp.einsum("qgph,kgh->gpqk", query_group, key_rows, preferred_element_type=jnp.float32)
            * score_scale
        )
        visible = segment_of(first_row, shard_rows.shape[0])[None, :] <= query_segments[:, None]
        weights = jnp.where(visible, jnp.exp(scores), 0.0).astype(jnp.bfloat16)
        return (weights, key_rows, value_rows)

    zero_sums = jnp.zeros((local_rows, pair_count, per_group, HEAD_DIM), jnp.float32)
    zero_totals = jnp.zeros((pair_count, per_group, local_rows), jnp.float32)
    numerator = zero_sums
    attend_denominator = zero_totals
    weights, key_rows, value_rows = score_weights(
        lax.all_gather(memory, "seq", axis=0, tiled=True), jnp.int32(0)
    )
    numerator = numerator + jnp.einsum(
        "gpqk,kgh->qgph", weights, value_rows, preferred_element_type=jnp.float32
    )
    attend_denominator = attend_denominator + jnp.sum(weights.astype(jnp.float32), axis=-1)
    numerator, denominator = (numerator, attend_denominator)
    attended = (numerator / denominator.transpose(2, 0, 1)[..., None]).astype(jnp.bfloat16)
    attended_rows = attended.reshape(local_rows, query_heads * HEAD_DIM)
    output_part = expert_pick(plan, output_weight, attended_rows)
    attention_out = lax.psum_scatter(
        output_part.astype(jnp.bfloat16), "tensor", scatter_dimension=1, tiled=True
    )
    back_attended = expert_back(plan, output_weight, whole_cotangent).astype(jnp.bfloat16)
    back_group = back_attended.reshape(local_rows, pair_count, per_group, HEAD_DIM)
    offset = jnp.sum(
        back_group.astype(jnp.float32) * attended.astype(jnp.float32), axis=-1
    ).transpose(1, 2, 0)
    zero_query = jnp.zeros((local_rows, pair_count, per_group, HEAD_DIM), jnp.float32)
    zero_memory = jnp.zeros((all_rows, 2 * pair_count, HEAD_DIM), jnp.float32)
    shard_rows = lax.all_gather(memory, "seq", axis=0, tiled=True)
    first_row = jnp.int32(0)
    back_query = zero_query
    back_memory = zero_memory
    weights, key_rows, value_rows = score_weights(shard_rows, first_row)
    probability = (weights.astype(jnp.float32) / denominator[..., None]).astype(jnp.bfloat16)
    back_prob = jnp.einsum(
        "qgph,kgh->gpqk", back_group, value_rows, preferred_element_type=jnp.float32
    )
    back_score = (probability.astype(jnp.float32) * (back_prob - offset[..., None])).astype(
        jnp.bfloat16
    )
    back_query = back_query + jnp.einsum(
        "gpqk,kgh->qgph", back_score, key_rows, preferred_element_type=jnp.float32
    )
    back_key = (
        jnp.einsum("gpqk,qgph->kgh", back_score, query_group, preferred_element_type=jnp.float32)
        * score_scale
    )
    back_value = jnp.einsum(
        "gpqk,qgph->kgh", probability, back_group, preferred_element_type=jnp.float32
    )
    stacked = jnp.stack([back_key, back_value], axis=2).reshape(
        shard_rows.shape[0], 2 * pair_count, HEAD_DIM
    )
    back_memory = lax.dynamic_update_slice_in_dim(back_memory, stacked, first_row, 0)
    back_query, back_memory = (back_query, back_memory)
    memory_sum = lax.psum_scatter(
        back_memory.astype(jnp.bfloat16), "seq", scatter_dimension=0, tiled=True
    ).astype(jnp.float32)
    if tensor_count > KV_HEADS:
        outgoing = jnp.where(is_even, memory_sum[:, 1:2], memory_sum[:, 0:1])
        incoming = partner_2(outgoing.astype(jnp.bfloat16), "tensor", 0).astype(outgoing.dtype)
        slice_grad = jnp.where(is_even, memory_sum[:, 0:1], memory_sum[:, 1:2]) + incoming
    else:
        slice_grad = memory_sum
    slice_back = jnp.where(
        is_key, norm_back(key_raw, key_factor, key_scaling, slice_grad), slice_grad
    ).astype(jnp.bfloat16)
    query_upstream = back_query.reshape(local_rows, query_heads, HEAD_DIM) * score_scale
    query_back = norm_back(query_raw, query_factor, query_scaling, query_upstream).astype(
        jnp.bfloat16
    )
    gradient_part = expert_back(
        plan, query_weight, query_back.reshape(local_rows, query_heads * HEAD_DIM)
    )
    gradient_part = gradient_part + expert_back(
        plan, key_weight, slice_back.reshape(local_rows, slice_blocks * HEAD_DIM)
    )
    back_normed = lax.psum_scatter(
        gradient_part.astype(jnp.bfloat16), "tensor", scatter_dimension=1, tiled=True
    ).astype(jnp.float32)
    column_start = tensor_rank * local_width
    local_scaling = lax.dynamic_slice_in_dim(row_scaling, column_start, local_width, 1)
    unit_rows = inputs.astype(jnp.float32) * row_factor
    partial_inner = jnp.sum(local_scaling * back_normed * unit_rows, axis=1)
    inner_total = lax.psum(partial_inner, "tensor")
    grad_input = (
        row_factor * (local_scaling * back_normed - unit_rows * (inner_total / D)[:, None])
    ).astype(jnp.bfloat16)
    return (attention_out, grad_input)


def solution(mesh):
    return jax.shard_map(
        local,
        mesh=mesh,
        in_specs=(
            P(("dp", "seq"), "tensor"),
            P(("dp", "seq"), "tensor"),
            P(),
            P(),
            P(None, None, "tensor"),
            P(None, None, "tensor"),
            P(None, "tensor", None),
            P(("dp", "seq")),
            P("dp"),
            P("dp"),
        ),
        out_specs=(P(("dp", "seq"), "tensor"), P(("dp", "seq"), "tensor")),
        check_vma=False,
    )
```

profile of v0, /device:TPU:0, one launch (start us, length us, event | category | flops | bytes accessed | tf_op | source)
XLA Modules:
  0.0 210.5 jit_solution(5124185873282323641)
XLA Ops:
  7.3 2.8 %all_gather.10 = bf16[128,3584]{1,0:T(8,128)(2,1)S(1)} all-gather(bf16[128,1792]{1,0:T(8,128)(2,1)} %param.10), channel_id=1, replica_groups=mesh['dp'=4,'seq'=4,'tensor'=2] {'tensor'}, dimensions={1}, use_global_device_ids=true | all-gather | bytes 1376256 | tf_op jit(solution)/shard_map/all_gather | solution.py:75
  10.0 0.3 fusion.4
  10.4 2.5 %sort.17 = (s32[128]{0:T(128)}, s32[128]{0:T(128)S(1)}) sort(s32[128]{0:T(128)S(1)} %copy-done.10, s32[128]{0:T(128)S(1)} %iota.26), dimensions={0}, to_apply=%region_1.2 | sort | flops 896 | bytes 2048 | tf_op jit(solution)/shard_map/jit(argsort)/sort | solution.py:35
  12.9 0.6 reduce_sum.82
  14.2 1.3 pad_add_fusion
  15.5 1.3 ragged-dot-metadata
  16.8 1.0 scatter_custom_fusion
  17.8 1.7 broadcast_select_fusion
  19.5 2.1 gather_fusion
  21.6 9.3 %ragged-dot-none.4 = f32[128,1024]{1,0:T(8,128)} custom-call(s32[1]{0:T(128)} %get-tuple-element.16, s32[3]{0:T(128)} %get-tuple-element.17, s32[2]{0:T(128)} %get-tuple-element.18, s32[2]{0:T(128)} %get-tuple-element.19, s32[1]{0:T(128)} %get-tuple-element.16, bf16[128,3584]{1,0:T(8,128)(2,1)} %gather_fusion, bf16[2,3584,1024]{2,1,0:T(8,128)(2,1)} %param.14), custom_call_target="tpu_custom_call" | custom-call | flops 939524096 | bytes 16121864 | tf_op jit(solution)/shard_map/ragged_dot_general/ragged-dot-none
  30.9 2.1 gather_fusion.4
  33.0 0.2 copy.109
  33.2 6.7 %ragged-dot-none.5 = f32[128,512]{1,0:T(8,128)} custom-call(s32[1]{0:T(128)} %get-tuple-element.16, s32[3]{0:T(128)} %get-tuple-element.17, s32[2]{0:T(128)} %get-tuple-element.18, s32[2]{0:T(128)} %get-tuple-element.19, s32[1]{0:T(128)} %get-tuple-element.16, bf16[128,3584]{1,0:T(8,128)(2,1)} %gather_fusion, bf16[2,3584,512]{2,1,0:T(8,128)(2,1)} %param.15), custom_call_target="tpu_custom_call" | custom-call | flops 469762048 | bytes 8519688 | tf_op jit(solution)/shard_map/ragged_dot_general/ragged-dot-none
  40.0 1.8 gather_fusion.1
  41.8 0.1 copy.106
  42.0 0.1 copy.107
  42.3 0.1 select_convert_fusion
  42.4 17.5 %all_gather.11 = bf16[512,4,128]{2,0,1:T(8,128)(2,1)S(1)} all-gather(bf16[128,4,128]{2,0,1:T(8,128)(2,1)S(1)} %select_convert_fusion), channel_id=1, replica_groups=mesh['dp'=4,'seq'=4,'tensor'=2] {'seq'}, dimensions={0}, use_global_device_ids=true | all-gather | bytes 655360 | tf_op jit(solution)/shard_map/all_gather | solution.py:134
  60.0 0.2 reduce_sum.84
  60.3 0.7 fusion.43
  61.0 2.6 %compare_select_fusion = s32[512,1]{0,1:T(1,128)S(1)} fusion(s32[]{:T(128)} %bitcast.6, s32[]{:T(128)} %bitcast.7, s32[]{:T(128)} %bitcast.9, s32[]{:T(128)} %bitcast.8), kind=kLoop, calls=%fused_computation.80 | loop fusion | flops 13312 | bytes 2064 | tf_op jit(solution)/shard_map/select_n | solution.py:114
  63.6 2.6 %fusion.39 = s32[128]{0:T(128)S(1)} fusion(s32[]{:T(128)} %bitcast.6, s32[]{:T(128)} %bitcast.7, s32[]{:T(128)} %bitcast.9, s32[]{:T(128)} %bitcast.8, s32[]{:T(128)S(6)} %mul.245), kind=kLoop, calls=%fused_computation.119 | loop fusion | flops 4352 | bytes 532 | tf_op jit(solution)/shard_map/select_n | solution.py:114
  66.3 1.3 gather_fusion.3
  67.6 3.5 %gather_fusion.2 = s32[512]{0:T(512)S(1)} fusion(s32[512]{0:T(512)S(1)} %copy-done, s32[1024]{0:T(1024)S(1)} %pad_clamp_fusion.1), kind=kCustom, calls=%fused_computation.2 | custom fusion | bytes 6144 | tf_op jit(solution)/shard_map/gather | solution.py:114
  71.2 2.7 %all_gather.12 = bf16[128,3584]{1,0:T(8,128)(2,1)S(1)} all-gather(bf16[128,1792]{1,0:T(8,128)(2,1)} %param.11), channel_id=1, replica_groups=mesh['dp'=4,'seq'=4,'tensor'=2] {'tensor'}, dimensions={1}, use_global_device_ids=true | all-gather | bytes 1376256 | tf_op jit(solution)/shard_map/all_gather | solution.py:76
  73.8 2.0 gather_fusion.7
  75.9 19.4 %copy.117 = bf16[2,1024,3584]{1,2,0:T(8,128)(2,1)} copy(bf16[2,1024,3584]{2,1,0:T(8,128)(2,1)} %param.16) | data formatting | bytes 29360128 | tf_op args[6]
  95.3 9.4 %ragged-dot-none.2 = f32[128,1024]{1,0:T(8,128)} custom-call(s32[1]{0:T(128)} %get-tuple-element.16, s32[3]{0:T(128)} %get-tuple-element.17, s32[2]{0:T(128)} %get-tuple-element.18, s32[2]{0:T(128)} %get-tuple-element.19, s32[1]{0:T(128)} %get-tuple-element.16, bf16[128,3584]{1,0:T(8,128)(2,1)} %gather_fusion.7, bf16[2,3584,1024]{2,1,0:T(8,128)(2,1)} %bitcast.135), custom_call_target="tpu_custom_call" | custom-call | flops 939524096 | bytes 16121864 | tf_op jit(solution)/shard_map/ragged_dot_general/ragged-dot-none
  104.7 2.1 gather_fusion.8
  106.8 0.2 copy.118
  106.9 0.1 broadcast_compare_fusion
  107.1 0.7 convert_reduce_fusion
  107.7 0.5 fusion.12
  108.2 1.1 multiply_reduce_fusion.1
  109.3 1.4 fusion.2
  110.7 0.5 fusion.13
  111.3 1.1 copy.128
  112.4 0.2 reduce-scatter.8.cloned.1.call-start
  112.6 10.0 %copy.131 = bf16[2,3584,512]{1,2,0:T(8,128)(2,1)} copy(bf16[2,3584,512]{2,1,0:T(8,128)(2,1)} %param.15) | data formatting | bytes 14680064 | tf_op args[5]
  122.7 18.8 %copy.125 = bf16[2,3584,1024]{1,2,0:T(8,128)(2,1)} copy(bf16[2,3584,1024]{2,1,0:T(8,128)(2,1)} %param.14) | data formatting | bytes 29360128 | tf_op args[4]
  141.6 1.3 fusion.18
  143.1 0.2 copy.122
  143.3 0.2 mul.270
  143.5 0.2 mul.257
  143.7 0.5 fusion.16
  144.2 1.6 gather_fusion.9
  145.8 9.6 %ragged-dot-none.1 = f32[128,3584]{1,0:T(8,128)} custom-call(s32[1]{0:T(128)} %get-tuple-element.16, s32[3]{0:T(128)} %get-tuple-element.17, s32[2]{0:T(128)} %get-tuple-element.18, s32[2]{0:T(128)} %get-tuple-element.19, s32[1]{0:T(128)} %get-tuple-element.16, bf16[128,1024]{1,0:T(8,128)(2,1)} %gather_fusion.9, bf16[2,1024,3584]{2,1,0:T(8,128)(2,1)} %bitcast.136), custom_call_target="tpu_custom_call" | custom-call | flops 939524096 | bytes 16777224 | tf_op jit(solution)/shard_map/ragged_dot_general/ragged-dot-none
  155.4 3.6 %gather_fusion.10 = f32[128,3584]{1,0:T(8,128)S(1)} fusion(f32[128,3584]{1,0:T(8,128)} %ragged-dot-none.1, s32[1024]{0:T(1024)S(1)} %pad_clamp_fusion.2), kind=kCustom, calls=%fused_computation.10 | custom fusion | bytes 3670528 | tf_op jit(solution)/shard_map/gather | solution.py:47
  159.0 1.1 fusion.21
  160.2 1.1 fusion.23
  161.3 0.1 copy.129
  161.4 0.1 copy.130
  161.5 1.5 gather_fusion.11
  163.0 7.1 %ragged-dot-none = f32[128,3584]{1,0:T(8,128)} custom-call(s32[1]{0:T(128)} %get-tuple-element.16, s32[3]{0:T(128)} %get-tuple-element.17, s32[2]{0:T(128)} %get-tuple-element.18, s32[2]{0:T(128)} %get-tuple-element.19, s32[1]{0:T(128)} %get-tuple-element.16, bf16[128,512]{1,0:T(8,128)(2,1)} %gather_fusion.11, bf16[2,512,3584]{2,1,0:T(8,128)(2,1)} %bitcast.137), custom_call_target="tpu_custom_call" | custom-call | flops 469762048 | bytes 9306120 | tf_op jit(solution)/shard_map/ragged_dot_general/ragged-dot-none
  170.1 4.7 %gather_fusion.12 = f32[128,3584]{1,0:T(8,128)} fusion(f32[128,3584]{1,0:T(8,128)} %ragged-dot-none, s32[1024]{0:T(1024)S(1)} %pad_clamp_fusion.2), kind=kCustom, calls=%fused_computation.12 | custom fusion | bytes 3670528 | tf_op jit(solution)/shard_map/gather | solution.py:47
  174.8 2.8 %add_convert_fusion = bf16[128,3584]{1,0:T(8,128)(2,1)} fusion(f32[128,3584]{1,0:T(8,128)S(1)} %gather_fusion.10, f32[128,3584]{1,0:T(8,128)} %gather_fusion.12), kind=kLoop, calls=%fused_computation.27 | loop fusion | flops 917504 | bytes 4587520 | tf_op jit(solution)/shard_map/convert_element_type | solution.py:204
  177.6 0.1 copy.115
  177.8 1.6 gather_fusion.5
  179.4 9.9 %ragged-dot-none.3 = f32[128,3584]{1,0:T(8,128)} custom-call(s32[1]{0:T(128)} %get-tuple-element.16, s32[3]{0:T(128)} %get-tuple-element.17, s32[2]{0:T(128)} %get-tuple-element.18, s32[2]{0:T(128)} %get-tuple-element.19, s32[1]{0:T(128)} %get-tuple-element.16, bf16[128,1024]{1,0:T(8,128)(2,1)} %gather_fusion.5, bf16[2,1024,3584]{2,1,0:T(8,128)(2,1)} %param.16), custom_call_target="tpu_custom_call" | custom-call | flops 939524096 | bytes 16777224 | tf_op jit(solution)/shard_map/ragged_dot_general/ragged-dot-none
  189.3 4.6 %gather_fusion.6 = bf16[128,3584]{1,0:T(8,128)(2,1)} fusion(f32[128,3584]{1,0:T(8,128)} %ragged-dot-none.3, s32[1024]{0:T(1024)S(1)} %pad_clamp_fusion.2), kind=kCustom, calls=%fused_computation.6 | custom fusion | bytes 1835520 | tf_op jit(solution)/shard_map/gather | solution.py:47
  194.0 1.4 multiply_reduce_fusion
  195.4 2.5 %psum.7 = f32[128]{0:T(128)S(1)} all-reduce(f32[128]{0:T(128)S(1)} %multiply_reduce_fusion), channel_id=1, replica_groups=mesh['dp'=4,'seq'=4,'tensor'=2] {'tensor'}, use_global_device_ids=true, to_apply=%region_14.15 | all-reduce | flops 128 | bytes 1024 | tf_op jit(solution)/shard_map/psum | solution.py:210
  197.8 1.1 multiply_convert_fusion
  198.9 5.0 %reduce-scatter.4.cloned.1.call-done = bf16[128,1792]{1,0:T(8,128)(2,1)} async-done(((bf16[128,3584]{1,0:T(8,128)(2,1)}), bf16[128,1792]{1,0:T(8,128)(2,1)}) %reduce-scatter.4.cloned.1.call-update) | async-done | bytes 458768 | tf_op jit(solution)/shard_map/reduce_scatter | solution.py:144
  (58 shorter events, 1.2 us)
Async XLA Ops:
  7.2 59.1 %copy-start = (s32[512]{0:T(512)S(1)}, s32[512]{0:T(512)}, u32[]{:S(2)}) copy-start(s32[512]{0:T(512)} %param.18) | copy-start | bytes 6148
  7.2 3.1 %copy-start.7 = (f32[2,3584]{1,0:T(2,128)S(1)}, f32[2,3584]{1,0:T(2,128)}, u32[]{:S(2)}) copy-start(f32[2,3584]{1,0:T(2,128)} %param.12) | copy-start | bytes 86020
  7.2 3.2 %copy-start.10 = (s32[128]{0:T(128)S(1)}, s32[128]{0:T(128)}, u32[]{:S(2)}) copy-start(s32[128]{0:T(128)} %param.17) | copy-start | bytes 1540
  7.2 151.8 %reduce-scatter.6.cloned.1.call-start = ((), (), s32[]{:S(2)}) async-start(), calls=%async_computation.4 | async-start | bytes 655360 | tf_op jit(solution)/shard_map/reduce_scatter | solution.py:181
  40.0 2.2 %copy-start.9 = (f32[2,2,128]{2,1,0:T(2,128)S(1)}, f32[2,2,128]{2,1,0:T(2,128)}, u32[]{:S(2)}) copy-start(f32[2,2,128]{2,1,0:T(2,128)} %param.13) | copy-start | bytes 6148
  42.0 18.3 %copy-start.8 = (s32[4]{0:T(128)S(1)}, s32[4]{0:T(128)}, u32[]{:S(2)}) copy-start(s32[4]{0:T(128)} %param.19) | copy-start | bytes 52
  59.9 48.3 %copy-start.5 = (bf16[512,4,128]{2,0,1:T(8,128)(2,1)}, bf16[512,4,128]{2,0,1:T(8,128)(2,1)S(1)}, u32[]{:S(2)}) copy-start(bf16[512,4,128]{2,0,1:T(8,128)(2,1)S(1)} %all_gather.11) | copy-start | bytes 1572868
  112.4 81.5 %reduce-scatter.8.cloned.1.call-start = ((), (), s32[]{:S(2)}) async-start(), calls=%async_computation.5 | async-start | bytes 1376256 | tf_op jit(solution)/shard_map/reduce_scatter | solution.py:203
  174.8 2.9 %copy-start.6 = (bf16[128,2,4,128]{0,3,2,1:T(8,128)(2,1)S(1)}, bf16[128,2,4,128]{0,3,2,1:T(8,128)(2,1)}, u32[]{:S(2)}) copy-start(bf16[128,2,4,128]{0,3,2,1:T(8,128)(2,1)} %get-tuple-element.46) | copy-start | bytes 786436
  177.6 26.4 %reduce-scatter.4.cloned.1.call-start = ((), (), s32[]{:S(2)}) async-start(), calls=%async_computation.3 | async-start | bytes 1376256 | tf_op jit(solution)/shard_map/reduce_scatter | solution.py:144
  189.3 4.7 %copy-start.2 = (f32[128,3584]{1,0:T(8,128)S(1)}, f32[128,3584]{1,0:T(8,128)}, u32[]{:S(2)}) copy-start(f32[128,3584]{1,0:T(8,128)} %get-tuple-element.30) | copy-start | bytes 5505028
  189.3 4.7 %copy-start.3 = (bf16[128,1792]{1,0:T(8,128)(2,1)S(1)}, bf16[128,1792]{1,0:T(8,128)(2,1)}, u32[]{:S(2)}) copy-start(bf16[128,1792]{1,0:T(8,128)(2,1)} %param.10) | copy-start | bytes 1376260
  193.9 3.9 %copy-start.4 = (bf16[128,1792]{1,0:T(8,128)(2,1)S(1)}, bf16[128,1792]{1,0:T(8,128)(2,1)}, u32[]{:S(2)}) copy-start(bf16[128,1792]{1,0:T(8,128)(2,1)} %reduce-scatter.8.cloned.1.call-done) | copy-start | bytes 1376260
  193.9 10.0 %copy-start.1 = (s32[512]{0:T(512)S(1)}, s32[512]{0:T(512)}, u32[]{:S(2)}) copy-start(s32[512]{0:T(512)} %param.18) | copy-start | bytes 6148
Sparse Core Ops, SparseCore 0:
  112.5 23.1 reduce-scatter.5
  177.7 9.9 reduce-scatter.7
  194.0 9.9 reduce-scatter.3
where the time goes:
time: 212 us; the launch traced here: 211 us
  local copies, waits for them, and re-layouts  85.6 us (40%)
  Pallas kernels  53.3 us (25%)
  blocking collectives  25.4 us (12%)
  other arithmetic  20.4 us (10%)
  between operations  14.9 us (7%)
  matrix products  5.43 us (3%)
  waiting for transfers between devices  5.13 us (2%)
    another operation x6, Pallas kernels  52 us
    unnamed x26, local copies, waits for them, and re-layouts  48.4 us
    gather x8, local copies, waits for them, and re-layouts, expert_pick(): return result[inverse]  19.1 us
    all_gather x1, blocking collectives, local(): lax.all_gather(memory, 'seq', axis=0, tiled=True)  17.5 us
    gather x5, local copies, waits for them, and re-layouts, expert_pick(): operand[ordering]  8.73 us
    select_n x2, other arithmetic, segment_of(): return segments[anchor]  5.23 us
    reduce_scatter x1, waiting for transfers between devices, local(): lax.psum_scatter(output_part.astype(jnp.bfloat16), 'tensor', scatter_dime...  5.04 us
    gather x2, local copies, waits for them, and re-layouts, segment_of(): return segments[anchor]  4.78 us
  transfers between devices with their start and end apart: 3, of which 1 were waited for; matrix products, arithmetic and copies ran while one was open for 22% of the time, Pallas kernels for 9%

commit v1 on v0

v1 whole, which is shorter than its diff:
```python
import functools
import math

import jax
import jax.numpy as jnp
from jax import lax
from jax.experimental import pallas as pl
from jax.experimental.pallas import tpu as pltpu
from jax.sharding import PartitionSpec as P

KV_HEADS = 4
HEAD_DIM = 128

epsilon = 1e-06
bf16 = jnp.bfloat16
f32 = jnp.float32


def inverse_norm(values):
    return lax.rsqrt(jnp.mean(values * values, axis=-1, keepdims=True) + epsilon)


def norm_back(values, factor, scaling, upstream):
    unit_rows = values * factor
    inner_mean = jnp.mean(scaling * upstream * unit_rows, axis=-1, keepdims=True)
    return factor * (scaling * upstream - unit_rows * inner_mean)


def seq_pairs(step, count):
    if count & (count - 1) == 0:
        return [(i, i ^ step) for i in range(count)]
    return [(i, (i + step) % count) for i in range(count)]


def seq_source(rank, step, count):
    if count & (count - 1) == 0:
        return rank ^ step
    return (rank - step) % count


def inverted(pairs):
    return [(b, a) for a, b in pairs]


def expert_pick(is_image, weights, operand):
    zero = jnp.zeros_like(operand)
    masked = jnp.concatenate(
        [jnp.where(is_image, zero, operand), jnp.where(is_image, operand, zero)], axis=1
    )
    flat = weights.reshape(-1, weights.shape[2])
    return jnp.dot(masked, flat, preferred_element_type=f32)


def expert_back(is_image, weights, operand):
    text_part = lax.dot_general(
        operand, weights[0], (((1,), (1,)), ((), ())), preferred_element_type=f32
    )
    image_part = lax.dot_general(
        operand, weights[1], (((1,), (1,)), ((), ())), preferred_element_type=f32
    )
    return jnp.where(is_image, image_part, text_part)


def dot_nt(a, b):
    return lax.dot_general(a, b, (((1,), (1,)), ((), ())), preferred_element_type=f32)


def dot_tn(a, b):
    return lax.dot_general(a, b, (((0,), (0,)), ((), ())), preferred_element_type=f32)


def attention_kernel(blocks, per_group, *refs):
    source_ref, segments_ref, query_ref, back_ref = refs[:4]
    memory_refs = refs[4 : 4 + blocks]
    attended_ref, back_query_ref = refs[4 + blocks : 6 + blocks]
    grad_refs = refs[6 + blocks :]
    rows = query_ref.shape[0]
    scale = 1.0 / math.sqrt(HEAD_DIM)

    def heads(ref):
        return jnp.concatenate(
            [ref[:, h * HEAD_DIM : (h + 1) * HEAD_DIM] for h in range(per_group)], axis=0
        )

    query, back = heads(query_ref), heads(back_ref)
    key = jnp.concatenate([m[:, :HEAD_DIM] for m in memory_refs], axis=0)
    value = jnp.concatenate([m[:, HEAD_DIM:] for m in memory_refs], axis=0)
    key_segments = jnp.concatenate(
        [segments_ref[pl.ds(source_ref[b], 1), :] for b in range(blocks)], axis=1
    )
    own = segments_ref[pl.ds(source_ref[0], 1), :]
    query_segments = jnp.broadcast_to(own.astype(f32), (rows, rows)).T[:, :1]
    visible = key_segments.astype(f32) <= query_segments
    visible = jnp.where(visible, 1.0, 0.0)
    visible = jnp.concatenate([visible] * per_group, axis=0)
    scores = dot_nt(query, key) * scale
    weights = jnp.where(visible > 0.0, jnp.exp(scores), 0.0).astype(bf16)
    weights32 = weights.astype(f32)
    denominator = jnp.sum(weights32, axis=1, keepdims=True)
    numerator = jnp.dot(weights, value, preferred_element_type=f32)
    attended = (numerator / denominator).astype(bf16)
    offset = jnp.sum(back.astype(f32) * attended.astype(f32), axis=1, keepdims=True)
    probability = (weights32 / denominator).astype(bf16)
    back_prob = dot_nt(back, value)
    back_score = (probability.astype(f32) * (back_prob - offset)).astype(bf16)
    back_query = jnp.dot(back_score, key, preferred_element_type=f32) * scale
    back_key = dot_tn(back_score, query) * scale
    back_value = dot_tn(probability, back)
    for h in range(per_group):
        part = slice(h * rows, (h + 1) * rows)
        columns = slice(h * HEAD_DIM, (h + 1) * HEAD_DIM)
        attended_ref[:, columns] = attended[part]
        back_query_ref[:, columns] = back_query[part]
    for b in range(blocks):
        part = slice(b * rows, (b + 1) * rows)
        grad_refs[b][:, :HEAD_DIM] = back_key[part].astype(grad_refs[b].dtype)
        grad_refs[b][:, HEAD_DIM:] = back_value[part].astype(grad_refs[b].dtype)


def attention(sources, segments, query, back, memories):
    rows, width = query.shape
    blocks = len(memories)
    pairs = memories[0].shape[1] // (2 * HEAD_DIM)
    per_group = width // HEAD_DIM // pairs
    wide = pl.BlockSpec((rows, per_group * HEAD_DIM), lambda g: (0, g))
    narrow = pl.BlockSpec((rows, 2 * HEAD_DIM), lambda g: (0, g))
    outs = [
        jax.ShapeDtypeStruct((rows, width), bf16),
        jax.ShapeDtypeStruct((rows, width), f32),
    ] + [
        jax.ShapeDtypeStruct((rows, pairs * 2 * HEAD_DIM), f32 if b == 0 else bf16)
        for b in range(blocks)
    ]
    return pl.pallas_call(
        functools.partial(attention_kernel, blocks, per_group),
        grid=(pairs,),
        out_shape=outs,
        in_specs=[
            pl.BlockSpec(memory_space=pltpu.SMEM),
            pl.BlockSpec(segments.shape, lambda g: (0, 0)),
            wide,
            wide,
        ]
        + [narrow] * blocks,
        out_specs=[wide, wide] + [narrow] * blocks,
        compiler_params=pltpu.CompilerParams(vmem_limit_bytes=40 * 1024 * 1024),
        cost_estimate=pl.CostEstimate(
            flops=12 * rows * rows * blocks * width,
            bytes_accessed=rows * width * 10,
            transcendentals=rows * rows * blocks * width // HEAD_DIM,
        ),
        name="attention",
    )(sources, segments, query, back, *memories)


def local(
    inputs,
    cotangent,
    norm_gain,
    head_gain,
    query_weight,
    key_weight,
    output_weight,
    modality,
    segments,
    block_order,
):
    tensor_rank = lax.axis_index("tensor")
    block_rank = lax.axis_index("seq")
    tensor_count = lax.axis_size("tensor")
    block_count = lax.axis_size("seq")
    local_rows = inputs.shape[0]
    local_width = inputs.shape[1]
    full_width = local_width * tensor_count
    swap = [(0, 1), (1, 0)]

    def spread(part):
        if tensor_count != 2:
            return lax.all_gather(part, "tensor", axis=1, tiled=True)
        other = lax.ppermute(part, "tensor", swap)
        first = tensor_rank == 0
        return jnp.concatenate(
            [jnp.where(first, part, other), jnp.where(first, other, part)], axis=1
        )

    def reduce_columns(part):
        if tensor_count != 2:
            return lax.psum_scatter(
                part.astype(bf16), "tensor", scatter_dimension=1, tiled=True
            ).astype(f32)
        first = tensor_rank == 0
        low, high = part[:, :local_width], part[:, local_width:]
        other = lax.ppermute(jnp.where(first, high, low).astype(bf16), "tensor", swap)
        return jnp.where(first, low, high) + other.astype(f32)

    whole_rows = lax.all_gather(inputs, "tensor", axis=1, tiled=True)
    is_image = (modality == 1)[:, None]
    head_image = is_image[:, :, None]
    row_scaling = jnp.where(is_image, norm_gain[1][None, :], norm_gain[0][None, :])
    rows_float = whole_rows.astype(f32)
    row_factor = inverse_norm(rows_float)
    normed = (rows_float * row_factor * row_scaling).astype(bf16)

    slice_blocks = key_weight.shape[2] // HEAD_DIM
    key_raw = expert_pick(is_image, key_weight, normed).reshape(local_rows, slice_blocks, HEAD_DIM)
    block_index = tensor_rank * slice_blocks + jnp.arange(slice_blocks, dtype=jnp.int32)
    is_key = (block_index % 2 == 0)[None, :, None]
    key_scaling = jnp.where(head_image, head_gain[1, 1], head_gain[0, 1])
    key_factor = inverse_norm(key_raw)
    slice_out = jnp.where(is_key, key_raw * key_factor * key_scaling, key_raw).astype(bf16)
    slice_out = slice_out.reshape(local_rows, slice_blocks * HEAD_DIM)
    shared = tensor_count > KV_HEADS
    is_even = tensor_rank % 2 == 0
    if shared:
        pair_swap = [(i, i ^ 1) for i in range(tensor_count)]
        partner = lax.ppermute(slice_out, "tensor", pair_swap)
        memory = jnp.where(
            is_even,
            jnp.concatenate([slice_out, partner], 1),
            jnp.concatenate([partner, slice_out], 1),
        )
    else:
        memory = slice_out
    memories, order = [memory], [block_rank]
    for step in range(1, block_count):
        memories.append(lax.ppermute(memory, "seq", seq_pairs(step, block_count)))
        order.append(seq_source(block_rank, step, block_count))
    sources = block_order[jnp.stack(order)]

    query_heads = query_weight.shape[2] // HEAD_DIM
    query_raw = expert_pick(is_image, query_weight, normed).reshape(
        local_rows, query_heads, HEAD_DIM
    )
    query_scaling = jnp.where(head_image, head_gain[1, 0], head_gain[0, 0])
    query_factor = inverse_norm(query_raw)
    query_normed = (query_raw * query_factor * query_scaling).astype(bf16)
    query_normed = query_normed.reshape(local_rows, query_heads * HEAD_DIM)

    back_attended = expert_back(is_image, output_weight, spread(cotangent)).astype(bf16)

    attended, back_query, own_grad, *grads = attention(
        sources,
        segments.reshape(block_count, local_rows),
        query_normed,
        back_attended,
        memories,
    )
    incoming = [
        lax.ppermute(grad, "seq", inverted(seq_pairs(step, block_count)))
        for step, grad in enumerate(grads, 1)
    ]

    output_part = expert_pick(is_image, output_weight, attended)
    attention_out = reduce_columns(output_part).astype(bf16)

    query_back = norm_back(
        query_raw,
        query_factor,
        query_scaling,
        back_query.reshape(local_rows, query_heads, HEAD_DIM),
    ).astype(bf16)
    inner_query = jnp.sum(query_back.astype(f32) * query_raw, axis=(1, 2))
    gradient_part = expert_back(
        is_image, query_weight, query_back.reshape(local_rows, query_heads * HEAD_DIM)
    )

    memory_sum = own_grad + sum(grad.astype(f32) for grad in incoming)
    if shared:
        low, high = memory_sum[:, :HEAD_DIM], memory_sum[:, HEAD_DIM:]
        outgoing = jnp.where(is_even, high, low).astype(bf16)
        slice_grad = jnp.where(is_even, low, high) + lax.ppermute(
            outgoing, "tensor", pair_swap
        ).astype(f32)
    else:
        slice_grad = memory_sum
    slice_grad = slice_grad.reshape(local_rows, slice_blocks, HEAD_DIM)
    slice_back = jnp.where(
        is_key, norm_back(key_raw, key_factor, key_scaling, slice_grad), slice_grad
    ).astype(bf16)
    inner = inner_query + jnp.sum(slice_back.astype(f32) * key_raw, axis=(1, 2))
    if tensor_count == 2:
        inner_total = inner + lax.ppermute(inner, "tensor", swap)
    else:
        inner_total = lax.psum(inner, "tensor")
    gradient_part = gradient_part + expert_back(
        is_image, key_weight, slice_back.reshape(local_rows, slice_blocks * HEAD_DIM)
    )
    back_normed = reduce_columns(gradient_part)
    local_scaling = lax.dynamic_slice_in_dim(
        row_scaling, tensor_rank * local_width, local_width, 1
    )
    unit_rows = inputs.astype(f32) * row_factor
    grad_input = (
        row_factor * (local_scaling * back_normed - unit_rows * (inner_total / full_width)[:, None])
    ).astype(bf16)
    return (attention_out, grad_input)


def solution(mesh):
    return jax.shard_map(
        local,
        mesh=mesh,
        in_specs=(
            P(("dp", "seq"), "tensor"),
            P(("dp", "seq"), "tensor"),
            P(),
            P(),
            P(None, None, "tensor"),
            P(None, None, "tensor"),
            P(None, "tensor", None),
            P(("dp", "seq")),
            P("dp"),
            P("dp"),
        ),
        out_specs=(P(("dp", "seq"), "tensor"), P(("dp", "seq"), "tensor")),
        check_vma=False,
    )
```

time: 212 us -> 111 us (0.52)
  local copies, waits for them, and re-layouts: 85.6 us -> 32.9 us
  Pallas kernels: 53.3 us -> 3.51 us
  matrix products: 5.43 us -> 45 us
  blocking collectives: 25.4 us -> 2.75 us
  between operations: 14.9 us -> 1.11 us
  other arithmetic: 20.4 us -> 9.13 us
  starting transfers between devices: 0.3 us -> 11.3 us
    another operation x6 -> x0, Pallas kernels: 52 us -> none
    unnamed x26 -> x28, local copies, waits for them, and re-layouts: 48.4 us -> 1.35 us
    dot_general x6 -> x9, matrix products: 5.43 us -> 45 us  [the longest x3 15.2 us: expert_pick(): return jnp.dot(masked, flat, preferred_element_type=f32)]
    gather x16 -> x1, local copies, waits for them, and re-layouts: 33.3 us -> 0.64 us  [local(): sources = block_order[jnp.stack(order)]]
    dot_general x0 -> x2, local copies, waits for them, and re-layouts: none -> 29.4 us  [expert_pick(): return jnp.dot(masked, flat, preferred_element_type=f32)]
    all_gather x3 -> x1, blocking collectives: 23 us -> 2.75 us  [local(): whole_rows = lax.all_gather(inputs, 'tensor', axis=1, tiled=True)]
    ppermute x0 -> x10, starting transfers between devices: none -> 11.3 us  [the longest x3 5.6 us: local(): memories.append(lax.ppermute(memory, 'seq', seq_pairs(step, block_count)))]
    reduce_scatter x3 -> x0, waiting for transfers between devices: 5.08 us -> none  [the longest x1 5.04 us: local(): lax.psum_scatter(output_part.astype(jnp.bfloat16), 'tensor', scatter_dime...]
  transfers between devices with their start and end apart: 3 -> 10, of which waited for: 1 -> 1; matrix products, arithmetic and copies ran while one was open for 22% -> 58% of each run, Pallas kernels for 9% -> 0%
where the time goes in v1:
time: 111 us; the launch traced here: 110 us
  matrix products  45 us (41%)
  local copies, waits for them, and re-layouts  32.9 us (30%)
  starting transfers between devices  11.3 us (10%)
  other arithmetic  9.13 us (8%)
  waiting for transfers between devices  3.95 us (4%)
  Pallas kernels  3.51 us (3%)
  blocking collectives  2.75 us (2%)
  between operations  1.11 us (1%)
    dot_general x2, local copies, waits for them, and re-layouts, expert_pick(): return jnp.dot(masked, flat, preferred_element_type=f32)  29.4 us
    dot_general x3, matrix products, expert_pick(): return jnp.dot(masked, flat, preferred_element_type=f32)  15.2 us
    dot_general x3, matrix products, expert_back(): lax.dot_general(operand, weights[0], (((1,), (1,)), ((), ())), preferred_...  15 us
    dot_general x3, matrix products, expert_back(): lax.dot_general(operand, weights[1], (((1,), (1,)), ((), ())), preferred_...  14.8 us
    ppermute x3, starting transfers between devices, local(): memories.append(lax.ppermute(memory, 'seq', seq_pairs(step, block_count)))  5.6 us
    ppermute x3, starting transfers between devices, local(): lax.ppermute(grad, 'seq', inverted(seq_pairs(step, block_count)))  4.53 us
    ppermute x3, waiting for transfers between devices, local(): lax.ppermute(grad, 'seq', inverted(seq_pairs(step, block_count)))  3.93 us
    pallas_call x1, Pallas kernels, attention(): pl.pallas_call(functools.partial(attention_kernel, blocks, per_group), gr...  3.51 us
  transfers between devices with their start and end apart: 10, of which 1 were waited for; matrix products, arithmetic and copies ran while one was open for 58% of the time, Pallas kernels for 0%

profile of v1, /device:TPU:0, one launch (start us, length us, event | category | flops | bytes accessed | tf_op | source)
XLA Modules:
  0.0 109.6 jit_solution(4798319421925040870)
XLA Ops:
  0.6 0.0 copy-start
  0.7 0.7 broadcast_compare_fusion
  1.3 0.9 slice_reduce_fusion.1
  2.2 2.8 %all_gather.3 = bf16[128,3584]{1,0:T(8,128)(2,1)S(1)} all-gather(bf16[128,1792]{1,0:T(8,128)(2,1)} %param.10), channel_id=1, replica_groups=mesh['dp'=4,'seq'=4,'tensor'=2] {'tensor'}, dimensions={1}, use_global_device_ids=true | all-gather | bytes 1376256 | tf_op jit(solution)/shard_map/all_gather | solution.py:196
  5.0 0.3 fusion.21
  5.3 10.0 %copy.21 = bf16[512,7168]{1,0:T(8,128)(2,1)} copy(bf16[512,7168]{0,1:T(8,128)(2,1)} %bitcast.77) | data formatting | bytes 14680064 | tf_op jit(solution)/shard_map/dot_general | solution.py:51
  15.3 0.5 broadcast_select_fusion.2
  15.8 5.5 %multiply_reduce_fusion.5 = (f32[128,4]{0,1:T(4,128)S(1)}, f32[128,4,128]{0,2,1:T(8,128)S(1)}) fusion(bf16[4,128,7168]{2,1,0:T(8,128)(2,1)} %bitcast.82, bf16[128,3584]{1,0:T(8,128)(2,1)S(1)} %get-tuple-element.21, bf16[128,3584]{1,0:T(8,128)(2,1)S(1)} %get-tuple-element.20), kind=kOutput, calls=%fused_computation.55 | convolution fusion | flops 943324672 | bytes 9439232 | tf_op jit(solution)/shard_map/dot_general | solution.py:51
  21.4 0.1 broadcast_select_fusion.7
  21.5 0.1 select_convert_fusion.3
  21.6 0.1 copy.27.refs_4_
  21.8 3.0 %collective-permute-start.1 = (bf16[128,512]{1,0:T(8,128)(2,1)S(1)}, bf16[128,512]{1,0:T(8,128)(2,1)S(1)}, u32[]{:S(2)}, u32[]{:S(2)}) collective-permute-start(bf16[128,512]{1,0:T(8,128)(2,1)S(1)} %copy.27.refs_4_), channel_id=1, source_target_pairs={{0,2},{2,0},{4,6},{6,4},{1,3},{3,1},{5,7},{7,5},{8,10},{10,8},{12,... | collective-permute-start | bytes 393224 | tf_op jit(solution)/shard_map/ppermute | solution.py:226
  24.8 2.6 %collective-permute-start.2 = (bf16[128,512]{1,0:T(8,128)(2,1)S(1)}, bf16[128,512]{1,0:T(8,128)(2,1)S(1)}, u32[]{:S(2)}, u32[]{:S(2)}) collective-permute-start(bf16[128,512]{1,0:T(8,128)(2,1)S(1)} %copy.27.refs_4_), channel_id=1, source_target_pairs={{0,4},{2,6},{4,0},{6,2},{1,5},{3,7},{5,1},{7,3},{8,12},{10,14},{12... | collective-permute-start | bytes 393224 | tf_op jit(solution)/shard_map/ppermute | solution.py:226
  27.4 1.5 %broadcast_select_fusion = f32[128,3584]{1,0:T(8,128)} fusion(f32[3584]{0:T(1024)S(1)} %get-tuple-element.15, f32[3584]{0:T(1024)S(1)} %get-tuple-element.14, pred[128]{0:T(512)(128)(4,1)S(1)} %broadcast_compare_fusion), kind=kLoop, calls=%fused_computation.36 | loop fusion | flops 458752 | bytes 1863808 | tf_op jit(solution)/shard_map/jit(_where)/select_n | solution.py:199
  28.9 19.3 %copy.19 = bf16[1024,7168]{1,0:T(8,128)(2,1)} copy(bf16[1024,7168]{0,1:T(8,128)(2,1)} %bitcast.76) | data formatting | bytes 29360128 | tf_op jit(solution)/shard_map/dot_general | solution.py:51
  48.2 7.5 %multiply_reduce_fusion.2 = (f32[128,8]{0,1:T(8,128)S(1)}, f32[128,8,128]{0,2,1:T(8,128)S(1)}) fusion(bf16[8,128,7168]{2,1,0:T(8,128)(2,1)} %bitcast.81, bf16[128,3584]{1,0:T(8,128)(2,1)} %copy-done.7, bf16[128,3584]{1,0:T(8,128)(2,1)S(1)} %get-tuple-element.20), kind=kOutput, calls=%fused_computation.47 | convolution fusion | flops 1882979328 | bytes 17043456 | tf_op jit(solution)/shard_map/dot_general | solution.py:51
  55.8 0.0 copy-start.8
  55.8 0.1 multiply_convert_fusion.2
  55.9 0.1 copy.26.refs_2_
  56.0 0.1 fusion.38
  56.1 0.6 gather_fusion
  56.8 0.0 collective-permute-done
  56.8 0.0 copy-done.8
  56.8 1.1 broadcast_select_fusion.4
  57.9 0.0 slice-start
  57.9 0.0 slice-start.1
  57.9 5.7 %fusion.4 = bf16[128,1024]{1,0:T(8,128)(2,1)S(1)} fusion(bf16[2,1024,3584]{2,1,0:T(8,128)(2,1)} %param.16, bf16[128,1792]{1,0:T(8,128)(2,1)S(1)} %get-tuple-element.23, bf16[128,1792]{1,0:T(8,128)(2,1)S(1)} %get-tuple-element.22), kind=kOutput, calls=%fused_computation.5 | convolution fusion | flops 941359104 | bytes 8519680 | tf_op jit(solution)/shard_map/dot_general | solution.py:55
  63.6 0.0 copy-start.2
  63.6 0.0 slice-start.2
  63.6 0.0 slice-start.3
  63.6 5.7 %fusion.29.refs_3_ = bf16[128,1024]{1,0:T(8,128)(2,1)S(1)} fusion(bf16[128,1024]{1,0:T(8,128)(2,1)S(1)} %fusion.4, bf16[2,1024,3584]{2,1,0:T(8,128)(2,1)} %param.16, bf16[128,1792]{1,0:T(8,128)(2,1)S(1)} %get-tuple-element.23, bf16[128,1792]{1,0:T(8,128)(2,1)S(1)} %get-tuple-element.22, pred[128]{0:T(512)(128)(4,1)S(1)} %broadcast_compare_fusion), kind=kOutput, calls=%fused_computation.30 | convolution fusion | flops 941490176 | bytes 8781952 | tf_op jit(solution)/shard_map/dot_general | solution.py:58
  69.3 0.0 collective-permute-done.2.refs_6_
  69.4 0.0 collective-permute-done.3.refs_7_
  69.4 3.5 %attention.1 = (bf16[128,1024]{1,0:T(8,128)(2,1)S(1)}, f32[128,1024]{1,0:T(8,128)S(1)}, f32[128,512]{1,0:T(8,128)S(1)}, bf16[128,512]{1,0:T(8,128)(2,1)S(1)}, bf...) custom-call(s32[4]{0:T(128)S(1)} %gather_fusion, s32[4,128]{1,0:T(4,128)S(1)} %bitcast.75, ...), custom_call_target="tpu_custom_call" | custom-call | flops 805306368 | bytes 1310720 | tf_op jit(solution)/shard_map/attention/pallas_call | solution.py:134
  72.9 0.1 broadcast_select_fusion.6
  73.0 2.2 %fusion.32 = f32[128,3584]{1,0:T(8,128)S(1)} fusion(bf16[2048,3584]{1,0:T(8,128)(2,1)S(1)} %bitcast.80, bf16[128,1024]{1,0:T(8,128)(2,1)S(1)} %get-tuple-element.25, bf16[128,1024]{1,0:T(8,128)(2,1)S(1)} %get-tuple-element.24), kind=kOutput, calls=%fused_computation.39 | convolution fusion | flops 1880096768 | bytes 17039360 | tf_op jit(solution)/shard_map/dot_general | solution.py:51
  75.2 1.2 %copy-done.3 = f32[128,3584]{1,0:T(8,128)} copy-done((f32[128,3584]{1,0:T(8,128)}, f32[128,3584]{1,0:T(8,128)S(1)}, u32[]{:S(2)}) %copy-start.3) | copy-done | bytes 1835032
  76.5 0.8 select_convert_fusion.1
  77.3 0.5 collective-permute-start.4
  77.8 0.2 copy.28
  78.0 0.1 multiply_reduce_fusion.1
  78.1 0.2 multiply_reduce_fusion
  78.3 5.7 %fusion = f32[128,3584]{1,0:T(8,128)S(1)} fusion(bf16[128,1024]{0,1:T(8,128)(2,1)S(1)} %bitcast.85, bf16[2,3584,1024]{2,1,0:T(8,128)(2,1)} %param.14), kind=kOutput, calls=%fused_computation.1 | convolution fusion | flops 939524096 | bytes 9437184 | tf_op jit(solution)/shard_map/dot_general | solution.py:55
  84.0 3.9 %collective-permute-start.7 = (bf16[128,512]{1,0:T(8,128)(2,1)S(1)}, bf16[128,512]{1,0:T(8,128)(2,1)S(1)}, u32[]{:S(2)}, u32[]{:S(2)}) collective-permute-start(bf16[128,512]{1,0:T(8,128)(2,1)S(1)} %get-tuple-element.13), channel_id=1, source_target_pairs={{6,0},{4,2},{2,4},{0,6},{7,1},{5,3},{3,5},{1,7},{14,8},{12,10},{10... | collective-permute-start | bytes 393224 | tf_op jit(solution)/shard_map/ppermute | solution.py:249
  87.9 0.0 collective-permute-start.6
  87.9 0.6 collective-permute-start.5
  88.5 5.7 %fusion.13 = f32[128,3584]{1,0:T(8,128)S(1)} fusion(f32[128,3584]{1,0:T(8,128)S(1)} %fusion, bf16[128,1024]{0,1:T(8,128)(2,1)S(1)} %bitcast.86, bf16[2,3584,1024]{2,1,0:T(8,128)(2,1)} %param.14, pred[128]{0:T(512)(128)(4,1)S(1)} %broadcast_compare_fusion), kind=kOutput, calls=%fused_computation.15 | convolution fusion | flops 939982848 | bytes 11272320 | tf_op jit(solution)/shard_map/dot_general | solution.py:58
  94.3 0.0 collective-permute-done.7
  94.3 3.9 %collective-permute-done.6 = bf16[128,512]{1,0:T(8,128)(2,1)S(1)} collective-permute-done((bf16[128,512]{1,0:T(8,128)(2,1)S(1)}, bf16[128,512]{1,0:T(8,128)(2,1)S(1)}, u32[]{:S(2)}, u32[]{:S(2)}) %collective-permute-start.6) | collective-permute-done | bytes 131104 | tf_op jit(solution)/shard_map/ppermute | solution.py:249
  98.2 0.0 collective-permute-done.5
  98.2 0.1 add_add_fusion
  98.3 0.1 copy.29
  98.4 0.1 multiply_reduce_fusion.4
  98.5 0.2 multiply_reduce_fusion.3
  98.6 3.4 %fusion.17 = f32[128,3584]{1,0:T(8,128)S(1)} fusion(bf16[128,512]{0,1:T(8,128)(2,1)S(1)} %bitcast.83, bf16[2,3584,512]{2,1,0:T(8,128)(2,1)} %param.15), kind=kOutput, calls=%fused_computation.17 | convolution fusion | flops 469762048 | bytes 5636096 | tf_op jit(solution)/shard_map/dot_general | solution.py:58
  102.0 0.1 collective-permute-start.9
  102.1 3.7 %fusion.12 = f32[128,3584]{1,0:T(8,128)S(1)} fusion(f32[128,3584]{1,0:T(8,128)S(1)} %fusion.13, f32[128,3584]{1,0:T(8,128)S(1)} %fusion.17, bf16[128,512]{0,1:T(8,128)(2,1)S(1)} %bitcast.84, bf16[2,3584,512]{2,1,0:T(8,128)(2,1)} %param.15, pred[128]{0:T(512)(128)(4,1)S(1)} %broadcast_compare_fusion), kind=kOutput, calls=%fused_computation.14 | convolution fusion | flops 470679552 | bytes 9306240 | tf_op jit(solution)/shard_map/dot_general | solution.py:55
  105.8 0.0 copy-start.6
  105.8 0.1 select_convert_fusion
  105.9 0.6 collective-permute-start.8
  106.4 0.0 collective-permute-done.9
  106.5 0.0 copy-start.1
  106.5 1.9 %add_convert_fusion = bf16[128,1792]{1,0:T(8,128)(2,1)} fusion(bf16[128,1792]{1,0:T(8,128)(2,1)} %collective-permute-done.4, f32[128,3584]{1,0:T(8,128)S(1)} %copy-done.4, pred[]{:T(512)S(6)} %eq.20), kind=kLoop, calls=%fused_computation.34 | loop fusion | flops 917504 | bytes 2752513 | tf_op jit(solution)/shard_map/convert_element_type | solution.py:254
  108.4 1.2 %multiply_convert_fusion = bf16[128,1792]{1,0:T(8,128)(2,1)} fusion(bf16[128,1792]{1,0:T(8,128)(2,1)S(1)} %copy-done.6, bf16[128,1792]{1,0:T(8,128)(2,1)S(1)} %collective-permute-done.8, f32[128,3584]{1,0:T(8,128)S(1)} %copy-done.5, s32[]{:T(128)S(6)} %select_n.125, f32[128,3584]{1,0:T(8,128)S(1)} %fusion.12, f32[128]{0:T(128)S(1)} %add_multiply_fusion, ...), kind=kLoop, calls=%fused_computation.32 | loop fusion | flops 2293760 | bytes 4129797 | tf_op jit(solution)/shard_map/convert_element_type | solution.py:295
  (33 shorter events, 0.1 us)
Async XLA Ops:
  0.6 55.5 %copy-start = (s32[4]{0:T(128)S(1)}, s32[4]{0:T(128)}, u32[]{:S(2)}) copy-start(s32[4]{0:T(128)} %param.19) | copy-start | bytes 52
  0.6 4.6 %copy-start.9 = (f32[2,2,128]{2,1,0:T(2,128)S(1)}, f32[2,2,128]{2,1,0:T(2,128)}, u32[]{:S(2)}) copy-start(f32[2,2,128]{2,1,0:T(2,128)} %param.13) | copy-start | bytes 6148
  15.8 5.5 %copy-start.7 = (bf16[128,3584]{1,0:T(8,128)(2,1)}, bf16[128,3584]{1,0:T(8,128)(2,1)S(1)}, u32[]{:S(2)}) copy-start(bf16[128,3584]{1,0:T(8,128)(2,1)S(1)} %get-tuple-element.21) | copy-start | bytes 2752516
  21.8 47.6 %collective-permute-start.1 = (bf16[128,512]{1,0:T(8,128)(2,1)S(1)}, bf16[128,512]{1,0:T(8,128)(2,1)S(1)}, u32[]{:S(2)}, u32[]{:S(2)}) collective-permute-start(bf16[128,512]{1,0:T(8,128)(2,1)S(1)} %copy.27.refs_4_), channel_id=1, source_target_pairs={{0,2},{2,0},{4,6},{6,4},{1,3},{3,1},{5,7},{7,5},{8,10},{10,8},{12,... | collective-permute-start | bytes 393224 | tf_op jit(solution)/shard_map/ppermute | solution.py:226
  24.8 44.6 %collective-permute-start.2 = (bf16[128,512]{1,0:T(8,128)(2,1)S(1)}, bf16[128,512]{1,0:T(8,128)(2,1)S(1)}, u32[]{:S(2)}, u32[]{:S(2)}) collective-permute-start(bf16[128,512]{1,0:T(8,128)(2,1)S(1)} %copy.27.refs_4_), channel_id=1, source_target_pairs={{0,4},{2,6},{4,0},{6,2},{1,5},{3,7},{5,1},{7,3},{8,12},{10,14},{12... | collective-permute-start | bytes 393224 | tf_op jit(solution)/shard_map/ppermute | solution.py:226
  27.4 42.0 %collective-permute-start.3 = (bf16[128,512]{1,0:T(8,128)(2,1)S(1)}, bf16[128,512]{1,0:T(8,128)(2,1)S(1)}, u32[]{:S(2)}, u32[]{:S(2)}) collective-permute-start(bf16[128,512]{1,0:T(8,128)(2,1)S(1)} %copy.27.refs_4_), channel_id=1, source_target_pairs={{0,6},{2,4},{4,2},{6,0},{1,7},{3,5},{5,3},{7,1},{8,14},{10,12},{12... | collective-permute-start | bytes 393224 | tf_op jit(solution)/shard_map/ppermute | solution.py:226
  27.4 29.4 %collective-permute-start = (bf16[128,1792]{1,0:T(8,128)(2,1)}, bf16[128,1792]{1,0:T(8,128)(2,1)}, u32[]{:S(2)}, u32[]{:S(2)}) collective-permute-start(bf16[128,1792]{1,0:T(8,128)(2,1)} %param.11), channel_id=1, source_target_pairs={{0,1},{1,0},{2,3},{3,2},{4,5},{5,4},{6,7},{7,6},{8,9},{9,8},{10,11... | collective-permute-start | bytes 1376264 | tf_op jit(solution)/shard_map/ppermute | solution.py:180
  55.8 1.0 copy-start.8
  57.9 15.1 %slice-start = ((s8[14680064]{0:T(1024)(128)(4,1)}), s8[4194304]{0:T(1024)(128)(4,1)S(1)}, s32[]{:S(2)}) async-start(s8[14680064]{0:T(1024)(128)(4,1)} %bitcast.78), calls=%async_computation | async-start | bytes 8388608
  57.9 15.1 %slice-start.1 = ((s8[14680064]{0:T(1024)(128)(4,1)}), s8[4194304]{0:T(1024)(128)(4,1)S(1)}, s32[]{:S(2)}) async-start(s8[14680064]{0:T(1024)(128)(4,1)} %bitcast.78), calls=%async_computation.1 | async-start | bytes 8388608
  63.6 5.8 %copy-start.2 = (s32[512]{0:T(512)S(1)}, s32[512]{0:T(512)}, u32[]{:S(2)}) copy-start(s32[512]{0:T(512)} %param.18) | copy-start | bytes 6148
  63.6 9.4 %slice-start.2 = ((s8[14680064]{0:T(1024)(128)(4,1)}), s8[4194304]{0:T(1024)(128)(4,1)S(1)}, s32[]{:S(2)}) async-start(s8[14680064]{0:T(1024)(128)(4,1)} %bitcast.78), calls=%async_computation.2 | async-start | bytes 8388608
  63.6 9.4 %slice-start.3 = ((s8[14680064]{0:T(1024)(128)(4,1)}), s8[2097152]{0:T(1024)(128)(4,1)S(1)}, s32[]{:S(2)}) async-start(s8[14680064]{0:T(1024)(128)(4,1)} %bitcast.78), calls=%async_computation.3 | async-start | bytes 4194304
  75.2 1.3 %copy-start.3 = (f32[128,3584]{1,0:T(8,128)}, f32[128,3584]{1,0:T(8,128)S(1)}, u32[]{:S(2)}) copy-start(f32[128,3584]{1,0:T(8,128)S(1)} %fusion.32) | copy-start | bytes 5505028
  77.3 29.1 %collective-permute-start.4 = (bf16[128,1792]{1,0:T(8,128)(2,1)}, bf16[128,1792]{1,0:T(8,128)(2,1)}, u32[]{:S(2)}, u32[]{:S(2)}) collective-permute-start(bf16[128,1792]{1,0:T(8,128)(2,1)} %select_convert_fusion.1), channel_id=1, source_target_pairs={{0,1},{1,0},{2,3},{3,2},{4,5},{5,4},{6,7},{7,6},{8,9},{9,8},{10,11... | collective-permute-start | bytes 1376264 | tf_op jit(solution)/shard_map/ppermute | solution.py:193
  84.0 10.3 %collective-permute-start.7 = (bf16[128,512]{1,0:T(8,128)(2,1)S(1)}, bf16[128,512]{1,0:T(8,128)(2,1)S(1)}, u32[]{:S(2)}, u32[]{:S(2)}) collective-permute-start(bf16[128,512]{1,0:T(8,128)(2,1)S(1)} %get-tuple-element.13), channel_id=1, source_target_pairs={{6,0},{4,2},{2,4},{0,6},{7,1},{5,3},{3,5},{1,7},{14,8},{12,10},{10... | collective-permute-start | bytes 393224 | tf_op jit(solution)/shard_map/ppermute | solution.py:249
  87.9 10.3 %collective-permute-start.6 = (bf16[128,512]{1,0:T(8,128)(2,1)S(1)}, bf16[128,512]{1,0:T(8,128)(2,1)S(1)}, u32[]{:S(2)}, u32[]{:S(2)}) collective-permute-start(bf16[128,512]{1,0:T(8,128)(2,1)S(1)} %get-tuple-element.12), channel_id=1, source_target_pairs={{4,0},{6,2},{0,4},{2,6},{5,1},{7,3},{1,5},{3,7},{12,8},{14,10},{8,... | collective-permute-start | bytes 393224 | tf_op jit(solution)/shard_map/ppermute | solution.py:249
  87.9 10.3 %collective-permute-start.5 = (bf16[128,512]{1,0:T(8,128)(2,1)S(1)}, bf16[128,512]{1,0:T(8,128)(2,1)S(1)}, u32[]{:S(2)}, u32[]{:S(2)}) collective-permute-start(bf16[128,512]{1,0:T(8,128)(2,1)S(1)} %get-tuple-element.11), channel_id=1, source_target_pairs={{2,0},{0,2},{6,4},{4,6},{3,1},{1,3},{7,5},{5,7},{10,8},{8,10},{14,... | collective-permute-start | bytes 393224 | tf_op jit(solution)/shard_map/ppermute | solution.py:249
  102.0 4.4 %collective-permute-start.9 = (f32[128]{0:T(128)S(1)}, f32[128]{0:T(128)S(1)}, u32[]{:S(2)}, u32[]{:S(2)}) collective-permute-start(f32[128]{0:T(128)S(1)} %add.107), channel_id=1, source_target_pairs={{0,1},{1,0},{2,3},{3,2},{4,5},{5,4},{6,7},{7,6},{8,9},{9,8},{10,11... | collective-permute-start | bytes 1544 | tf_op jit(solution)/shard_map/ppermute | solution.py:282
  102.1 4.4 %copy-start.4 = (f32[128,3584]{1,0:T(8,128)S(1)}, f32[128,3584]{1,0:T(8,128)}, u32[]{:S(2)}) copy-start(f32[128,3584]{1,0:T(8,128)} %copy-done.3) | copy-start | bytes 5505028
  105.8 2.6 %copy-start.5 = (f32[128,3584]{1,0:T(8,128)S(1)}, f32[128,3584]{1,0:T(8,128)}, u32[]{:S(2)}) copy-start(f32[128,3584]{1,0:T(8,128)} %broadcast_select_fusion) | copy-start | bytes 5505028
  105.8 2.6 %copy-start.6 = (bf16[128,1792]{1,0:T(8,128)(2,1)S(1)}, bf16[128,1792]{1,0:T(8,128)(2,1)}, u32[]{:S(2)}) copy-start(bf16[128,1792]{1,0:T(8,128)(2,1)} %param.10) | copy-start | bytes 1376260
  105.9 2.5 %collective-permute-start.8 = (bf16[128,1792]{1,0:T(8,128)(2,1)S(1)}, bf16[128,1792]{1,0:T(8,128)(2,1)S(1)}, u32[]{:S(2)}, u32[]{:S(2)}) collective-permute-start(bf16[128,1792]{1,0:T(8,128)(2,1)S(1)} %select_convert_fusion), channel_id=1, source_target_pairs={{0,1},{1,0},{2,3},{3,2},{4,5},{5,4},{6,7},{7,6},{8,9},{9,8},{10,11... | collective-permute-start | bytes 1376264 | tf_op jit(solution)/shard_map/ppermute | solution.py:193
  106.5 3.1 %copy-start.1 = (s32[4]{0:T(128)S(1)}, s32[4]{0:T(128)}, u32[]{:S(2)}) copy-start(s32[4]{0:T(128)} %param.19) | copy-start | bytes 52

commit v2 on v1

v2 whole, which is shorter than its diff:
```python
import functools
import math

import jax
import jax.numpy as jnp
from jax import lax
from jax.experimental import pallas as pl
from jax.experimental.pallas import tpu as pltpu
from jax.sharding import PartitionSpec as P

KV_HEADS = 4
HEAD_DIM = 128
MIB = 1024 * 1024

epsilon = 1e-06
bf16 = jnp.bfloat16
f32 = jnp.float32
SMEM = pl.BlockSpec(memory_space=pltpu.SMEM)


def seq_pairs(step, count):
    if count & (count - 1) == 0:
        return [(i, i ^ step) for i in range(count)]
    return [(i, (i + step) % count) for i in range(count)]


def seq_source(rank, step, count):
    if count & (count - 1) == 0:
        return rank ^ step
    return (rank - step) % count


def inverted(pairs):
    return [(b, a) for a, b in pairs]


def tile_of(extent, most):
    best = HEAD_DIM
    for size in range(HEAD_DIM, min(extent, most) + 1, HEAD_DIM):
        if extent % size == 0:
            best = size
    return best


def dot_nt(a, b):
    return lax.dot_general(a, b, (((1,), (1,)), ((), ())), preferred_element_type=f32)


def dot_tn(a, b):
    return lax.dot_general(a, b, (((0,), (0,)), ((), ())), preferred_element_type=f32)


def column(row):
    count = row.shape[1]
    return jnp.broadcast_to(row.astype(f32), (count, count)).T[:, :1]


def row_of(col):
    count = col.shape[0]
    return jnp.broadcast_to(col, (count, count)).T[:1, :]


def inverse_norm(values):
    return lax.rsqrt(jnp.mean(values * values, axis=-1, keepdims=True) + epsilon)


def norm_back(values, factor, scaling, upstream):
    unit_rows = values * factor
    inner_mean = jnp.mean(scaling * upstream * unit_rows, axis=-1, keepdims=True)
    return factor * (scaling * upstream - unit_rows * inner_mean)


def whole(shape):
    return pl.BlockSpec(shape, lambda *_: (0,) * len(shape))


def params(mib):
    return pltpu.CompilerParams(vmem_limit_bytes=mib * MIB)


def cost(micros):
    return pl.CostEstimate(
        flops=int(micros * 1e9), bytes_accessed=int(micros * 2e6), transcendentals=0
    )


def in_order(rank, part_refs):
    if len(part_refs) == 1:
        return part_refs[0][...]
    own, other = part_refs[0][...], part_refs[1][...]
    first = rank == 0
    return jnp.concatenate([jnp.where(first, own, other), jnp.where(first, other, own)], axis=1)


def both_experts(image, rows, weights):
    zero = jnp.zeros_like(rows)
    masked = jnp.concatenate([jnp.where(image, zero, rows), jnp.where(image, rows, zero)], axis=1)
    flat = weights.reshape(2 * weights.shape[1], weights.shape[2])
    return jnp.dot(masked, flat, preferred_element_type=f32)


def both_back(image, rows, weights):
    return jnp.where(image, dot_nt(rows, weights[1]), dot_nt(rows, weights[0]))


def key_kernel(count, chunk, *refs):
    rank_ref, modality_ref, gain_ref, head_ref, weight_ref = refs[:5]
    part_refs = refs[5 : 5 + count]
    memory_ref, raw_ref, normed_ref, factor_ref, total = refs[5 + count :]
    step = pl.program_id(0)
    image = column(modality_ref[...]) > 0.0

    @pl.when(step == 0)
    def _():
        rows = in_order(rank_ref[0], part_refs).astype(f32)
        factor = inverse_norm(rows)
        scaling = jnp.where(image, gain_ref[1:2, :], gain_ref[0:1, :])
        normed_ref[...] = (rows * factor * scaling).astype(bf16)
        factor_ref[...] = row_of(factor)
        total[...] = jnp.zeros_like(total)

    columns = pl.ds(pl.multiple_of(step * chunk, HEAD_DIM), chunk)
    total[...] += both_experts(image, normed_ref[:, columns], weight_ref[...])

    @pl.when(step == pl.num_programs(0) - 1)
    def _():
        blocks = total.shape[1] // HEAD_DIM
        scaling = jnp.where(image, head_ref[1, 1:2, :], head_ref[0, 1:2, :])
        raw_ref[...] = total[...]
        for b in range(blocks):
            part = slice(b * HEAD_DIM, (b + 1) * HEAD_DIM)
            raw = total[:, part]
            normed = raw * inverse_norm(raw) * scaling
            is_key = (rank_ref[0] * blocks + b) % 2 == 0
            memory_ref[:, part] = jnp.where(is_key, normed, raw).astype(bf16)


def key_stage(rank, modality, norm_gain, head_gain, weights, parts):
    _, depth, width = weights.shape
    rows = parts[0].shape[0]
    chunk = tile_of(depth, 1792)
    return pl.pallas_call(
        functools.partial(key_kernel, len(parts), chunk),
        grid=(depth // chunk,),
        out_shape=[
            jax.ShapeDtypeStruct((rows, width), bf16),
            jax.ShapeDtypeStruct((rows, width), f32),
            jax.ShapeDtypeStruct((rows, depth), bf16),
            jax.ShapeDtypeStruct((1, rows), f32),
        ],
        in_specs=[
            SMEM,
            whole(modality.shape),
            whole(norm_gain.shape),
            whole(head_gain.shape),
            pl.BlockSpec((2, chunk, width), lambda i: (0, i, 0)),
        ]
        + [whole(p.shape) for p in parts],
        out_specs=[
            whole((rows, width)),
            whole((rows, width)),
            whole((rows, depth)),
            whole((1, rows)),
        ],
        scratch_shapes=[pltpu.VMEM((rows, width), f32)],
        compiler_params=params(20),
        cost_estimate=cost(3),
        name="key_stage",
    )(rank, modality, norm_gain, head_gain, weights, *parts)


def query_kernel(chunk, modality_ref, head_ref, weight_ref, normed_ref, query_ref, raw_ref):
    step = pl.program_id(0)
    image = column(modality_ref[...]) > 0.0
    columns = pl.ds(pl.multiple_of(step * chunk, HEAD_DIM), chunk)
    product = both_experts(image, normed_ref[:, columns], weight_ref[...])

    @pl.when(step == 0)
    def _():
        raw_ref[...] = product

    @pl.when(step > 0)
    def _():
        raw_ref[...] += product

    @pl.when(step == pl.num_programs(0) - 1)
    def _():
        scaling = jnp.where(image, head_ref[1, 0:1, :], head_ref[0, 0:1, :])
        for h in range(raw_ref.shape[1] // HEAD_DIM):
            part = slice(h * HEAD_DIM, (h + 1) * HEAD_DIM)
            raw = raw_ref[:, part]
            query_ref[:, part] = (raw * inverse_norm(raw) * scaling).astype(bf16)


def query_stage(modality, head_gain, weights, normed):
    _, depth, width = weights.shape
    rows = normed.shape[0]
    chunk = tile_of(depth, 896)
    return pl.pallas_call(
        functools.partial(query_kernel, chunk),
        grid=(depth // chunk,),
        out_shape=[
            jax.ShapeDtypeStruct((rows, width), bf16),
            jax.ShapeDtypeStruct((rows, width), f32),
        ],
        in_specs=[
            whole(modality.shape),
            whole(head_gain.shape),
            pl.BlockSpec((2, chunk, width), lambda i: (0, i, 0)),
            whole(normed.shape),
        ],
        out_specs=[whole((rows, width)), whole((rows, width))],
        compiler_params=params(20),
        cost_estimate=cost(5),
        name="query_stage",
    )(modality, head_gain, weights, normed)


def cotangent_kernel(count, *refs):
    rank_ref, modality_ref, weight_ref = refs[:3]
    part_refs = refs[3 : 3 + count]
    back_ref, held = refs[3 + count :]
    image = column(modality_ref[...]) > 0.0

    @pl.when(pl.program_id(0) == 0)
    def _():
        held[...] = in_order(rank_ref[0], part_refs)

    back_ref[...] = both_back(image, held[...], weight_ref[...]).astype(bf16)


def cotangent_stage(rank, modality, weights, parts):
    _, width, depth = weights.shape
    rows = parts[0].shape[0]
    tile = tile_of(width, 256)
    return pl.pallas_call(
        functools.partial(cotangent_kernel, len(parts)),
        grid=(width // tile,),
        out_shape=jax.ShapeDtypeStruct((rows, width), bf16),
        in_specs=[
            SMEM,
            whole(modality.shape),
            pl.BlockSpec((2, tile, depth), lambda i: (0, i, 0)),
        ]
        + [whole(p.shape) for p in parts],
        out_specs=pl.BlockSpec((rows, tile), lambda i: (0, i)),
        scratch_shapes=[pltpu.VMEM((rows, depth), bf16)],
        compiler_params=params(20),
        cost_estimate=cost(7),
        name="cotangent_stage",
    )(rank, modality, weights, *parts)


def attention_kernel(blocks, per_group, *refs):
    source_ref, segments_ref, modality_ref, head_ref, query_ref, raw_ref, back_ref = refs[:7]
    memory_refs = refs[7 : 7 + blocks]
    attended_ref, query_back_ref, inner_ref = refs[7 + blocks : 10 + blocks]
    grad_refs = refs[10 + blocks :]
    rows = query_ref.shape[0]
    scale = 1.0 / math.sqrt(HEAD_DIM)

    def heads(ref):
        return jnp.concatenate(
            [ref[:, h * HEAD_DIM : (h + 1) * HEAD_DIM] for h in range(per_group)], axis=0
        )

    query, back = heads(query_ref), heads(back_ref)
    key = jnp.concatenate([m[:, :HEAD_DIM] for m in memory_refs], axis=0)
    value = jnp.concatenate([m[:, HEAD_DIM:] for m in memory_refs], axis=0)
    key_segments = jnp.concatenate(
        [segments_ref[pl.ds(source_ref[b], 1), :] for b in range(blocks)], axis=1
    )
    query_segments = column(segments_ref[pl.ds(source_ref[0], 1), :])
    visible = jnp.where(key_segments.astype(f32) <= query_segments, 1.0, 0.0)
    visible = jnp.concatenate([visible] * per_group, axis=0)
    scores = dot_nt(query, key) * scale
    weights = jnp.where(visible > 0.0, jnp.exp(scores), 0.0).astype(bf16)
    weights32 = weights.astype(f32)
    denominator = jnp.sum(weights32, axis=1, keepdims=True)
    numerator = jnp.dot(weights, value, preferred_element_type=f32)
    attended = (numerator / denominator).astype(bf16)
    offset = jnp.sum(back.astype(f32) * attended.astype(f32), axis=1, keepdims=True)
    probability = (weights32 / denominator).astype(bf16)
    back_prob = dot_nt(back, value)
    back_score = (probability.astype(f32) * (back_prob - offset)).astype(bf16)
    back_query = jnp.dot(back_score, key, preferred_element_type=f32) * scale
    back_key = dot_tn(back_score, query) * scale
    back_value = dot_tn(probability, back)
    for b in range(blocks):
        part = slice(b * rows, (b + 1) * rows)
        grad_refs[b][:, :HEAD_DIM] = back_key[part].astype(grad_refs[b].dtype)
        grad_refs[b][:, HEAD_DIM:] = back_value[part].astype(grad_refs[b].dtype)
    image = column(modality_ref[...]) > 0.0
    scaling = jnp.where(image, head_ref[1, 0:1, :], head_ref[0, 0:1, :])
    inner = jnp.zeros((rows, 1), f32)
    for h in range(per_group):
        part = slice(h * rows, (h + 1) * rows)
        columns = slice(h * HEAD_DIM, (h + 1) * HEAD_DIM)
        attended_ref[:, columns] = attended[part]
        raw = raw_ref[:, columns]
        query_back = norm_back(raw, inverse_norm(raw), scaling, back_query[part]).astype(bf16)
        query_back_ref[:, columns] = query_back
        inner += jnp.sum(query_back.astype(f32) * raw, axis=1, keepdims=True)
    inner = row_of(inner)

    @pl.when(pl.program_id(0) == 0)
    def _():
        inner_ref[...] = inner

    @pl.when(pl.program_id(0) > 0)
    def _():
        inner_ref[...] += inner


def attention_stage(sources, segments, modality, head_gain, query, raw, back, memories):
    rows, width = query.shape
    blocks = len(memories)
    pairs = memories[0].shape[1] // (2 * HEAD_DIM)
    per_group = width // HEAD_DIM // pairs
    wide = pl.BlockSpec((rows, per_group * HEAD_DIM), lambda g: (0, g))
    narrow = pl.BlockSpec((rows, 2 * HEAD_DIM), lambda g: (0, g))
    outs = [
        jax.ShapeDtypeStruct((rows, width), bf16),
        jax.ShapeDtypeStruct((rows, width), bf16),
        jax.ShapeDtypeStruct((1, rows), f32),
    ] + [
        jax.ShapeDtypeStruct((rows, pairs * 2 * HEAD_DIM), f32 if b == 0 else bf16)
        for b in range(blocks)
    ]
    return pl.pallas_call(
        functools.partial(attention_kernel, blocks, per_group),
        grid=(pairs,),
        out_shape=outs,
        in_specs=[
            SMEM,
            whole(segments.shape),
            whole(modality.shape),
            whole(head_gain.shape),
            wide,
            wide,
            wide,
        ]
        + [narrow] * blocks,
        out_specs=[wide, wide, whole((1, rows))] + [narrow] * blocks,
        compiler_params=params(32),
        cost_estimate=cost(3.5),
        name="attention_stage",
    )(sources, segments, modality, head_gain, query, raw, back, *memories)


def output_kernel(turns, rank_ref, modality_ref, weight_ref, attended_ref, *out_refs):
    image = column(modality_ref[...]) > 0.0
    product = both_experts(image, attended_ref[...], weight_ref[...])
    if len(out_refs) == 1:
        out_refs[0][...] = product.astype(bf16)
        return
    sent_ref, kept_ref = out_refs

    @pl.when(pl.program_id(0) < turns)
    def _():
        sent_ref[...] = product.astype(bf16)

    @pl.when(pl.program_id(0) >= turns)
    def _():
        kept_ref[...] = product


def output_stage(rank, modality, weights, attended, split):
    _, depth, width = weights.shape
    rows = attended.shape[0]
    tile = tile_of(width // 2, 896)
    turns = width // 2 // tile
    if split:
        def place(i, rank_ref):
            half = jnp.where(i < turns, 1 - rank_ref[0], rank_ref[0])
            return half * turns + lax.rem(i, turns)

        outs = [
            jax.ShapeDtypeStruct((rows, width // 2), bf16),
            jax.ShapeDtypeStruct((rows, width // 2), f32),
        ]
        out_specs = [
            pl.BlockSpec((rows, tile), lambda i, r: (0, jnp.minimum(i, turns - 1))),
            pl.BlockSpec((rows, tile), lambda i, r: (0, jnp.maximum(i - turns, 0))),
        ]
    else:
        def place(i, rank_ref):
            return i

        outs = [jax.ShapeDtypeStruct((rows, width), bf16)]
        out_specs = [pl.BlockSpec((rows, tile), lambda i, r: (0, i))]
    return pl.pallas_call(
        functools.partial(output_kernel, turns),
        grid_spec=pltpu.PrefetchScalarGridSpec(
            num_scalar_prefetch=1,
            grid=(2 * turns,),
            in_specs=[
                whole(modality.shape),
                pl.BlockSpec((2, depth, tile), lambda i, r: (0, 0, place(i, r))),
                whole(attended.shape),
            ],
            out_specs=out_specs,
        ),
        out_shape=outs,
        compiler_params=params(20),
        cost_estimate=cost(5),
        name="output_stage",
    )(rank, modality, weights, attended)


def query_back_kernel(modality_ref, weight_ref, back_ref, out_ref):
    image = column(modality_ref[...]) > 0.0
    out_ref[...] = both_back(image, back_ref[...], weight_ref[...])


def query_back_stage(modality, weights, back):
    _, depth, width = weights.shape
    rows = back.shape[0]
    tile = tile_of(depth, 896)
    return pl.pallas_call(
        query_back_kernel,
        grid=(depth // tile,),
        out_shape=jax.ShapeDtypeStruct((rows, depth), f32),
        in_specs=[
            whole(modality.shape),
            pl.BlockSpec((2, tile, width), lambda i: (0, i, 0)),
            whole(back.shape),
        ],
        out_specs=pl.BlockSpec((rows, tile), lambda i: (0, i)),
        compiler_params=params(20),
        cost_estimate=cost(7),
        name="query_back_stage",
    )(modality, weights, back)


def key_back_kernel(
    count, rank_ref, modality_ref, head_ref, raw_ref, inner_in_ref, part_ref, weight_ref, *refs
):
    grad_refs = refs[:count]
    out_ref, back_ref, inner_ref = refs[count:]
    image = column(modality_ref[...]) > 0.0
    blocks = raw_ref.shape[1] // HEAD_DIM

    @pl.when(pl.program_id(0) == 0)
    def _():
        scaling = jnp.where(image, head_ref[1, 1:2, :], head_ref[0, 1:2, :])
        inner = jnp.zeros((raw_ref.shape[0], 1), f32)
        for b in range(blocks):
            part = slice(b * HEAD_DIM, (b + 1) * HEAD_DIM)
            raw = raw_ref[:, part]
            upstream = grad_refs[0][:, part].astype(f32)
            for grad_ref in grad_refs[1:]:
                upstream += grad_ref[:, part].astype(f32)
            is_key = (rank_ref[0] * blocks + b) % 2 == 0
            normed_back = norm_back(raw, inverse_norm(raw), scaling, upstream)
            back = jnp.where(is_key, normed_back, upstream).astype(bf16)
            back_ref[:, part] = back
            inner += jnp.sum(back.astype(f32) * raw, axis=1, keepdims=True)
        inner_ref[...] = inner_in_ref[...] + row_of(inner)

    product = both_back(image, back_ref[...], weight_ref[...])
    out_ref[...] = (product + part_ref[...]).astype(bf16)


def key_back_stage(rank, modality, head_gain, raw, inner, part, weights, grads, split):
    _, depth, width = weights.shape
    rows = raw.shape[0]
    tile = tile_of(depth // 2, 896)
    turns = depth // 2 // tile
    steps = turns if split else 2 * turns

    def place(i, rank_ref):
        return (1 - rank_ref[0]) * turns + i if split else i

    return pl.pallas_call(
        functools.partial(key_back_kernel, len(grads)),
        grid_spec=pltpu.PrefetchScalarGridSpec(
            num_scalar_prefetch=1,
            grid=(steps,),
            in_specs=[
                whole(modality.shape),
                whole(head_gain.shape),
                whole(raw.shape),
                whole(inner.shape),
                pl.BlockSpec((rows, tile), lambda i, r: (0, place(i, r))),
                pl.BlockSpec((2, tile, width), lambda i, r: (0, place(i, r), 0)),
            ]
            + [whole(g.shape) for g in grads],
            out_specs=[
                pl.BlockSpec((rows, tile), lambda i, r: (0, i)),
                whole((rows, width)),
                whole((1, rows)),
            ],
        ),
        out_shape=[
            jax.ShapeDtypeStruct((rows, steps * tile), bf16),
            jax.ShapeDtypeStruct((rows, width), bf16),
            jax.ShapeDtypeStruct((1, rows), f32),
        ],
        compiler_params=params(20),
        cost_estimate=cost(2),
        name="key_back_stage",
    )(rank, modality, head_gain, raw, inner, part, weights, *grads)


def kept_kernel(rank_ref, modality_ref, part_ref, weight_ref, back_ref, out_ref):
    image = column(modality_ref[...]) > 0.0
    out_ref[...] = both_back(image, back_ref[...], weight_ref[...]) + part_ref[...]


def kept_stage(rank, modality, part, weights, back):
    _, depth, width = weights.shape
    rows = back.shape[0]
    tile = tile_of(depth // 2, 896)
    turns = depth // 2 // tile
    return pl.pallas_call(
        kept_kernel,
        grid_spec=pltpu.PrefetchScalarGridSpec(
            num_scalar_prefetch=1,
            grid=(turns,),
            in_specs=[
                whole(modality.shape),
                pl.BlockSpec((rows, tile), lambda i, r: (0, r[0] * turns + i)),
                pl.BlockSpec((2, tile, width), lambda i, r: (0, r[0] * turns + i, 0)),
                whole(back.shape),
            ],
            out_specs=pl.BlockSpec((rows, tile), lambda i, r: (0, i)),
        ),
        out_shape=jax.ShapeDtypeStruct((rows, depth // 2), f32),
        compiler_params=params(20),
        cost_estimate=cost(2),
        name="kept_stage",
    )(rank, modality, part, weights, back)


def finish(total_width, count, modality, gain, factor, inputs, backs, inners):
    rows, width = inputs.shape

    def kernel(modality_ref, gain_ref, factor_ref, inputs_ref, *refs):
        back_refs = refs[:count]
        inner_refs, out_ref = refs[count:-1], refs[-1]
        image = column(modality_ref[...]) > 0.0
        scaling = jnp.where(image, gain_ref[1:2, :], gain_ref[0:1, :])
        factor_column = column(factor_ref[...])
        back = back_refs[0][...].astype(f32)
        for ref in back_refs[1:]:
            back += ref[...].astype(f32)
        inner = inner_refs[0][...]
        for ref in inner_refs[1:]:
            inner += ref[...]
        unit_rows = inputs_ref[...].astype(f32) * factor_column
        inner_mean = column(inner) * (1.0 / total_width)
        out_ref[...] = (factor_column * (scaling * back - unit_rows * inner_mean)).astype(bf16)

    arrays = [modality, gain, factor, inputs, *backs, *inners]
    return pl.pallas_call(
        kernel,
        out_shape=jax.ShapeDtypeStruct((rows, width), bf16),
        in_specs=[whole(a.shape) for a in arrays],
        out_specs=whole((rows, width)),
        grid=(1,),
        compiler_params=params(20),
        cost_estimate=cost(1),
        name="finish",
    )(*arrays)


def local(
    inputs,
    cotangent,
    norm_gain,
    head_gain,
    query_weight,
    key_weight,
    output_weight,
    modality,
    segments,
    block_order,
):
    tensor_rank = lax.axis_index("tensor")
    block_rank = lax.axis_index("seq")
    tensor_count = lax.axis_size("tensor")
    block_count = lax.axis_size("seq")
    local_rows, local_width = inputs.shape
    full_width = local_width * tensor_count
    split = tensor_count == 2
    swap = [(0, 1), (1, 0)]
    rank = tensor_rank.astype(jnp.int32).reshape(1)
    modality = modality.reshape(1, local_rows)
    segments = segments.reshape(block_count, local_rows)

    def spread(part):
        if split:
            return [part, lax.ppermute(part, "tensor", swap)]
        return [lax.all_gather(part, "tensor", axis=1, tiled=True)]

    def scatter_columns(part):
        return lax.psum_scatter(part, "tensor", scatter_dimension=1, tiled=True)

    memory, key_raw, normed, row_factor = key_stage(
        rank, modality, norm_gain, head_gain, key_weight, spread(inputs)
    )
    shared = tensor_count > KV_HEADS
    is_even = tensor_rank % 2 == 0
    pair_swap = [(i, i ^ 1) for i in range(tensor_count)]
    if shared:
        partner = lax.ppermute(memory, "tensor", pair_swap)
        memory = jnp.where(
            is_even,
            jnp.concatenate([memory, partner], 1),
            jnp.concatenate([partner, memory], 1),
        )
    memories, order = [memory], [block_rank]
    for step in range(1, block_count):
        memories.append(lax.ppermute(memory, "seq", seq_pairs(step, block_count)))
        order.append(seq_source(block_rank, step, block_count))
    sources = block_order[jnp.stack(order)]

    query, query_raw = query_stage(modality, head_gain, query_weight, normed)
    back_attended = cotangent_stage(rank, modality, output_weight, spread(cotangent))
    attended, query_back, inner, own_grad, *grads = attention_stage(
        sources, segments, modality, head_gain, query, query_raw, back_attended, memories
    )
    incoming = [
        lax.ppermute(grad, "seq", inverted(seq_pairs(step, block_count)))
        for step, grad in enumerate(grads, 1)
    ]

    projected = output_stage(rank, modality, output_weight, attended, split)
    if split:
        sent, kept = projected
        attention_out = (kept + lax.ppermute(sent, "tensor", swap).astype(f32)).astype(bf16)
    else:
        attention_out = scatter_columns(projected[0])

    gradient_part = query_back_stage(modality, query_weight, query_back)

    if shared:
        total = own_grad + sum(grad.astype(f32) for grad in incoming)
        low, high = total[:, :HEAD_DIM], total[:, HEAD_DIM:]
        outgoing = jnp.where(is_even, high, low).astype(bf16)
        sums = [jnp.where(is_even, low, high), lax.ppermute(outgoing, "tensor", pair_swap)]
    else:
        sums = [own_grad, *incoming]
    sent, slice_back, inner = key_back_stage(
        rank, modality, head_gain, key_raw, inner, gradient_part, key_weight, sums, split
    )
    if split:
        inners = [inner, lax.ppermute(inner, "tensor", swap)]
        other = lax.ppermute(sent, "tensor", swap)
        kept = kept_stage(rank, modality, gradient_part, key_weight, slice_back)
        backs = [kept, other]
    else:
        inners = [lax.psum(inner, "tensor")]
        backs = [scatter_columns(sent)]
    gain = lax.dynamic_slice_in_dim(norm_gain, tensor_rank * local_width, local_width, 1)
    grad_input = finish(
        full_width, len(backs), modality, gain, row_factor, inputs, backs, inners
    )
    return (attention_out, grad_input)


def solution(mesh):
    return jax.shard_map(
        local,
        mesh=mesh,
        in_specs=(
            P(("dp", "seq"), "tensor"),
            P(("dp", "seq"), "tensor"),
            P(),
            P(),
            P(None, None, "tensor"),
            P(None, None, "tensor"),
            P(None, "tensor", None),
            P(("dp", "seq")),
            P("dp"),
            P("dp"),
        ),
        out_specs=(P(("dp", "seq"), "tensor"), P(("dp", "seq"), "tensor")),
        check_vma=False,
    )
```

time: 111 us -> 73 us (0.66)
  matrix products: 45 us -> 0 us
  Pallas kernels: 3.51 us -> 35 us
  local copies, waits for them, and re-layouts: 32.9 us -> 24.3 us
  other arithmetic: 9.13 us -> 0.95 us
  waiting for transfers between devices: 3.95 us -> 0.15 us
  blocking collectives: 2.75 us -> 0 us
    dot_general x9 -> x0, matrix products: 45 us -> none  [the longest x3 15.2 us: expert_pick(): return jnp.dot(masked, flat, preferred_element_type=f32)]
    pallas_call x1 -> x9, Pallas kernels: 3.51 us -> 35 us  [the longest x1 6.68 us: cotangent_stage(): pl.pallas_call(functools.partial(cotangent_kernel, len(parts)), grid=(wid...]
    dot_general x2 -> x0, local copies, waits for them, and re-layouts: 29.4 us -> none  [expert_pick(): return jnp.dot(masked, flat, preferred_element_type=f32)]
    unnamed x28 -> x40, local copies, waits for them, and re-layouts: 1.35 us -> 22.9 us
    ppermute x3, waiting for transfers between devices: 3.93 us -> 0.01 us  [local(): lax.ppermute(grad, 'seq', inverted(seq_pairs(step, block_count)))]
    convert_element_type x6 -> x1, other arithmetic: 4.19 us -> 0.87 us  [local(): (kept + lax.ppermute(sent, 'tensor', swap).astype(f32)).astype(bf16)]
    select_n x5 -> x0, other arithmetic: 3.32 us -> none  [the longest x1 1.5 us: local(): jnp.where(is_image, norm_gain[1][None, :], norm_gain[0][None, :])]
    all_gather x1 -> x0, blocking collectives: 2.75 us -> none  [local(): whole_rows = lax.all_gather(inputs, 'tensor', axis=1, tiled=True)]
  transfers between devices with their start and end apart: 10 -> 11, of which waited for: 1 -> 1; matrix products, arithmetic and copies ran while one was open for 58% -> 3% of each run, Pallas kernels for 0% -> 41%
where the time goes in v2:
time: 73 us; the launch traced here: 72.6 us
  Pallas kernels  35 us (48%)
  local copies, waits for them, and re-layouts  24.3 us (33%)
  starting transfers between devices  11.3 us (15%)
  other arithmetic  0.95 us (1%)
  between operations  0.92 us (1%)
    unnamed x40, local copies, waits for them, and re-layouts  22.9 us
    pallas_call x1, Pallas kernels, cotangent_stage(): pl.pallas_call(functools.partial(cotangent_kernel, len(parts)), grid=(wid...  6.68 us
    pallas_call x1, Pallas kernels, query_back_stage(): pl.pallas_call(query_back_kernel, grid=(depth // tile,), out_shape=jax.Sh...  6.22 us
    ppermute x3, starting transfers between devices, local(): memories.append(lax.ppermute(memory, 'seq', seq_pairs(step, block_count)))  5.6 us
    pallas_call x1, Pallas kernels, output_stage(): pl.pallas_call(functools.partial(output_kernel, turns), grid_spec=pltpu.P...  4.99 us
    pallas_call x1, Pallas kernels, query_stage(): pl.pallas_call(functools.partial(query_kernel, chunk), grid=(depth // chu...  4.52 us
    ppermute x3, starting transfers between devices, local(): lax.ppermute(grad, 'seq', inverted(seq_pairs(step, block_count)))  4.45 us
    pallas_call x1, Pallas kernels, attention_stage(): pl.pallas_call(functools.partial(attention_kernel, blocks, per_group), gr...  4.1 us
  transfers between devices with their start and end apart: 11, of which 1 were waited for; matrix products, arithmetic and copies ran while one was open for 3% of the time, Pallas kernels for 41%

profile of v2, /device:TPU:0, one launch (start us, length us, event | category | flops | bytes accessed | tf_op | source)
XLA Modules:
  0.0 72.6 jit_solution(6112449783100415234)
XLA Ops:
  0.6 0.0 copy-start
  0.6 0.5 collective-permute-start
  1.2 0.1 collective-permute-start.1
  1.2 0.1 fusion
  1.3 0.0 copy-done
  1.3 0.6 gather_fusion
  2.0 0.7 constant_dynamic-slice_fusion.gain_ref
  2.7 0.1 collective-permute-done.refs_6_
  2.8 0.0 copy-start.1
  2.8 3.1 %copy-done.1 = bf16[2,3584,512]{2,1,0:T(8,128)(2,1)S(1)} copy-done((bf16[2,3584,512]{2,1,0:T(8,128)(2,1)S(1)}, bf16[2,3584,512]{2,1,0:T(8,128)(2,1)}, u32[]{:S(2)}) %copy-start.1) | copy-done | bytes 7340056
  5.9 0.7 %copy-done.2 = f32[2,3584]{1,0:T(2,128)S(1)} copy-done((f32[2,3584]{1,0:T(2,128)S(1)}, f32[2,3584]{1,0:T(2,128)}, u32[]{:S(2)}) %copy-start.2) | copy-done | bytes 28696
  6.7 0.7 copy-done.3
  7.3 0.7 copy-done.5
  8.0 1.0 %copy-done.11 = bf16[128,1792]{1,0:T(8,128)(2,1)S(1)} copy-done((bf16[128,1792]{1,0:T(8,128)(2,1)S(1)}, bf16[128,1792]{1,0:T(8,128)(2,1)}, u32[]{:S(2)}) %copy-start.11) | copy-done | bytes 458776
  9.0 2.9 %key_stage.1 = (bf16[128,512]{1,0:T(8,128)(2,1)S(1)}, f32[128,512]{1,0:T(8,128)S(1)}, bf16[128,3584]{1,0:T(8,128)(2,1)S(1)}, f32[1,128]{1,0:T(1,128)S(1)}) custom-call(s32[1]{0:T(128)} %bitcast.refs_0_.rank_ref, s32[1,128]{1,0:T(1,128)S(1)} %bitcast.11, f32[2,3584]{1,0:T(2,128)S(1)} %copy-done.2, f32[2,2,128]{2,1,0:T(2,128)S(1)} %copy-done.3, ...), custom_call_target="tpu_custom_call" | custom-call | flops 3000000000 | bytes 6000000 | tf_op jit(solution)/shard_map/key_stage/pallas_call | solution.py:142
  11.9 0.0 copy-start.4
  11.9 3.0 %collective-permute-start.2 = (bf16[128,512]{1,0:T(8,128)(2,1)S(1)}, bf16[128,512]{1,0:T(8,128)(2,1)S(1)}, u32[]{:S(2)}, u32[]{:S(2)}) collective-permute-start(bf16[128,512]{1,0:T(8,128)(2,1)S(1)} %get-tuple-element.23.refs_7_), channel_id=1, source_target_pairs={{0,2},{2,0},{4,6},{6,4},{1,3},{3,1},{5,7},{7,5},{8,10},{10,8},{12,... | collective-permute-start | bytes 393224 | tf_op jit(solution)/shard_map/ppermute | solution.py:615
  14.9 2.6 %collective-permute-start.3 = (bf16[128,512]{1,0:T(8,128)(2,1)S(1)}, bf16[128,512]{1,0:T(8,128)(2,1)S(1)}, u32[]{:S(2)}, u32[]{:S(2)}) collective-permute-start(bf16[128,512]{1,0:T(8,128)(2,1)S(1)} %get-tuple-element.23.refs_7_), channel_id=1, source_target_pairs={{0,4},{2,6},{4,0},{6,2},{1,5},{3,7},{5,1},{7,3},{8,12},{10,14},{12... | collective-permute-start | bytes 393224 | tf_op jit(solution)/shard_map/ppermute | solution.py:615
  17.5 0.0 collective-permute-start.4
  17.5 0.0 collective-permute-done.1.refs_4_
  17.5 5.2 %copy-done.7 = bf16[2,1024,3584]{2,1,0:T(8,128)(2,1)S(1)} copy-done((bf16[2,1024,3584]{2,1,0:T(8,128)(2,1)S(1)}, bf16[2,1024,3584]{2,1,0:T(8,128)(2,1)}, u32[]{:S(2)}) %copy-start.7) | copy-done | bytes 14680088
  22.7 1.0 %copy-done.10 = bf16[128,1792]{1,0:T(8,128)(2,1)S(1)} copy-done((bf16[128,1792]{1,0:T(8,128)(2,1)S(1)}, bf16[128,1792]{1,0:T(8,128)(2,1)}, u32[]{:S(2)}) %copy-start.10) | copy-done | bytes 458776
  23.7 6.7 %cotangent_stage.1.refs_6_ = bf16[128,1024]{1,0:T(8,128)(2,1)S(1)} custom-call(s32[1]{0:T(128)} %bitcast.refs_0_.rank_ref, s32[1,128]{1,0:T(1,128)S(1)} %bitcast.12, bf16[2,1024,3584]{2,1,0:T(8,128)(2,1)S(1)} %copy-done.7, bf16[128,1792]{1,0:T(8,128)(2,1)S(1)} %copy-done.10, bf16[128,1792]{1,0:T(8,128)(2,1)S(1)} %collective-permute-done.1.refs_4_), custom_call_target="tpu_custom_call" | custom-call | flops 7000000000 | bytes 14000000 | tf_op jit(solution)/shard_map/cotangent_stage/pallas_call | solution.py:236
  30.4 0.0 copy-start.6
  30.4 0.0 copy-done.4
  30.4 0.0 copy-start.8
  30.4 5.2 %copy-done.8 = bf16[2,3584,1024]{2,1,0:T(8,128)(2,1)S(1)} copy-done((bf16[2,3584,1024]{2,1,0:T(8,128)(2,1)S(1)}, bf16[2,3584,1024]{2,1,0:T(8,128)(2,1)}, u32[]{:S(2)}) %copy-start.8) | copy-done | bytes 14680088
  35.6 4.5 %query_stage.1 = (bf16[128,1024]{1,0:T(8,128)(2,1)S(1)}, f32[128,1024]{1,0:T(8,128)S(1)}) custom-call(s32[1,128]{1,0:T(1,128)S(1)} %bitcast.13, f32[2,2,128]{2,1,0:T(2,128)S(1)} %copy-done.4, bf16[2,3584,1024]{2,1,0:T(8,128)(2,1)S(1)} %copy-done.8, bf16[128,3584]{1,0:T(8,128)(2,1)S(1)} %get-tuple-element.20.normed_ref), custom_call_target="tpu_custom_call" | custom-call | flops 5000000000 | bytes 10000000 | tf_op jit(solution)/shard_map/query_stage/pallas_call | solution.py:199
  40.1 0.0 collective-permute-done.2.refs_8_
  40.1 0.0 collective-permute-done.3.refs_9_
  40.1 0.0 collective-permute-done.4.refs_10_
  40.1 0.0 copy-done.6
  40.2 0.0 copy-done.13
  40.2 0.0 slice-start.5
  40.2 4.1 %attention_stage.1 = (bf16[128,1024]{1,0:T(8,128)(2,1)S(1)}, bf16[128,1024]{1,0:T(8,128)(2,1)S(1)}, f32[1,128]{1,0:T(1,128)S(1)}, f32[128,512]{1,0:T(8,128)S(1)}...) custom-call(s32[4]{0:T(128)S(1)} %gather_fusion, ...), custom_call_target="tpu_custom_call" | custom-call | flops 3500000000 | bytes 7000000 | tf_op jit(solution)/shard_map/attention_stage/pallas_call | solution.py:330
  44.3 1.0 %collective-permute-start.6 = (bf16[128,512]{1,0:T(8,128)(2,1)S(1)}, bf16[128,512]{1,0:T(8,128)(2,1)S(1)}, u32[]{:S(2)}, u32[]{:S(2)}) collective-permute-start(bf16[128,512]{1,0:T(8,128)(2,1)S(1)} %get-tuple-element.32), channel_id=1, source_target_pairs={{2,0},{0,2},{6,4},{4,6},{3,1},{1,3},{7,5},{5,7},{10,8},{8,10},{14,... | collective-permute-start | bytes 393224 | tf_op jit(solution)/shard_map/ppermute | solution.py:625
  45.3 3.5 %collective-permute-start.7 = (bf16[128,512]{1,0:T(8,128)(2,1)S(1)}, bf16[128,512]{1,0:T(8,128)(2,1)S(1)}, u32[]{:S(2)}, u32[]{:S(2)}) collective-permute-start(bf16[128,512]{1,0:T(8,128)(2,1)S(1)} %get-tuple-element.33), channel_id=1, source_target_pairs={{4,0},{6,2},{0,4},{2,6},{5,1},{7,3},{1,5},{3,7},{12,8},{14,10},{8,... | collective-permute-start | bytes 393224 | tf_op jit(solution)/shard_map/ppermute | solution.py:625
  48.7 0.0 collective-permute-start.8
  48.7 0.0 slice-done.2
  48.7 0.0 slice-done.3
  48.7 0.0 slice-done.4
  48.8 0.0 slice-done.5
  48.8 5.0 %output_stage.1 = (bf16[128,1792]{1,0:T(8,128)(2,1)S(1)}, f32[128,1792]{1,0:T(8,128)S(1)}) custom-call(s32[1]{0:T(128)} %bitcast.refs_0_.rank_ref, s32[1,128]{1,0:T(1,128)S(1)} %bitcast.15, bf16[2,1024,3584]{2,1,0:T(8,128)(2,1)S(1)} %bitcast.21, bf16[128,1024]{1,0:T(8,128)(2,1)S(1)} %get-tuple-element.24.attended_ref), custom_call_target="tpu_custom_call" | custom-call | flops 5000000000 | bytes 10000000 | tf_op jit(solution)/shard_map/output_stage/pallas_call | solution.py:392
  53.8 0.0 slice-start
  53.8 0.1 collective-permute-start.5
  53.9 0.0 copy-start.9
  53.9 5.3 %copy-done.9 = bf16[2,3584,1024]{2,1,0:T(8,128)(2,1)S(1)} copy-done((bf16[2,3584,1024]{2,1,0:T(8,128)(2,1)S(1)}, bf16[2,3584,1024]{2,1,0:T(8,128)(2,1)}, u32[]{:S(2)}) %copy-start.9) | copy-done | bytes 14680088
  59.2 6.2 %query_back_stage.1.part_ref = f32[128,3584]{1,0:T(8,128)S(1)} custom-call(s32[1,128]{1,0:T(1,128)S(1)} %bitcast.16, bf16[2,3584,1024]{2,1,0:T(8,128)(2,1)S(1)} %copy-done.9, bf16[128,1024]{1,0:T(8,128)(2,1)S(1)} %get-tuple-element.28.back_ref), custom_call_target="tpu_custom_call" | custom-call | flops 7000000000 | bytes 14000000 | tf_op jit(solution)/shard_map/query_back_stage/pallas_call | solution.py:420
  65.4 0.0 copy-start.12
  65.4 0.0 collective-permute-done.6.refs_1_
  65.4 0.0 collective-permute-done.7.refs_2_
  65.4 0.0 collective-permute-done.8.refs_3_
  65.5 0.0 slice-done
  65.5 0.0 slice-done.1
  65.5 2.5 %key_back_stage.1 = (bf16[128,1792]{1,0:T(8,128)(2,1)S(1)}, bf16[128,512]{1,0:T(8,128)(2,1)S(1)}, f32[1,128]{1,0:T(1,128)S(1)}) custom-call(s32[1]{0:T(128)} %bitcast.refs_0_.rank_ref, s32[1,128]{1,0:T(1,128)S(1)} %bitcast.17, f32[2,2,128]{2,1,0:T(2,128)S(1)} %copy-done.4, f32[128,512]{1,0:T(8,128)S(1)} %get-tuple-element.29.raw_ref, ...), custom_call_target="tpu_custom_call" | custom-call | flops 2000000000 | bytes 4000000 | tf_op jit(solution)/shard_map/key_back_stage/pallas_call | solution.py:475
  68.0 0.4 collective-permute-start.9
  68.4 0.2 collective-permute-start.10
  68.6 1.8 %kept_stage.1.refs_0_ = f32[128,1792]{1,0:T(8,128)S(1)} custom-call(s32[1]{0:T(128)} %bitcast.refs_0_.rank_ref, s32[1,128]{1,0:T(1,128)S(1)} %bitcast.18, f32[128,3584]{1,0:T(8,128)S(1)} %query_back_stage.1.part_ref, bf16[2,3584,512]{2,1,0:T(8,128)(2,1)S(1)} %bitcast.10, bf16[128,512]{1,0:T(8,128)(2,1)S(1)} %get-tuple-element.35.back_ref), custom_call_target="tpu_custom_call" | custom-call | flops 2000000000 | bytes 4000000 | tf_op jit(solution)/shard_map/kept_stage/pallas_call | solution.py:516
  70.5 0.0 collective-permute-done.5
  70.5 0.9 %add_convert_fusion = bf16[128,1792]{1,0:T(8,128)(2,1)} fusion(f32[128,1792]{1,0:T(8,128)S(1)} %get-tuple-element.25, bf16[128,1792]{1,0:T(8,128)(2,1)S(1)} %collective-permute-done.5), kind=kLoop, calls=%fused_computation.1 | loop fusion | flops 688128 | bytes 1835008 | tf_op jit(solution)/shard_map/convert_element_type | solution.py:632
  71.3 0.0 collective-permute-done.10.refs_3_
  71.3 0.0 collective-permute-done.9.refs_1_
  71.3 0.0 copy-done.12
  71.3 1.2 %finish.1 = bf16[128,1792]{1,0:T(8,128)(2,1)} custom-call(s32[1,128]{1,0:T(1,128)S(1)} %bitcast.19, f32[2,1792]{1,0:T(2,128)S(1)} %constant_dynamic-slice_fusion.gain_ref, f32[1,128]{1,0:T(1,128)S(1)} %get-tuple-element.27.factor_ref, bf16[128,1792]{1,0:T(8,128)(2,1)S(1)} %copy-done.12, f32[128,1792]{1,0:T(8,128)S(1)} %kept_stage.1.refs_0_, ...), custom_call_target="tpu_custom_call" | custom-call | flops 1000000000 | bytes 2000000 | tf_op jit(solution)/shard_map/finish/pallas_call | solution.py:556
  (14 shorter events, 0.0 us)
Async XLA Ops:
  0.6 0.7 copy-start
  0.6 2.2 %collective-permute-start = (bf16[128,1792]{1,0:T(8,128)(2,1)}, bf16[128,1792]{1,0:T(8,128)(2,1)S(1)}, u32[]{:S(2)}, u32[]{:S(2)}) collective-permute-start(bf16[128,1792]{1,0:T(8,128)(2,1)} %inputs_ref.1), channel_id=1, source_target_pairs={{0,1},{1,0},{2,3},{3,2},{4,5},{5,4},{6,7},{7,6},{8,9},{9,8},{10,11... | collective-permute-start | bytes 1376264 | tf_op jit(solution)/shard_map/ppermute | solution.py:594
  1.2 16.3 %collective-permute-start.1 = (bf16[128,1792]{1,0:T(8,128)(2,1)}, bf16[128,1792]{1,0:T(8,128)(2,1)S(1)}, u32[]{:S(2)}, u32[]{:S(2)}) collective-permute-start(bf16[128,1792]{1,0:T(8,128)(2,1)} %refs_3_.4), channel_id=1, source_target_pairs={{0,1},{1,0},{2,3},{3,2},{4,5},{5,4},{6,7},{7,6},{8,9},{9,8},{10,11... | collective-permute-start | bytes 1376264 | tf_op jit(solution)/shard_map/ppermute | solution.py:594
  2.8 3.1 %copy-start.1 = (bf16[2,3584,512]{2,1,0:T(8,128)(2,1)S(1)}, bf16[2,3584,512]{2,1,0:T(8,128)(2,1)}, u32[]{:S(2)}) copy-start(bf16[2,3584,512]{2,1,0:T(8,128)(2,1)} %weight_ref.9) | copy-start | bytes 22020100
  5.9 0.7 %copy-start.2 = (f32[2,3584]{1,0:T(2,128)S(1)}, f32[2,3584]{1,0:T(2,128)}, u32[]{:S(2)}) copy-start(f32[2,3584]{1,0:T(2,128)} %refs_2_.2) | copy-start | bytes 86020
  6.6 0.7 copy-start.3
  7.3 0.7 copy-start.5
  8.0 1.0 %copy-start.11 = (bf16[128,1792]{1,0:T(8,128)(2,1)S(1)}, bf16[128,1792]{1,0:T(8,128)(2,1)}, u32[]{:S(2)}) copy-start(bf16[128,1792]{1,0:T(8,128)(2,1)} %inputs_ref.1) | copy-start | bytes 1376260
  11.9 18.5 %copy-start.4 = (f32[2,2,128]{2,1,0:T(2,128)S(1)}, f32[2,2,128]{2,1,0:T(2,128)}, u32[]{:S(2)}) copy-start(f32[2,2,128]{2,1,0:T(2,128)} %head_ref.3) | copy-start | bytes 6148
  11.9 28.2 %collective-permute-start.2 = (bf16[128,512]{1,0:T(8,128)(2,1)S(1)}, bf16[128,512]{1,0:T(8,128)(2,1)S(1)}, u32[]{:S(2)}, u32[]{:S(2)}) collective-permute-start(bf16[128,512]{1,0:T(8,128)(2,1)S(1)} %get-tuple-element.23.refs_7_), channel_id=1, source_target_pairs={{0,2},{2,0},{4,6},{6,4},{1,3},{3,1},{5,7},{7,5},{8,10},{10,8},{12,... | collective-permute-start | bytes 393224 | tf_op jit(solution)/shard_map/ppermute | solution.py:615
  14.9 25.2 %collective-permute-start.3 = (bf16[128,512]{1,0:T(8,128)(2,1)S(1)}, bf16[128,512]{1,0:T(8,128)(2,1)S(1)}, u32[]{:S(2)}, u32[]{:S(2)}) collective-permute-start(bf16[128,512]{1,0:T(8,128)(2,1)S(1)} %get-tuple-element.23.refs_7_), channel_id=1, source_target_pairs={{0,4},{2,6},{4,0},{6,2},{1,5},{3,7},{5,1},{7,3},{8,12},{10,14},{12... | collective-permute-start | bytes 393224 | tf_op jit(solution)/shard_map/ppermute | solution.py:615
  17.5 22.7 %collective-permute-start.4 = (bf16[128,512]{1,0:T(8,128)(2,1)S(1)}, bf16[128,512]{1,0:T(8,128)(2,1)S(1)}, u32[]{:S(2)}, u32[]{:S(2)}) collective-permute-start(bf16[128,512]{1,0:T(8,128)(2,1)S(1)} %get-tuple-element.23.refs_7_), channel_id=1, source_target_pairs={{0,6},{2,4},{4,2},{6,0},{1,7},{3,5},{5,3},{7,1},{8,14},{10,12},{12... | collective-permute-start | bytes 393224 | tf_op jit(solution)/shard_map/ppermute | solution.py:615
  17.5 5.2 %copy-start.7 = (bf16[2,1024,3584]{2,1,0:T(8,128)(2,1)S(1)}, bf16[2,1024,3584]{2,1,0:T(8,128)(2,1)}, u32[]{:S(2)}) copy-start(bf16[2,1024,3584]{2,1,0:T(8,128)(2,1)} %weight_ref.6) | copy-start | bytes 44040196
  22.7 1.0 %copy-start.10 = (bf16[128,1792]{1,0:T(8,128)(2,1)S(1)}, bf16[128,1792]{1,0:T(8,128)(2,1)}, u32[]{:S(2)}) copy-start(bf16[128,1792]{1,0:T(8,128)(2,1)} %refs_3_.4) | copy-start | bytes 1376260
  30.4 9.8 %copy-start.6 = (s32[128]{0:T(128)S(1)}, s32[128]{0:T(128)}, u32[]{:S(2)}) copy-start(s32[128]{0:T(128)} %param.17) | copy-start | bytes 1540
  30.4 5.2 %copy-start.8 = (bf16[2,3584,1024]{2,1,0:T(8,128)(2,1)S(1)}, bf16[2,3584,1024]{2,1,0:T(8,128)(2,1)}, u32[]{:S(2)}) copy-start(bf16[2,3584,1024]{2,1,0:T(8,128)(2,1)} %weight_ref.7) | copy-start | bytes 44040196
  35.6 4.6 %copy-start.13 = (s32[512]{0:T(512)S(1)}, s32[512]{0:T(512)}, u32[]{:S(2)}) copy-start(s32[512]{0:T(512)} %param.18) | copy-start | bytes 6148
  35.6 13.2 %slice-start.2 = ((s8[14680064]{0:T(1024)(128)(4,1)}), s8[4194304]{0:T(1024)(128)(4,1)S(1)}, s32[]{:S(2)}) async-start(s8[14680064]{0:T(1024)(128)(4,1)} %bitcast.20), calls=%async_computation.2 | async-start | bytes 8388608
  35.6 13.2 %slice-start.3 = ((s8[14680064]{0:T(1024)(128)(4,1)}), s8[4194304]{0:T(1024)(128)(4,1)S(1)}, s32[]{:S(2)}) async-start(s8[14680064]{0:T(1024)(128)(4,1)} %bitcast.20), calls=%async_computation.3 | async-start | bytes 8388608
  35.6 13.2 %slice-start.4 = ((s8[14680064]{0:T(1024)(128)(4,1)}), s8[4194304]{0:T(1024)(128)(4,1)S(1)}, s32[]{:S(2)}) async-start(s8[14680064]{0:T(1024)(128)(4,1)} %bitcast.20), calls=%async_computation.4 | async-start | bytes 8388608
  40.2 8.6 %slice-start.5 = ((s8[14680064]{0:T(1024)(128)(4,1)}), s8[2097152]{0:T(1024)(128)(4,1)S(1)}, s32[]{:S(2)}) async-start(s8[14680064]{0:T(1024)(128)(4,1)} %bitcast.20), calls=%async_computation.5 | async-start | bytes 4194304
  44.3 21.1 %collective-permute-start.6 = (bf16[128,512]{1,0:T(8,128)(2,1)S(1)}, bf16[128,512]{1,0:T(8,128)(2,1)S(1)}, u32[]{:S(2)}, u32[]{:S(2)}) collective-permute-start(bf16[128,512]{1,0:T(8,128)(2,1)S(1)} %get-tuple-element.32), channel_id=1, source_target_pairs={{2,0},{0,2},{6,4},{4,6},{3,1},{1,3},{7,5},{5,7},{10,8},{8,10},{14,... | collective-permute-start | bytes 393224 | tf_op jit(solution)/shard_map/ppermute | solution.py:625
  45.3 20.2 %collective-permute-start.7 = (bf16[128,512]{1,0:T(8,128)(2,1)S(1)}, bf16[128,512]{1,0:T(8,128)(2,1)S(1)}, u32[]{:S(2)}, u32[]{:S(2)}) collective-permute-start(bf16[128,512]{1,0:T(8,128)(2,1)S(1)} %get-tuple-element.33), channel_id=1, source_target_pairs={{4,0},{6,2},{0,4},{2,6},{5,1},{7,3},{1,5},{3,7},{12,8},{14,10},{8,... | collective-permute-start | bytes 393224 | tf_op jit(solution)/shard_map/ppermute | solution.py:625
  48.7 16.7 %collective-permute-start.8 = (bf16[128,512]{1,0:T(8,128)(2,1)S(1)}, bf16[128,512]{1,0:T(8,128)(2,1)S(1)}, u32[]{:S(2)}, u32[]{:S(2)}) collective-permute-start(bf16[128,512]{1,0:T(8,128)(2,1)S(1)} %get-tuple-element.34), channel_id=1, source_target_pairs={{6,0},{4,2},{2,4},{0,6},{7,1},{5,3},{3,5},{1,7},{14,8},{12,10},{10... | collective-permute-start | bytes 393224 | tf_op jit(solution)/shard_map/ppermute | solution.py:625
  53.8 11.7 %slice-start = ((s8[7340032]{0:T(1024)(128)(4,1)}), s8[4194304]{0:T(1024)(128)(4,1)S(1)}, s32[]{:S(2)}) async-start(s8[7340032]{0:T(1024)(128)(4,1)} %bitcast.9), calls=%async_computation | async-start | bytes 8388608
  53.8 16.7 %collective-permute-start.5 = (bf16[128,1792]{1,0:T(8,128)(2,1)S(1)}, bf16[128,1792]{1,0:T(8,128)(2,1)S(1)}, u32[]{:S(2)}, u32[]{:S(2)}) collective-permute-start(bf16[128,1792]{1,0:T(8,128)(2,1)S(1)} %get-tuple-element.26), channel_id=1, source_target_pairs={{0,1},{1,0},{2,3},{3,2},{4,5},{5,4},{6,7},{7,6},{8,9},{9,8},{10,11... | collective-permute-start | bytes 1376264 | tf_op jit(solution)/shard_map/ppermute | solution.py:632
  53.9 5.3 %copy-start.9 = (bf16[2,3584,1024]{2,1,0:T(8,128)(2,1)S(1)}, bf16[2,3584,1024]{2,1,0:T(8,128)(2,1)}, u32[]{:S(2)}) copy-start(bf16[2,3584,1024]{2,1,0:T(8,128)(2,1)} %weight_ref.7) | copy-start | bytes 44040196
  59.2 6.3 %slice-start.1 = ((s8[7340032]{0:T(1024)(128)(4,1)}), s8[3145728]{0:T(1024)(128)(4,1)S(1)}, s32[]{:S(2)}) async-start(s8[7340032]{0:T(1024)(128)(4,1)} %bitcast.9), calls=%async_computation.1 | async-start | bytes 6291456
  65.4 5.9 %copy-start.12 = (bf16[128,1792]{1,0:T(8,128)(2,1)S(1)}, bf16[128,1792]{1,0:T(8,128)(2,1)}, u32[]{:S(2)}) copy-start(bf16[128,1792]{1,0:T(8,128)(2,1)} %inputs_ref.1) | copy-start | bytes 1376260
  68.0 3.3 %collective-permute-start.9 = (bf16[128,1792]{1,0:T(8,128)(2,1)S(1)}, bf16[128,1792]{1,0:T(8,128)(2,1)S(1)}, u32[]{:S(2)}, u32[]{:S(2)}) collective-permute-start(bf16[128,1792]{1,0:T(8,128)(2,1)S(1)} %get-tuple-element.36), channel_id=1, source_target_pairs={{0,1},{1,0},{2,3},{3,2},{4,5},{5,4},{6,7},{7,6},{8,9},{9,8},{10,11... | collective-permute-start | bytes 1376264 | tf_op jit(solution)/shard_map/ppermute | solution.py:650
  68.4 2.9 %collective-permute-start.10 = (f32[1,128]{1,0:T(1,128)S(1)}, f32[1,128]{1,0:T(1,128)S(1)}, u32[]{:S(2)}, u32[]{:S(2)}) collective-permute-start(f32[1,128]{1,0:T(1,128)S(1)} %get-tuple-element.37.refs_2_), channel_id=1, source_target_pairs={{0,1},{1,0},{2,3},{3,2},{4,5},{5,4},{6,7},{7,6},{8,9},{9,8},{10,11... | collective-permute-start | bytes 1544 | tf_op jit(solution)/shard_map/ppermute | solution.py:649

commit v3 on v2

--- a/solution.py
+++ b/solution.py
@@ -68,6 +68,10 @@
     unit_rows = values * factor
     inner_mean = jnp.mean(scaling * upstream * unit_rows, axis=-1, keepdims=True)
     return factor * (scaling * upstream - unit_rows * inner_mean)
+
+
+def streamed(weights):
+    return pltpu.with_memory_space_constraint(weights, pltpu.HBM)
 
 
 def whole(shape):
@@ -138,7 +142,7 @@
 def key_stage(rank, modality, norm_gain, head_gain, weights, parts):
     _, depth, width = weights.shape
     rows = parts[0].shape[0]
-    chunk = tile_of(depth, 1792)
+    chunk = tile_of(depth, 896)
     return pl.pallas_call(
         functools.partial(key_kernel, len(parts), chunk),
         grid=(depth // chunk,),
@@ -195,7 +199,7 @@
 def query_stage(modality, head_gain, weights, normed):
     _, depth, width = weights.shape
     rows = normed.shape[0]
-    chunk = tile_of(depth, 896)
+    chunk = tile_of(depth, 512)
     return pl.pallas_call(
         functools.partial(query_kernel, chunk),
         grid=(depth // chunk,),
@@ -232,7 +236,7 @@
 def cotangent_stage(rank, modality, weights, parts):
     _, width, depth = weights.shape
     rows = parts[0].shape[0]
-    tile = tile_of(width, 256)
+    tile = tile_of(width, 128)
     return pl.pallas_call(
         functools.partial(cotangent_kernel, len(parts)),
         grid=(width // tile,),
@@ -416,7 +420,7 @@
 def query_back_stage(modality, weights, back):
     _, depth, width = weights.shape
     rows = back.shape[0]
-    tile = tile_of(depth, 896)
+    tile = tile_of(depth, 512)
     return pl.pallas_call(
         query_back_kernel,
         grid=(depth // tile,),
@@ -586,19 +590,20 @@
     split = tensor_count == 2
     swap = [(0, 1), (1, 0)]
     rank = tensor_rank.astype(jnp.int32).reshape(1)
-    modality = modality.reshape(1, local_rows)
-    segments = segments.reshape(block_count, local_rows)
+    modality = streamed(modality.reshape(1, local_rows))
+    segments = streamed(segments.reshape(block_count, local_rows))
+    head_gain = streamed(head_gain)
 
     def spread(part):
         if split:
-            return [part, lax.ppermute(part, "tensor", swap)]
+            return [streamed(part), lax.ppermute(part, "tensor", swap)]
         return [lax.all_gather(part, "tensor", axis=1, tiled=True)]
 
     def scatter_columns(part):
         return lax.psum_scatter(part, "tensor", scatter_dimension=1, tiled=True)
 
     memory, key_raw, normed, row_factor = key_stage(
-        rank, modality, norm_gain, head_gain, key_weight, spread(inputs)
+        rank, modality, streamed(norm_gain), head_gain, streamed(key_weight), spread(inputs)
     )
     shared = tensor_count > KV_HEADS
     is_even = tensor_rank % 2 == 0
@@ -616,8 +621,10 @@
         order.append(seq_source(block_rank, step, block_count))
     sources = block_order[jnp.stack(order)]
 
-    query, query_raw = query_stage(modality, head_gain, query_weight, normed)
-    back_attended = cotangent_stage(rank, modality, output_weight, spread(cotangent))
+    query, query_raw = query_stage(modality, head_gain, streamed(query_weight), normed)
+    back_attended = cotangent_stage(
+        rank, modality, streamed(output_weight), spread(cotangent)
+    )
     attended, query_back, inner, own_grad, *grads = attention_stage(
         sources, segments, modality, head_gain, query, query_raw, back_attended, memories
     )
@@ -633,7 +640,7 @@
     else:
         attention_out = scatter_columns(projected[0])
 
-    gradient_part = query_back_stage(modality, query_weight, query_back)
+    gradient_part = query_back_stage(modality, streamed(query_weight), query_back)
 
     if shared:
         total = own_grad + sum(grad.astype(f32) for grad in incoming)
@@ -655,7 +662,7 @@
         backs = [scatter_columns(sent)]
     gain = lax.dynamic_slice_in_dim(norm_gain, tensor_rank * local_width, local_width, 1)
     grad_input = finish(
-        full_width, len(backs), modality, gain, row_factor, inputs, backs, inners
+        full_width, len(backs), modality, gain, row_factor, streamed(inputs), backs, inners
     )
     return (attention_out, grad_input)
 

time: 73 us -> 70.3 us (0.963)
  local copies, waits for them, and re-layouts: 24.3 us -> 1.4 us
  Pallas kernels: 35 us -> 55.2 us
    unnamed x40 -> x14, local copies, waits for them, and re-layouts: 22.9 us -> 0.05 us
    pallas_call x1, Pallas kernels: 4.52 us -> 10.8 us  [query_stage(): pl.pallas_call(functools.partial(query_kernel, chunk), grid=(depth // chu...]
    pallas_call x1, Pallas kernels: 6.22 us -> 10.7 us  [query_back_stage(): pl.pallas_call(query_back_kernel, grid=(depth // tile,), out_shape=jax.Sh...]
    pallas_call x1, Pallas kernels: 6.68 us -> 10.4 us  [cotangent_stage(): pl.pallas_call(functools.partial(cotangent_kernel, len(parts)), grid=(wid...]
    pallas_call x1, Pallas kernels: 2.87 us -> 5.82 us  [key_stage(): pl.pallas_call(functools.partial(key_kernel, len(parts), chunk), grid=(de...]
    pallas_call x1, Pallas kernels: 1.22 us -> 2.26 us  [finish(): pl.pallas_call(kernel, out_shape=jax.ShapeDtypeStruct((rows, width), bf16...]
  transfers between devices with their start and end apart: 11 -> 11, of which waited for: 1 -> 1; matrix products, arithmetic and copies ran while one was open for 3% -> 3% of each run, Pallas kernels for 41% -> 69%
where the time goes in v3:
time: 70.3 us; the launch traced here: 69.9 us
  Pallas kernels  55.2 us (79%)
  starting transfers between devices  11.3 us (16%)
  local copies, waits for them, and re-layouts  1.4 us (2%)
  other arithmetic  0.95 us (1%)
  between operations  0.88 us (1%)
    pallas_call x1, Pallas kernels, query_stage(): pl.pallas_call(functools.partial(query_kernel, chunk), grid=(depth // chu...  10.8 us
    pallas_call x1, Pallas kernels, query_back_stage(): pl.pallas_call(query_back_kernel, grid=(depth // tile,), out_shape=jax.Sh...  10.7 us
    pallas_call x1, Pallas kernels, cotangent_stage(): pl.pallas_call(functools.partial(cotangent_kernel, len(parts)), grid=(wid...  10.4 us
    pallas_call x1, Pallas kernels, key_stage(): pl.pallas_call(functools.partial(key_kernel, len(parts), chunk), grid=(de...  5.82 us
    ppermute x3, starting transfers between devices, local(): memories.append(lax.ppermute(memory, 'seq', seq_pairs(step, block_count)))  5.6 us
    pallas_call x1, Pallas kernels, output_stage(): pl.pallas_call(functools.partial(output_kernel, turns), grid_spec=pltpu.P...  5.26 us
    pallas_call x1, Pallas kernels, attention_stage(): pl.pallas_call(functools.partial(attention_kernel, blocks, per_group), gr...  4.46 us
    ppermute x3, starting transfers between devices, local(): lax.ppermute(grad, 'seq', inverted(seq_pairs(step, block_count)))  4.45 us
  transfers between devices with their start and end apart: 11, of which 1 were waited for; matrix products, arithmetic and copies ran while one was open for 3% of the time, Pallas kernels for 69%

profile of v3, /device:TPU:0, one launch (start us, length us, event | category | flops | bytes accessed | tf_op | source)
XLA Modules:
  0.0 69.9 jit_solution(15746784161933642647)
XLA Ops:
  0.6 0.0 copy-start
  0.6 0.5 collective-permute-start
  1.2 0.1 collective-permute-start.1
  1.2 0.1 fusion
  1.3 0.0 copy-done
  1.3 0.6 gather_fusion
  2.0 0.7 %constant_dynamic-slice_fusion.gain_ref = f32[2,1792]{1,0:T(2,128)S(1)} fusion(f32[2,3584]{1,0:T(2,128)} %refs_2_.2, s32[]{:T(128)S(6)} %select_n.14), kind=kLoop, calls=%fused_computation.5 | loop fusion | bytes 28676 | tf_op jit(solution)/shard_map/dynamic_slice | solution.py:663
  2.7 0.1 collective-permute-done.refs_6_
  2.8 5.8 %key_stage.1 = (bf16[128,512]{1,0:T(8,128)(2,1)S(1)}, f32[128,512]{1,0:T(8,128)S(1)}, bf16[128,3584]{1,0:T(8,128)(2,1)S(1)}, f32[1,128]{1,0:T(1,128)S(1)}) custom-call(s32[1]{0:T(128)} %bitcast.refs_0_.rank_ref, s32[1,128]{1,0:T(1,128)} %bitcast.13, f32[2,3584]{1,0:T(2,128)} %refs_2_.2, f32[2,2,128]{2,1,0:T(2,128)} %head_ref.3, ...), custom_call_target="tpu_custom_call" | custom-call | flops 3000000000 | bytes 6000000 | tf_op jit(solution)/shard_map/key_stage/pallas_call | solution.py:146
  8.6 3.0 %collective-permute-start.2 = (bf16[128,512]{1,0:T(8,128)(2,1)S(1)}, bf16[128,512]{1,0:T(8,128)(2,1)S(1)}, u32[]{:S(2)}, u32[]{:S(2)}) collective-permute-start(bf16[128,512]{1,0:T(8,128)(2,1)S(1)} %get-tuple-element.23.refs_7_), channel_id=1, source_target_pairs={{0,2},{2,0},{4,6},{6,4},{1,3},{3,1},{5,7},{7,5},{8,10},{10,8},{12,... | collective-permute-start | bytes 393224 | tf_op jit(solution)/shard_map/ppermute | solution.py:620
  11.7 2.6 %collective-permute-start.3 = (bf16[128,512]{1,0:T(8,128)(2,1)S(1)}, bf16[128,512]{1,0:T(8,128)(2,1)S(1)}, u32[]{:S(2)}, u32[]{:S(2)}) collective-permute-start(bf16[128,512]{1,0:T(8,128)(2,1)S(1)} %get-tuple-element.23.refs_7_), channel_id=1, source_target_pairs={{0,4},{2,6},{4,0},{6,2},{1,5},{3,7},{5,1},{7,3},{8,12},{10,14},{12... | collective-permute-start | bytes 393224 | tf_op jit(solution)/shard_map/ppermute | solution.py:620
  14.2 0.0 collective-permute-start.4
  14.3 0.0 collective-permute-done.1.refs_4_
  14.3 10.4 %cotangent_stage.1.refs_6_ = bf16[128,1024]{1,0:T(8,128)(2,1)S(1)} custom-call(s32[1]{0:T(128)} %bitcast.refs_0_.rank_ref, s32[1,128]{1,0:T(1,128)} %bitcast.14, bf16[2,1024,3584]{2,1,0:T(8,128)(2,1)} %weight_ref.6, bf16[128,1792]{1,0:T(8,128)(2,1)} %refs_3_.4, bf16[128,1792]{1,0:T(8,128)(2,1)S(1)} %collective-permute-done.1.refs_4_), custom_call_target="tpu_custom_call" | custom-call | flops 7000000000 | bytes 14000000 | tf_op jit(solution)/shard_map/cotangent_stage/pallas_call | solution.py:240
  24.7 0.0 slice-start.2
  24.7 0.0 slice-start.3
  24.7 0.0 slice-start.4
  24.7 10.8 %query_stage.1 = (bf16[128,1024]{1,0:T(8,128)(2,1)S(1)}, f32[128,1024]{1,0:T(8,128)S(1)}) custom-call(s32[1,128]{1,0:T(1,128)} %bitcast.15, f32[2,2,128]{2,1,0:T(2,128)} %head_ref.3, bf16[2,3584,1024]{2,1,0:T(8,128)(2,1)} %weight_ref.7, bf16[128,3584]{1,0:T(8,128)(2,1)S(1)} %get-tuple-element.20.normed_ref), custom_call_target="tpu_custom_call" | custom-call | flops 5000000000 | bytes 10000000 | tf_op jit(solution)/shard_map/query_stage/pallas_call | solution.py:203
  35.6 0.0 collective-permute-done.2.refs_8_
  35.6 0.0 collective-permute-done.3.refs_9_
  35.6 0.0 collective-permute-done.4.refs_10_
  35.6 0.0 slice-start.5
  35.6 4.5 %attention_stage.1 = (bf16[128,1024]{1,0:T(8,128)(2,1)S(1)}, bf16[128,1024]{1,0:T(8,128)(2,1)S(1)}, f32[1,128]{1,0:T(1,128)S(1)}, f32[128,512]{1,0:T(8,128)S(1)}...) custom-call(s32[4]{0:T(128)S(1)} %gather_fusion, s32[4,128]{1,0:T(4,128)} %bitcast.22, ...), custom_call_target="tpu_custom_call" | custom-call | flops 3500000000 | bytes 7000000 | tf_op jit(solution)/shard_map/attention_stage/pallas_call | solution.py:334
  40.1 1.0 %collective-permute-start.6 = (bf16[128,512]{1,0:T(8,128)(2,1)S(1)}, bf16[128,512]{1,0:T(8,128)(2,1)S(1)}, u32[]{:S(2)}, u32[]{:S(2)}) collective-permute-start(bf16[128,512]{1,0:T(8,128)(2,1)S(1)} %get-tuple-element.32), channel_id=1, source_target_pairs={{2,0},{0,2},{6,4},{4,6},{3,1},{1,3},{7,5},{5,7},{10,8},{8,10},{14,... | collective-permute-start | bytes 393224 | tf_op jit(solution)/shard_map/ppermute | solution.py:632
  41.0 3.5 %collective-permute-start.7 = (bf16[128,512]{1,0:T(8,128)(2,1)S(1)}, bf16[128,512]{1,0:T(8,128)(2,1)S(1)}, u32[]{:S(2)}, u32[]{:S(2)}) collective-permute-start(bf16[128,512]{1,0:T(8,128)(2,1)S(1)} %get-tuple-element.33), channel_id=1, source_target_pairs={{4,0},{6,2},{0,4},{2,6},{5,1},{7,3},{1,5},{3,7},{12,8},{14,10},{8,... | collective-permute-start | bytes 393224 | tf_op jit(solution)/shard_map/ppermute | solution.py:632
  44.5 0.0 collective-permute-start.8
  44.5 0.0 slice-done.2
  44.5 0.0 slice-done.3
  44.5 0.0 slice-done.4
  44.5 0.0 slice-done.5
  44.6 5.3 %output_stage.1 = (bf16[128,1792]{1,0:T(8,128)(2,1)S(1)}, f32[128,1792]{1,0:T(8,128)S(1)}) custom-call(s32[1]{0:T(128)} %bitcast.refs_0_.rank_ref, s32[1,128]{1,0:T(1,128)} %bitcast.17, bf16[2,1024,3584]{2,1,0:T(8,128)(2,1)S(1)} %bitcast.12, bf16[128,1024]{1,0:T(8,128)(2,1)S(1)} %get-tuple-element.24.attended_ref), custom_call_target="tpu_custom_call" | custom-call | flops 5000000000 | bytes 10000000 | tf_op jit(solution)/shard_map/output_stage/pallas_call | solution.py:396
  49.8 0.0 slice-start
  49.8 0.1 collective-permute-start.5
  49.9 0.0 slice-start.1
  49.9 10.7 %query_back_stage.1.part_ref = f32[128,3584]{1,0:T(8,128)S(1)} custom-call(s32[1,128]{1,0:T(1,128)} %bitcast.18, bf16[2,3584,1024]{2,1,0:T(8,128)(2,1)} %weight_ref.7, bf16[128,1024]{1,0:T(8,128)(2,1)S(1)} %get-tuple-element.28.back_ref), custom_call_target="tpu_custom_call" | custom-call | flops 7000000000 | bytes 14000000 | tf_op jit(solution)/shard_map/query_back_stage/pallas_call | solution.py:424
  60.6 0.0 collective-permute-done.6.refs_1_
  60.7 0.0 collective-permute-done.7.refs_2_
  60.7 0.0 collective-permute-done.8.refs_3_
  60.7 0.0 slice-done
  60.7 0.0 slice-done.1
  60.7 3.1 %key_back_stage.1 = (bf16[128,1792]{1,0:T(8,128)(2,1)S(1)}, bf16[128,512]{1,0:T(8,128)(2,1)S(1)}, f32[1,128]{1,0:T(1,128)S(1)}) custom-call(s32[1]{0:T(128)} %bitcast.refs_0_.rank_ref, s32[1,128]{1,0:T(1,128)} %bitcast.19, f32[2,2,128]{2,1,0:T(2,128)} %head_ref.3, f32[128,512]{1,0:T(8,128)S(1)} %get-tuple-element.29.raw_ref, ...), custom_call_target="tpu_custom_call" | custom-call | flops 2000000000 | bytes 4000000 | tf_op jit(solution)/shard_map/key_back_stage/pallas_call | solution.py:479
  63.8 0.1 collective-permute-start.9
  63.9 0.5 collective-permute-start.10
  64.4 2.3 %kept_stage.1.refs_0_ = f32[128,1792]{1,0:T(8,128)S(1)} custom-call(s32[1]{0:T(128)} %bitcast.refs_0_.rank_ref, s32[1,128]{1,0:T(1,128)} %bitcast.20, f32[128,3584]{1,0:T(8,128)S(1)} %query_back_stage.1.part_ref, bf16[2,3584,512]{2,1,0:T(8,128)(2,1)S(1)} %bitcast.10, bf16[128,512]{1,0:T(8,128)(2,1)S(1)} %get-tuple-element.35.back_ref), custom_call_target="tpu_custom_call" | custom-call | flops 2000000000 | bytes 4000000 | tf_op jit(solution)/shard_map/kept_stage/pallas_call | solution.py:520
  66.7 0.0 collective-permute-done.5
  66.7 0.9 %add_convert_fusion = bf16[128,1792]{1,0:T(8,128)(2,1)} fusion(f32[128,1792]{1,0:T(8,128)S(1)} %get-tuple-element.25, bf16[128,1792]{1,0:T(8,128)(2,1)S(1)} %collective-permute-done.5), kind=kLoop, calls=%fused_computation.1 | loop fusion | flops 688128 | bytes 1835008 | tf_op jit(solution)/shard_map/convert_element_type | solution.py:639
  67.6 0.0 collective-permute-done.10.refs_3_
  67.6 0.0 collective-permute-done.9.refs_1_
  67.6 2.3 %finish.1 = bf16[128,1792]{1,0:T(8,128)(2,1)} custom-call(s32[1,128]{1,0:T(1,128)} %bitcast.21, f32[2,1792]{1,0:T(2,128)S(1)} %constant_dynamic-slice_fusion.gain_ref, f32[1,128]{1,0:T(1,128)S(1)} %get-tuple-element.27.factor_ref, bf16[128,1792]{1,0:T(8,128)(2,1)} %inputs_ref.1, f32[128,1792]{1,0:T(8,128)S(1)} %kept_stage.1.refs_0_, ...), custom_call_target="tpu_custom_call" | custom-call | flops 1000000000 | bytes 2000000 | tf_op jit(solution)/shard_map/finish/pallas_call | solution.py:560
  (3 shorter events, 0.0 us)
Async XLA Ops:
  0.6 0.7 %copy-start = (s32[4]{0:T(128)S(1)}, s32[4]{0:T(128)}, u32[]{:S(2)}) copy-start(s32[4]{0:T(128)} %param.19) | copy-start | bytes 52
  0.6 2.2 %collective-permute-start = (bf16[128,1792]{1,0:T(8,128)(2,1)}, bf16[128,1792]{1,0:T(8,128)(2,1)S(1)}, u32[]{:S(2)}, u32[]{:S(2)}) collective-permute-start(bf16[128,1792]{1,0:T(8,128)(2,1)} %inputs_ref.1), channel_id=1, source_target_pairs={{0,1},{1,0},{2,3},{3,2},{4,5},{5,4},{6,7},{7,6},{8,9},{9,8},{10,11... | collective-permute-start | bytes 1376264 | tf_op jit(solution)/shard_map/ppermute | solution.py:599
  1.2 13.1 %collective-permute-start.1 = (bf16[128,1792]{1,0:T(8,128)(2,1)}, bf16[128,1792]{1,0:T(8,128)(2,1)S(1)}, u32[]{:S(2)}, u32[]{:S(2)}) collective-permute-start(bf16[128,1792]{1,0:T(8,128)(2,1)} %refs_3_.4), channel_id=1, source_target_pairs={{0,1},{1,0},{2,3},{3,2},{4,5},{5,4},{6,7},{7,6},{8,9},{9,8},{10,11... | collective-permute-start | bytes 1376264 | tf_op jit(solution)/shard_map/ppermute | solution.py:599
  8.6 26.9 %collective-permute-start.2 = (bf16[128,512]{1,0:T(8,128)(2,1)S(1)}, bf16[128,512]{1,0:T(8,128)(2,1)S(1)}, u32[]{:S(2)}, u32[]{:S(2)}) collective-permute-start(bf16[128,512]{1,0:T(8,128)(2,1)S(1)} %get-tuple-element.23.refs_7_), channel_id=1, source_target_pairs={{0,2},{2,0},{4,6},{6,4},{1,3},{3,1},{5,7},{7,5},{8,10},{10,8},{12,... | collective-permute-start | bytes 393224 | tf_op jit(solution)/shard_map/ppermute | solution.py:620
  11.7 23.9 %collective-permute-start.3 = (bf16[128,512]{1,0:T(8,128)(2,1)S(1)}, bf16[128,512]{1,0:T(8,128)(2,1)S(1)}, u32[]{:S(2)}, u32[]{:S(2)}) collective-permute-start(bf16[128,512]{1,0:T(8,128)(2,1)S(1)} %get-tuple-element.23.refs_7_), channel_id=1, source_target_pairs={{0,4},{2,6},{4,0},{6,2},{1,5},{3,7},{5,1},{7,3},{8,12},{10,14},{12... | collective-permute-start | bytes 393224 | tf_op jit(solution)/shard_map/ppermute | solution.py:620
  14.2 21.3 %collective-permute-start.4 = (bf16[128,512]{1,0:T(8,128)(2,1)S(1)}, bf16[128,512]{1,0:T(8,128)(2,1)S(1)}, u32[]{:S(2)}, u32[]{:S(2)}) collective-permute-start(bf16[128,512]{1,0:T(8,128)(2,1)S(1)} %get-tuple-element.23.refs_7_), channel_id=1, source_target_pairs={{0,6},{2,4},{4,2},{6,0},{1,7},{3,5},{5,3},{7,1},{8,14},{10,12},{12... | collective-permute-start | bytes 393224 | tf_op jit(solution)/shard_map/ppermute | solution.py:620
  24.7 19.9 %slice-start.2 = ((s8[14680064]{0:T(1024)(128)(4,1)}), s8[4194304]{0:T(1024)(128)(4,1)S(1)}, s32[]{:S(2)}) async-start(s8[14680064]{0:T(1024)(128)(4,1)} %bitcast.11), calls=%async_computation.2 | async-start | bytes 8388608
  24.7 19.8 %slice-start.3 = ((s8[14680064]{0:T(1024)(128)(4,1)}), s8[4194304]{0:T(1024)(128)(4,1)S(1)}, s32[]{:S(2)}) async-start(s8[14680064]{0:T(1024)(128)(4,1)} %bitcast.11), calls=%async_computation.3 | async-start | bytes 8388608
  24.7 19.8 %slice-start.4 = ((s8[14680064]{0:T(1024)(128)(4,1)}), s8[4194304]{0:T(1024)(128)(4,1)S(1)}, s32[]{:S(2)}) async-start(s8[14680064]{0:T(1024)(128)(4,1)} %bitcast.11), calls=%async_computation.4 | async-start | bytes 8388608
  35.6 9.0 %slice-start.5 = ((s8[14680064]{0:T(1024)(128)(4,1)}), s8[2097152]{0:T(1024)(128)(4,1)S(1)}, s32[]{:S(2)}) async-start(s8[14680064]{0:T(1024)(128)(4,1)} %bitcast.11), calls=%async_computation.5 | async-start | bytes 4194304
  40.1 20.6 %collective-permute-start.6 = (bf16[128,512]{1,0:T(8,128)(2,1)S(1)}, bf16[128,512]{1,0:T(8,128)(2,1)S(1)}, u32[]{:S(2)}, u32[]{:S(2)}) collective-permute-start(bf16[128,512]{1,0:T(8,128)(2,1)S(1)} %get-tuple-element.32), channel_id=1, source_target_pairs={{2,0},{0,2},{6,4},{4,6},{3,1},{1,3},{7,5},{5,7},{10,8},{8,10},{14,... | collective-permute-start | bytes 393224 | tf_op jit(solution)/shard_map/ppermute | solution.py:632
  41.0 19.6 %collective-permute-start.7 = (bf16[128,512]{1,0:T(8,128)(2,1)S(1)}, bf16[128,512]{1,0:T(8,128)(2,1)S(1)}, u32[]{:S(2)}, u32[]{:S(2)}) collective-permute-start(bf16[128,512]{1,0:T(8,128)(2,1)S(1)} %get-tuple-element.33), channel_id=1, source_target_pairs={{4,0},{6,2},{0,4},{2,6},{5,1},{7,3},{1,5},{3,7},{12,8},{14,10},{8,... | collective-permute-start | bytes 393224 | tf_op jit(solution)/shard_map/ppermute | solution.py:632
  44.5 16.2 %collective-permute-start.8 = (bf16[128,512]{1,0:T(8,128)(2,1)S(1)}, bf16[128,512]{1,0:T(8,128)(2,1)S(1)}, u32[]{:S(2)}, u32[]{:S(2)}) collective-permute-start(bf16[128,512]{1,0:T(8,128)(2,1)S(1)} %get-tuple-element.34), channel_id=1, source_target_pairs={{6,0},{4,2},{2,4},{0,6},{7,1},{5,3},{3,5},{1,7},{14,8},{12,10},{10... | collective-permute-start | bytes 393224 | tf_op jit(solution)/shard_map/ppermute | solution.py:632
  49.8 10.9 %slice-start = ((s8[7340032]{0:T(1024)(128)(4,1)}), s8[4194304]{0:T(1024)(128)(4,1)S(1)}, s32[]{:S(2)}) async-start(s8[7340032]{0:T(1024)(128)(4,1)} %bitcast.9), calls=%async_computation | async-start | bytes 8388608
  49.8 16.9 %collective-permute-start.5 = (bf16[128,1792]{1,0:T(8,128)(2,1)S(1)}, bf16[128,1792]{1,0:T(8,128)(2,1)S(1)}, u32[]{:S(2)}, u32[]{:S(2)}) collective-permute-start(bf16[128,1792]{1,0:T(8,128)(2,1)S(1)} %get-tuple-element.26), channel_id=1, source_target_pairs={{0,1},{1,0},{2,3},{3,2},{4,5},{5,4},{6,7},{7,6},{8,9},{9,8},{10,11... | collective-permute-start | bytes 1376264 | tf_op jit(solution)/shard_map/ppermute | solution.py:639
  49.9 10.8 %slice-start.1 = ((s8[7340032]{0:T(1024)(128)(4,1)}), s8[3145728]{0:T(1024)(128)(4,1)S(1)}, s32[]{:S(2)}) async-start(s8[7340032]{0:T(1024)(128)(4,1)} %bitcast.9), calls=%async_computation.1 | async-start | bytes 6291456
  63.8 3.8 %collective-permute-start.9 = (bf16[128,1792]{1,0:T(8,128)(2,1)S(1)}, bf16[128,1792]{1,0:T(8,128)(2,1)S(1)}, u32[]{:S(2)}, u32[]{:S(2)}) collective-permute-start(bf16[128,1792]{1,0:T(8,128)(2,1)S(1)} %get-tuple-element.36), channel_id=1, source_target_pairs={{0,1},{1,0},{2,3},{3,2},{4,5},{5,4},{6,7},{7,6},{8,9},{9,8},{10,11... | collective-permute-start | bytes 1376264 | tf_op jit(solution)/shard_map/ppermute | solution.py:657
  63.9 3.7 %collective-permute-start.10 = (f32[1,128]{1,0:T(1,128)S(1)}, f32[1,128]{1,0:T(1,128)S(1)}, u32[]{:S(2)}, u32[]{:S(2)}) collective-permute-start(f32[1,128]{1,0:T(1,128)S(1)} %get-tuple-element.37.refs_2_), channel_id=1, source_target_pairs={{0,1},{1,0},{2,3},{3,2},{4,5},{5,4},{6,7},{7,6},{8,9},{9,8},{10,11... | collective-permute-start | bytes 1544 | tf_op jit(solution)/shard_map/ppermute | solution.py:656

commit v4 on v2

v4 whole, which is shorter than its diff:
```python
import functools
import math

import jax
import jax.numpy as jnp
from jax import lax
from jax.experimental import pallas as pl
from jax.experimental.pallas import tpu as pltpu
from jax.sharding import PartitionSpec as P

KV_HEADS = 4
HEAD_DIM = 128
MIB = 1024 * 1024

epsilon = 1e-06
bf16 = jnp.bfloat16
f32 = jnp.float32
SMEM = pl.BlockSpec(memory_space=pltpu.SMEM)
VMEM = pl.BlockSpec(memory_space=pltpu.VMEM)
ANY = pl.BlockSpec(memory_space=pl.ANY)


def seq_pairs(step, count):
    if count & (count - 1) == 0:
        return [(i, i ^ step) for i in range(count)]
    return [(i, (i + step) % count) for i in range(count)]


def seq_source(rank, step, count):
    if count & (count - 1) == 0:
        return rank ^ step
    return (rank - step) % count


def inverted(pairs):
    return [(b, a) for a, b in pairs]


def tile_of(extent, most):
    best = HEAD_DIM
    for size in range(HEAD_DIM, min(extent, most) + 1, HEAD_DIM):
        if extent % size == 0:
            best = size
    return best


def dot_nt(a, b):
    return lax.dot_general(a, b, (((1,), (1,)), ((), ())), preferred_element_type=f32)


def dot_tn(a, b):
    return lax.dot_general(a, b, (((0,), (0,)), ((), ())), preferred_element_type=f32)


def column(row):
    count = row.shape[1]
    return jnp.broadcast_to(row.astype(f32), (count, count)).T[:, :1]


def row_of(col):
    count = col.shape[0]
    return jnp.broadcast_to(col, (count, count)).T[:1, :]


def inverse_norm(values):
    return lax.rsqrt(jnp.mean(values * values, axis=-1, keepdims=True) + epsilon)


def norm_back(values, factor, scaling, upstream):
    unit_rows = values * factor
    inner_mean = jnp.mean(scaling * upstream * unit_rows, axis=-1, keepdims=True)
    return factor * (scaling * upstream - unit_rows * inner_mean)


def streamed(weights):
    return pltpu.with_memory_space_constraint(weights, pltpu.HBM)


def params(mib):
    return pltpu.CompilerParams(vmem_limit_bytes=mib * MIB)


def cost(micros):
    return pl.CostEstimate(
        flops=int(micros * 1e9), bytes_accessed=int(micros * 2e6), transcendentals=0
    )


def in_order(rank, part_refs):
    if len(part_refs) == 1:
        return part_refs[0][...]
    own, other = part_refs[0][...], part_refs[1][...]
    first = rank == 0
    return jnp.concatenate([jnp.where(first, own, other), jnp.where(first, other, own)], axis=1)


def both_experts(image, rows, weights):
    zero = jnp.zeros_like(rows)
    masked = jnp.concatenate([jnp.where(image, zero, rows), jnp.where(image, rows, zero)], axis=1)
    flat = weights.reshape(2 * weights.shape[1], weights.shape[2])
    return jnp.dot(masked, flat, preferred_element_type=f32)


def both_back(image, rows, weights):
    return jnp.where(image, dot_nt(rows, weights[1]), dot_nt(rows, weights[0]))


def chunks_of(extent, most):
    size = tile_of(extent, most)
    return [(start, size) for start in range(0, extent, size)]


AHEAD = 4


def copies_of(source_ref, target_ref, sem_ref, pieces, base=0, slots=0):
    copies = []
    for index, (start, size) in enumerate(pieces):
        pair = []
        for e in range(2):
            if slots:
                target = target_ref.at[index % slots, e]
            else:
                target = target_ref.at[e, pl.ds(start, size), :]
            source = source_ref.at[e, pl.ds(base + start, size), :]
            pair.append(pltpu.make_async_copy(source, target, sem_ref.at[index, e]))
        copies.append(pair)
    return copies


def begin(copies, index):
    if index < len(copies):
        for copy in copies[index]:
            copy.start()


def begin_first(copies):
    for index in range(AHEAD):
        begin(copies, index)


def arrive(copies, index):
    for copy in copies[index]:
        copy.wait()


def ring(weights, pieces):
    return pltpu.VMEM((AHEAD, 2, pieces[0][1], weights.shape[2]), weights.dtype)


def resident(weights):
    return pltpu.VMEM(weights.shape, weights.dtype)


def fetch_kernel(pieces, weight_ref, held_ref, sem_ref):
    copies = copies_of(weight_ref, held_ref, sem_ref, pieces)
    for pair in copies:
        for copy in pair:
            copy.start()
    for pair in copies:
        for copy in pair:
            copy.wait()


def fetch(weights):
    pieces = chunks_of(weights.shape[1], 896)
    return pl.pallas_call(
        functools.partial(fetch_kernel, pieces),
        out_shape=resident(weights),
        in_specs=[ANY],
        out_specs=VMEM,
        scratch_shapes=[pltpu.SemaphoreType.DMA((len(pieces), 2))],
        compiler_params=params(4),
        cost_estimate=cost(0.2),
        name="fetch",
    )(streamed(weights))


def key_kernel(count, *refs):
    rank_ref, modality_ref, gain_ref, head_ref, weight_ref = refs[:5]
    part_refs = refs[5 : 5 + count]
    memory_ref, raw_ref, normed_ref, factor_ref = refs[5 + count :]
    image = column(modality_ref[...]) > 0.0
    rows = in_order(rank_ref[0], part_refs).astype(f32)
    factor = inverse_norm(rows)
    scaling = jnp.where(image, gain_ref[1:2, :], gain_ref[0:1, :])
    normed_ref[...] = (rows * factor * scaling).astype(bf16)
    factor_ref[...] = row_of(factor)
    for index, (start, size) in enumerate(chunks_of(normed_ref.shape[1], 1792)):
        part = slice(start, start + size)
        product = both_experts(image, normed_ref[:, part], weight_ref[:, part, :])
        if index == 0:
            raw_ref[...] = product
        else:
            raw_ref[...] += product
    blocks = raw_ref.shape[1] // HEAD_DIM
    scaling = jnp.where(image, head_ref[1, 1:2, :], head_ref[0, 1:2, :])
    for b in range(blocks):
        part = slice(b * HEAD_DIM, (b + 1) * HEAD_DIM)
        raw = raw_ref[:, part]
        normed = raw * inverse_norm(raw) * scaling
        is_key = (rank_ref[0] * blocks + b) % 2 == 0
        memory_ref[:, part] = jnp.where(is_key, normed, raw).astype(bf16)


def key_stage(rank, modality, norm_gain, head_gain, weights, parts):
    _, depth, width = weights.shape
    rows = parts[0].shape[0]
    return pl.pallas_call(
        functools.partial(key_kernel, len(parts)),
        out_shape=[
            jax.ShapeDtypeStruct((rows, width), bf16),
            jax.ShapeDtypeStruct((rows, width), f32),
            jax.ShapeDtypeStruct((rows, depth), bf16),
            jax.ShapeDtypeStruct((1, rows), f32),
        ],
        in_specs=[SMEM] + [VMEM] * (4 + len(parts)),
        out_specs=[VMEM] * 4,
        compiler_params=params(12),
        cost_estimate=cost(0.2),
        name="key_stage",
    )(rank, modality, norm_gain, head_gain, weights, *parts)


def middle_kernel(count, output_pieces, query_pieces, *refs):
    rank_ref, modality_ref, head_ref, normed_ref, output_ref, query_weight_ref = refs[:6]
    part_refs = refs[6 : 6 + count]
    query_ref, raw_ref, back_ref, output_held = refs[6 + count : 10 + count]
    query_slots, output_sems, query_sems = refs[10 + count :]
    copies = copies_of(output_ref, output_held, output_sems, output_pieces)
    copies += copies_of(query_weight_ref, query_slots, query_sems, query_pieces, slots=AHEAD)
    begin_first(copies)
    image = column(modality_ref[...]) > 0.0
    cotangent = in_order(rank_ref[0], part_refs)
    for index, (start, size) in enumerate(output_pieces):
        arrive(copies, index)
        part = slice(start, start + size)
        back_ref[:, part] = both_back(image, cotangent, output_held[:, part, :]).astype(bf16)
        begin(copies, index + AHEAD)
    for index, (start, size) in enumerate(query_pieces):
        place = len(output_pieces) + index
        arrive(copies, place)
        part = slice(start, start + size)
        product = both_experts(image, normed_ref[:, part], query_slots[index % AHEAD])
        if index == 0:
            raw_ref[...] = product
        else:
            raw_ref[...] += product
        begin(copies, place + AHEAD)
    scaling = jnp.where(image, head_ref[1, 0:1, :], head_ref[0, 0:1, :])
    for h in range(raw_ref.shape[1] // HEAD_DIM):
        part = slice(h * HEAD_DIM, (h + 1) * HEAD_DIM)
        raw = raw_ref[:, part]
        query_ref[:, part] = (raw * inverse_norm(raw) * scaling).astype(bf16)


def middle_stage(rank, modality, head_gain, normed, output_weight, query_weight, parts):
    rows = normed.shape[0]
    width = query_weight.shape[2]
    output_pieces = chunks_of(output_weight.shape[1], 128)
    query_pieces = chunks_of(query_weight.shape[1], 512)
    return pl.pallas_call(
        functools.partial(middle_kernel, len(parts), output_pieces, query_pieces),
        out_shape=[
            jax.ShapeDtypeStruct((rows, width), bf16),
            jax.ShapeDtypeStruct((rows, width), f32),
            jax.ShapeDtypeStruct((rows, width), bf16),
            resident(output_weight),
        ],
        in_specs=[SMEM, VMEM, VMEM, VMEM, ANY, ANY] + [VMEM] * len(parts),
        out_specs=[VMEM] * 4,
        scratch_shapes=[
            ring(query_weight, query_pieces),
            pltpu.SemaphoreType.DMA((len(output_pieces), 2)),
            pltpu.SemaphoreType.DMA((len(query_pieces), 2)),
        ],
        compiler_params=params(16),
        cost_estimate=cost(0.2),
        name="middle_stage",
    )(rank, modality, head_gain, normed, streamed(output_weight), streamed(query_weight), *parts)


def attention_kernel(blocks, pairs, per_group, *refs):
    for pair in range(pairs):
        wide = pl.ds(pair * per_group * HEAD_DIM, per_group * HEAD_DIM)
        narrow = pl.ds(pair * 2 * HEAD_DIM, 2 * HEAD_DIM)
        views = list(refs[:4]) + [ref.at[:, wide] for ref in refs[4:7]]
        views += [ref.at[:, narrow] for ref in refs[7 : 7 + blocks]]
        views += [ref.at[:, wide] for ref in refs[7 + blocks : 9 + blocks]]
        views += [refs[9 + blocks]]
        views += [ref.at[:, narrow] for ref in refs[10 + blocks :]]
        attention_pair(blocks, per_group, pair == 0, *views)


def attention_pair(blocks, per_group, fresh, *refs):
    source_ref, segments_ref, modality_ref, head_ref, query_ref, raw_ref, back_ref = refs[:7]
    memory_refs = refs[7 : 7 + blocks]
    attended_ref, query_back_ref, inner_ref = refs[7 + blocks : 10 + blocks]
    grad_refs = refs[10 + blocks :]
    rows = query_ref.shape[0]
    scale = 1.0 / math.sqrt(HEAD_DIM)

    def heads(ref):
        return jnp.concatenate(
            [ref[:, h * HEAD_DIM : (h + 1) * HEAD_DIM] for h in range(per_group)], axis=0
        )

    query, back = heads(query_ref), heads(back_ref)
    key = jnp.concatenate([m[:, :HEAD_DIM] for m in memory_refs], axis=0)
    value = jnp.concatenate([m[:, HEAD_DIM:] for m in memory_refs], axis=0)
    key_segments = jnp.concatenate(
        [segments_ref[pl.ds(source_ref[b], 1), :] for b in range(blocks)], axis=1
    )
    query_segments = column(segments_ref[pl.ds(source_ref[0], 1), :])
    visible = jnp.where(key_segments.astype(f32) <= query_segments, 1.0, 0.0)
    visible = jnp.concatenate([visible] * per_group, axis=0)
    scores = dot_nt(query, key) * scale
    weights = jnp.where(visible > 0.0, jnp.exp(scores), 0.0).astype(bf16)
    weights32 = weights.astype(f32)
    denominator = jnp.sum(weights32, axis=1, keepdims=True)
    numerator = jnp.dot(weights, value, preferred_element_type=f32)
    attended = (numerator / denominator).astype(bf16)
    offset = jnp.sum(back.astype(f32) * attended.astype(f32), axis=1, keepdims=True)
    probability = (weights32 / denominator).astype(bf16)
    back_prob = dot_nt(back, value)
    back_score = (probability.astype(f32) * (back_prob - offset)).astype(bf16)
    back_query = jnp.dot(back_score, key, preferred_element_type=f32) * scale
    back_key = dot_tn(back_score, query) * scale
    back_value = dot_tn(probability, back)
    for b in range(blocks):
        part = slice(b * rows, (b + 1) * rows)
        grad_refs[b][:, :HEAD_DIM] = back_key[part].astype(grad_refs[b].dtype)
        grad_refs[b][:, HEAD_DIM:] = back_value[part].astype(grad_refs[b].dtype)
    image = column(modality_ref[...]) > 0.0
    scaling = jnp.where(image, head_ref[1, 0:1, :], head_ref[0, 0:1, :])
    inner = jnp.zeros((rows, 1), f32)
    for h in range(per_group):
        part = slice(h * rows, (h + 1) * rows)
        columns = slice(h * HEAD_DIM, (h + 1) * HEAD_DIM)
        attended_ref[:, columns] = attended[part]
        raw = raw_ref[:, columns]
        query_back = norm_back(raw, inverse_norm(raw), scaling, back_query[part]).astype(bf16)
        query_back_ref[:, columns] = query_back
        inner += jnp.sum(query_back.astype(f32) * raw, axis=1, keepdims=True)
    inner = row_of(inner)

    if fresh:
        inner_ref[...] = inner
    else:
        inner_ref[...] += inner


def attention_stage(sources, segments, modality, head_gain, query, raw, back, memories):
    rows, width = query.shape
    blocks = len(memories)
    pairs = memories[0].shape[1] // (2 * HEAD_DIM)
    per_group = width // HEAD_DIM // pairs
    outs = [
        jax.ShapeDtypeStruct((rows, width), bf16),
        jax.ShapeDtypeStruct((rows, width), bf16),
        jax.ShapeDtypeStruct((1, rows), f32),
    ] + [
        jax.ShapeDtypeStruct((rows, pairs * 2 * HEAD_DIM), f32 if b == 0 else bf16)
        for b in range(blocks)
    ]
    return pl.pallas_call(
        functools.partial(attention_kernel, blocks, pairs, per_group),
        out_shape=outs,
        in_specs=[SMEM] + [VMEM] * (6 + blocks),
        out_specs=[VMEM] * (3 + blocks),
        compiler_params=params(16),
        cost_estimate=cost(0.2),
        name="attention_stage",
    )(sources, segments, modality, head_gain, query, raw, back, *memories)


def half(rank, extent, other):
    size = extent // 2
    place = 1 - rank if other else rank
    return pl.ds(pl.multiple_of(place * size, HEAD_DIM), size)


def turn_kernel(pieces, outputs, *refs):
    rank_ref, modality_ref, output_ref, attended_ref, back_ref, query_ref = refs[:6]
    out_refs = refs[6 : 6 + outputs]
    part_ref, slots, sems = refs[6 + outputs :]
    copies = copies_of(query_ref, slots, sems, pieces, slots=AHEAD)
    begin_first(copies)
    image = column(modality_ref[...]) > 0.0
    attended = attended_ref[...]
    width = output_ref.shape[2]
    if outputs == 1:
        out_refs[0][...] = both_experts(image, attended, output_ref[...]).astype(bf16)
    else:
        sent_ref, kept_ref = out_refs
        weights = output_ref[:, :, half(rank_ref[0], width, True)]
        sent_ref[...] = both_experts(image, attended, weights).astype(bf16)
        weights = output_ref[:, :, half(rank_ref[0], width, False)]
        kept_ref[...] = both_experts(image, attended, weights)
    for index, (start, size) in enumerate(pieces):
        arrive(copies, index)
        part = slice(start, start + size)
        part_ref[:, part] = both_back(image, back_ref[...], slots[index % AHEAD])
        begin(copies, index + AHEAD)


def turn_stage(rank, modality, output_held, attended, query_back, query_weight, split):
    depth = query_weight.shape[1]
    width = output_held.shape[2]
    rows = attended.shape[0]
    pieces = chunks_of(depth, 512)
    if split:
        outs = [
            jax.ShapeDtypeStruct((rows, width // 2), bf16),
            jax.ShapeDtypeStruct((rows, width // 2), f32),
        ]
    else:
        outs = [jax.ShapeDtypeStruct((rows, width), bf16)]
    *projected, part = pl.pallas_call(
        functools.partial(turn_kernel, pieces, len(outs)),
        out_shape=outs + [jax.ShapeDtypeStruct((rows, depth), f32)],
        in_specs=[SMEM, VMEM, VMEM, VMEM, VMEM, ANY],
        out_specs=[VMEM] * (len(outs) + 1),
        scratch_shapes=[
            ring(query_weight, pieces),
            pltpu.SemaphoreType.DMA((len(pieces), 2)),
        ],
        compiler_params=params(16),
        cost_estimate=cost(0.2),
        name="turn_stage",
    )(rank, modality, output_held, attended, query_back, streamed(query_weight))
    return projected, part


def back_pieces(depth, split):
    return chunks_of(depth // 2 if split else depth, 896)


def key_back_kernel(split, *refs):
    rank_ref, modality_ref, head_ref, raw_ref, inner_in_ref, part_ref, weight_ref = refs[:7]
    grad_refs = refs[8:-6]
    out_ref, back_ref, inner_ref = refs[-6:-3]
    held, sems = refs[-2:]
    depth = part_ref.shape[1]
    base = pl.multiple_of((1 - rank_ref[0]) * (depth // 2), HEAD_DIM) if split else 0
    pieces = back_pieces(depth, split)
    copies = copies_of(weight_ref, held, sems, pieces, base)
    for index in range(len(copies)):
        begin(copies, index)
    image = column(modality_ref[...]) > 0.0
    blocks = raw_ref.shape[1] // HEAD_DIM
    scaling = jnp.where(image, head_ref[1, 1:2, :], head_ref[0, 1:2, :])
    inner = jnp.zeros((raw_ref.shape[0], 1), f32)
    for b in range(blocks):
        part = slice(b * HEAD_DIM, (b + 1) * HEAD_DIM)
        raw = raw_ref[:, part]
        upstream = grad_refs[0][:, part].astype(f32)
        for grad_ref in grad_refs[1:]:
            upstream += grad_ref[:, part].astype(f32)
        is_key = (rank_ref[0] * blocks + b) % 2 == 0
        normed_back = norm_back(raw, inverse_norm(raw), scaling, upstream)
        back = jnp.where(is_key, normed_back, upstream).astype(bf16)
        back_ref[:, part] = back
        inner += jnp.sum(back.astype(f32) * raw, axis=1, keepdims=True)
    inner_ref[...] = inner_in_ref[...] + row_of(inner)
    for index, (start, size) in enumerate(pieces):
        arrive(copies, index)
        part = slice(start, start + size)
        product = both_back(image, back_ref[...], held[:, part, :])
        given = part_ref[:, pl.ds(base + start, size)]
        out_ref[:, part] = (product + given).astype(bf16)


def key_back_stage(rank, modality, head_gain, raw, inner, part, weights, passed, grads, split):
    _, depth, width = weights.shape
    rows = raw.shape[0]
    pieces = back_pieces(depth, split)
    extent = depth // 2 if split else depth
    return pl.pallas_call(
        functools.partial(key_back_kernel, split),
        out_shape=[
            jax.ShapeDtypeStruct((rows, extent), bf16),
            jax.ShapeDtypeStruct((rows, width), bf16),
            jax.ShapeDtypeStruct((1, rows), f32),
            jax.ShapeDtypeStruct(passed.shape, passed.dtype),
        ],
        in_specs=[SMEM] + [VMEM] * 5 + [ANY, ANY] + [VMEM] * len(grads),
        out_specs=[VMEM] * 3 + [ANY],
        scratch_shapes=[
            pltpu.VMEM((2, extent, width), bf16),
            pltpu.SemaphoreType.DMA((len(pieces), 2)),
        ],
        input_output_aliases={7: 3},
        compiler_params=params(12),
        cost_estimate=cost(0.2),
        name="key_back_stage",
    )(rank, modality, head_gain, raw, inner, part, streamed(weights), passed, *grads)


def kept_kernel(rank_ref, modality_ref, part_ref, weight_ref, back_ref, out_ref, held, sems):
    depth = part_ref.shape[1]
    base = pl.multiple_of(rank_ref[0] * (depth // 2), HEAD_DIM)
    pieces = back_pieces(depth, True)
    copies = copies_of(weight_ref, held, sems, pieces, base)
    for index in range(len(copies)):
        begin(copies, index)
    image = column(modality_ref[...]) > 0.0
    for index, (start, size) in enumerate(pieces):
        arrive(copies, index)
        part = slice(start, start + size)
        product = both_back(image, back_ref[...], held[:, part, :])
        out_ref[:, part] = product + part_ref[:, pl.ds(base + start, size)]


def kept_stage(rank, modality, part, weights, back):
    _, depth, width = weights.shape
    pieces = back_pieces(depth, True)
    return pl.pallas_call(
        kept_kernel,
        out_shape=jax.ShapeDtypeStruct((back.shape[0], depth // 2), f32),
        in_specs=[SMEM, VMEM, VMEM, ANY, VMEM],
        out_specs=VMEM,
        scratch_shapes=[
            pltpu.VMEM((2, depth // 2, width), bf16),
            pltpu.SemaphoreType.DMA((len(pieces), 2)),
        ],
        compiler_params=params(12),
        cost_estimate=cost(0.2),
        name="kept_stage",
    )(rank, modality, part, streamed(weights), back)


def finish(total_width, count, modality, gain, factor, inputs, backs, inners):
    rows, width = inputs.shape

    def kernel(modality_ref, gain_ref, factor_ref, inputs_ref, *refs):
        back_refs = refs[:count]
        inner_refs, out_ref = refs[count:-1], refs[-1]
        image = column(modality_ref[...]) > 0.0
        scaling = jnp.where(image, gain_ref[1:2, :], gain_ref[0:1, :])
        factor_column = column(factor_ref[...])
        back = back_refs[0][...].astype(f32)
        for ref in back_refs[1:]:
            back += ref[...].astype(f32)
        inner = inner_refs[0][...]
        for ref in inner_refs[1:]:
            inner += ref[...]
        unit_rows = inputs_ref[...].astype(f32) * factor_column
        inner_mean = column(inner) * (1.0 / total_width)
        out_ref[...] = (factor_column * (scaling * back - unit_rows * inner_mean)).astype(bf16)

    arrays = [modality, gain, factor, inputs, *backs, *inners]
    return pl.pallas_call(
        kernel,
        out_shape=jax.ShapeDtypeStruct((rows, width), bf16),
        in_specs=[VMEM] * len(arrays),
        out_specs=VMEM,
        compiler_params=params(12),
        cost_estimate=cost(0.2),
        name="finish",
    )(*arrays)


def local(
    inputs,
    cotangent,
    norm_gain,
    head_gain,
    query_weight,
    key_weight,
    output_weight,
    modality,
    segments,
    block_order,
):
    tensor_rank = lax.axis_index("tensor")
    block_rank = lax.axis_index("seq")
    tensor_count = lax.axis_size("tensor")
    block_count = lax.axis_size("seq")
    local_rows, local_width = inputs.shape
    full_width = local_width * tensor_count
    split = tensor_count == 2
    swap = [(0, 1), (1, 0)]
    rank = tensor_rank.astype(jnp.int32).reshape(1)
    modality = modality.reshape(1, local_rows)
    segments = segments.reshape(block_count, local_rows)

    def spread(part):
        if split:
            return [part, lax.ppermute(part, "tensor", swap)]
        return [lax.all_gather(part, "tensor", axis=1, tiled=True)]

    def scatter_columns(part):
        return lax.psum_scatter(part, "tensor", scatter_dimension=1, tiled=True)

    memory, key_raw, normed, row_factor = key_stage(
        rank, modality, norm_gain, head_gain, fetch(key_weight), spread(inputs)
    )
    shared = tensor_count > KV_HEADS
    is_even = tensor_rank % 2 == 0
    pair_swap = [(i, i ^ 1) for i in range(tensor_count)]
    if shared:
        partner = lax.ppermute(memory, "tensor", pair_swap)
        memory = jnp.where(
            is_even,
            jnp.concatenate([memory, partner], 1),
            jnp.concatenate([partner, memory], 1),
        )
    memories, order = [memory], [block_rank]
    for step in range(1, block_count):
        memories.append(lax.ppermute(memory, "seq", seq_pairs(step, block_count)))
        order.append(seq_source(block_rank, step, block_count))
    sources = block_order[jnp.stack(order)]

    query, query_raw, back_attended, output_held = middle_stage(
        rank, modality, head_gain, normed, output_weight, query_weight, spread(cotangent)
    )
    attended, query_back, inner, own_grad, *grads = attention_stage(
        sources, segments, modality, head_gain, query, query_raw, back_attended, memories
    )
    incoming = [
        lax.ppermute(grad, "seq", inverted(seq_pairs(step, block_count)))
        for step, grad in enumerate(grads, 1)
    ]

    projected, gradient_part = turn_stage(
        rank, modality, output_held, attended, query_back, query_weight, split
    )
    if shared:
        total = own_grad + sum(grad.astype(f32) for grad in incoming)
        low, high = total[:, :HEAD_DIM], total[:, HEAD_DIM:]
        outgoing = jnp.where(is_even, high, low).astype(bf16)
        sums = [jnp.where(is_even, low, high), lax.ppermute(outgoing, "tensor", pair_swap)]
    else:
        sums = [own_grad, *incoming]
    sent, slice_back, inner, passed = key_back_stage(
        rank,
        modality,
        head_gain,
        key_raw,
        inner,
        gradient_part,
        key_weight,
        projected[0],
        sums,
        split,
    )
    if split:
        inners = [inner, lax.ppermute(inner, "tensor", swap)]
        other = lax.ppermute(sent, "tensor", swap)
        kept = kept_stage(rank, modality, gradient_part, key_weight, slice_back)
        backs = [kept, other]
        attention_out = projected[1] + lax.ppermute(passed, "tensor", swap).astype(f32)
        attention_out = attention_out.astype(bf16)
    else:
        inners = [lax.psum(inner, "tensor")]
        backs = [scatter_columns(sent)]
        attention_out = scatter_columns(passed)
    gain = lax.dynamic_slice_in_dim(norm_gain, tensor_rank * local_width, local_width, 1)
    grad_input = finish(
        full_width, len(backs), modality, gain, row_factor, inputs, backs, inners
    )
    return (attention_out, grad_input)


def solution(mesh):
    return jax.shard_map(
        local,
        mesh=mesh,
        in_specs=(
            P(("dp", "seq"), "tensor"),
            P(("dp", "seq"), "tensor"),
            P(),
            P(),
            P(None, None, "tensor"),
            P(None, None, "tensor"),
            P(None, "tensor", None),
            P(("dp", "seq")),
            P("dp"),
            P("dp"),
        ),
        out_specs=(P(("dp", "seq"), "tensor"), P(("dp", "seq"), "tensor")),
        check_vma=False,
    )
```

time: 73 us -> 54 us (0.74)
  local copies, waits for them, and re-layouts: 24.3 us -> 3.02 us
  Pallas kernels: 35 us -> 36.7 us
  other arithmetic: 0.95 us -> 1.97 us
    unnamed x40 -> x22, local copies, waits for them, and re-layouts: 22.9 us -> 2.38 us
    pallas_call x8 -> x7, Pallas kernels: 33.8 us -> 35.5 us  [the longest x1 10.8 us: middle_stage(): pl.pallas_call(functools.partial(middle_kernel, len(parts), output_pieces...]
    convert_element_type x1, other arithmetic: 0.87 us -> 1.88 us  [local(): attention_out = attention_out.astype(bf16)]
  transfers between devices with their start and end apart: 11 -> 11, of which waited for: 1 -> 0; matrix products, arithmetic and copies ran while one was open for 3% -> 5% of each run, Pallas kernels for 41% -> 53%
where the time goes in v4:
time: 54 us; the launch traced here: 53.8 us
  Pallas kernels  36.7 us (68%)
  starting transfers between devices  11.2 us (21%)
  local copies, waits for them, and re-layouts  3.02 us (6%)
  other arithmetic  1.97 us (4%)
  between operations  0.85 us (2%)
    pallas_call x1, Pallas kernels, middle_stage(): pl.pallas_call(functools.partial(middle_kernel, len(parts), output_pieces...  10.8 us
    pallas_call x1, Pallas kernels, turn_stage(): pl.pallas_call(functools.partial(turn_kernel, pieces, len(outs)), out_sha...  10 us
    ppermute x3, starting transfers between devices, local(): memories.append(lax.ppermute(memory, 'seq', seq_pairs(step, block_count)))  5.66 us
    ppermute x3, starting transfers between devices, local(): lax.ppermute(grad, 'seq', inverted(seq_pairs(step, block_count)))  4.42 us
    pallas_call x1, Pallas kernels, attention_stage(): pl.pallas_call(functools.partial(attention_kernel, blocks, pairs, per_gro...  3.87 us
    pallas_call x1, Pallas kernels, fetch(): pl.pallas_call(functools.partial(fetch_kernel, pieces), out_shape=residen...  3.17 us
    pallas_call x1, Pallas kernels, key_back_stage(): pl.pallas_call(functools.partial(key_back_kernel, split), out_shape=[jax....  3.13 us
    pallas_call x1, Pallas kernels, kept_stage(): pl.pallas_call(kept_kernel, out_shape=jax.ShapeDtypeStruct((back.shape[0]...  2.91 us
  transfers between devices with their start and end apart: 11, of which 0 were waited for; matrix products, arithmetic and copies ran while one was open for 5% of the time, Pallas kernels for 53%

profile of v4, /device:TPU:0, one launch (start us, length us, event | category | flops | bytes accessed | tf_op | source)
XLA Modules:
  0.0 53.8 jit_solution(9698732772267953572)
XLA Ops:
  0.6 0.0 copy-start
  0.6 0.0 copy-start.2
  0.7 0.0 copy-start.3
  0.7 0.0 copy-start.8
  0.7 0.0 copy-start.6
  0.7 0.0 copy-start.7
  0.7 0.5 collective-permute-start
  1.2 0.1 collective-permute-start.1
  1.3 3.2 %fetch.1.refs_4_ = bf16[2,3584,512]{2,1,0:T(8,128)(2,1)S(1)} custom-call(bf16[2,3584,512]{2,1,0:T(8,128)(2,1)} %weight_ref.3), custom_call_target="tpu_custom_call" | custom-call | flops 200000000 | bytes 400000 | tf_op jit(solution)/shard_map/fetch/pallas_call | solution.py:167
  4.5 0.1 fusion
  4.6 0.0 collective-permute-done.refs_6_
  4.6 0.0 copy-done.2
  4.6 0.0 copy-done.8
  4.6 0.0 copy-done.6
  4.6 0.0 copy-done.7
  4.6 1.6 %key_stage.1 = (bf16[128,512]{1,0:T(8,128)(2,1)S(1)}, f32[128,512]{1,0:T(8,128)S(1)}, bf16[128,3584]{1,0:T(8,128)(2,1)S(1)}, f32[1,128]{1,0:T(1,128)S(1)}) custom-call(s32[1]{0:T(128)} %bitcast.refs_0_.rank_ref, s32[1,128]{1,0:T(1,128)S(1)} %bitcast.9, f32[2,3584]{1,0:T(2,128)S(1)} %copy-done.6, f32[2,2,128]{2,1,0:T(2,128)S(1)} %copy-done.7, ...), custom_call_target="tpu_custom_call" | custom-call | flops 200000000 | bytes 400000 | tf_op jit(solution)/shard_map/key_stage/pallas_call | solution.py:209
  6.2 3.1 %collective-permute-start.2 = (bf16[128,512]{1,0:T(8,128)(2,1)S(1)}, bf16[128,512]{1,0:T(8,128)(2,1)S(1)}, u32[]{:S(2)}, u32[]{:S(2)}) collective-permute-start(bf16[128,512]{1,0:T(8,128)(2,1)S(1)} %get-tuple-element.29.refs_7_), channel_id=1, source_target_pairs={{0,2},{2,0},{4,6},{6,4},{1,3},{3,1},{5,7},{7,5},{8,10},{10,8},{12,... | collective-permute-start | bytes 393224 | tf_op jit(solution)/shard_map/ppermute | solution.py:611
  9.3 2.6 %collective-permute-start.3 = (bf16[128,512]{1,0:T(8,128)(2,1)S(1)}, bf16[128,512]{1,0:T(8,128)(2,1)S(1)}, u32[]{:S(2)}, u32[]{:S(2)}) collective-permute-start(bf16[128,512]{1,0:T(8,128)(2,1)S(1)} %get-tuple-element.29.refs_7_), channel_id=1, source_target_pairs={{0,4},{2,6},{4,0},{6,2},{1,5},{3,7},{5,1},{7,3},{8,12},{10,14},{12... | collective-permute-start | bytes 393224 | tf_op jit(solution)/shard_map/ppermute | solution.py:611
  11.9 0.0 collective-permute-start.4
  11.9 0.0 copy-done
  11.9 0.6 %gather_fusion = s32[4]{0:T(128)S(1)} fusion(s32[4]{0:T(128)S(1)} %copy-done, s32[1024]{0:T(1024)S(1)} %pad_clamp_fusion), kind=kCustom, calls=%fused_computation | custom fusion | bytes 48 | tf_op jit(solution)/shard_map/gather | solution.py:613
  12.5 0.0 collective-permute-done.1.refs_7_
  12.5 0.0 copy-done.3
  12.5 0.0 copy-start.9
  12.6 10.8 %middle_stage.1 = (bf16[128,1024]{1,0:T(8,128)(2,1)S(1)}, f32[128,1024]{1,0:T(8,128)S(1)}, bf16[128,1024]{1,0:T(8,128)(2,1)S(1)}, bf16[2,1024,3584]{2,1,0:T(8,128)(2,1)S(1)}) custom-call(s32[1]{0:T(128)} %bitcast.refs_0_.rank_ref, s32[1,128]{1,0:T(1,128)S(1)} %bitcast.10, f32[2,2,128]{2,1,0:T(2,128)S(1)} %copy-done.7, ...), custom_call_target="tpu_custom_call" | custom-call | flops 200000000 | bytes 400000 | tf_op jit(solution)/shard_map/middle_stage/pallas_call | solution.py:262
  23.4 0.0 collective-permute-done.2.refs_8_
  23.4 0.0 collective-permute-done.3.refs_9_
  23.4 0.0 collective-permute-done.4.refs_10_
  23.4 0.0 copy-done.9
  23.4 3.9 %attention_stage.1 = (bf16[128,1024]{1,0:T(8,128)(2,1)S(1)}, bf16[128,1024]{1,0:T(8,128)(2,1)S(1)}, f32[1,128]{1,0:T(1,128)S(1)}, f32[128,512]{1,0:T(8,128)S(1)}...) custom-call(s32[4]{0:T(128)S(1)} %gather_fusion, ...), custom_call_target="tpu_custom_call" | custom-call | flops 200000000 | bytes 400000 | tf_op jit(solution)/shard_map/attention_stage/pallas_call | solution.py:366
  27.3 1.0 %collective-permute-start.5 = (bf16[128,512]{1,0:T(8,128)(2,1)S(1)}, bf16[128,512]{1,0:T(8,128)(2,1)S(1)}, u32[]{:S(2)}, u32[]{:S(2)}) collective-permute-start(bf16[128,512]{1,0:T(8,128)(2,1)S(1)} %get-tuple-element.38), channel_id=1, source_target_pairs={{2,0},{0,2},{6,4},{4,6},{3,1},{1,3},{7,5},{5,7},{10,8},{8,10},{14,... | collective-permute-start | bytes 393224 | tf_op jit(solution)/shard_map/ppermute | solution.py:622
  28.3 3.4 %collective-permute-start.6 = (bf16[128,512]{1,0:T(8,128)(2,1)S(1)}, bf16[128,512]{1,0:T(8,128)(2,1)S(1)}, u32[]{:S(2)}, u32[]{:S(2)}) collective-permute-start(bf16[128,512]{1,0:T(8,128)(2,1)S(1)} %get-tuple-element.39), channel_id=1, source_target_pairs={{4,0},{6,2},{0,4},{2,6},{5,1},{7,3},{1,5},{3,7},{12,8},{14,10},{8,... | collective-permute-start | bytes 393224 | tf_op jit(solution)/shard_map/ppermute | solution.py:622
  31.7 0.0 collective-permute-start.7
  31.7 0.0 copy-start.1
  31.7 10.0 %turn_stage.1 = (bf16[128,1792]{1,0:T(8,128)(2,1)}, f32[128,1792]{1,0:T(8,128)S(1)}, f32[128,3584]{1,0:T(8,128)S(1)}) custom-call(s32[1]{0:T(128)} %bitcast.refs_0_.rank_ref, s32[1,128]{1,0:T(1,128)S(1)} %bitcast.12, bf16[2,1024,3584]{2,1,0:T(8,128)(2,1)S(1)} %get-tuple-element.25.refs_2_, bf16[128,1024]{1,0:T(8,128)(2,1)S(1)} %get-tuple-element.30.refs_3_, ...), custom_call_target="tpu_custom_call" | custom-call | flops 200000000 | bytes 400000 | tf_op jit(solution)/shard_map/turn_stage/pallas_call | solution.py:419
  41.7 0.0 collective-permute-done.5.refs_9_
  41.7 0.0 collective-permute-done.6.refs_10_
  41.7 0.0 collective-permute-done.7.refs_11_
  41.8 3.1 %key_back_stage.1 = (bf16[128,1792]{1,0:T(8,128)(2,1)S(1)}, bf16[128,512]{1,0:T(8,128)(2,1)S(1)}, f32[1,128]{1,0:T(1,128)S(1)}, bf16[128,1792]{1,0:T(8,128)(2,1)}) custom-call(s32[1]{0:T(128)} %bitcast.refs_0_.rank_ref, s32[1,128]{1,0:T(1,128)S(1)} %bitcast.13, f32[2,2,128]{2,1,0:T(2,128)S(1)} %copy-done.7, ...), custom_call_target="tpu_custom_call", output_to_operand_aliasing={{3}: (7, {})} | custom-call | flops 200000000 | bytes 400000 | tf_op jit(solution)/shard_map/key_back_stage/pallas_call | solution.py:479
  44.9 0.0 copy-start.4
  44.9 0.6 %copy-done.4 = bf16[128,512]{1,0:T(8,128)(2,1)} copy-done((bf16[128,512]{1,0:T(8,128)(2,1)}, bf16[128,512]{1,0:T(8,128)(2,1)S(1)}, u32[]{:S(2)}) %copy-start.4) | copy-done | bytes 131096
  45.6 0.0 copy-start.10
  45.6 0.8 %copy-done.10 = bf16[128,1792]{1,0:T(8,128)(2,1)} copy-done((bf16[128,1792]{1,0:T(8,128)(2,1)}, bf16[128,1792]{1,0:T(8,128)(2,1)S(1)}, u32[]{:S(2)}) %copy-start.10) | copy-done | bytes 458776
  46.3 0.0 collective-permute-start.8
  46.3 0.5 collective-permute-start.9
  46.9 0.0 collective-permute-start.10
  46.9 0.0 copy-start.5
  46.9 0.9 %copy-done.5 = bf16[128,512]{1,0:T(8,128)(2,1)S(1)} copy-done((bf16[128,512]{1,0:T(8,128)(2,1)S(1)}, bf16[128,512]{1,0:T(8,128)(2,1)}, u32[]{:S(2)}) %copy-start.5) | copy-done | bytes 131096
  47.8 2.9 %kept_stage.1.refs_0_ = f32[128,1792]{1,0:T(8,128)S(1)} custom-call(s32[1]{0:T(128)} %bitcast.refs_0_.rank_ref, s32[1,128]{1,0:T(1,128)S(1)} %bitcast.14, f32[128,3584]{1,0:T(8,128)S(1)} %get-tuple-element.35.refs_5_.part_ref, bf16[2,3584,512]{2,1,0:T(8,128)(2,1)} %weight_ref.3, bf16[128,512]{1,0:T(8,128)(2,1)S(1)} %copy-done.5), custom_call_target="tpu_custom_call" | custom-call | flops 200000000 | bytes 400000 | tf_op jit(solution)/shard_map/kept_stage/pallas_call | solution.py:518
  50.7 0.0 collective-permute-done.8
  50.7 1.9 %add_convert_fusion = bf16[128,1792]{1,0:T(8,128)(2,1)} fusion(f32[128,1792]{1,0:T(8,128)S(1)} %get-tuple-element.32, bf16[128,1792]{1,0:T(8,128)(2,1)} %collective-permute-done.8), kind=kLoop, calls=%fused_computation.1 | loop fusion | flops 688128 | bytes 1835008 | tf_op jit(solution)/shard_map/convert_element_type | solution.py:654
  52.6 0.0 collective-permute-done.10.refs_3_
  52.6 0.0 collective-permute-done.9.refs_1_
  52.6 1.2 %finish.1 = bf16[128,1792]{1,0:T(8,128)(2,1)} custom-call(s32[1,128]{1,0:T(1,128)S(1)} %bitcast.15, f32[2,1792]{1,0:T(2,128)S(1)} %constant_dynamic-slice_fusion.gain_ref, f32[1,128]{1,0:T(1,128)S(1)} %get-tuple-element.42.factor_ref, bf16[128,1792]{1,0:T(8,128)(2,1)S(1)} %copy-done.2, f32[128,1792]{1,0:T(8,128)S(1)} %kept_stage.1.refs_0_, ...), custom_call_target="tpu_custom_call" | custom-call | flops 200000000 | bytes 400000 | tf_op jit(solution)/shard_map/finish/pallas_call | solution.py:553
  53.8 0.0 copy-done.1
  (2 shorter events, 0.0 us)
Async XLA Ops:
  0.6 11.3 %copy-start = (s32[4]{0:T(128)S(1)}, s32[4]{0:T(128)}, u32[]{:S(2)}) copy-start(s32[4]{0:T(128)} %param.19) | copy-start | bytes 52
  0.6 3.9 %copy-start.2 = (bf16[128,1792]{1,0:T(8,128)(2,1)S(1)}, bf16[128,1792]{1,0:T(8,128)(2,1)}, u32[]{:S(2)}) copy-start(bf16[128,1792]{1,0:T(8,128)(2,1)} %inputs_ref.1) | copy-start | bytes 1376260
  0.7 11.9 %copy-start.3 = (bf16[128,1792]{1,0:T(8,128)(2,1)S(1)}, bf16[128,1792]{1,0:T(8,128)(2,1)}, u32[]{:S(2)}) copy-start(bf16[128,1792]{1,0:T(8,128)(2,1)} %refs_6_.2) | copy-start | bytes 1376260
  0.7 3.9 %copy-start.8 = (s32[128]{0:T(128)S(1)}, s32[128]{0:T(128)}, u32[]{:S(2)}) copy-start(s32[128]{0:T(128)} %param.17) | copy-start | bytes 1540
  0.7 3.9 %copy-start.6 = (f32[2,3584]{1,0:T(2,128)S(1)}, f32[2,3584]{1,0:T(2,128)}, u32[]{:S(2)}) copy-start(f32[2,3584]{1,0:T(2,128)} %refs_2_.3) | copy-start | bytes 86020
  0.7 3.9 %copy-start.7 = (f32[2,2,128]{2,1,0:T(2,128)S(1)}, f32[2,2,128]{2,1,0:T(2,128)}, u32[]{:S(2)}) copy-start(f32[2,2,128]{2,1,0:T(2,128)} %refs_2_.5) | copy-start | bytes 6148
  0.7 3.9 %collective-permute-start = (bf16[128,1792]{1,0:T(8,128)(2,1)}, bf16[128,1792]{1,0:T(8,128)(2,1)S(1)}, u32[]{:S(2)}, u32[]{:S(2)}) collective-permute-start(bf16[128,1792]{1,0:T(8,128)(2,1)} %inputs_ref.1), channel_id=1, source_target_pairs={{0,1},{1,0},{2,3},{3,2},{4,5},{5,4},{6,7},{7,6},{8,9},{9,8},{10,11... | collective-permute-start | bytes 1376264 | tf_op jit(solution)/shard_map/ppermute | solution.py:590
  1.2 11.3 %collective-permute-start.1 = (bf16[128,1792]{1,0:T(8,128)(2,1)}, bf16[128,1792]{1,0:T(8,128)(2,1)S(1)}, u32[]{:S(2)}, u32[]{:S(2)}) collective-permute-start(bf16[128,1792]{1,0:T(8,128)(2,1)} %refs_6_.2), channel_id=1, source_target_pairs={{0,1},{1,0},{2,3},{3,2},{4,5},{5,4},{6,7},{7,6},{8,9},{9,8},{10,11... | collective-permute-start | bytes 1376264 | tf_op jit(solution)/shard_map/ppermute | solution.py:590
  6.2 17.2 %collective-permute-start.2 = (bf16[128,512]{1,0:T(8,128)(2,1)S(1)}, bf16[128,512]{1,0:T(8,128)(2,1)S(1)}, u32[]{:S(2)}, u32[]{:S(2)}) collective-permute-start(bf16[128,512]{1,0:T(8,128)(2,1)S(1)} %get-tuple-element.29.refs_7_), channel_id=1, source_target_pairs={{0,2},{2,0},{4,6},{6,4},{1,3},{3,1},{5,7},{7,5},{8,10},{10,8},{12,... | collective-permute-start | bytes 393224 | tf_op jit(solution)/shard_map/ppermute | solution.py:611
  9.3 14.1 %collective-permute-start.3 = (bf16[128,512]{1,0:T(8,128)(2,1)S(1)}, bf16[128,512]{1,0:T(8,128)(2,1)S(1)}, u32[]{:S(2)}, u32[]{:S(2)}) collective-permute-start(bf16[128,512]{1,0:T(8,128)(2,1)S(1)} %get-tuple-element.29.refs_7_), channel_id=1, source_target_pairs={{0,4},{2,6},{4,0},{6,2},{1,5},{3,7},{5,1},{7,3},{8,12},{10,14},{12... | collective-permute-start | bytes 393224 | tf_op jit(solution)/shard_map/ppermute | solution.py:611
  11.9 11.5 %collective-permute-start.4 = (bf16[128,512]{1,0:T(8,128)(2,1)S(1)}, bf16[128,512]{1,0:T(8,128)(2,1)S(1)}, u32[]{:S(2)}, u32[]{:S(2)}) collective-permute-start(bf16[128,512]{1,0:T(8,128)(2,1)S(1)} %get-tuple-element.29.refs_7_), channel_id=1, source_target_pairs={{0,6},{2,4},{4,2},{6,0},{1,7},{3,5},{5,3},{7,1},{8,14},{10,12},{12... | collective-permute-start | bytes 393224 | tf_op jit(solution)/shard_map/ppermute | solution.py:611
  12.5 10.9 %copy-start.9 = (s32[512]{0:T(512)S(1)}, s32[512]{0:T(512)}, u32[]{:S(2)}) copy-start(s32[512]{0:T(512)} %param.18) | copy-start | bytes 6148
  27.3 14.4 %collective-permute-start.5 = (bf16[128,512]{1,0:T(8,128)(2,1)S(1)}, bf16[128,512]{1,0:T(8,128)(2,1)S(1)}, u32[]{:S(2)}, u32[]{:S(2)}) collective-permute-start(bf16[128,512]{1,0:T(8,128)(2,1)S(1)} %get-tuple-element.38), channel_id=1, source_target_pairs={{2,0},{0,2},{6,4},{4,6},{3,1},{1,3},{7,5},{5,7},{10,8},{8,10},{14,... | collective-permute-start | bytes 393224 | tf_op jit(solution)/shard_map/ppermute | solution.py:622
  28.3 13.4 %collective-permute-start.6 = (bf16[128,512]{1,0:T(8,128)(2,1)S(1)}, bf16[128,512]{1,0:T(8,128)(2,1)S(1)}, u32[]{:S(2)}, u32[]{:S(2)}) collective-permute-start(bf16[128,512]{1,0:T(8,128)(2,1)S(1)} %get-tuple-element.39), channel_id=1, source_target_pairs={{4,0},{6,2},{0,4},{2,6},{5,1},{7,3},{1,5},{3,7},{12,8},{14,10},{8,... | collective-permute-start | bytes 393224 | tf_op jit(solution)/shard_map/ppermute | solution.py:622
  31.7 10.0 %collective-permute-start.7 = (bf16[128,512]{1,0:T(8,128)(2,1)S(1)}, bf16[128,512]{1,0:T(8,128)(2,1)S(1)}, u32[]{:S(2)}, u32[]{:S(2)}) collective-permute-start(bf16[128,512]{1,0:T(8,128)(2,1)S(1)} %get-tuple-element.40), channel_id=1, source_target_pairs={{6,0},{4,2},{2,4},{0,6},{7,1},{5,3},{3,5},{1,7},{14,8},{12,10},{10... | collective-permute-start | bytes 393224 | tf_op jit(solution)/shard_map/ppermute | solution.py:622
  31.7 22.1 %copy-start.1 = (s32[4]{0:T(128)S(1)}, s32[4]{0:T(128)}, u32[]{:S(2)}) copy-start(s32[4]{0:T(128)} %param.19) | copy-start | bytes 52
  44.9 0.7 %copy-start.4 = (bf16[128,512]{1,0:T(8,128)(2,1)}, bf16[128,512]{1,0:T(8,128)(2,1)S(1)}, u32[]{:S(2)}) copy-start(bf16[128,512]{1,0:T(8,128)(2,1)S(1)} %get-tuple-element.43.back_ref) | copy-start | bytes 393220
  45.6 0.8 %copy-start.10 = (bf16[128,1792]{1,0:T(8,128)(2,1)}, bf16[128,1792]{1,0:T(8,128)(2,1)S(1)}, u32[]{:S(2)}) copy-start(bf16[128,1792]{1,0:T(8,128)(2,1)S(1)} %get-tuple-element.44) | copy-start | bytes 1376260
  46.3 4.3 %collective-permute-start.8 = (bf16[128,1792]{1,0:T(8,128)(2,1)}, bf16[128,1792]{1,0:T(8,128)(2,1)}, u32[]{:S(2)}, u32[]{:S(2)}) collective-permute-start(bf16[128,1792]{1,0:T(8,128)(2,1)} %get-tuple-element.41), channel_id=1, source_target_pairs={{0,1},{1,0},{2,3},{3,2},{4,5},{5,4},{6,7},{7,6},{8,9},{9,8},{10,11... | collective-permute-start | bytes 1376264 | tf_op jit(solution)/shard_map/ppermute | solution.py:653
  46.3 6.2 %collective-permute-start.9 = (bf16[128,1792]{1,0:T(8,128)(2,1)}, bf16[128,1792]{1,0:T(8,128)(2,1)S(1)}, u32[]{:S(2)}, u32[]{:S(2)}) collective-permute-start(bf16[128,1792]{1,0:T(8,128)(2,1)} %copy-done.10), channel_id=1, source_target_pairs={{0,1},{1,0},{2,3},{3,2},{4,5},{5,4},{6,7},{7,6},{8,9},{9,8},{10,11... | collective-permute-start | bytes 1376264 | tf_op jit(solution)/shard_map/ppermute | solution.py:650
  46.9 5.7 %collective-permute-start.10 = (f32[1,128]{1,0:T(1,128)S(1)}, f32[1,128]{1,0:T(1,128)S(1)}, u32[]{:S(2)}, u32[]{:S(2)}) collective-permute-start(f32[1,128]{1,0:T(1,128)S(1)} %get-tuple-element.45.refs_2_), channel_id=1, source_target_pairs={{0,1},{1,0},{2,3},{3,2},{4,5},{5,4},{6,7},{7,6},{8,9},{9,8},{10,11... | collective-permute-start | bytes 1544 | tf_op jit(solution)/shard_map/ppermute | solution.py:649
  46.9 0.9 %copy-start.5 = (bf16[128,512]{1,0:T(8,128)(2,1)S(1)}, bf16[128,512]{1,0:T(8,128)(2,1)}, u32[]{:S(2)}) copy-start(bf16[128,512]{1,0:T(8,128)(2,1)} %copy-done.4) | copy-start | bytes 393220

commit v5 on v4

--- a/solution.py
+++ b/solution.py
@@ -170,7 +170,7 @@
         in_specs=[ANY],
         out_specs=VMEM,
         scratch_shapes=[pltpu.SemaphoreType.DMA((len(pieces), 2))],
-        compiler_params=params(4),
+        compiler_params=params(1),
         cost_estimate=cost(0.2),
         name="fetch",
     )(streamed(weights))
@@ -216,37 +216,32 @@
         ],
         in_specs=[SMEM] + [VMEM] * (4 + len(parts)),
         out_specs=[VMEM] * 4,
-        compiler_params=params(12),
-        cost_estimate=cost(0.2),
+        compiler_params=params(8),
+        cost_estimate=cost(10),
         name="key_stage",
     )(rank, modality, norm_gain, head_gain, weights, *parts)
 
 
-def middle_kernel(count, output_pieces, query_pieces, *refs):
+def middle_kernel(count, pieces, *refs):
     rank_ref, modality_ref, head_ref, normed_ref, output_ref, query_weight_ref = refs[:6]
     part_refs = refs[6 : 6 + count]
-    query_ref, raw_ref, back_ref, output_held = refs[6 + count : 10 + count]
-    query_slots, output_sems, query_sems = refs[10 + count :]
-    copies = copies_of(output_ref, output_held, output_sems, output_pieces)
-    copies += copies_of(query_weight_ref, query_slots, query_sems, query_pieces, slots=AHEAD)
+    query_ref, raw_ref, back_ref, slots, sems = refs[6 + count :]
+    copies = copies_of(query_weight_ref, slots, sems, pieces, slots=AHEAD)
     begin_first(copies)
     image = column(modality_ref[...]) > 0.0
     cotangent = in_order(rank_ref[0], part_refs)
-    for index, (start, size) in enumerate(output_pieces):
+    for start, size in chunks_of(output_ref.shape[1], 256):
+        part = slice(start, start + size)
+        back_ref[:, part] = both_back(image, cotangent, output_ref[:, part, :]).astype(bf16)
+    for index, (start, size) in enumerate(pieces):
         arrive(copies, index)
         part = slice(start, start + size)
-        back_ref[:, part] = both_back(image, cotangent, output_held[:, part, :]).astype(bf16)
-        begin(copies, index + AHEAD)
-    for index, (start, size) in enumerate(query_pieces):
-        place = len(output_pieces) + index
-        arrive(copies, place)
-        part = slice(start, start + size)
-        product = both_experts(image, normed_ref[:, part], query_slots[index % AHEAD])
+        product = both_experts(image, normed_ref[:, part], slots[index % AHEAD])
         if index == 0:
             raw_ref[...] = product
         else:
             raw_ref[...] += product
-        begin(copies, place + AHEAD)
+        begin(copies, index + AHEAD)
     scaling = jnp.where(image, head_ref[1, 0:1, :], head_ref[0, 0:1, :])
     for h in range(raw_ref.shape[1] // HEAD_DIM):
         part = slice(h * HEAD_DIM, (h + 1) * HEAD_DIM)
@@ -257,46 +252,44 @@
 def middle_stage(rank, modality, head_gain, normed, output_weight, query_weight, parts):
     rows = normed.shape[0]
     width = query_weight.shape[2]
-    output_pieces = chunks_of(output_weight.shape[1], 128)
-    query_pieces = chunks_of(query_weight.shape[1], 512)
+    pieces = chunks_of(query_weight.shape[1], 512)
     return pl.pallas_call(
-        functools.partial(middle_kernel, len(parts), output_pieces, query_pieces),
+        functools.partial(middle_kernel, len(parts), pieces),
         out_shape=[
             jax.ShapeDtypeStruct((rows, width), bf16),
             jax.ShapeDtypeStruct((rows, width), f32),
             jax.ShapeDtypeStruct((rows, width), bf16),
-            resident(output_weight),
         ],
-        in_specs=[SMEM, VMEM, VMEM, VMEM, ANY, ANY] + [VMEM] * len(parts),
-        out_specs=[VMEM] * 4,
+        in_specs=[SMEM, VMEM, VMEM, VMEM, VMEM, ANY] + [VMEM] * len(parts),
+        out_specs=[VMEM] * 3,
         scratch_shapes=[
-            ring(query_weight, query_pieces),
-            pltpu.SemaphoreType.DMA((len(output_pieces), 2)),
-            pltpu.SemaphoreType.DMA((len(query_pieces), 2)),
+            ring(query_weight, pieces),
+            pltpu.SemaphoreType.DMA((len(pieces), 2)),
         ],
-        compiler_params=params(16),
-        cost_estimate=cost(0.2),
+        compiler_params=params(14),
+        cost_estimate=cost(8),
         name="middle_stage",
-    )(rank, modality, head_gain, normed, streamed(output_weight), streamed(query_weight), *parts)
+    )(rank, modality, head_gain, normed, output_weight, streamed(query_weight), *parts)
 
 
 def attention_kernel(blocks, pairs, per_group, *refs):
     for pair in range(pairs):
         wide = pl.ds(pair * per_group * HEAD_DIM, per_group * HEAD_DIM)
         narrow = pl.ds(pair * 2 * HEAD_DIM, 2 * HEAD_DIM)
-        views = list(refs[:4]) + [ref.at[:, wide] for ref in refs[4:7]]
-        views += [ref.at[:, narrow] for ref in refs[7 : 7 + blocks]]
-        views += [ref.at[:, wide] for ref in refs[7 + blocks : 9 + blocks]]
-        views += [refs[9 + blocks]]
-        views += [ref.at[:, narrow] for ref in refs[10 + blocks :]]
+        views = list(refs[:5]) + [ref.at[:, wide] for ref in refs[5:8]]
+        views += [ref.at[:, narrow] for ref in refs[8 : 8 + blocks]]
+        views += [ref.at[:, wide] for ref in refs[8 + blocks : 10 + blocks]]
+        views += [refs[10 + blocks]]
+        views += [ref.at[:, narrow] for ref in refs[11 + blocks :]]
         attention_pair(blocks, per_group, pair == 0, *views)
 
 
 def attention_pair(blocks, per_group, fresh, *refs):
-    source_ref, segments_ref, modality_ref, head_ref, query_ref, raw_ref, back_ref = refs[:7]
-    memory_refs = refs[7 : 7 + blocks]
-    attended_ref, query_back_ref, inner_ref = refs[7 + blocks : 10 + blocks]
-    grad_refs = refs[10 + blocks :]
+    place_ref, order_ref, segments_ref, modality_ref, head_ref = refs[:5]
+    query_ref, raw_ref, back_ref = refs[5:8]
+    memory_refs = refs[8 : 8 + blocks]
+    attended_ref, query_back_ref, inner_ref = refs[8 + blocks : 11 + blocks]
+    grad_refs = refs[11 + blocks :]
     rows = query_ref.shape[0]
     scale = 1.0 / math.sqrt(HEAD_DIM)
 
@@ -308,10 +301,12 @@
     query, back = heads(query_ref), heads(back_ref)
     key = jnp.concatenate([m[:, :HEAD_DIM] for m in memory_refs], axis=0)
     value = jnp.concatenate([m[:, HEAD_DIM:] for m in memory_refs], axis=0)
-    key_segments = jnp.concatenate(
-        [segments_ref[pl.ds(source_ref[b], 1), :] for b in range(blocks)], axis=1
-    )
-    query_segments = column(segments_ref[pl.ds(source_ref[0], 1), :])
+    lines = [
+        segments_ref[pl.ds(order_ref[seq_source(place_ref[0], b, blocks)], 1), :]
+        for b in range(blocks)
+    ]
+    key_segments = jnp.concatenate(lines, axis=1)
+    query_segments = column(lines[0])
     visible = jnp.where(key_segments.astype(f32) <= query_segments, 1.0, 0.0)
     visible = jnp.concatenate([visible] * per_group, axis=0)
     scores = dot_nt(query, key) * scale
@@ -350,7 +345,7 @@
         inner_ref[...] += inner
 
 
-def attention_stage(sources, segments, modality, head_gain, query, raw, back, memories):
+def attention_stage(place, order, segments, modality, head_gain, query, raw, back, memories):
     rows, width = query.shape
     blocks = len(memories)
     pairs = memories[0].shape[1] // (2 * HEAD_DIM)
@@ -366,18 +361,12 @@
     return pl.pallas_call(
         functools.partial(attention_kernel, blocks, pairs, per_group),
         out_shape=outs,
-        in_specs=[SMEM] + [VMEM] * (6 + blocks),
+        in_specs=[SMEM, SMEM] + [VMEM] * (6 + blocks),
         out_specs=[VMEM] * (3 + blocks),
-        compiler_params=params(16),
-        cost_estimate=cost(0.2),
+        compiler_params=params(12),
+        cost_estimate=cost(4),
         name="attention_stage",
-    )(sources, segments, modality, head_gain, query, raw, back, *memories)
-
-
-def half(rank, extent, other):
-    size = extent // 2
-    place = 1 - rank if other else rank
-    return pl.ds(pl.multiple_of(place * size, HEAD_DIM), size)
+    )(place, order, segments, modality, head_gain, query, raw, back, *memories)
 
 
 def turn_kernel(pieces, outputs, *refs):
@@ -388,15 +377,24 @@
     begin_first(copies)
     image = column(modality_ref[...]) > 0.0
     attended = attended_ref[...]
-    width = output_ref.shape[2]
+    extent = output_ref.shape[2] // 2
+
+    def project(rank):
+        sent_ref, kept_ref = out_refs
+        for start, size in chunks_of(extent, 896):
+            part = slice(start, start + size)
+            first = (1 - rank) * extent + start
+            product = both_experts(image, attended, output_ref[:, :, first : first + size])
+            sent_ref[:, part] = product.astype(bf16)
+            first = rank * extent + start
+            product = both_experts(image, attended, output_ref[:, :, first : first + size])
+            kept_ref[:, part] = product
+
     if outputs == 1:
         out_refs[0][...] = both_experts(image, attended, output_ref[...]).astype(bf16)
     else:
-        sent_ref, kept_ref = out_refs
-        weights = output_ref[:, :, half(rank_ref[0], width, True)]
-        sent_ref[...] = both_experts(image, attended, weights).astype(bf16)
-        weights = output_ref[:, :, half(rank_ref[0], width, False)]
-        kept_ref[...] = both_experts(image, attended, weights)
+        for rank in range(2):
+            pl.when(rank_ref[0] == rank)(functools.partial(project, rank))
     for index, (start, size) in enumerate(pieces):
         arrive(copies, index)
         part = slice(start, start + size)
@@ -404,9 +402,9 @@
         begin(copies, index + AHEAD)
 
 
-def turn_stage(rank, modality, output_held, attended, query_back, query_weight, split):
+def turn_stage(rank, modality, output_weight, attended, query_back, query_weight, split):
     depth = query_weight.shape[1]
-    width = output_held.shape[2]
+    width = output_weight.shape[2]
     rows = attended.shape[0]
     pieces = chunks_of(depth, 512)
     if split:
@@ -426,27 +424,17 @@
             pltpu.SemaphoreType.DMA((len(pieces), 2)),
         ],
         compiler_params=params(16),
-        cost_estimate=cost(0.2),
+        cost_estimate=cost(10),
         name="turn_stage",
-    )(rank, modality, output_held, attended, query_back, streamed(query_weight))
+    )(rank, modality, output_weight, attended, query_back, streamed(query_weight))
     return projected, part
-
-
-def back_pieces(depth, split):
-    return chunks_of(depth // 2 if split else depth, 896)
 
 
 def key_back_kernel(split, *refs):
     rank_ref, modality_ref, head_ref, raw_ref, inner_in_ref, part_ref, weight_ref = refs[:7]
-    grad_refs = refs[8:-6]
-    out_ref, back_ref, inner_ref = refs[-6:-3]
-    held, sems = refs[-2:]
-    depth = part_ref.shape[1]
-    base = pl.multiple_of((1 - rank_ref[0]) * (depth // 2), HEAD_DIM) if split else 0
-    pieces = back_pieces(depth, split)
-    copies = copies_of(weight_ref, held, sems, pieces, base)
-    for index in range(len(copies)):
-        begin(copies, index)
+    grad_refs = refs[8:-4]
+    out_ref, back_ref, inner_ref = refs[-4:-1]
+    base = pl.multiple_of((1 - rank_ref[0]) * out_ref.shape[1], HEAD_DIM) if split else 0
     image = column(modality_ref[...]) > 0.0
     blocks = raw_ref.shape[1] // HEAD_DIM
     scaling = jnp.where(image, head_ref[1, 1:2, :], head_ref[0, 1:2, :])
@@ -463,102 +451,93 @@
         back_ref[:, part] = back
         inner += jnp.sum(back.astype(f32) * raw, axis=1, keepdims=True)
     inner_ref[...] = inner_in_ref[...] + row_of(inner)
-    for index, (start, size) in enumerate(pieces):
-        arrive(copies, index)
-        part = slice(start, start + size)
-        product = both_back(image, back_ref[...], held[:, part, :])
-        given = part_ref[:, pl.ds(base + start, size)]
-        out_ref[:, part] = (product + given).astype(bf16)
+    for start, size in chunks_of(out_ref.shape[1], 896):
+        place = pl.ds(base + start, size)
+        product = both_back(image, back_ref[...], weight_ref[:, place, :])
+        out_ref[:, start : start + size] = (product + part_ref[:, place]).astype(bf16)
 
 
 def key_back_stage(rank, modality, head_gain, raw, inner, part, weights, passed, grads, split):
     _, depth, width = weights.shape
     rows = raw.shape[0]
-    pieces = back_pieces(depth, split)
-    extent = depth // 2 if split else depth
     return pl.pallas_call(
         functools.partial(key_back_kernel, split),
         out_shape=[
-            jax.ShapeDtypeStruct((rows, extent), bf16),
+            jax.ShapeDtypeStruct((rows, depth // 2 if split else depth), bf16),
             jax.ShapeDtypeStruct((rows, width), bf16),
             jax.ShapeDtypeStruct((1, rows), f32),
             jax.ShapeDtypeStruct(passed.shape, passed.dtype),
         ],
-        in_specs=[SMEM] + [VMEM] * 5 + [ANY, ANY] + [VMEM] * len(grads),
+        in_specs=[SMEM] + [VMEM] * 6 + [ANY] + [VMEM] * len(grads),
         out_specs=[VMEM] * 3 + [ANY],
-        scratch_shapes=[
-            pltpu.VMEM((2, extent, width), bf16),
-            pltpu.SemaphoreType.DMA((len(pieces), 2)),
-        ],
         input_output_aliases={7: 3},
-        compiler_params=params(12),
-        cost_estimate=cost(0.2),
+        compiler_params=params(6),
+        cost_estimate=cost(2),
         name="key_back_stage",
-    )(rank, modality, head_gain, raw, inner, part, streamed(weights), passed, *grads)
-
-
-def kept_kernel(rank_ref, modality_ref, part_ref, weight_ref, back_ref, out_ref, held, sems):
-    depth = part_ref.shape[1]
-    base = pl.multiple_of(rank_ref[0] * (depth // 2), HEAD_DIM)
-    pieces = back_pieces(depth, True)
-    copies = copies_of(weight_ref, held, sems, pieces, base)
-    for index in range(len(copies)):
-        begin(copies, index)
+    )(rank, modality, head_gain, raw, inner, part, weights, passed, *grads)
+
+
+def kept_kernel(rank_ref, modality_ref, part_ref, weight_ref, back_ref, out_ref):
+    base = pl.multiple_of(rank_ref[0] * out_ref.shape[1], HEAD_DIM)
     image = column(modality_ref[...]) > 0.0
-    for index, (start, size) in enumerate(pieces):
-        arrive(copies, index)
-        part = slice(start, start + size)
-        product = both_back(image, back_ref[...], held[:, part, :])
-        out_ref[:, part] = product + part_ref[:, pl.ds(base + start, size)]
+    for start, size in chunks_of(out_ref.shape[1], 896):
+        place = pl.ds(base + start, size)
+        product = both_back(image, back_ref[...], weight_ref[:, place, :])
+        out_ref[:, start : start + size] = product + part_ref[:, place]
 
 
 def kept_stage(rank, modality, part, weights, back):
-    _, depth, width = weights.shape
-    pieces = back_pieces(depth, True)
     return pl.pallas_call(
         kept_kernel,
-        out_shape=jax.ShapeDtypeStruct((back.shape[0], depth // 2), f32),
-        in_specs=[SMEM, VMEM, VMEM, ANY, VMEM],
+        out_shape=jax.ShapeDtypeStruct((back.shape[0], weights.shape[1] // 2), f32),
+        in_specs=[SMEM] + [VMEM] * 4,
         out_specs=VMEM,
-        scratch_shapes=[
-            pltpu.VMEM((2, depth // 2, width), bf16),
-            pltpu.SemaphoreType.DMA((len(pieces), 2)),
-        ],
-        compiler_params=params(12),
-        cost_estimate=cost(0.2),
+        compiler_params=params(6),
+        cost_estimate=cost(2),
         name="kept_stage",
-    )(rank, modality, part, streamed(weights), back)
-
-
-def finish(total_width, count, modality, gain, factor, inputs, backs, inners):
-    rows, width = inputs.shape
-
-    def kernel(modality_ref, gain_ref, factor_ref, inputs_ref, *refs):
-        back_refs = refs[:count]
-        inner_refs, out_ref = refs[count:-1], refs[-1]
-        image = column(modality_ref[...]) > 0.0
-        scaling = jnp.where(image, gain_ref[1:2, :], gain_ref[0:1, :])
-        factor_column = column(factor_ref[...])
-        back = back_refs[0][...].astype(f32)
-        for ref in back_refs[1:]:
-            back += ref[...].astype(f32)
-        inner = inner_refs[0][...]
-        for ref in inner_refs[1:]:
-            inner += ref[...]
-        unit_rows = inputs_ref[...].astype(f32) * factor_column
-        inner_mean = column(inner) * (1.0 / total_width)
-        out_ref[...] = (factor_column * (scaling * back - unit_rows * inner_mean)).astype(bf16)
-
-    arrays = [modality, gain, factor, inputs, *backs, *inners]
+    )(rank, modality, part, weights, back)
+
+
+def finish_kernel(backs, inners, total_width, *refs):
+    rank_ref, modality_ref, gain_ref, factor_ref, inputs_ref = refs[:5]
+    back_refs = refs[5 : 5 + backs]
+    inner_refs = refs[5 + backs : 5 + backs + inners]
+    rest = refs[5 + backs + inners :]
+    out_ref = rest[-1]
+    width = inputs_ref.shape[1]
+    image = column(modality_ref[...]) > 0.0
+    gain = gain_ref[...]
+    if gain.shape[1] != width:
+        gain = gain_ref[:, pl.ds(pl.multiple_of(rank_ref[0] * width, HEAD_DIM), width)]
+    scaling = jnp.where(image, gain[1:2, :], gain[0:1, :])
+    factor = column(factor_ref[...])
+    back = back_refs[0][...].astype(f32)
+    for ref in back_refs[1:]:
+        back += ref[...].astype(f32)
+    inner = inner_refs[0][...]
+    for ref in inner_refs[1:]:
+        inner += ref[...]
+    unit_rows = inputs_ref[...].astype(f32) * factor
+    inner_mean = column(inner) * (1.0 / total_width)
+    out_ref[...] = (factor * (scaling * back - unit_rows * inner_mean)).astype(bf16)
+    if len(rest) == 4:
+        kept_ref, other_ref, attention_ref, _ = rest
+        attention_ref[...] = (kept_ref[...] + other_ref[...].astype(f32)).astype(bf16)
+
+
+def finish(rank, total_width, modality, gain, factor, inputs, backs, inners, projected):
+    shape = jax.ShapeDtypeStruct(inputs.shape, bf16)
+    arrays = [modality, gain, factor, inputs, *backs, *inners, *projected]
+    outs = [shape] * (2 if projected else 1)
     return pl.pallas_call(
-        kernel,
-        out_shape=jax.ShapeDtypeStruct((rows, width), bf16),
-        in_specs=[VMEM] * len(arrays),
-        out_specs=VMEM,
-        compiler_params=params(12),
-        cost_estimate=cost(0.2),
+        functools.partial(finish_kernel, len(backs), len(inners), total_width),
+        out_shape=outs,
+        in_specs=[SMEM] + [VMEM] * len(arrays),
+        out_specs=[VMEM] * len(outs),
+        compiler_params=params(6),
+        cost_estimate=cost(1),
         name="finish",
-    )(*arrays)
+    )(rank, *arrays)
 
 
 def local(
@@ -606,17 +585,23 @@
             jnp.concatenate([memory, partner], 1),
             jnp.concatenate([partner, memory], 1),
         )
-    memories, order = [memory], [block_rank]
+    memories = [memory]
     for step in range(1, block_count):
         memories.append(lax.ppermute(memory, "seq", seq_pairs(step, block_count)))
-        order.append(seq_source(block_rank, step, block_count))
-    sources = block_order[jnp.stack(order)]
-
-    query, query_raw, back_attended, output_held = middle_stage(
+
+    query, query_raw, back_attended = middle_stage(
         rank, modality, head_gain, normed, output_weight, query_weight, spread(cotangent)
     )
     attended, query_back, inner, own_grad, *grads = attention_stage(
-        sources, segments, modality, head_gain, query, query_raw, back_attended, memories
+        block_rank.astype(jnp.int32).reshape(1),
+        block_order,
+        segments,
+        modality,
+        head_gain,
+        query,
+        query_raw,
+        back_attended,
+        memories,
     )
     incoming = [
         lax.ppermute(grad, "seq", inverted(seq_pairs(step, block_count)))
@@ -624,7 +609,7 @@
     ]
 
     projected, gradient_part = turn_stage(
-        rank, modality, output_held, attended, query_back, query_weight, split
+        rank, modality, output_weight, attended, query_back, query_weight, split
     )
     if shared:
         total = own_grad + sum(grad.astype(f32) for grad in incoming)
@@ -650,17 +635,20 @@
         other = lax.ppermute(sent, "tensor", swap)
         kept = kept_stage(rank, modality, gradient_part, key_weight, slice_back)
         backs = [kept, other]
-        attention_out = projected[1] + lax.ppermute(passed, "tensor", swap).astype(f32)
-        attention_out = attention_out.astype(bf16)
+        projected = [projected[1], lax.ppermute(passed, "tensor", swap)]
+        gain = norm_gain
     else:
         inners = [lax.psum(inner, "tensor")]
         backs = [scatter_columns(sent)]
         attention_out = scatter_columns(passed)
-    gain = lax.dynamic_slice_in_dim(norm_gain, tensor_rank * local_width, local_width, 1)
-    grad_input = finish(
-        full_width, len(backs), modality, gain, row_factor, inputs, backs, inners
-    )
-    return (attention_out, grad_input)
+        projected = []
+        gain = lax.dynamic_slice_in_dim(norm_gain, tensor_rank * local_width, local_width, 1)
+    results = finish(
+        rank, full_width, modality, gain, row_factor, inputs, backs, inners, projected
+    )
+    if split:
+        attention_out = results[0]
+    return (attention_out, results[-1])
 
 
 def solution(mesh):

time: 54 us -> 46.2 us (0.86)
  Pallas kernels: 36.7 us -> 32.2 us
  local copies, waits for them, and re-layouts: 3.02 us -> 0.07 us
  other arithmetic: 1.97 us -> 0.01 us
  waiting for transfers between devices: 0.03 us -> 1.62 us
    unnamed x22 -> x26, local copies, waits for them, and re-layouts: 2.38 us -> 0.07 us
    convert_element_type x1 -> x0, other arithmetic: 1.88 us -> none  [local(): attention_out = attention_out.astype(bf16)]
    pallas_call x1, Pallas kernels: 3.13 us -> 1.47 us  [key_back_stage(): pl.pallas_call(functools.partial(key_back_kernel, split), out_shape=[jax....]
    pallas_call x1, Pallas kernels: 2.91 us -> 1.28 us  [kept_stage(): pl.pallas_call(kept_kernel, out_shape=jax.ShapeDtypeStruct((back.shape[0]...]
    pallas_call x1, Pallas kernels: 10 us -> 8.59 us  [turn_stage(): pl.pallas_call(functools.partial(turn_kernel, pieces, len(outs)), out_sha...]
    ppermute x3, waiting for transfers between devices: 0.01 us -> 1.01 us  [local(): lax.ppermute(grad, 'seq', inverted(seq_pairs(step, block_count)))]
    gather x1 -> x0, local copies, waits for them, and re-layouts: 0.64 us -> none  [local(): sources = block_order[jnp.stack(order)]]
    ppermute x1, waiting for transfers between devices: 0.01 us -> 0.6 us  [local(): inners = [inner, lax.ppermute(inner, 'tensor', swap)]]
  transfers between devices with their start and end apart: 11 -> 11, of which waited for: 0 -> 2; matrix products, arithmetic and copies ran while one was open for 5% -> 0% of each run, Pallas kernels for 53% -> 55%
where the time goes in v5:
time: 46.2 us; the launch traced here: 46.1 us
  Pallas kernels  32.2 us (70%)
  starting transfers between devices  11.3 us (24%)
  waiting for transfers between devices  1.62 us (4%)
  between operations  0.9 us (2%)
    pallas_call x1, Pallas kernels, middle_stage(): pl.pallas_call(functools.partial(middle_kernel, len(parts), pieces), out_...  10.7 us
    pallas_call x1, Pallas kernels, turn_stage(): pl.pallas_call(functools.partial(turn_kernel, pieces, len(outs)), out_sha...  8.59 us
    ppermute x3, starting transfers between devices, local(): memories.append(lax.ppermute(memory, 'seq', seq_pairs(step, block_count)))  5.66 us
    ppermute x3, starting transfers between devices, local(): lax.ppermute(grad, 'seq', inverted(seq_pairs(step, block_count)))  4.42 us
    pallas_call x1, Pallas kernels, attention_stage(): pl.pallas_call(functools.partial(attention_kernel, blocks, pairs, per_gro...  3.86 us
    pallas_call x1, Pallas kernels, fetch(): pl.pallas_call(functools.partial(fetch_kernel, pieces), out_shape=residen...  3.32 us
    pallas_call x1, Pallas kernels, key_stage(): pl.pallas_call(functools.partial(key_kernel, len(parts)), out_shape=[jax....  1.57 us
    pallas_call x1, Pallas kernels, key_back_stage(): pl.pallas_call(functools.partial(key_back_kernel, split), out_shape=[jax....  1.47 us
  transfers between devices with their start and end apart: 11, of which 2 were waited for; matrix products, arithmetic and copies ran while one was open for 0% of the time, Pallas kernels for 55%

profile of v5, /device:TPU:0, one launch (start us, length us, event | category | flops | bytes accessed | tf_op | source)
XLA Modules:
  0.0 46.1 jit_solution(7203481891460338140)
XLA Ops:
  0.6 0.5 %collective-permute-start = (bf16[128,1792]{1,0:T(8,128)(2,1)}, bf16[128,1792]{1,0:T(8,128)(2,1)S(1)}, u32[]{:S(2)}, u32[]{:S(2)}) collective-permute-start(bf16[128,1792]{1,0:T(8,128)(2,1)} %refs_4_.5), channel_id=1, source_target_pairs={{0,1},{1,0},{2,3},{3,2},{4,5},{5,4},{6,7},{7,6},{8,9},{9,8},{10,11... | collective-permute-start | bytes 1376264 | tf_op jit(solution)/shard_map/ppermute | solution.py:569
  1.1 0.1 collective-permute-start.1
  1.2 0.0 copy-start.1
  1.2 0.0 copy-start.2
  1.2 0.0 copy-start.3
  1.2 0.0 copy-start.4
  1.2 0.0 slice-start.2
  1.3 0.0 slice-start.3
  1.3 3.3 %fetch.1.refs_4_ = bf16[2,3584,512]{2,1,0:T(8,128)(2,1)S(1)} custom-call(bf16[2,3584,512]{2,1,0:T(8,128)(2,1)} %weight_ref.3), custom_call_target="tpu_custom_call" | custom-call | flops 200000000 | bytes 400000 | tf_op jit(solution)/shard_map/fetch/pallas_call | solution.py:167
  4.6 0.0 collective-permute-done.refs_6_
  4.6 0.0 copy-done.1
  4.6 0.0 copy-done.2
  4.6 0.0 copy-done.3
  4.6 0.0 copy-done.4
  4.6 0.0 slice-start.4
  4.7 0.0 slice-start.5
  4.7 0.0 copy-start
  4.7 1.6 %key_stage.1 = (bf16[128,512]{1,0:T(8,128)(2,1)S(1)}, f32[128,512]{1,0:T(8,128)S(1)}, bf16[128,3584]{1,0:T(8,128)(2,1)S(1)}, f32[1,128]{1,0:T(1,128)S(1)}) custom-call(s32[1]{0:T(128)} %bitcast.refs_0_.rank_ref, s32[1,128]{1,0:T(1,128)S(1)} %bitcast.8, f32[2,3584]{1,0:T(2,128)S(1)} %copy-done.4, f32[2,2,128]{2,1,0:T(2,128)S(1)} %copy-done.1, ...), custom_call_target="tpu_custom_call" | custom-call | flops 10000000000 | bytes 20000000 | tf_op jit(solution)/shard_map/key_stage/pallas_call | solution.py:209
  6.2 3.1 %collective-permute-start.2 = (bf16[128,512]{1,0:T(8,128)(2,1)S(1)}, bf16[128,512]{1,0:T(8,128)(2,1)S(1)}, u32[]{:S(2)}, u32[]{:S(2)}) collective-permute-start(bf16[128,512]{1,0:T(8,128)(2,1)S(1)} %get-tuple-element.28.refs_8_), channel_id=1, source_target_pairs={{0,2},{2,0},{4,6},{6,4},{1,3},{3,1},{5,7},{7,5},{8,10},{10,8},{12,... | collective-permute-start | bytes 393224 | tf_op jit(solution)/shard_map/ppermute | solution.py:590
  9.3 2.6 %collective-permute-start.3 = (bf16[128,512]{1,0:T(8,128)(2,1)S(1)}, bf16[128,512]{1,0:T(8,128)(2,1)S(1)}, u32[]{:S(2)}, u32[]{:S(2)}) collective-permute-start(bf16[128,512]{1,0:T(8,128)(2,1)S(1)} %get-tuple-element.28.refs_8_), channel_id=1, source_target_pairs={{0,4},{2,6},{4,0},{6,2},{1,5},{3,7},{5,1},{7,3},{8,12},{10,14},{12... | collective-permute-start | bytes 393224 | tf_op jit(solution)/shard_map/ppermute | solution.py:590
  11.9 0.0 collective-permute-start.4
  11.9 0.0 collective-permute-done.1.refs_7_
  11.9 0.0 slice-done.2
  11.9 0.0 slice-done.3
  11.9 0.0 slice-done.4
  11.9 0.0 slice-done.5
  11.9 0.0 copy-done
  12.0 0.0 copy-start.5
  12.0 0.0 copy-start.6
  12.0 10.7 %middle_stage.1 = (bf16[128,1024]{1,0:T(8,128)(2,1)S(1)}, f32[128,1024]{1,0:T(8,128)S(1)}, bf16[128,1024]{1,0:T(8,128)(2,1)S(1)}) custom-call(s32[1]{0:T(128)} %bitcast.refs_0_.rank_ref, s32[1,128]{1,0:T(1,128)S(1)} %bitcast.9, f32[2,2,128]{2,1,0:T(2,128)S(1)} %copy-done.1, bf16[128,3584]{1,0:T(8,128)(2,1)S(1)} %get-tuple-element.24.refs_3_, ...), custom_call_target="tpu_custom_call" | custom-call | flops 8000000000 | bytes 16000000 | tf_op jit(solution)/shard_map/middle_stage/pallas_call | solution.py:256
  22.7 0.0 collective-permute-done.2.refs_9_
  22.7 0.0 collective-permute-done.3.refs_10_
  22.7 0.0 collective-permute-done.4.refs_11_
  22.7 0.0 copy-done.5
  22.7 0.0 copy-done.6
  22.7 0.0 slice-start
  22.7 3.9 %attention_stage.1 = (bf16[128,1024]{1,0:T(8,128)(2,1)S(1)}, bf16[128,1024]{1,0:T(8,128)(2,1)S(1)}, f32[1,128]{1,0:T(1,128)S(1)}, f32[128,512]{1,0:T(8,128)S(1)}...) custom-call(s32[1]{0:T(128)} %bitcast.2.refs_0_, s32[4]{0:T(128)S(1)} %copy-done.6, ...), custom_call_target="tpu_custom_call" | custom-call | flops 4000000000 | bytes 8000000 | tf_op jit(solution)/shard_map/attention_stage/pallas_call | solution.py:361
  26.6 1.8 %collective-permute-start.5 = (bf16[128,512]{1,0:T(8,128)(2,1)S(1)}, bf16[128,512]{1,0:T(8,128)(2,1)S(1)}, u32[]{:S(2)}, u32[]{:S(2)}) collective-permute-start(bf16[128,512]{1,0:T(8,128)(2,1)S(1)} %get-tuple-element.36), channel_id=1, source_target_pairs={{2,0},{0,2},{6,4},{4,6},{3,1},{1,3},{7,5},{5,7},{10,8},{8,10},{14,... | collective-permute-start | bytes 393224 | tf_op jit(solution)/shard_map/ppermute | solution.py:607
  28.4 2.7 %collective-permute-start.6 = (bf16[128,512]{1,0:T(8,128)(2,1)S(1)}, bf16[128,512]{1,0:T(8,128)(2,1)S(1)}, u32[]{:S(2)}, u32[]{:S(2)}) collective-permute-start(bf16[128,512]{1,0:T(8,128)(2,1)S(1)} %get-tuple-element.37), channel_id=1, source_target_pairs={{4,0},{6,2},{0,4},{2,6},{5,1},{7,3},{1,5},{3,7},{12,8},{14,10},{8,... | collective-permute-start | bytes 393224 | tf_op jit(solution)/shard_map/ppermute | solution.py:607
  31.0 0.0 collective-permute-start.7
  31.0 0.0 slice-start.1
  31.0 8.6 %turn_stage.1 = (bf16[128,1792]{1,0:T(8,128)(2,1)S(1)}, f32[128,1792]{1,0:T(8,128)S(1)}, f32[128,3584]{1,0:T(8,128)S(1)}) custom-call(s32[1]{0:T(128)} %bitcast.refs_0_.rank_ref, s32[1,128]{1,0:T(1,128)S(1)} %bitcast.11, bf16[2,1024,3584]{2,1,0:T(8,128)(2,1)S(1)} %bitcast.7, bf16[128,1024]{1,0:T(8,128)(2,1)S(1)} %get-tuple-element.29.refs_3_, ...), custom_call_target="tpu_custom_call" | custom-call | flops 10000000000 | bytes 20000000 | tf_op jit(solution)/shard_map/turn_stage/pallas_call | solution.py:417
  39.6 0.0 collective-permute-done.5.refs_9_
  39.6 1.0 %collective-permute-done.6.refs_10_ = bf16[128,512]{1,0:T(8,128)(2,1)S(1)} collective-permute-done((bf16[128,512]{1,0:T(8,128)(2,1)S(1)}, bf16[128,512]{1,0:T(8,128)(2,1)S(1)}, u32[]{:S(2)}, u32[]{:S(2)}) %collective-permute-start.6) | collective-permute-done | bytes 131104 | tf_op jit(solution)/shard_map/ppermute | solution.py:607
  40.6 0.0 collective-permute-done.7.refs_11_
  40.6 0.0 slice-done
  40.6 0.0 slice-done.1
  40.6 1.5 %key_back_stage.1 = (bf16[128,1792]{1,0:T(8,128)(2,1)S(1)}, bf16[128,512]{1,0:T(8,128)(2,1)S(1)}, f32[1,128]{1,0:T(1,128)S(1)}, bf16[128,1792]{1,0:T(8,128)(2,1)S(1)}) custom-call(s32[1]{0:T(128)} %bitcast.refs_0_.rank_ref, s32[1,128]{1,0:T(1,128)S(1)} %bitcast.12, f32[2,2,128]{2,1,0:T(2,128)S(1)} %copy-done.1, ...), custom_call_target="tpu_custom_call", output_to_operand_aliasing={{3}: (7, {})} | custom-call | flops 2000000000 | bytes 4000000 | tf_op jit(solution)/shard_map/key_back_stage/pallas_call | solution.py:463
  42.1 0.1 collective-permute-start.10
  42.2 0.5 %collective-permute-start.8 = (bf16[128,1792]{1,0:T(8,128)(2,1)S(1)}, bf16[128,1792]{1,0:T(8,128)(2,1)S(1)}, u32[]{:S(2)}, u32[]{:S(2)}) collective-permute-start(bf16[128,1792]{1,0:T(8,128)(2,1)S(1)} %get-tuple-element.40), channel_id=1, source_target_pairs={{0,1},{1,0},{2,3},{3,2},{4,5},{5,4},{6,7},{7,6},{8,9},{9,8},{10,11... | collective-permute-start | bytes 1376264 | tf_op jit(solution)/shard_map/ppermute | solution.py:635
  42.7 0.1 collective-permute-start.9
  42.8 1.3 %kept_stage.1.refs_5_ = f32[128,1792]{1,0:T(8,128)S(1)} custom-call(s32[1]{0:T(128)} %bitcast.refs_0_.rank_ref, s32[1,128]{1,0:T(1,128)S(1)} %bitcast.13, f32[128,3584]{1,0:T(8,128)S(1)} %get-tuple-element.31.refs_5_.part_ref, bf16[2,3584,512]{2,1,0:T(8,128)(2,1)S(1)} %bitcast.5, bf16[128,512]{1,0:T(8,128)(2,1)S(1)} %get-tuple-element.39.back_ref), custom_call_target="tpu_custom_call" | custom-call | flops 2000000000 | bytes 4000000 | tf_op jit(solution)/shard_map/kept_stage/pallas_call | solution.py:490
  44.1 0.6 %collective-permute-done.9.refs_8_ = f32[1,128]{1,0:T(1,128)S(1)} collective-permute-done((f32[1,128]{1,0:T(1,128)S(1)}, f32[1,128]{1,0:T(1,128)S(1)}, u32[]{:S(2)}, u32[]{:S(2)}) %collective-permute-start.9) | collective-permute-done | bytes 544 | tf_op jit(solution)/shard_map/ppermute | solution.py:634
  44.7 0.0 collective-permute-done.10.refs_10_
  44.7 0.0 collective-permute-done.8.refs_6_
  44.7 1.4 %finish.1 = (bf16[128,1792]{1,0:T(8,128)(2,1)}, bf16[128,1792]{1,0:T(8,128)(2,1)}) custom-call(s32[1]{0:T(128)} %bitcast.refs_0_.rank_ref, s32[1,128]{1,0:T(1,128)S(1)} %bitcast.14, f32[2,3584]{1,0:T(2,128)S(1)} %copy-done.4, f32[1,128]{1,0:T(1,128)S(1)} %get-tuple-element.23.refs_3_, bf16[128,1792]{1,0:T(8,128)(2,1)S(1)} %copy-done.3, ...), custom_call_target="tpu_custom_call" | custom-call | flops 1000000000 | bytes 2000000 | tf_op jit(solution)/shard_map/finish/pallas_call | solution.py:532
  (2 shorter events, 0.0 us)
Async XLA Ops:
  0.6 4.0 %collective-permute-start = (bf16[128,1792]{1,0:T(8,128)(2,1)}, bf16[128,1792]{1,0:T(8,128)(2,1)S(1)}, u32[]{:S(2)}, u32[]{:S(2)}) collective-permute-start(bf16[128,1792]{1,0:T(8,128)(2,1)} %refs_4_.5), channel_id=1, source_target_pairs={{0,1},{1,0},{2,3},{3,2},{4,5},{5,4},{6,7},{7,6},{8,9},{9,8},{10,11... | collective-permute-start | bytes 1376264 | tf_op jit(solution)/shard_map/ppermute | solution.py:569
  1.1 10.8 %collective-permute-start.1 = (bf16[128,1792]{1,0:T(8,128)(2,1)}, bf16[128,1792]{1,0:T(8,128)(2,1)S(1)}, u32[]{:S(2)}, u32[]{:S(2)}) collective-permute-start(bf16[128,1792]{1,0:T(8,128)(2,1)} %refs_6_.2), channel_id=1, source_target_pairs={{0,1},{1,0},{2,3},{3,2},{4,5},{5,4},{6,7},{7,6},{8,9},{9,8},{10,11... | collective-permute-start | bytes 1376264 | tf_op jit(solution)/shard_map/ppermute | solution.py:569
  1.2 3.4 %copy-start.1 = (f32[2,2,128]{2,1,0:T(2,128)S(1)}, f32[2,2,128]{2,1,0:T(2,128)}, u32[]{:S(2)}) copy-start(f32[2,2,128]{2,1,0:T(2,128)} %refs_2_.8) | copy-start | bytes 6148
  1.2 3.4 %copy-start.2 = (s32[128]{0:T(128)S(1)}, s32[128]{0:T(128)}, u32[]{:S(2)}) copy-start(s32[128]{0:T(128)} %param.17) | copy-start | bytes 1540
  1.2 3.4 %copy-start.3 = (bf16[128,1792]{1,0:T(8,128)(2,1)S(1)}, bf16[128,1792]{1,0:T(8,128)(2,1)}, u32[]{:S(2)}) copy-start(bf16[128,1792]{1,0:T(8,128)(2,1)} %refs_4_.5) | copy-start | bytes 1376260
  1.2 3.4 %copy-start.4 = (f32[2,3584]{1,0:T(2,128)S(1)}, f32[2,3584]{1,0:T(2,128)}, u32[]{:S(2)}) copy-start(f32[2,3584]{1,0:T(2,128)} %refs_2_.9) | copy-start | bytes 86020
  1.2 10.7 %slice-start.2 = ((s8[14680064]{0:T(1024)(128)(4,1)}), s8[4194304]{0:T(1024)(128)(4,1)S(1)}, s32[]{:S(2)}) async-start(s8[14680064]{0:T(1024)(128)(4,1)} %bitcast.6), calls=%async_computation.2 | async-start | bytes 8388608
  1.3 10.7 %slice-start.3 = ((s8[14680064]{0:T(1024)(128)(4,1)}), s8[4194304]{0:T(1024)(128)(4,1)S(1)}, s32[]{:S(2)}) async-start(s8[14680064]{0:T(1024)(128)(4,1)} %bitcast.6), calls=%async_computation.3 | async-start | bytes 8388608
  4.6 7.3 %slice-start.4 = ((s8[14680064]{0:T(1024)(128)(4,1)}), s8[4194304]{0:T(1024)(128)(4,1)S(1)}, s32[]{:S(2)}) async-start(s8[14680064]{0:T(1024)(128)(4,1)} %bitcast.6), calls=%async_computation.4 | async-start | bytes 8388608
  4.7 7.3 %slice-start.5 = ((s8[14680064]{0:T(1024)(128)(4,1)}), s8[2097152]{0:T(1024)(128)(4,1)S(1)}, s32[]{:S(2)}) async-start(s8[14680064]{0:T(1024)(128)(4,1)} %bitcast.6), calls=%async_computation.5 | async-start | bytes 4194304
  4.7 7.3 %copy-start = (bf16[128,1792]{1,0:T(8,128)(2,1)S(1)}, bf16[128,1792]{1,0:T(8,128)(2,1)}, u32[]{:S(2)}) copy-start(bf16[128,1792]{1,0:T(8,128)(2,1)} %refs_6_.2) | copy-start | bytes 1376260
  6.2 16.4 %collective-permute-start.2 = (bf16[128,512]{1,0:T(8,128)(2,1)S(1)}, bf16[128,512]{1,0:T(8,128)(2,1)S(1)}, u32[]{:S(2)}, u32[]{:S(2)}) collective-permute-start(bf16[128,512]{1,0:T(8,128)(2,1)S(1)} %get-tuple-element.28.refs_8_), channel_id=1, source_target_pairs={{0,2},{2,0},{4,6},{6,4},{1,3},{3,1},{5,7},{7,5},{8,10},{10,8},{12,... | collective-permute-start | bytes 393224 | tf_op jit(solution)/shard_map/ppermute | solution.py:590
  9.3 13.4 %collective-permute-start.3 = (bf16[128,512]{1,0:T(8,128)(2,1)S(1)}, bf16[128,512]{1,0:T(8,128)(2,1)S(1)}, u32[]{:S(2)}, u32[]{:S(2)}) collective-permute-start(bf16[128,512]{1,0:T(8,128)(2,1)S(1)} %get-tuple-element.28.refs_8_), channel_id=1, source_target_pairs={{0,4},{2,6},{4,0},{6,2},{1,5},{3,7},{5,1},{7,3},{8,12},{10,14},{12... | collective-permute-start | bytes 393224 | tf_op jit(solution)/shard_map/ppermute | solution.py:590
  11.9 10.8 %collective-permute-start.4 = (bf16[128,512]{1,0:T(8,128)(2,1)S(1)}, bf16[128,512]{1,0:T(8,128)(2,1)S(1)}, u32[]{:S(2)}, u32[]{:S(2)}) collective-permute-start(bf16[128,512]{1,0:T(8,128)(2,1)S(1)} %get-tuple-element.28.refs_8_), channel_id=1, source_target_pairs={{0,6},{2,4},{4,2},{6,0},{1,7},{3,5},{5,3},{7,1},{8,14},{10,12},{12... | collective-permute-start | bytes 393224 | tf_op jit(solution)/shard_map/ppermute | solution.py:590
  12.0 10.7 %copy-start.5 = (s32[512]{0:T(512)S(1)}, s32[512]{0:T(512)}, u32[]{:S(2)}) copy-start(s32[512]{0:T(512)} %param.18) | copy-start | bytes 6148
  12.0 10.7 %copy-start.6 = (s32[4]{0:T(128)S(1)}, s32[4]{0:T(128)}, u32[]{:S(2)}) copy-start(s32[4]{0:T(128)} %refs_1_.1) | copy-start | bytes 52
  22.7 17.9 %slice-start = ((s8[7340032]{0:T(1024)(128)(4,1)}), s8[4194304]{0:T(1024)(128)(4,1)S(1)}, s32[]{:S(2)}) async-start(s8[7340032]{0:T(1024)(128)(4,1)} %bitcast.4), calls=%async_computation | async-start | bytes 8388608
  26.6 13.0 %collective-permute-start.5 = (bf16[128,512]{1,0:T(8,128)(2,1)S(1)}, bf16[128,512]{1,0:T(8,128)(2,1)S(1)}, u32[]{:S(2)}, u32[]{:S(2)}) collective-permute-start(bf16[128,512]{1,0:T(8,128)(2,1)S(1)} %get-tuple-element.36), channel_id=1, source_target_pairs={{2,0},{0,2},{6,4},{4,6},{3,1},{1,3},{7,5},{5,7},{10,8},{8,10},{14,... | collective-permute-start | bytes 393224 | tf_op jit(solution)/shard_map/ppermute | solution.py:607
  28.4 12.3 %collective-permute-start.6 = (bf16[128,512]{1,0:T(8,128)(2,1)S(1)}, bf16[128,512]{1,0:T(8,128)(2,1)S(1)}, u32[]{:S(2)}, u32[]{:S(2)}) collective-permute-start(bf16[128,512]{1,0:T(8,128)(2,1)S(1)} %get-tuple-element.37), channel_id=1, source_target_pairs={{4,0},{6,2},{0,4},{2,6},{5,1},{7,3},{1,5},{3,7},{12,8},{14,10},{8,... | collective-permute-start | bytes 393224 | tf_op jit(solution)/shard_map/ppermute | solution.py:607
  31.0 9.6 %collective-permute-start.7 = (bf16[128,512]{1,0:T(8,128)(2,1)S(1)}, bf16[128,512]{1,0:T(8,128)(2,1)S(1)}, u32[]{:S(2)}, u32[]{:S(2)}) collective-permute-start(bf16[128,512]{1,0:T(8,128)(2,1)S(1)} %get-tuple-element.38), channel_id=1, source_target_pairs={{6,0},{4,2},{2,4},{0,6},{7,1},{5,3},{3,5},{1,7},{14,8},{12,10},{10... | collective-permute-start | bytes 393224 | tf_op jit(solution)/shard_map/ppermute | solution.py:607
  31.0 9.6 %slice-start.1 = ((s8[7340032]{0:T(1024)(128)(4,1)}), s8[3145728]{0:T(1024)(128)(4,1)S(1)}, s32[]{:S(2)}) async-start(s8[7340032]{0:T(1024)(128)(4,1)} %bitcast.4), calls=%async_computation.1 | async-start | bytes 6291456
  42.1 2.5 %collective-permute-start.10 = (bf16[128,1792]{1,0:T(8,128)(2,1)S(1)}, bf16[128,1792]{1,0:T(8,128)(2,1)S(1)}, u32[]{:S(2)}, u32[]{:S(2)}) collective-permute-start(bf16[128,1792]{1,0:T(8,128)(2,1)S(1)} %get-tuple-element.43), channel_id=1, source_target_pairs={{0,1},{1,0},{2,3},{3,2},{4,5},{5,4},{6,7},{7,6},{8,9},{9,8},{10,11... | collective-permute-start | bytes 1376264 | tf_op jit(solution)/shard_map/ppermute | solution.py:638
  42.2 2.5 %collective-permute-start.8 = (bf16[128,1792]{1,0:T(8,128)(2,1)S(1)}, bf16[128,1792]{1,0:T(8,128)(2,1)S(1)}, u32[]{:S(2)}, u32[]{:S(2)}) collective-permute-start(bf16[128,1792]{1,0:T(8,128)(2,1)S(1)} %get-tuple-element.40), channel_id=1, source_target_pairs={{0,1},{1,0},{2,3},{3,2},{4,5},{5,4},{6,7},{7,6},{8,9},{9,8},{10,11... | collective-permute-start | bytes 1376264 | tf_op jit(solution)/shard_map/ppermute | solution.py:635
  42.7 2.0 %collective-permute-start.9 = (f32[1,128]{1,0:T(1,128)S(1)}, f32[1,128]{1,0:T(1,128)S(1)}, u32[]{:S(2)}, u32[]{:S(2)}) collective-permute-start(f32[1,128]{1,0:T(1,128)S(1)} %get-tuple-element.41.refs_7_), channel_id=1, source_target_pairs={{0,1},{1,0},{2,3},{3,2},{4,5},{5,4},{6,7},{7,6},{8,9},{9,8},{10,11... | collective-permute-start | bytes 1544 | tf_op jit(solution)/shard_map/ppermute | solution.py:634

commit v6 on v5

--- a/solution.py
+++ b/solution.py
@@ -24,6 +24,10 @@
     if count & (count - 1) == 0:
         return [(i, i ^ step) for i in range(count)]
     return [(i, (i + step) % count) for i in range(count)]
+
+
+def seq_steps(count):
+    return sorted(range(1, count), key=lambda step: (step != count // 2, step))
 
 
 def seq_source(rank, step, count):
@@ -230,18 +234,23 @@
     begin_first(copies)
     image = column(modality_ref[...]) > 0.0
     cotangent = in_order(rank_ref[0], part_refs)
-    for start, size in chunks_of(output_ref.shape[1], 256):
+    tiles = chunks_of(output_ref.shape[1], 256)
+    done = 0
+    for turn, (start, size) in enumerate(tiles, 1):
         part = slice(start, start + size)
         back_ref[:, part] = both_back(image, cotangent, output_ref[:, part, :]).astype(bf16)
-    for index, (start, size) in enumerate(pieces):
-        arrive(copies, index)
-        part = slice(start, start + size)
-        product = both_experts(image, normed_ref[:, part], slots[index % AHEAD])
-        if index == 0:
-            raw_ref[...] = product
-        else:
-            raw_ref[...] += product
-        begin(copies, index + AHEAD)
+        until = len(pieces) * turn // len(tiles)
+        for index in range(done, until):
+            arrive(copies, index)
+            start, size = pieces[index]
+            part = slice(start, start + size)
+            product = both_experts(image, normed_ref[:, part], slots[index % AHEAD])
+            if index == 0:
+                raw_ref[...] = product
+            else:
+                raw_ref[...] += product
+            begin(copies, index + AHEAD)
+        done = until
     scaling = jnp.where(image, head_ref[1, 0:1, :], head_ref[0, 0:1, :])
     for h in range(raw_ref.shape[1] // HEAD_DIM):
         part = slice(h * HEAD_DIM, (h + 1) * HEAD_DIM)
@@ -302,8 +311,8 @@
     key = jnp.concatenate([m[:, :HEAD_DIM] for m in memory_refs], axis=0)
     value = jnp.concatenate([m[:, HEAD_DIM:] for m in memory_refs], axis=0)
     lines = [
-        segments_ref[pl.ds(order_ref[seq_source(place_ref[0], b, blocks)], 1), :]
-        for b in range(blocks)
+        segments_ref[pl.ds(order_ref[seq_source(place_ref[0], step, blocks)], 1), :]
+        for step in [0, *seq_steps(blocks)]
     ]
     key_segments = jnp.concatenate(lines, axis=1)
     query_segments = column(lines[0])
@@ -586,7 +595,7 @@
             jnp.concatenate([partner, memory], 1),
         )
     memories = [memory]
-    for step in range(1, block_count):
+    for step in seq_steps(block_count):
         memories.append(lax.ppermute(memory, "seq", seq_pairs(step, block_count)))
 
     query, query_raw, back_attended = middle_stage(
@@ -605,7 +614,7 @@
     )
     incoming = [
         lax.ppermute(grad, "seq", inverted(seq_pairs(step, block_count)))
-        for step, grad in enumerate(grads, 1)
+        for step, grad in zip(seq_steps(block_count), grads)
     ]
 
     projected, gradient_part = turn_stage(

time: 46.2 us -> 45.1 us (0.976)
  Pallas kernels: 32.2 us -> 30.7 us
  starting transfers between devices: 11.3 us -> 12.3 us
  waiting for transfers between devices: 1.62 us -> 0.98 us
    pallas_call x1, Pallas kernels: 10.7 us -> 9.23 us  [middle_stage(): pl.pallas_call(functools.partial(middle_kernel, len(parts), pieces), out_...]
    ppermute x3, starting transfers between devices: 4.42 us -> 5.42 us  [local(): lax.ppermute(grad, 'seq', inverted(seq_pairs(step, block_count)))]
    ppermute x3, waiting for transfers between devices: 1.01 us -> 0.37 us  [local(): lax.ppermute(grad, 'seq', inverted(seq_pairs(step, block_count)))]
  transfers between devices with their start and end apart: 11 -> 11, of which waited for: 2 -> 2; matrix products, arithmetic and copies ran while one was open for 0% -> 0% of each run, Pallas kernels for 55% -> 53%
where the time goes in v6:
time: 45.1 us; the launch traced here: 45 us
  Pallas kernels  30.7 us (68%)
  starting transfers between devices  12.3 us (27%)
  waiting for transfers between devices  0.98 us (2%)
  between operations  0.9 us (2%)
    pallas_call x1, Pallas kernels, middle_stage(): pl.pallas_call(functools.partial(middle_kernel, len(parts), pieces), out_...  9.23 us
    pallas_call x1, Pallas kernels, turn_stage(): pl.pallas_call(functools.partial(turn_kernel, pieces, len(outs)), out_sha...  8.59 us
    ppermute x3, starting transfers between devices, local(): memories.append(lax.ppermute(memory, 'seq', seq_pairs(step, block_count)))  5.66 us
    ppermute x3, starting transfers between devices, local(): lax.ppermute(grad, 'seq', inverted(seq_pairs(step, block_count)))  5.42 us
    pallas_call x1, Pallas kernels, attention_stage(): pl.pallas_call(functools.partial(attention_kernel, blocks, pairs, per_gro...  3.86 us
    pallas_call x1, Pallas kernels, fetch(): pl.pallas_call(functools.partial(fetch_kernel, pieces), out_shape=residen...  3.32 us
    pallas_call x1, Pallas kernels, key_stage(): pl.pallas_call(functools.partial(key_kernel, len(parts)), out_shape=[jax....  1.57 us
    pallas_call x1, Pallas kernels, key_back_stage(): pl.pallas_call(functools.partial(key_back_kernel, split), out_shape=[jax....  1.47 us
  transfers between devices with their start and end apart: 11, of which 2 were waited for; matrix products, arithmetic and copies ran while one was open for 0% of the time, Pallas kernels for 53%

profile of v6, /device:TPU:0, one launch (start us, length us, event | category | flops | bytes accessed | tf_op | source)
XLA Modules:
  0.0 45.0 jit_solution(504961494732154373)
XLA Ops:
  0.6 0.5 %collective-permute-start = (bf16[128,1792]{1,0:T(8,128)(2,1)}, bf16[128,1792]{1,0:T(8,128)(2,1)S(1)}, u32[]{:S(2)}, u32[]{:S(2)}) collective-permute-start(bf16[128,1792]{1,0:T(8,128)(2,1)} %refs_4_.5), channel_id=1, source_target_pairs={{0,1},{1,0},{2,3},{3,2},{4,5},{5,4},{6,7},{7,6},{8,9},{9,8},{10,11... | collective-permute-start | bytes 1376264 | tf_op jit(solution)/shard_map/ppermute | solution.py:578
  1.1 0.1 collective-permute-start.1
  1.2 0.0 copy-start.1
  1.2 0.0 copy-start.2
  1.2 0.0 copy-start.3
  1.2 0.0 copy-start.4
  1.2 0.0 slice-start.2
  1.3 0.0 slice-start.3
  1.3 3.3 %fetch.1.refs_4_ = bf16[2,3584,512]{2,1,0:T(8,128)(2,1)S(1)} custom-call(bf16[2,3584,512]{2,1,0:T(8,128)(2,1)} %weight_ref.3), custom_call_target="tpu_custom_call" | custom-call | flops 200000000 | bytes 400000 | tf_op jit(solution)/shard_map/fetch/pallas_call | solution.py:171
  4.6 0.0 collective-permute-done.refs_6_
  4.6 0.0 copy-done.1
  4.6 0.0 copy-done.2
  4.6 0.0 copy-done.3
  4.6 0.0 copy-done.4
  4.6 0.0 slice-start.4
  4.7 0.0 slice-start.5
  4.7 0.0 copy-start
  4.7 1.6 %key_stage.1 = (bf16[128,512]{1,0:T(8,128)(2,1)S(1)}, f32[128,512]{1,0:T(8,128)S(1)}, bf16[128,3584]{1,0:T(8,128)(2,1)S(1)}, f32[1,128]{1,0:T(1,128)S(1)}) custom-call(s32[1]{0:T(128)} %bitcast.refs_0_.rank_ref, s32[1,128]{1,0:T(1,128)S(1)} %bitcast.8, f32[2,3584]{1,0:T(2,128)S(1)} %copy-done.4, f32[2,2,128]{2,1,0:T(2,128)S(1)} %copy-done.1, ...), custom_call_target="tpu_custom_call" | custom-call | flops 10000000000 | bytes 20000000 | tf_op jit(solution)/shard_map/key_stage/pallas_call | solution.py:213
  6.2 4.1 %collective-permute-start.2 = (bf16[128,512]{1,0:T(8,128)(2,1)S(1)}, bf16[128,512]{1,0:T(8,128)(2,1)S(1)}, u32[]{:S(2)}, u32[]{:S(2)}) collective-permute-start(bf16[128,512]{1,0:T(8,128)(2,1)S(1)} %get-tuple-element.28.refs_8_), channel_id=1, source_target_pairs={{0,4},{2,6},{4,0},{6,2},{1,5},{3,7},{5,1},{7,3},{8,12},{10,14},{12... | collective-permute-start | bytes 393224 | tf_op jit(solution)/shard_map/ppermute | solution.py:599
  10.3 1.6 %collective-permute-start.3 = (bf16[128,512]{1,0:T(8,128)(2,1)S(1)}, bf16[128,512]{1,0:T(8,128)(2,1)S(1)}, u32[]{:S(2)}, u32[]{:S(2)}) collective-permute-start(bf16[128,512]{1,0:T(8,128)(2,1)S(1)} %get-tuple-element.28.refs_8_), channel_id=1, source_target_pairs={{0,2},{2,0},{4,6},{6,4},{1,3},{3,1},{5,7},{7,5},{8,10},{10,8},{12,... | collective-permute-start | bytes 393224 | tf_op jit(solution)/shard_map/ppermute | solution.py:599
  11.9 0.0 collective-permute-start.4
  11.9 0.0 collective-permute-done.1.refs_7_
  11.9 0.0 slice-done.2
  11.9 0.0 slice-done.3
  11.9 0.0 slice-done.4
  11.9 0.0 slice-done.5
  11.9 0.0 copy-done
  12.0 0.0 copy-start.5
  12.0 0.0 copy-start.6
  12.0 9.2 %middle_stage.1 = (bf16[128,1024]{1,0:T(8,128)(2,1)S(1)}, f32[128,1024]{1,0:T(8,128)S(1)}, bf16[128,1024]{1,0:T(8,128)(2,1)S(1)}) custom-call(s32[1]{0:T(128)} %bitcast.refs_0_.rank_ref, s32[1,128]{1,0:T(1,128)S(1)} %bitcast.9, f32[2,2,128]{2,1,0:T(2,128)S(1)} %copy-done.1, bf16[128,3584]{1,0:T(8,128)(2,1)S(1)} %get-tuple-element.24.refs_3_, ...), custom_call_target="tpu_custom_call" | custom-call | flops 8000000000 | bytes 16000000 | tf_op jit(solution)/shard_map/middle_stage/pallas_call | solution.py:265
  21.2 0.0 collective-permute-done.2.refs_9_
  21.2 0.0 collective-permute-done.3.refs_10_
  21.2 0.0 collective-permute-done.4.refs_11_
  21.3 0.0 copy-done.5
  21.3 0.0 copy-done.6
  21.3 0.0 slice-start
  21.3 3.9 %attention_stage.1 = (bf16[128,1024]{1,0:T(8,128)(2,1)S(1)}, bf16[128,1024]{1,0:T(8,128)(2,1)S(1)}, f32[1,128]{1,0:T(1,128)S(1)}, f32[128,512]{1,0:T(8,128)S(1)}...) custom-call(s32[1]{0:T(128)} %bitcast.2.refs_0_, s32[4]{0:T(128)S(1)} %copy-done.6, ...), custom_call_target="tpu_custom_call" | custom-call | flops 4000000000 | bytes 8000000 | tf_op jit(solution)/shard_map/attention_stage/pallas_call | solution.py:370
  25.1 3.9 %collective-permute-start.5 = (bf16[128,512]{1,0:T(8,128)(2,1)S(1)}, bf16[128,512]{1,0:T(8,128)(2,1)S(1)}, u32[]{:S(2)}, u32[]{:S(2)}) collective-permute-start(bf16[128,512]{1,0:T(8,128)(2,1)S(1)} %get-tuple-element.36), channel_id=1, source_target_pairs={{4,0},{6,2},{0,4},{2,6},{5,1},{7,3},{1,5},{3,7},{12,8},{14,10},{8,... | collective-permute-start | bytes 393224 | tf_op jit(solution)/shard_map/ppermute | solution.py:616
  29.0 0.5 %collective-permute-start.6 = (bf16[128,512]{1,0:T(8,128)(2,1)S(1)}, bf16[128,512]{1,0:T(8,128)(2,1)S(1)}, u32[]{:S(2)}, u32[]{:S(2)}) collective-permute-start(bf16[128,512]{1,0:T(8,128)(2,1)S(1)} %get-tuple-element.37), channel_id=1, source_target_pairs={{2,0},{0,2},{6,4},{4,6},{3,1},{1,3},{7,5},{5,7},{10,8},{8,10},{14,... | collective-permute-start | bytes 393224 | tf_op jit(solution)/shard_map/ppermute | solution.py:616
  29.6 1.0 %collective-permute-start.7 = (bf16[128,512]{1,0:T(8,128)(2,1)S(1)}, bf16[128,512]{1,0:T(8,128)(2,1)S(1)}, u32[]{:S(2)}, u32[]{:S(2)}) collective-permute-start(bf16[128,512]{1,0:T(8,128)(2,1)S(1)} %get-tuple-element.38), channel_id=1, source_target_pairs={{6,0},{4,2},{2,4},{0,6},{7,1},{5,3},{3,5},{1,7},{14,8},{12,10},{10... | collective-permute-start | bytes 393224 | tf_op jit(solution)/shard_map/ppermute | solution.py:616
  30.6 0.0 slice-start.1
  30.6 8.6 %turn_stage.1 = (bf16[128,1792]{1,0:T(8,128)(2,1)S(1)}, f32[128,1792]{1,0:T(8,128)S(1)}, f32[128,3584]{1,0:T(8,128)S(1)}) custom-call(s32[1]{0:T(128)} %bitcast.refs_0_.rank_ref, s32[1,128]{1,0:T(1,128)S(1)} %bitcast.11, bf16[2,1024,3584]{2,1,0:T(8,128)(2,1)S(1)} %bitcast.7, bf16[128,1024]{1,0:T(8,128)(2,1)S(1)} %get-tuple-element.29.refs_3_, ...), custom_call_target="tpu_custom_call" | custom-call | flops 10000000000 | bytes 20000000 | tf_op jit(solution)/shard_map/turn_stage/pallas_call | solution.py:426
  39.2 0.0 collective-permute-done.5.refs_9_
  39.2 0.4 collective-permute-done.6.refs_10_
  39.5 0.0 collective-permute-done.7.refs_11_
  39.5 0.0 slice-done
  39.6 0.0 slice-done.1
  39.6 1.5 %key_back_stage.1 = (bf16[128,1792]{1,0:T(8,128)(2,1)S(1)}, bf16[128,512]{1,0:T(8,128)(2,1)S(1)}, f32[1,128]{1,0:T(1,128)S(1)}, bf16[128,1792]{1,0:T(8,128)(2,1)S(1)}) custom-call(s32[1]{0:T(128)} %bitcast.refs_0_.rank_ref, s32[1,128]{1,0:T(1,128)S(1)} %bitcast.12, f32[2,2,128]{2,1,0:T(2,128)S(1)} %copy-done.1, ...), custom_call_target="tpu_custom_call", output_to_operand_aliasing={{3}: (7, {})} | custom-call | flops 2000000000 | bytes 4000000 | tf_op jit(solution)/shard_map/key_back_stage/pallas_call | solution.py:472
  41.0 0.1 collective-permute-start.10
  41.1 0.5 %collective-permute-start.8 = (bf16[128,1792]{1,0:T(8,128)(2,1)S(1)}, bf16[128,1792]{1,0:T(8,128)(2,1)S(1)}, u32[]{:S(2)}, u32[]{:S(2)}) collective-permute-start(bf16[128,1792]{1,0:T(8,128)(2,1)S(1)} %get-tuple-element.40), channel_id=1, source_target_pairs={{0,1},{1,0},{2,3},{3,2},{4,5},{5,4},{6,7},{7,6},{8,9},{9,8},{10,11... | collective-permute-start | bytes 1376264 | tf_op jit(solution)/shard_map/ppermute | solution.py:644
  41.6 0.1 collective-permute-start.9
  41.7 1.3 %kept_stage.1.refs_5_ = f32[128,1792]{1,0:T(8,128)S(1)} custom-call(s32[1]{0:T(128)} %bitcast.refs_0_.rank_ref, s32[1,128]{1,0:T(1,128)S(1)} %bitcast.13, f32[128,3584]{1,0:T(8,128)S(1)} %get-tuple-element.31.refs_5_.part_ref, bf16[2,3584,512]{2,1,0:T(8,128)(2,1)S(1)} %bitcast.5, bf16[128,512]{1,0:T(8,128)(2,1)S(1)} %get-tuple-element.39.back_ref), custom_call_target="tpu_custom_call" | custom-call | flops 2000000000 | bytes 4000000 | tf_op jit(solution)/shard_map/kept_stage/pallas_call | solution.py:499
  43.0 0.6 %collective-permute-done.9.refs_8_ = f32[1,128]{1,0:T(1,128)S(1)} collective-permute-done((f32[1,128]{1,0:T(1,128)S(1)}, f32[1,128]{1,0:T(1,128)S(1)}, u32[]{:S(2)}, u32[]{:S(2)}) %collective-permute-start.9) | collective-permute-done | bytes 544 | tf_op jit(solution)/shard_map/ppermute | solution.py:643
  43.6 0.0 collective-permute-done.10.refs_10_
  43.6 0.0 collective-permute-done.8.refs_6_
  43.6 1.4 %finish.1 = (bf16[128,1792]{1,0:T(8,128)(2,1)}, bf16[128,1792]{1,0:T(8,128)(2,1)}) custom-call(s32[1]{0:T(128)} %bitcast.refs_0_.rank_ref, s32[1,128]{1,0:T(1,128)S(1)} %bitcast.14, f32[2,3584]{1,0:T(2,128)S(1)} %copy-done.4, f32[1,128]{1,0:T(1,128)S(1)} %get-tuple-element.23.refs_3_, bf16[128,1792]{1,0:T(8,128)(2,1)S(1)} %copy-done.3, ...), custom_call_target="tpu_custom_call" | custom-call | flops 1000000000 | bytes 2000000 | tf_op jit(solution)/shard_map/finish/pallas_call | solution.py:541
  (2 shorter events, 0.0 us)
Async XLA Ops:
  0.6 4.0 %collective-permute-start = (bf16[128,1792]{1,0:T(8,128)(2,1)}, bf16[128,1792]{1,0:T(8,128)(2,1)S(1)}, u32[]{:S(2)}, u32[]{:S(2)}) collective-permute-start(bf16[128,1792]{1,0:T(8,128)(2,1)} %refs_4_.5), channel_id=1, source_target_pairs={{0,1},{1,0},{2,3},{3,2},{4,5},{5,4},{6,7},{7,6},{8,9},{9,8},{10,11... | collective-permute-start | bytes 1376264 | tf_op jit(solution)/shard_map/ppermute | solution.py:578
  1.1 10.8 %collective-permute-start.1 = (bf16[128,1792]{1,0:T(8,128)(2,1)}, bf16[128,1792]{1,0:T(8,128)(2,1)S(1)}, u32[]{:S(2)}, u32[]{:S(2)}) collective-permute-start(bf16[128,1792]{1,0:T(8,128)(2,1)} %refs_6_.2), channel_id=1, source_target_pairs={{0,1},{1,0},{2,3},{3,2},{4,5},{5,4},{6,7},{7,6},{8,9},{9,8},{10,11... | collective-permute-start | bytes 1376264 | tf_op jit(solution)/shard_map/ppermute | solution.py:578
  1.2 3.4 %copy-start.1 = (f32[2,2,128]{2,1,0:T(2,128)S(1)}, f32[2,2,128]{2,1,0:T(2,128)}, u32[]{:S(2)}) copy-start(f32[2,2,128]{2,1,0:T(2,128)} %refs_2_.8) | copy-start | bytes 6148
  1.2 3.4 %copy-start.2 = (s32[128]{0:T(128)S(1)}, s32[128]{0:T(128)}, u32[]{:S(2)}) copy-start(s32[128]{0:T(128)} %param.17) | copy-start | bytes 1540
  1.2 3.4 %copy-start.3 = (bf16[128,1792]{1,0:T(8,128)(2,1)S(1)}, bf16[128,1792]{1,0:T(8,128)(2,1)}, u32[]{:S(2)}) copy-start(bf16[128,1792]{1,0:T(8,128)(2,1)} %refs_4_.5) | copy-start | bytes 1376260
  1.2 3.4 %copy-start.4 = (f32[2,3584]{1,0:T(2,128)S(1)}, f32[2,3584]{1,0:T(2,128)}, u32[]{:S(2)}) copy-start(f32[2,3584]{1,0:T(2,128)} %refs_2_.9) | copy-start | bytes 86020
  1.2 10.7 %slice-start.2 = ((s8[14680064]{0:T(1024)(128)(4,1)}), s8[4194304]{0:T(1024)(128)(4,1)S(1)}, s32[]{:S(2)}) async-start(s8[14680064]{0:T(1024)(128)(4,1)} %bitcast.6), calls=%async_computation.2 | async-start | bytes 8388608
  1.3 10.7 %slice-start.3 = ((s8[14680064]{0:T(1024)(128)(4,1)}), s8[4194304]{0:T(1024)(128)(4,1)S(1)}, s32[]{:S(2)}) async-start(s8[14680064]{0:T(1024)(128)(4,1)} %bitcast.6), calls=%async_computation.3 | async-start | bytes 8388608
  4.6 7.3 %slice-start.4 = ((s8[14680064]{0:T(1024)(128)(4,1)}), s8[4194304]{0:T(1024)(128)(4,1)S(1)}, s32[]{:S(2)}) async-start(s8[14680064]{0:T(1024)(128)(4,1)} %bitcast.6), calls=%async_computation.4 | async-start | bytes 8388608
  4.7 7.3 %slice-start.5 = ((s8[14680064]{0:T(1024)(128)(4,1)}), s8[2097152]{0:T(1024)(128)(4,1)S(1)}, s32[]{:S(2)}) async-start(s8[14680064]{0:T(1024)(128)(4,1)} %bitcast.6), calls=%async_computation.5 | async-start | bytes 4194304
  4.7 7.3 %copy-start = (bf16[128,1792]{1,0:T(8,128)(2,1)S(1)}, bf16[128,1792]{1,0:T(8,128)(2,1)}, u32[]{:S(2)}) copy-start(bf16[128,1792]{1,0:T(8,128)(2,1)} %refs_6_.2) | copy-start | bytes 1376260
  6.2 15.0 %collective-permute-start.2 = (bf16[128,512]{1,0:T(8,128)(2,1)S(1)}, bf16[128,512]{1,0:T(8,128)(2,1)S(1)}, u32[]{:S(2)}, u32[]{:S(2)}) collective-permute-start(bf16[128,512]{1,0:T(8,128)(2,1)S(1)} %get-tuple-element.28.refs_8_), channel_id=1, source_target_pairs={{0,4},{2,6},{4,0},{6,2},{1,5},{3,7},{5,1},{7,3},{8,12},{10,14},{12... | collective-permute-start | bytes 393224 | tf_op jit(solution)/shard_map/ppermute | solution.py:599
  10.3 10.9 %collective-permute-start.3 = (bf16[128,512]{1,0:T(8,128)(2,1)S(1)}, bf16[128,512]{1,0:T(8,128)(2,1)S(1)}, u32[]{:S(2)}, u32[]{:S(2)}) collective-permute-start(bf16[128,512]{1,0:T(8,128)(2,1)S(1)} %get-tuple-element.28.refs_8_), channel_id=1, source_target_pairs={{0,2},{2,0},{4,6},{6,4},{1,3},{3,1},{5,7},{7,5},{8,10},{10,8},{12,... | collective-permute-start | bytes 393224 | tf_op jit(solution)/shard_map/ppermute | solution.py:599
  11.9 9.3 %collective-permute-start.4 = (bf16[128,512]{1,0:T(8,128)(2,1)S(1)}, bf16[128,512]{1,0:T(8,128)(2,1)S(1)}, u32[]{:S(2)}, u32[]{:S(2)}) collective-permute-start(bf16[128,512]{1,0:T(8,128)(2,1)S(1)} %get-tuple-element.28.refs_8_), channel_id=1, source_target_pairs={{0,6},{2,4},{4,2},{6,0},{1,7},{3,5},{5,3},{7,1},{8,14},{10,12},{12... | collective-permute-start | bytes 393224 | tf_op jit(solution)/shard_map/ppermute | solution.py:599
  12.0 9.3 %copy-start.5 = (s32[512]{0:T(512)S(1)}, s32[512]{0:T(512)}, u32[]{:S(2)}) copy-start(s32[512]{0:T(512)} %param.18) | copy-start | bytes 6148
  12.0 9.3 %copy-start.6 = (s32[4]{0:T(128)S(1)}, s32[4]{0:T(128)}, u32[]{:S(2)}) copy-start(s32[4]{0:T(128)} %refs_1_.1) | copy-start | bytes 52
  21.3 18.3 %slice-start = ((s8[7340032]{0:T(1024)(128)(4,1)}), s8[4194304]{0:T(1024)(128)(4,1)S(1)}, s32[]{:S(2)}) async-start(s8[7340032]{0:T(1024)(128)(4,1)} %bitcast.4), calls=%async_computation | async-start | bytes 8388608
  25.1 14.0 %collective-permute-start.5 = (bf16[128,512]{1,0:T(8,128)(2,1)S(1)}, bf16[128,512]{1,0:T(8,128)(2,1)S(1)}, u32[]{:S(2)}, u32[]{:S(2)}) collective-permute-start(bf16[128,512]{1,0:T(8,128)(2,1)S(1)} %get-tuple-element.36), channel_id=1, source_target_pairs={{4,0},{6,2},{0,4},{2,6},{5,1},{7,3},{1,5},{3,7},{12,8},{14,10},{8,... | collective-permute-start | bytes 393224 | tf_op jit(solution)/shard_map/ppermute | solution.py:616
  29.0 10.5 %collective-permute-start.6 = (bf16[128,512]{1,0:T(8,128)(2,1)S(1)}, bf16[128,512]{1,0:T(8,128)(2,1)S(1)}, u32[]{:S(2)}, u32[]{:S(2)}) collective-permute-start(bf16[128,512]{1,0:T(8,128)(2,1)S(1)} %get-tuple-element.37), channel_id=1, source_target_pairs={{2,0},{0,2},{6,4},{4,6},{3,1},{1,3},{7,5},{5,7},{10,8},{8,10},{14,... | collective-permute-start | bytes 393224 | tf_op jit(solution)/shard_map/ppermute | solution.py:616
  29.6 10.0 %collective-permute-start.7 = (bf16[128,512]{1,0:T(8,128)(2,1)S(1)}, bf16[128,512]{1,0:T(8,128)(2,1)S(1)}, u32[]{:S(2)}, u32[]{:S(2)}) collective-permute-start(bf16[128,512]{1,0:T(8,128)(2,1)S(1)} %get-tuple-element.38), channel_id=1, source_target_pairs={{6,0},{4,2},{2,4},{0,6},{7,1},{5,3},{3,5},{1,7},{14,8},{12,10},{10... | collective-permute-start | bytes 393224 | tf_op jit(solution)/shard_map/ppermute | solution.py:616
  30.6 9.0 %slice-start.1 = ((s8[7340032]{0:T(1024)(128)(4,1)}), s8[3145728]{0:T(1024)(128)(4,1)S(1)}, s32[]{:S(2)}) async-start(s8[7340032]{0:T(1024)(128)(4,1)} %bitcast.4), calls=%async_computation.1 | async-start | bytes 6291456
  41.0 2.5 %collective-permute-start.10 = (bf16[128,1792]{1,0:T(8,128)(2,1)S(1)}, bf16[128,1792]{1,0:T(8,128)(2,1)S(1)}, u32[]{:S(2)}, u32[]{:S(2)}) collective-permute-start(bf16[128,1792]{1,0:T(8,128)(2,1)S(1)} %get-tuple-element.43), channel_id=1, source_target_pairs={{0,1},{1,0},{2,3},{3,2},{4,5},{5,4},{6,7},{7,6},{8,9},{9,8},{10,11... | collective-permute-start | bytes 1376264 | tf_op jit(solution)/shard_map/ppermute | solution.py:647
  41.1 2.5 %collective-permute-start.8 = (bf16[128,1792]{1,0:T(8,128)(2,1)S(1)}, bf16[128,1792]{1,0:T(8,128)(2,1)S(1)}, u32[]{:S(2)}, u32[]{:S(2)}) collective-permute-start(bf16[128,1792]{1,0:T(8,128)(2,1)S(1)} %get-tuple-element.40), channel_id=1, source_target_pairs={{0,1},{1,0},{2,3},{3,2},{4,5},{5,4},{6,7},{7,6},{8,9},{9,8},{10,11... | collective-permute-start | bytes 1376264 | tf_op jit(solution)/shard_map/ppermute | solution.py:644
  41.6 2.0 %collective-permute-start.9 = (f32[1,128]{1,0:T(1,128)S(1)}, f32[1,128]{1,0:T(1,128)S(1)}, u32[]{:S(2)}, u32[]{:S(2)}) collective-permute-start(f32[1,128]{1,0:T(1,128)S(1)} %get-tuple-element.41.refs_7_), channel_id=1, source_target_pairs={{0,1},{1,0},{2,3},{3,2},{4,5},{5,4},{6,7},{7,6},{8,9},{9,8},{10,11... | collective-permute-start | bytes 1544 | tf_op jit(solution)/shard_map/ppermute | solution.py:643

commit v7 on v6

--- a/solution.py
+++ b/solution.py
@@ -27,7 +27,7 @@
 
 
 def seq_steps(count):
-    return sorted(range(1, count), key=lambda step: (step != count // 2, step))
+    return sorted(range(1, count), key=lambda step: (step == count // 2, -step))
 
 
 def seq_source(rank, step, count):
@@ -150,34 +150,6 @@
 
 def ring(weights, pieces):
     return pltpu.VMEM((AHEAD, 2, pieces[0][1], weights.shape[2]), weights.dtype)
-
-
-def resident(weights):
-    return pltpu.VMEM(weights.shape, weights.dtype)
-
-
-def fetch_kernel(pieces, weight_ref, held_ref, sem_ref):
-    copies = copies_of(weight_ref, held_ref, sem_ref, pieces)
-    for pair in copies:
-        for copy in pair:
-            copy.start()
-    for pair in copies:
-        for copy in pair:
-            copy.wait()
-
-
-def fetch(weights):
-    pieces = chunks_of(weights.shape[1], 896)
-    return pl.pallas_call(
-        functools.partial(fetch_kernel, pieces),
-        out_shape=resident(weights),
-        in_specs=[ANY],
-        out_specs=VMEM,
-        scratch_shapes=[pltpu.SemaphoreType.DMA((len(pieces), 2))],
-        compiler_params=params(1),
-        cost_estimate=cost(0.2),
-        name="fetch",
-    )(streamed(weights))
 
 
 def key_kernel(count, *refs):
@@ -234,7 +206,7 @@
     begin_first(copies)
     image = column(modality_ref[...]) > 0.0
     cotangent = in_order(rank_ref[0], part_refs)
-    tiles = chunks_of(output_ref.shape[1], 256)
+    tiles = chunks_of(output_ref.shape[1], HEAD_DIM)
     done = 0
     for turn, (start, size) in enumerate(tiles, 1):
         part = slice(start, start + size)
@@ -282,18 +254,6 @@
 
 
 def attention_kernel(blocks, pairs, per_group, *refs):
-    for pair in range(pairs):
-        wide = pl.ds(pair * per_group * HEAD_DIM, per_group * HEAD_DIM)
-        narrow = pl.ds(pair * 2 * HEAD_DIM, 2 * HEAD_DIM)
-        views = list(refs[:5]) + [ref.at[:, wide] for ref in refs[5:8]]
-        views += [ref.at[:, narrow] for ref in refs[8 : 8 + blocks]]
-        views += [ref.at[:, wide] for ref in refs[8 + blocks : 10 + blocks]]
-        views += [refs[10 + blocks]]
-        views += [ref.at[:, narrow] for ref in refs[11 + blocks :]]
-        attention_pair(blocks, per_group, pair == 0, *views)
-
-
-def attention_pair(blocks, per_group, fresh, *refs):
     place_ref, order_ref, segments_ref, modality_ref, head_ref = refs[:5]
     query_ref, raw_ref, back_ref = refs[5:8]
     memory_refs = refs[8 : 8 + blocks]
@@ -301,57 +261,53 @@
     grad_refs = refs[11 + blocks :]
     rows = query_ref.shape[0]
     scale = 1.0 / math.sqrt(HEAD_DIM)
-
-    def heads(ref):
-        return jnp.concatenate(
-            [ref[:, h * HEAD_DIM : (h + 1) * HEAD_DIM] for h in range(per_group)], axis=0
-        )
-
-    query, back = heads(query_ref), heads(back_ref)
-    key = jnp.concatenate([m[:, :HEAD_DIM] for m in memory_refs], axis=0)
-    value = jnp.concatenate([m[:, HEAD_DIM:] for m in memory_refs], axis=0)
     lines = [
         segments_ref[pl.ds(order_ref[seq_source(place_ref[0], step, blocks)], 1), :]
         for step in [0, *seq_steps(blocks)]
     ]
-    key_segments = jnp.concatenate(lines, axis=1)
-    query_segments = column(lines[0])
-    visible = jnp.where(key_segments.astype(f32) <= query_segments, 1.0, 0.0)
-    visible = jnp.concatenate([visible] * per_group, axis=0)
-    scores = dot_nt(query, key) * scale
-    weights = jnp.where(visible > 0.0, jnp.exp(scores), 0.0).astype(bf16)
-    weights32 = weights.astype(f32)
-    denominator = jnp.sum(weights32, axis=1, keepdims=True)
-    numerator = jnp.dot(weights, value, preferred_element_type=f32)
-    attended = (numerator / denominator).astype(bf16)
-    offset = jnp.sum(back.astype(f32) * attended.astype(f32), axis=1, keepdims=True)
-    probability = (weights32 / denominator).astype(bf16)
-    back_prob = dot_nt(back, value)
-    back_score = (probability.astype(f32) * (back_prob - offset)).astype(bf16)
-    back_query = jnp.dot(back_score, key, preferred_element_type=f32) * scale
-    back_key = dot_tn(back_score, query) * scale
-    back_value = dot_tn(probability, back)
-    for b in range(blocks):
-        part = slice(b * rows, (b + 1) * rows)
-        grad_refs[b][:, :HEAD_DIM] = back_key[part].astype(grad_refs[b].dtype)
-        grad_refs[b][:, HEAD_DIM:] = back_value[part].astype(grad_refs[b].dtype)
+    key_segments = jnp.concatenate(lines, axis=1).astype(f32)
+    visible = key_segments <= column(lines[0])
     image = column(modality_ref[...]) > 0.0
     scaling = jnp.where(image, head_ref[1, 0:1, :], head_ref[0, 0:1, :])
     inner = jnp.zeros((rows, 1), f32)
-    for h in range(per_group):
-        part = slice(h * rows, (h + 1) * rows)
-        columns = slice(h * HEAD_DIM, (h + 1) * HEAD_DIM)
-        attended_ref[:, columns] = attended[part]
-        raw = raw_ref[:, columns]
-        query_back = norm_back(raw, inverse_norm(raw), scaling, back_query[part]).astype(bf16)
-        query_back_ref[:, columns] = query_back
-        inner += jnp.sum(query_back.astype(f32) * raw, axis=1, keepdims=True)
-    inner = row_of(inner)
-
-    if fresh:
-        inner_ref[...] = inner
-    else:
-        inner_ref[...] += inner
+    for pair in range(pairs):
+        columns = [
+            slice(h * HEAD_DIM, (h + 1) * HEAD_DIM)
+            for h in range(pair * per_group, (pair + 1) * per_group)
+        ]
+        parts = [slice(h * rows, (h + 1) * rows) for h in range(per_group)]
+        keys = slice(2 * pair * HEAD_DIM, (2 * pair + 1) * HEAD_DIM)
+        values = slice((2 * pair + 1) * HEAD_DIM, (2 * pair + 2) * HEAD_DIM)
+        query = jnp.concatenate([query_ref[:, c] for c in columns], axis=0)
+        back = jnp.concatenate([back_ref[:, c] for c in columns], axis=0)
+        key = jnp.concatenate([m[:, keys] for m in memory_refs], axis=0)
+        value = jnp.concatenate([m[:, values] for m in memory_refs], axis=0)
+        scores = dot_nt(query, key) * (scale * math.log2(math.e))
+        weights = jnp.concatenate(
+            [jnp.where(visible, jnp.exp2(scores[p]), 0.0).astype(bf16) for p in parts], axis=0
+        )
+        weights32 = weights.astype(f32)
+        inverse = 1.0 / jnp.sum(weights32, axis=1, keepdims=True)
+        numerator = jnp.dot(weights, value, preferred_element_type=f32)
+        attended = (numerator * inverse).astype(bf16)
+        offset = jnp.sum(back.astype(f32) * attended.astype(f32), axis=1, keepdims=True)
+        probability = (weights32 * inverse).astype(bf16)
+        back_prob = dot_nt(back, value)
+        back_score = (probability.astype(f32) * (back_prob - offset)).astype(bf16)
+        back_query = jnp.dot(back_score, key, preferred_element_type=f32) * scale
+        back_key = dot_tn(back_score, query) * scale
+        back_value = dot_tn(probability, back)
+        for b, grad_ref in enumerate(grad_refs):
+            part = slice(b * rows, (b + 1) * rows)
+            grad_ref[:, keys] = back_key[part].astype(grad_ref.dtype)
+            grad_ref[:, values] = back_value[part].astype(grad_ref.dtype)
+        for part, place in zip(parts, columns):
+            attended_ref[:, place] = attended[part]
+            raw = raw_ref[:, place]
+            query_back = norm_back(raw, inverse_norm(raw), scaling, back_query[part]).astype(bf16)
+            query_back_ref[:, place] = query_back
+            inner += jnp.sum(query_back.astype(f32) * raw, axis=1, keepdims=True)
+    inner_ref[...] = row_of(inner)
 
 
 def attention_stage(place, order, segments, modality, head_gain, query, raw, back, memories):
@@ -406,8 +362,10 @@
             pl.when(rank_ref[0] == rank)(functools.partial(project, rank))
     for index, (start, size) in enumerate(pieces):
         arrive(copies, index)
-        part = slice(start, start + size)
-        part_ref[:, part] = both_back(image, back_ref[...], slots[index % AHEAD])
+        for inside, tile in chunks_of(size, HEAD_DIM):
+            weights = slots[index % AHEAD, :, inside : inside + tile, :]
+            part = slice(start + inside, start + inside + tile)
+            part_ref[:, part] = both_back(image, back_ref[...], weights)
         begin(copies, index + AHEAD)
 
 
@@ -460,7 +418,7 @@
         back_ref[:, part] = back
         inner += jnp.sum(back.astype(f32) * raw, axis=1, keepdims=True)
     inner_ref[...] = inner_in_ref[...] + row_of(inner)
-    for start, size in chunks_of(out_ref.shape[1], 896):
+    for start, size in chunks_of(out_ref.shape[1], HEAD_DIM):
         place = pl.ds(base + start, size)
         product = both_back(image, back_ref[...], weight_ref[:, place, :])
         out_ref[:, start : start + size] = (product + part_ref[:, place]).astype(bf16)
@@ -489,7 +447,7 @@
 def kept_kernel(rank_ref, modality_ref, part_ref, weight_ref, back_ref, out_ref):
     base = pl.multiple_of(rank_ref[0] * out_ref.shape[1], HEAD_DIM)
     image = column(modality_ref[...]) > 0.0
-    for start, size in chunks_of(out_ref.shape[1], 896):
+    for start, size in chunks_of(out_ref.shape[1], HEAD_DIM):
         place = pl.ds(base + start, size)
         product = both_back(image, back_ref[...], weight_ref[:, place, :])
         out_ref[:, start : start + size] = product + part_ref[:, place]
@@ -582,7 +540,7 @@
         return lax.psum_scatter(part, "tensor", scatter_dimension=1, tiled=True)
 
     memory, key_raw, normed, row_factor = key_stage(
-        rank, modality, norm_gain, head_gain, fetch(key_weight), spread(inputs)
+        rank, modality, norm_gain, head_gain, key_weight, spread(inputs)
     )
     shared = tensor_count > KV_HEADS
     is_even = tensor_rank % 2 == 0
@@ -614,7 +572,7 @@
     )
     incoming = [
         lax.ppermute(grad, "seq", inverted(seq_pairs(step, block_count)))
-        for step, grad in zip(seq_steps(block_count), grads)
+        for step, grad in reversed(list(zip(seq_steps(block_count), grads)))
     ]
 
     projected, gradient_part = turn_stage(

time: 45.1 us -> 48.9 us (1.084)
  local copies, waits for them, and re-layouts: 0.07 us -> 6.23 us
  Pallas kernels: 30.7 us -> 24.8 us
  waiting for transfers between devices: 0.98 us -> 4.17 us
    unnamed x26 -> x30, local copies, waits for them, and re-layouts: 0.07 us -> 6.23 us
    pallas_call x1 -> x0, Pallas kernels: 3.32 us -> none  [fetch(): pl.pallas_call(functools.partial(fetch_kernel, pieces), out_shape=residen...]
    ppermute x2, waiting for transfers between devices: 0.01 us -> 1.58 us  [spread(): return [part, lax.ppermute(part, 'tensor', swap)]]
    pallas_call x1, Pallas kernels: 9.23 us -> 8.23 us  [middle_stage(): pl.pallas_call(functools.partial(middle_kernel, len(parts), pieces), out_...]
    pallas_call x1, Pallas kernels: 3.86 us -> 3.1 us  [attention_stage(): pl.pallas_call(functools.partial(attention_kernel, blocks, pairs, per_gro...]
    pallas_call x1, Pallas kernels: 8.59 us -> 7.84 us  [turn_stage(): pl.pallas_call(functools.partial(turn_kernel, pieces, len(outs)), out_sha...]
    ppermute x3, waiting for transfers between devices: 0.37 us -> 1.11 us  [local(): lax.ppermute(grad, 'seq', inverted(seq_pairs(step, block_count)))]
    ppermute x3, waiting for transfers between devices: 0.01 us -> 0.73 us  [local(): memories.append(lax.ppermute(memory, 'seq', seq_pairs(step, block_count)))]
  transfers between devices with their start and end apart: 11 -> 11, of which waited for: 2 -> 5; matrix products, arithmetic and copies ran while one was open for 0% -> 0% of each run, Pallas kernels for 53% -> 39%
where the time goes in v7:
time: 48.9 us; the launch traced here: 48.6 us
  Pallas kernels  24.8 us (51%)
  starting transfers between devices  12.7 us (26%)
  local copies, waits for them, and re-layouts  6.23 us (13%)
  waiting for transfers between devices  4.17 us (9%)
  between operations  0.79 us (2%)
    pallas_call x1, Pallas kernels, middle_stage(): pl.pallas_call(functools.partial(middle_kernel, len(parts), pieces), out_...  8.23 us
    pallas_call x1, Pallas kernels, turn_stage(): pl.pallas_call(functools.partial(turn_kernel, pieces, len(outs)), out_sha...  7.84 us
    unnamed x30, local copies, waits for them, and re-layouts  6.23 us
    ppermute x3, starting transfers between devices, local(): lax.ppermute(grad, 'seq', inverted(seq_pairs(step, block_count)))  5.82 us
    ppermute x3, starting transfers between devices, local(): memories.append(lax.ppermute(memory, 'seq', seq_pairs(step, block_count)))  5.6 us
    pallas_call x1, Pallas kernels, attention_stage(): pl.pallas_call(functools.partial(attention_kernel, blocks, pairs, per_gro...  3.1 us
    ppermute x2, waiting for transfers between devices, spread(): return [part, lax.ppermute(part, 'tensor', swap)]  1.58 us
    pallas_call x1, Pallas kernels, key_stage(): pl.pallas_call(functools.partial(key_kernel, len(parts)), out_shape=[jax....  1.57 us
  transfers between devices with their start and end apart: 11, of which 5 were waited for; matrix products, arithmetic and copies ran while one was open for 0% of the time, Pallas kernels for 39%

profile of v7, /device:TPU:0, one launch (start us, length us, event | category | flops | bytes accessed | tf_op | source)
XLA Modules:
  0.0 48.6 jit_solution(13289668780738885652)
XLA Ops:
  0.6 0.5 %collective-permute-start = (bf16[128,1792]{1,0:T(8,128)(2,1)}, bf16[128,1792]{1,0:T(8,128)(2,1)S(1)}, u32[]{:S(2)}, u32[]{:S(2)}) collective-permute-start(bf16[128,1792]{1,0:T(8,128)(2,1)} %refs_4_.7), channel_id=1, source_target_pairs={{0,1},{1,0},{2,3},{3,2},{4,5},{5,4},{6,7},{7,6},{8,9},{9,8},{10,11... | collective-permute-start | bytes 1376264 | tf_op jit(solution)/shard_map/ppermute | solution.py:536
  1.1 0.1 collective-permute-start.1
  1.2 1.6 %collective-permute-done.refs_6_ = bf16[128,1792]{1,0:T(8,128)(2,1)S(1)} collective-permute-done((bf16[128,1792]{1,0:T(8,128)(2,1)}, bf16[128,1792]{1,0:T(8,128)(2,1)S(1)}, u32[]{:S(2)}, u32[]{:S(2)}) %collective-permute-start) | collective-permute-done | bytes 458784 | tf_op jit(solution)/shard_map/ppermute | solution.py:536
  2.8 0.0 copy-start
  2.8 3.1 %copy-done = bf16[2,3584,512]{2,1,0:T(8,128)(2,1)S(1)} copy-done((bf16[2,3584,512]{2,1,0:T(8,128)(2,1)S(1)}, bf16[2,3584,512]{2,1,0:T(8,128)(2,1)}, u32[]{:S(2)}) %copy-start) | copy-done | bytes 7340056
  5.9 0.0 copy-start.3
  5.9 0.7 %copy-done.3 = f32[2,2,128]{2,1,0:T(2,128)S(1)} copy-done((f32[2,2,128]{2,1,0:T(2,128)S(1)}, f32[2,2,128]{2,1,0:T(2,128)}, u32[]{:S(2)}) %copy-start.3) | copy-done | bytes 2072
  6.6 0.0 copy-start.5
  6.6 0.7 %copy-done.5 = s32[128]{0:T(128)S(1)} copy-done((s32[128]{0:T(128)S(1)}, s32[128]{0:T(128)}, u32[]{:S(2)}) %copy-start.5) | copy-done | bytes 536
  7.2 0.0 copy-start.7
  7.2 1.0 %copy-done.7 = bf16[128,1792]{1,0:T(8,128)(2,1)S(1)} copy-done((bf16[128,1792]{1,0:T(8,128)(2,1)S(1)}, bf16[128,1792]{1,0:T(8,128)(2,1)}, u32[]{:S(2)}) %copy-start.7) | copy-done | bytes 458776
  8.2 0.0 copy-start.9
  8.2 0.7 %copy-done.9 = f32[2,3584]{1,0:T(2,128)S(1)} copy-done((f32[2,3584]{1,0:T(2,128)S(1)}, f32[2,3584]{1,0:T(2,128)}, u32[]{:S(2)}) %copy-start.9) | copy-done | bytes 28696
  9.0 0.0 copy-start.1
  9.0 0.0 copy-start.2
  9.0 0.0 copy-start.4
  9.0 0.0 copy-start.6
  9.0 1.6 %key_stage.1 = (bf16[128,512]{1,0:T(8,128)(2,1)S(1)}, f32[128,512]{1,0:T(8,128)S(1)}, bf16[128,3584]{1,0:T(8,128)(2,1)S(1)}, f32[1,128]{1,0:T(1,128)S(1)}) custom-call(s32[1]{0:T(128)} %bitcast.refs_0_.rank_ref, s32[1,128]{1,0:T(1,128)S(1)} %bitcast.6, f32[2,3584]{1,0:T(2,128)S(1)} %copy-done.9, f32[2,2,128]{2,1,0:T(2,128)S(1)} %copy-done.3, ...), custom_call_target="tpu_custom_call" | custom-call | flops 10000000000 | bytes 20000000 | tf_op jit(solution)/shard_map/key_stage/pallas_call | solution.py:185
  10.6 4.0 %collective-permute-start.4 = (bf16[128,512]{1,0:T(8,128)(2,1)S(1)}, bf16[128,512]{1,0:T(8,128)(2,1)S(1)}, u32[]{:S(2)}, u32[]{:S(2)}) collective-permute-start(bf16[128,512]{1,0:T(8,128)(2,1)S(1)} %get-tuple-element.28.refs_8_), channel_id=1, source_target_pairs={{0,4},{2,6},{4,0},{6,2},{1,5},{3,7},{5,1},{7,3},{8,12},{10,14},{12... | collective-permute-start | bytes 393224 | tf_op jit(solution)/shard_map/ppermute | solution.py:557
  14.6 1.6 %collective-permute-start.3 = (bf16[128,512]{1,0:T(8,128)(2,1)S(1)}, bf16[128,512]{1,0:T(8,128)(2,1)S(1)}, u32[]{:S(2)}, u32[]{:S(2)}) collective-permute-start(bf16[128,512]{1,0:T(8,128)(2,1)S(1)} %get-tuple-element.28.refs_8_), channel_id=1, source_target_pairs={{0,2},{2,0},{4,6},{6,4},{1,3},{3,1},{5,7},{7,5},{8,10},{10,8},{12,... | collective-permute-start | bytes 393224 | tf_op jit(solution)/shard_map/ppermute | solution.py:557
  16.2 0.0 collective-permute-start.2
  16.2 0.0 collective-permute-done.1.refs_7_
  16.2 0.0 copy-done.1
  16.2 0.0 copy-done.2
  16.2 0.0 copy-done.4
  16.2 0.0 copy-done.6
  16.2 0.0 copy-start.11
  16.2 0.0 copy-start.12
  16.2 8.2 %middle_stage.1 = (bf16[128,1024]{1,0:T(8,128)(2,1)S(1)}, f32[128,1024]{1,0:T(8,128)S(1)}, bf16[128,1024]{1,0:T(8,128)(2,1)S(1)}) custom-call(s32[1]{0:T(128)} %bitcast.refs_0_.rank_ref, s32[1,128]{1,0:T(1,128)S(1)} %bitcast.7, f32[2,2,128]{2,1,0:T(2,128)S(1)} %copy-done.4, bf16[128,3584]{1,0:T(8,128)(2,1)S(1)} %get-tuple-element.24.refs_3_, ...), custom_call_target="tpu_custom_call" | custom-call | flops 8000000000 | bytes 16000000 | tf_op jit(solution)/shard_map/middle_stage/pallas_call | solution.py:237
  24.5 0.0 collective-permute-done.4.refs_11_
  24.5 0.0 collective-permute-done.3.refs_10_
  24.5 0.7 %collective-permute-done.2.refs_9_ = bf16[128,512]{1,0:T(8,128)(2,1)S(1)} collective-permute-done((bf16[128,512]{1,0:T(8,128)(2,1)S(1)}, bf16[128,512]{1,0:T(8,128)(2,1)S(1)}, u32[]{:S(2)}, u32[]{:S(2)}) %collective-permute-start.2) | collective-permute-done | bytes 131104 | tf_op jit(solution)/shard_map/ppermute | solution.py:557
  25.2 0.0 copy-done.11
  25.2 0.0 copy-done.12
  25.2 0.0 slice-start
  25.2 3.1 %attention_stage.1 = (bf16[128,1024]{1,0:T(8,128)(2,1)S(1)}, bf16[128,1024]{1,0:T(8,128)(2,1)S(1)}, f32[1,128]{1,0:T(1,128)S(1)}, f32[128,512]{1,0:T(8,128)S(1)}...) custom-call(s32[1]{0:T(128)} %bitcast.2.refs_0_, s32[4]{0:T(128)S(1)} %copy-done.12, ...), custom_call_target="tpu_custom_call" | custom-call | flops 4000000000 | bytes 8000000 | tf_op jit(solution)/shard_map/attention_stage/pallas_call | solution.py:326
  28.3 4.3 %collective-permute-start.5 = (bf16[128,512]{1,0:T(8,128)(2,1)S(1)}, bf16[128,512]{1,0:T(8,128)(2,1)S(1)}, u32[]{:S(2)}, u32[]{:S(2)}) collective-permute-start(bf16[128,512]{1,0:T(8,128)(2,1)S(1)} %get-tuple-element.36), channel_id=1, source_target_pairs={{4,0},{6,2},{0,4},{2,6},{5,1},{7,3},{1,5},{3,7},{12,8},{14,10},{8,... | collective-permute-start | bytes 393224 | tf_op jit(solution)/shard_map/ppermute | solution.py:574
  32.6 0.0 collective-permute-start.6
  32.6 1.5 %collective-permute-start.7 = (bf16[128,512]{1,0:T(8,128)(2,1)S(1)}, bf16[128,512]{1,0:T(8,128)(2,1)S(1)}, u32[]{:S(2)}, u32[]{:S(2)}) collective-permute-start(bf16[128,512]{1,0:T(8,128)(2,1)S(1)} %get-tuple-element.38), channel_id=1, source_target_pairs={{6,0},{4,2},{2,4},{0,6},{7,1},{5,3},{3,5},{1,7},{14,8},{12,10},{10... | collective-permute-start | bytes 393224 | tf_op jit(solution)/shard_map/ppermute | solution.py:574
  34.2 0.0 slice-start.1
  34.2 7.8 %turn_stage.1 = (bf16[128,1792]{1,0:T(8,128)(2,1)S(1)}, f32[128,1792]{1,0:T(8,128)S(1)}, f32[128,3584]{1,0:T(8,128)S(1)}) custom-call(s32[1]{0:T(128)} %bitcast.refs_0_.rank_ref, s32[1,128]{1,0:T(1,128)S(1)} %bitcast.9, bf16[2,1024,3584]{2,1,0:T(8,128)(2,1)S(1)} %copy-done.1, bf16[128,1024]{1,0:T(8,128)(2,1)S(1)} %get-tuple-element.29.refs_3_, ...), custom_call_target="tpu_custom_call" | custom-call | flops 10000000000 | bytes 20000000 | tf_op jit(solution)/shard_map/turn_stage/pallas_call | solution.py:384
  42.0 0.0 copy-start.8
  42.0 0.0 copy-start.10
  42.0 0.2 collective-permute-done.5.refs_9_
  42.2 0.9 %collective-permute-done.6.refs_10_ = bf16[128,512]{1,0:T(8,128)(2,1)S(1)} collective-permute-done((bf16[128,512]{1,0:T(8,128)(2,1)S(1)}, bf16[128,512]{1,0:T(8,128)(2,1)S(1)}, u32[]{:S(2)}, u32[]{:S(2)}) %collective-permute-start.6) | collective-permute-done | bytes 131104 | tf_op jit(solution)/shard_map/ppermute | solution.py:574
  43.1 0.0 collective-permute-done.7.refs_11_
  43.1 0.0 slice-done
  43.1 0.0 slice-done.1
  43.1 1.5 %key_back_stage.1 = (bf16[128,1792]{1,0:T(8,128)(2,1)S(1)}, bf16[128,512]{1,0:T(8,128)(2,1)S(1)}, f32[1,128]{1,0:T(1,128)S(1)}, bf16[128,1792]{1,0:T(8,128)(2,1)S(1)}) custom-call(s32[1]{0:T(128)} %bitcast.refs_0_.rank_ref, s32[1,128]{1,0:T(1,128)S(1)} %bitcast.10, f32[2,2,128]{2,1,0:T(2,128)S(1)} %copy-done.4, ...), custom_call_target="tpu_custom_call", output_to_operand_aliasing={{3}: (7, {})} | custom-call | flops 2000000000 | bytes 4000000 | tf_op jit(solution)/shard_map/key_back_stage/pallas_call | solution.py:430
  44.6 0.1 collective-permute-start.8
  44.7 0.5 %collective-permute-start.10 = (bf16[128,1792]{1,0:T(8,128)(2,1)S(1)}, bf16[128,1792]{1,0:T(8,128)(2,1)S(1)}, u32[]{:S(2)}, u32[]{:S(2)}) collective-permute-start(bf16[128,1792]{1,0:T(8,128)(2,1)S(1)} %get-tuple-element.43), channel_id=1, source_target_pairs={{0,1},{1,0},{2,3},{3,2},{4,5},{5,4},{6,7},{7,6},{8,9},{9,8},{10,11... | collective-permute-start | bytes 1376264 | tf_op jit(solution)/shard_map/ppermute | solution.py:605
  45.2 0.1 collective-permute-start.9
  45.3 1.1 %kept_stage.1.refs_5_ = f32[128,1792]{1,0:T(8,128)S(1)} custom-call(s32[1]{0:T(128)} %bitcast.refs_0_.rank_ref, s32[1,128]{1,0:T(1,128)S(1)} %bitcast.11, f32[128,3584]{1,0:T(8,128)S(1)} %get-tuple-element.31.refs_5_.part_ref, bf16[2,3584,512]{2,1,0:T(8,128)(2,1)S(1)} %bitcast.5, bf16[128,512]{1,0:T(8,128)(2,1)S(1)} %get-tuple-element.39.back_ref), custom_call_target="tpu_custom_call" | custom-call | flops 2000000000 | bytes 4000000 | tf_op jit(solution)/shard_map/kept_stage/pallas_call | solution.py:457
  46.4 0.7 %collective-permute-done.9.refs_8_ = f32[1,128]{1,0:T(1,128)S(1)} collective-permute-done((f32[1,128]{1,0:T(1,128)S(1)}, f32[1,128]{1,0:T(1,128)S(1)}, u32[]{:S(2)}, u32[]{:S(2)}) %collective-permute-start.9) | collective-permute-done | bytes 544 | tf_op jit(solution)/shard_map/ppermute | solution.py:601
  47.2 0.0 collective-permute-done.8.refs_6_
  47.2 0.0 collective-permute-done.10.refs_10_
  47.2 0.0 copy-done.8
  47.2 0.0 copy-done.10
  47.2 1.4 %finish.1 = (bf16[128,1792]{1,0:T(8,128)(2,1)}, bf16[128,1792]{1,0:T(8,128)(2,1)}) custom-call(s32[1]{0:T(128)} %bitcast.refs_0_.rank_ref, s32[1,128]{1,0:T(1,128)S(1)} %bitcast.12, f32[2,3584]{1,0:T(2,128)S(1)} %copy-done.10, f32[1,128]{1,0:T(1,128)S(1)} %get-tuple-element.23.refs_3_, bf16[128,1792]{1,0:T(8,128)(2,1)S(1)} %copy-done.8, ...), custom_call_target="tpu_custom_call" | custom-call | flops 1000000000 | bytes 2000000 | tf_op jit(solution)/shard_map/finish/pallas_call | solution.py:499
  (1 shorter events, 0.0 us)
Async XLA Ops:
  0.6 2.2 %collective-permute-start = (bf16[128,1792]{1,0:T(8,128)(2,1)}, bf16[128,1792]{1,0:T(8,128)(2,1)S(1)}, u32[]{:S(2)}, u32[]{:S(2)}) collective-permute-start(bf16[128,1792]{1,0:T(8,128)(2,1)} %refs_4_.7), channel_id=1, source_target_pairs={{0,1},{1,0},{2,3},{3,2},{4,5},{5,4},{6,7},{7,6},{8,9},{9,8},{10,11... | collective-permute-start | bytes 1376264 | tf_op jit(solution)/shard_map/ppermute | solution.py:536
  1.1 15.0 %collective-permute-start.1 = (bf16[128,1792]{1,0:T(8,128)(2,1)}, bf16[128,1792]{1,0:T(8,128)(2,1)S(1)}, u32[]{:S(2)}, u32[]{:S(2)}) collective-permute-start(bf16[128,1792]{1,0:T(8,128)(2,1)} %refs_6_.2), channel_id=1, source_target_pairs={{0,1},{1,0},{2,3},{3,2},{4,5},{5,4},{6,7},{7,6},{8,9},{9,8},{10,11... | collective-permute-start | bytes 1376264 | tf_op jit(solution)/shard_map/ppermute | solution.py:536
  2.8 3.1 %copy-start = (bf16[2,3584,512]{2,1,0:T(8,128)(2,1)S(1)}, bf16[2,3584,512]{2,1,0:T(8,128)(2,1)}, u32[]{:S(2)}) copy-start(bf16[2,3584,512]{2,1,0:T(8,128)(2,1)} %weight_ref.1) | copy-start | bytes 22020100
  5.9 0.7 %copy-start.3 = (f32[2,2,128]{2,1,0:T(2,128)S(1)}, f32[2,2,128]{2,1,0:T(2,128)}, u32[]{:S(2)}) copy-start(f32[2,2,128]{2,1,0:T(2,128)} %refs_2_.8) | copy-start | bytes 6148
  6.6 0.7 %copy-start.5 = (s32[128]{0:T(128)S(1)}, s32[128]{0:T(128)}, u32[]{:S(2)}) copy-start(s32[128]{0:T(128)} %param.17) | copy-start | bytes 1540
  7.2 1.0 %copy-start.7 = (bf16[128,1792]{1,0:T(8,128)(2,1)S(1)}, bf16[128,1792]{1,0:T(8,128)(2,1)}, u32[]{:S(2)}) copy-start(bf16[128,1792]{1,0:T(8,128)(2,1)} %refs_4_.7) | copy-start | bytes 1376260
  8.2 0.7 %copy-start.9 = (f32[2,3584]{1,0:T(2,128)S(1)}, f32[2,3584]{1,0:T(2,128)}, u32[]{:S(2)}) copy-start(f32[2,3584]{1,0:T(2,128)} %refs_2_.9) | copy-start | bytes 86020
  9.0 7.2 %copy-start.1 = (bf16[2,1024,3584]{2,1,0:T(8,128)(2,1)S(1)}, bf16[2,1024,3584]{2,1,0:T(8,128)(2,1)}, u32[]{:S(2)}) copy-start(bf16[2,1024,3584]{2,1,0:T(8,128)(2,1)} %refs_2_.7) | copy-start | bytes 44040196
  9.0 7.2 %copy-start.2 = (bf16[128,1792]{1,0:T(8,128)(2,1)S(1)}, bf16[128,1792]{1,0:T(8,128)(2,1)}, u32[]{:S(2)}) copy-start(bf16[128,1792]{1,0:T(8,128)(2,1)} %refs_6_.2) | copy-start | bytes 1376260
  9.0 7.2 %copy-start.4 = (f32[2,2,128]{2,1,0:T(2,128)S(1)}, f32[2,2,128]{2,1,0:T(2,128)}, u32[]{:S(2)}) copy-start(f32[2,2,128]{2,1,0:T(2,128)} %refs_2_.8) | copy-start | bytes 6148
  9.0 7.2 %copy-start.6 = (s32[128]{0:T(128)S(1)}, s32[128]{0:T(128)}, u32[]{:S(2)}) copy-start(s32[128]{0:T(128)} %param.17) | copy-start | bytes 1540
  10.6 13.9 %collective-permute-start.4 = (bf16[128,512]{1,0:T(8,128)(2,1)S(1)}, bf16[128,512]{1,0:T(8,128)(2,1)S(1)}, u32[]{:S(2)}, u32[]{:S(2)}) collective-permute-start(bf16[128,512]{1,0:T(8,128)(2,1)S(1)} %get-tuple-element.28.refs_8_), channel_id=1, source_target_pairs={{0,4},{2,6},{4,0},{6,2},{1,5},{3,7},{5,1},{7,3},{8,12},{10,14},{12... | collective-permute-start | bytes 393224 | tf_op jit(solution)/shard_map/ppermute | solution.py:557
  14.6 9.9 %collective-permute-start.3 = (bf16[128,512]{1,0:T(8,128)(2,1)S(1)}, bf16[128,512]{1,0:T(8,128)(2,1)S(1)}, u32[]{:S(2)}, u32[]{:S(2)}) collective-permute-start(bf16[128,512]{1,0:T(8,128)(2,1)S(1)} %get-tuple-element.28.refs_8_), channel_id=1, source_target_pairs={{0,2},{2,0},{4,6},{6,4},{1,3},{3,1},{5,7},{7,5},{8,10},{10,8},{12,... | collective-permute-start | bytes 393224 | tf_op jit(solution)/shard_map/ppermute | solution.py:557
  16.2 9.1 %collective-permute-start.2 = (bf16[128,512]{1,0:T(8,128)(2,1)S(1)}, bf16[128,512]{1,0:T(8,128)(2,1)S(1)}, u32[]{:S(2)}, u32[]{:S(2)}) collective-permute-start(bf16[128,512]{1,0:T(8,128)(2,1)S(1)} %get-tuple-element.28.refs_8_), channel_id=1, source_target_pairs={{0,6},{2,4},{4,2},{6,0},{1,7},{3,5},{5,3},{7,1},{8,14},{10,12},{12... | collective-permute-start | bytes 393224 | tf_op jit(solution)/shard_map/ppermute | solution.py:557
  16.2 9.0 %copy-start.11 = (s32[512]{0:T(512)S(1)}, s32[512]{0:T(512)}, u32[]{:S(2)}) copy-start(s32[512]{0:T(512)} %param.18) | copy-start | bytes 6148
  16.2 9.0 %copy-start.12 = (s32[4]{0:T(128)S(1)}, s32[4]{0:T(128)}, u32[]{:S(2)}) copy-start(s32[4]{0:T(128)} %refs_1_.1) | copy-start | bytes 52
  25.2 17.9 %slice-start = ((s8[7340032]{0:T(1024)(128)(4,1)}), s8[4194304]{0:T(1024)(128)(4,1)S(1)}, s32[]{:S(2)}) async-start(s8[7340032]{0:T(1024)(128)(4,1)} %bitcast.4), calls=%async_computation | async-start | bytes 8388608
  28.3 13.9 %collective-permute-start.5 = (bf16[128,512]{1,0:T(8,128)(2,1)S(1)}, bf16[128,512]{1,0:T(8,128)(2,1)S(1)}, u32[]{:S(2)}, u32[]{:S(2)}) collective-permute-start(bf16[128,512]{1,0:T(8,128)(2,1)S(1)} %get-tuple-element.36), channel_id=1, source_target_pairs={{4,0},{6,2},{0,4},{2,6},{5,1},{7,3},{1,5},{3,7},{12,8},{14,10},{8,... | collective-permute-start | bytes 393224 | tf_op jit(solution)/shard_map/ppermute | solution.py:574
  32.6 10.5 %collective-permute-start.6 = (bf16[128,512]{1,0:T(8,128)(2,1)S(1)}, bf16[128,512]{1,0:T(8,128)(2,1)S(1)}, u32[]{:S(2)}, u32[]{:S(2)}) collective-permute-start(bf16[128,512]{1,0:T(8,128)(2,1)S(1)} %get-tuple-element.37), channel_id=1, source_target_pairs={{2,0},{0,2},{6,4},{4,6},{3,1},{1,3},{7,5},{5,7},{10,8},{8,10},{14,... | collective-permute-start | bytes 393224 | tf_op jit(solution)/shard_map/ppermute | solution.py:574
  32.6 10.5 %collective-permute-start.7 = (bf16[128,512]{1,0:T(8,128)(2,1)S(1)}, bf16[128,512]{1,0:T(8,128)(2,1)S(1)}, u32[]{:S(2)}, u32[]{:S(2)}) collective-permute-start(bf16[128,512]{1,0:T(8,128)(2,1)S(1)} %get-tuple-element.38), channel_id=1, source_target_pairs={{6,0},{4,2},{2,4},{0,6},{7,1},{5,3},{3,5},{1,7},{14,8},{12,10},{10... | collective-permute-start | bytes 393224 | tf_op jit(solution)/shard_map/ppermute | solution.py:574
  34.2 9.0 %slice-start.1 = ((s8[7340032]{0:T(1024)(128)(4,1)}), s8[3145728]{0:T(1024)(128)(4,1)S(1)}, s32[]{:S(2)}) async-start(s8[7340032]{0:T(1024)(128)(4,1)} %bitcast.4), calls=%async_computation.1 | async-start | bytes 6291456
  42.0 5.2 %copy-start.8 = (bf16[128,1792]{1,0:T(8,128)(2,1)S(1)}, bf16[128,1792]{1,0:T(8,128)(2,1)}, u32[]{:S(2)}) copy-start(bf16[128,1792]{1,0:T(8,128)(2,1)} %refs_4_.7) | copy-start | bytes 1376260
  42.0 5.2 %copy-start.10 = (f32[2,3584]{1,0:T(2,128)S(1)}, f32[2,3584]{1,0:T(2,128)}, u32[]{:S(2)}) copy-start(f32[2,3584]{1,0:T(2,128)} %refs_2_.9) | copy-start | bytes 86020
  44.6 2.5 %collective-permute-start.8 = (bf16[128,1792]{1,0:T(8,128)(2,1)S(1)}, bf16[128,1792]{1,0:T(8,128)(2,1)S(1)}, u32[]{:S(2)}, u32[]{:S(2)}) collective-permute-start(bf16[128,1792]{1,0:T(8,128)(2,1)S(1)} %get-tuple-element.40), channel_id=1, source_target_pairs={{0,1},{1,0},{2,3},{3,2},{4,5},{5,4},{6,7},{7,6},{8,9},{9,8},{10,11... | collective-permute-start | bytes 1376264 | tf_op jit(solution)/shard_map/ppermute | solution.py:602
  44.7 2.5 %collective-permute-start.10 = (bf16[128,1792]{1,0:T(8,128)(2,1)S(1)}, bf16[128,1792]{1,0:T(8,128)(2,1)S(1)}, u32[]{:S(2)}, u32[]{:S(2)}) collective-permute-start(bf16[128,1792]{1,0:T(8,128)(2,1)S(1)} %get-tuple-element.43), channel_id=1, source_target_pairs={{0,1},{1,0},{2,3},{3,2},{4,5},{5,4},{6,7},{7,6},{8,9},{9,8},{10,11... | collective-permute-start | bytes 1376264 | tf_op jit(solution)/shard_map/ppermute | solution.py:605
  45.2 2.0 %collective-permute-start.9 = (f32[1,128]{1,0:T(1,128)S(1)}, f32[1,128]{1,0:T(1,128)S(1)}, u32[]{:S(2)}, u32[]{:S(2)}) collective-permute-start(f32[1,128]{1,0:T(1,128)S(1)} %get-tuple-element.41.refs_7_), channel_id=1, source_target_pairs={{0,1},{1,0},{2,3},{3,2},{4,5},{5,4},{6,7},{7,6},{8,9},{9,8},{10,11... | collective-permute-start | bytes 1544 | tf_op jit(solution)/shard_map/ppermute | solution.py:601

commit v8 on v7

--- a/solution.py
+++ b/solution.py
@@ -27,7 +27,7 @@
 
 
 def seq_steps(count):
-    return sorted(range(1, count), key=lambda step: (step == count // 2, -step))
+    return sorted(range(1, count), key=lambda step: (step != count // 2, step))
 
 
 def seq_source(rank, step, count):
@@ -150,6 +150,34 @@
 
 def ring(weights, pieces):
     return pltpu.VMEM((AHEAD, 2, pieces[0][1], weights.shape[2]), weights.dtype)
+
+
+def resident(weights):
+    return pltpu.VMEM(weights.shape, weights.dtype)
+
+
+def fetch_kernel(pieces, weight_ref, held_ref, sem_ref):
+    copies = copies_of(weight_ref, held_ref, sem_ref, pieces)
+    for pair in copies:
+        for copy in pair:
+            copy.start()
+    for pair in copies:
+        for copy in pair:
+            copy.wait()
+
+
+def fetch(weights):
+    pieces = chunks_of(weights.shape[1], 896)
+    return pl.pallas_call(
+        functools.partial(fetch_kernel, pieces),
+        out_shape=resident(weights),
+        in_specs=[ANY],
+        out_specs=VMEM,
+        scratch_shapes=[pltpu.SemaphoreType.DMA((len(pieces), 2))],
+        compiler_params=params(1),
+        cost_estimate=cost(0.2),
+        name="fetch",
+    )(streamed(weights))
 
 
 def key_kernel(count, *refs):
@@ -397,10 +425,42 @@
     return projected, part
 
 
+def tie(passed, arrived):
+    def kernel(passed_ref, arrived_ref, out_ref):
+        del passed_ref, arrived_ref, out_ref
+
+    return pl.pallas_call(
+        kernel,
+        out_shape=jax.ShapeDtypeStruct(passed.shape, passed.dtype),
+        in_specs=[ANY, ANY],
+        out_specs=ANY,
+        input_output_aliases={0: 0},
+        compiler_params=params(1),
+        cost_estimate=cost(0.1),
+        name="tie",
+    )(passed, arrived)
+
+
+def merge_kernel(kept_ref, other_ref, out_ref):
+    out_ref[...] = (kept_ref[...] + other_ref[...].astype(f32)).astype(bf16)
+
+
+def merge(kept, other):
+    return pl.pallas_call(
+        merge_kernel,
+        out_shape=jax.ShapeDtypeStruct(other.shape, bf16),
+        in_specs=[VMEM, VMEM],
+        out_specs=VMEM,
+        compiler_params=params(4),
+        cost_estimate=cost(0.5),
+        name="merge",
+    )(kept, other)
+
+
 def key_back_kernel(split, *refs):
     rank_ref, modality_ref, head_ref, raw_ref, inner_in_ref, part_ref, weight_ref = refs[:7]
-    grad_refs = refs[8:-4]
-    out_ref, back_ref, inner_ref = refs[-4:-1]
+    grad_refs = refs[7:-3]
+    out_ref, back_ref, inner_ref = refs[-3:]
     base = pl.multiple_of((1 - rank_ref[0]) * out_ref.shape[1], HEAD_DIM) if split else 0
     image = column(modality_ref[...]) > 0.0
     blocks = raw_ref.shape[1] // HEAD_DIM
@@ -424,7 +484,7 @@
         out_ref[:, start : start + size] = (product + part_ref[:, place]).astype(bf16)
 
 
-def key_back_stage(rank, modality, head_gain, raw, inner, part, weights, passed, grads, split):
+def key_back_stage(rank, modality, head_gain, raw, inner, part, weights, grads, split):
     _, depth, width = weights.shape
     rows = raw.shape[0]
     return pl.pallas_call(
@@ -433,15 +493,13 @@
             jax.ShapeDtypeStruct((rows, depth // 2 if split else depth), bf16),
             jax.ShapeDtypeStruct((rows, width), bf16),
             jax.ShapeDtypeStruct((1, rows), f32),
-            jax.ShapeDtypeStruct(passed.shape, passed.dtype),
         ],
-        in_specs=[SMEM] + [VMEM] * 6 + [ANY] + [VMEM] * len(grads),
-        out_specs=[VMEM] * 3 + [ANY],
-        input_output_aliases={7: 3},
+        in_specs=[SMEM] + [VMEM] * (6 + len(grads)),
+        out_specs=[VMEM] * 3,
         compiler_params=params(6),
         cost_estimate=cost(2),
         name="key_back_stage",
-    )(rank, modality, head_gain, raw, inner, part, weights, passed, *grads)
+    )(rank, modality, head_gain, raw, inner, part, weights, *grads)
 
 
 def kept_kernel(rank_ref, modality_ref, part_ref, weight_ref, back_ref, out_ref):
@@ -469,8 +527,7 @@
     rank_ref, modality_ref, gain_ref, factor_ref, inputs_ref = refs[:5]
     back_refs = refs[5 : 5 + backs]
     inner_refs = refs[5 + backs : 5 + backs + inners]
-    rest = refs[5 + backs + inners :]
-    out_ref = rest[-1]
+    out_ref = refs[-1]
     width = inputs_ref.shape[1]
     image = column(modality_ref[...]) > 0.0
     gain = gain_ref[...]
@@ -487,20 +544,15 @@
     unit_rows = inputs_ref[...].astype(f32) * factor
     inner_mean = column(inner) * (1.0 / total_width)
     out_ref[...] = (factor * (scaling * back - unit_rows * inner_mean)).astype(bf16)
-    if len(rest) == 4:
-        kept_ref, other_ref, attention_ref, _ = rest
-        attention_ref[...] = (kept_ref[...] + other_ref[...].astype(f32)).astype(bf16)
-
-
-def finish(rank, total_width, modality, gain, factor, inputs, backs, inners, projected):
-    shape = jax.ShapeDtypeStruct(inputs.shape, bf16)
-    arrays = [modality, gain, factor, inputs, *backs, *inners, *projected]
-    outs = [shape] * (2 if projected else 1)
+
+
+def finish(rank, total_width, modality, gain, factor, inputs, backs, inners):
+    arrays = [modality, gain, factor, inputs, *backs, *inners]
     return pl.pallas_call(
         functools.partial(finish_kernel, len(backs), len(inners), total_width),
-        out_shape=outs,
+        out_shape=jax.ShapeDtypeStruct(inputs.shape, bf16),
         in_specs=[SMEM] + [VMEM] * len(arrays),
-        out_specs=[VMEM] * len(outs),
+        out_specs=VMEM,
         compiler_params=params(6),
         cost_estimate=cost(1),
         name="finish",
@@ -540,7 +592,7 @@
         return lax.psum_scatter(part, "tensor", scatter_dimension=1, tiled=True)
 
     memory, key_raw, normed, row_factor = key_stage(
-        rank, modality, norm_gain, head_gain, key_weight, spread(inputs)
+        rank, modality, norm_gain, head_gain, fetch(key_weight), spread(inputs)
     )
     shared = tensor_count > KV_HEADS
     is_even = tensor_rank % 2 == 0
@@ -572,12 +624,18 @@
     )
     incoming = [
         lax.ppermute(grad, "seq", inverted(seq_pairs(step, block_count)))
-        for step, grad in reversed(list(zip(seq_steps(block_count), grads)))
+        for step, grad in zip(seq_steps(block_count), grads)
     ]
 
     projected, gradient_part = turn_stage(
         rank, modality, output_weight, attended, query_back, query_weight, split
     )
+    if split:
+        passed = tie(projected[0], incoming[0])
+        attention_out = merge(projected[1], lax.ppermute(passed, "tensor", swap))
+    else:
+        attention_out = scatter_columns(projected[0])
+
     if shared:
         total = own_grad + sum(grad.astype(f32) for grad in incoming)
         low, high = total[:, :HEAD_DIM], total[:, HEAD_DIM:]
@@ -585,7 +643,7 @@
         sums = [jnp.where(is_even, low, high), lax.ppermute(outgoing, "tensor", pair_swap)]
     else:
         sums = [own_grad, *incoming]
-    sent, slice_back, inner, passed = key_back_stage(
+    sent, slice_back, inner = key_back_stage(
         rank,
         modality,
         head_gain,
@@ -593,7 +651,6 @@
         inner,
         gradient_part,
         key_weight,
-        projected[0],
         sums,
         split,
     )
@@ -602,20 +659,13 @@
         other = lax.ppermute(sent, "tensor", swap)
         kept = kept_stage(rank, modality, gradient_part, key_weight, slice_back)
         backs = [kept, other]
-        projected = [projected[1], lax.ppermute(passed, "tensor", swap)]
         gain = norm_gain
     else:
         inners = [lax.psum(inner, "tensor")]
         backs = [scatter_columns(sent)]
-        attention_out = scatter_columns(passed)
-        projected = []
         gain = lax.dynamic_slice_in_dim(norm_gain, tensor_rank * local_width, local_width, 1)
-    results = finish(
-        rank, full_width, modality, gain, row_factor, inputs, backs, inners, projected
-    )
-    if split:
-        attention_out = results[0]
-    return (attention_out, results[-1])
+    grad_input = finish(rank, full_width, modality, gain, row_factor, inputs, backs, inners)
+    return (attention_out, grad_input)
 
 
 def solution(mesh):

time: 48.9 us -> 44.3 us (0.906)
  local copies, waits for them, and re-layouts: 6.23 us -> 0.07 us
  Pallas kernels: 24.8 us -> 28.7 us
  waiting for transfers between devices: 4.17 us -> 1.81 us
    unnamed x30 -> x26, local copies, waits for them, and re-layouts: 6.23 us -> 0.07 us
    pallas_call x0 -> x3, Pallas kernels: none -> 4.19 us  [the longest x1 3.32 us: fetch(): pl.pallas_call(functools.partial(fetch_kernel, pieces), out_shape=residen...]
    ppermute x2, waiting for transfers between devices: 1.58 us -> 0.01 us  [spread(): return [part, lax.ppermute(part, 'tensor', swap)]]
    ppermute x1, waiting for transfers between devices: 0.75 us -> 0.01 us  [local(): inners = [inner, lax.ppermute(inner, 'tensor', swap)]]
    ppermute x1, starting transfers between devices: 0.5 us -> 0.01 us  [local(): attention_out = merge(projected[1], lax.ppermute(passed, 'tensor', swap))]
  transfers between devices with their start and end apart: 11 -> 11, of which waited for: 5 -> 3; matrix products, arithmetic and copies ran while one was open for 0% -> 0% of each run, Pallas kernels for 39% -> 55%
where the time goes in v8:
time: 44.3 us; the launch traced here: 44.1 us
  Pallas kernels  28.7 us (65%)
  starting transfers between devices  12.6 us (28%)
  waiting for transfers between devices  1.81 us (4%)
  between operations  0.87 us (2%)
    pallas_call x1, Pallas kernels, middle_stage(): pl.pallas_call(functools.partial(middle_kernel, len(parts), pieces), out_...  8.23 us
    pallas_call x1, Pallas kernels, turn_stage(): pl.pallas_call(functools.partial(turn_kernel, pieces, len(outs)), out_sha...  7.82 us
    ppermute x3, starting transfers between devices, local(): lax.ppermute(grad, 'seq', inverted(seq_pairs(step, block_count)))  5.81 us
    ppermute x3, starting transfers between devices, local(): memories.append(lax.ppermute(memory, 'seq', seq_pairs(step, block_count)))  5.66 us
    pallas_call x1, Pallas kernels, fetch(): pl.pallas_call(functools.partial(fetch_kernel, pieces), out_shape=residen...  3.32 us
    pallas_call x1, Pallas kernels, attention_stage(): pl.pallas_call(functools.partial(attention_kernel, blocks, pairs, per_gro...  3.1 us
    pallas_call x1, Pallas kernels, key_stage(): pl.pallas_call(functools.partial(key_kernel, len(parts)), out_shape=[jax....  1.56 us
    pallas_call x1, Pallas kernels, key_back_stage(): pl.pallas_call(functools.partial(key_back_kernel, split), out_shape=[jax....  1.49 us
  transfers between devices with their start and end apart: 11, of which 3 were waited for; matrix products, arithmetic and copies ran while one was open for 0% of the time, Pallas kernels for 55%

profile of v8, /device:TPU:0, one launch (start us, length us, event | category | flops | bytes accessed | tf_op | source)
XLA Modules:
  0.0 44.1 jit_solution(7332491203056511964)
XLA Ops:
  0.6 0.5 %collective-permute-start = (bf16[128,1792]{1,0:T(8,128)(2,1)}, bf16[128,1792]{1,0:T(8,128)(2,1)S(1)}, u32[]{:S(2)}, u32[]{:S(2)}) collective-permute-start(bf16[128,1792]{1,0:T(8,128)(2,1)} %refs_4_.5), channel_id=1, source_target_pairs={{0,1},{1,0},{2,3},{3,2},{4,5},{5,4},{6,7},{7,6},{8,9},{9,8},{10,11... | collective-permute-start | bytes 1376264 | tf_op jit(solution)/shard_map/ppermute | solution.py:588
  1.1 0.1 collective-permute-start.1
  1.2 0.0 copy-start.1
  1.2 0.0 copy-start.2
  1.2 0.0 copy-start.3
  1.2 0.0 copy-start.4
  1.2 0.0 slice-start.2
  1.3 0.0 slice-start.3
  1.3 3.3 %fetch.1.refs_4_ = bf16[2,3584,512]{2,1,0:T(8,128)(2,1)S(1)} custom-call(bf16[2,3584,512]{2,1,0:T(8,128)(2,1)} %weight_ref.3), custom_call_target="tpu_custom_call" | custom-call | flops 200000000 | bytes 400000 | tf_op jit(solution)/shard_map/fetch/pallas_call | solution.py:171
  4.6 0.0 collective-permute-done.refs_6_
  4.6 0.0 copy-done.1
  4.6 0.0 copy-done.2
  4.6 0.0 copy-done.3
  4.6 0.0 copy-done.4
  4.6 0.0 slice-start.4
  4.7 0.0 slice-start.5
  4.7 0.0 copy-start
  4.7 1.6 %key_stage.1 = (bf16[128,512]{1,0:T(8,128)(2,1)S(1)}, f32[128,512]{1,0:T(8,128)S(1)}, bf16[128,3584]{1,0:T(8,128)(2,1)S(1)}, f32[1,128]{1,0:T(1,128)S(1)}) custom-call(s32[1]{0:T(128)} %bitcast.refs_0_.rank_ref, s32[1,128]{1,0:T(1,128)S(1)} %bitcast.8, f32[2,3584]{1,0:T(2,128)S(1)} %copy-done.4, f32[2,2,128]{2,1,0:T(2,128)S(1)} %copy-done.1, ...), custom_call_target="tpu_custom_call" | custom-call | flops 10000000000 | bytes 20000000 | tf_op jit(solution)/shard_map/key_stage/pallas_call | solution.py:213
  6.2 4.1 %collective-permute-start.2 = (bf16[128,512]{1,0:T(8,128)(2,1)S(1)}, bf16[128,512]{1,0:T(8,128)(2,1)S(1)}, u32[]{:S(2)}, u32[]{:S(2)}) collective-permute-start(bf16[128,512]{1,0:T(8,128)(2,1)S(1)} %get-tuple-element.26.refs_8_), channel_id=1, source_target_pairs={{0,4},{2,6},{4,0},{6,2},{1,5},{3,7},{5,1},{7,3},{8,12},{10,14},{12... | collective-permute-start | bytes 393224 | tf_op jit(solution)/shard_map/ppermute | solution.py:609
  10.3 1.6 %collective-permute-start.3 = (bf16[128,512]{1,0:T(8,128)(2,1)S(1)}, bf16[128,512]{1,0:T(8,128)(2,1)S(1)}, u32[]{:S(2)}, u32[]{:S(2)}) collective-permute-start(bf16[128,512]{1,0:T(8,128)(2,1)S(1)} %get-tuple-element.26.refs_8_), channel_id=1, source_target_pairs={{0,2},{2,0},{4,6},{6,4},{1,3},{3,1},{5,7},{7,5},{8,10},{10,8},{12,... | collective-permute-start | bytes 393224 | tf_op jit(solution)/shard_map/ppermute | solution.py:609
  11.9 0.0 collective-permute-start.4
  11.9 0.0 collective-permute-done.1.refs_7_
  11.9 0.0 slice-done.2
  11.9 0.0 slice-done.3
  11.9 0.0 slice-done.4
  11.9 0.0 slice-done.5
  11.9 0.0 copy-done
  12.0 0.0 copy-start.5
  12.0 0.0 copy-start.6
  12.0 8.2 %middle_stage.1 = (bf16[128,1024]{1,0:T(8,128)(2,1)S(1)}, f32[128,1024]{1,0:T(8,128)S(1)}, bf16[128,1024]{1,0:T(8,128)(2,1)S(1)}) custom-call(s32[1]{0:T(128)} %bitcast.refs_0_.rank_ref, s32[1,128]{1,0:T(1,128)S(1)} %bitcast.9, f32[2,2,128]{2,1,0:T(2,128)S(1)} %copy-done.1, bf16[128,3584]{1,0:T(8,128)(2,1)S(1)} %get-tuple-element.22.refs_3_, ...), custom_call_target="tpu_custom_call" | custom-call | flops 8000000000 | bytes 16000000 | tf_op jit(solution)/shard_map/middle_stage/pallas_call | solution.py:265
  20.2 0.0 collective-permute-done.2.refs_9_
  20.2 0.0 collective-permute-done.3.refs_10_
  20.2 0.6 %collective-permute-done.4.refs_11_ = bf16[128,512]{1,0:T(8,128)(2,1)S(1)} collective-permute-done((bf16[128,512]{1,0:T(8,128)(2,1)S(1)}, bf16[128,512]{1,0:T(8,128)(2,1)S(1)}, u32[]{:S(2)}, u32[]{:S(2)}) %collective-permute-start.4) | collective-permute-done | bytes 131104 | tf_op jit(solution)/shard_map/ppermute | solution.py:609
  20.9 0.0 copy-done.5
  20.9 0.0 copy-done.6
  20.9 0.0 slice-start
  20.9 3.1 %attention_stage.1 = (bf16[128,1024]{1,0:T(8,128)(2,1)S(1)}, bf16[128,1024]{1,0:T(8,128)(2,1)S(1)}, f32[1,128]{1,0:T(1,128)S(1)}, f32[128,512]{1,0:T(8,128)S(1)}...) custom-call(s32[1]{0:T(128)} %bitcast.2.refs_0_, s32[4]{0:T(128)S(1)} %copy-done.6, ...), custom_call_target="tpu_custom_call" | custom-call | flops 4000000000 | bytes 8000000 | tf_op jit(solution)/shard_map/attention_stage/pallas_call | solution.py:354
  24.0 4.3 %collective-permute-start.5 = (bf16[128,512]{1,0:T(8,128)(2,1)S(1)}, bf16[128,512]{1,0:T(8,128)(2,1)S(1)}, u32[]{:S(2)}, u32[]{:S(2)}) collective-permute-start(bf16[128,512]{1,0:T(8,128)(2,1)S(1)} %get-tuple-element.31), channel_id=1, source_target_pairs={{4,0},{6,2},{0,4},{2,6},{5,1},{7,3},{1,5},{3,7},{12,8},{14,10},{8,... | collective-permute-start | bytes 393224 | tf_op jit(solution)/shard_map/ppermute | solution.py:626
  28.3 0.0 collective-permute-start.7
  28.3 1.5 %collective-permute-start.8 = (bf16[128,512]{1,0:T(8,128)(2,1)S(1)}, bf16[128,512]{1,0:T(8,128)(2,1)S(1)}, u32[]{:S(2)}, u32[]{:S(2)}) collective-permute-start(bf16[128,512]{1,0:T(8,128)(2,1)S(1)} %get-tuple-element.38), channel_id=1, source_target_pairs={{6,0},{4,2},{2,4},{0,6},{7,1},{5,3},{3,5},{1,7},{14,8},{12,10},{10... | collective-permute-start | bytes 393224 | tf_op jit(solution)/shard_map/ppermute | solution.py:626
  29.8 0.0 slice-start.1
  29.8 7.8 %turn_stage.1 = (bf16[128,1792]{1,0:T(8,128)(2,1)S(1)}, f32[128,1792]{1,0:T(8,128)S(1)}, f32[128,3584]{1,0:T(8,128)S(1)}) custom-call(s32[1]{0:T(128)} %bitcast.refs_0_.rank_ref, s32[1,128]{1,0:T(1,128)S(1)} %bitcast.11, bf16[2,1024,3584]{2,1,0:T(8,128)(2,1)S(1)} %bitcast.7, bf16[128,1024]{1,0:T(8,128)(2,1)S(1)} %get-tuple-element.27.refs_3_, ...), custom_call_target="tpu_custom_call" | custom-call | flops 10000000000 | bytes 20000000 | tf_op jit(solution)/shard_map/turn_stage/pallas_call | solution.py:412
  37.6 0.2 collective-permute-done.5.arrived_ref.refs_8_
  37.9 0.0 collective-permute-start.6
  37.9 0.9 %collective-permute-done.7.refs_9_ = bf16[128,512]{1,0:T(8,128)(2,1)S(1)} collective-permute-done((bf16[128,512]{1,0:T(8,128)(2,1)S(1)}, bf16[128,512]{1,0:T(8,128)(2,1)S(1)}, u32[]{:S(2)}, u32[]{:S(2)}) %collective-permute-start.7) | collective-permute-done | bytes 131104 | tf_op jit(solution)/shard_map/ppermute | solution.py:626
  38.8 0.0 collective-permute-done.8.refs_10_
  38.8 0.0 slice-done
  38.8 0.0 slice-done.1
  38.8 1.5 %key_back_stage.1 = (bf16[128,1792]{1,0:T(8,128)(2,1)S(1)}, bf16[128,512]{1,0:T(8,128)(2,1)S(1)}, f32[1,128]{1,0:T(1,128)S(1)}) custom-call(s32[1]{0:T(128)} %bitcast.refs_0_.rank_ref, s32[1,128]{1,0:T(1,128)S(1)} %bitcast.12, f32[2,2,128]{2,1,0:T(2,128)S(1)} %copy-done.1, f32[128,512]{1,0:T(8,128)S(1)} %get-tuple-element.34.refs_3_, ...), custom_call_target="tpu_custom_call" | custom-call | flops 2000000000 | bytes 4000000 | tf_op jit(solution)/shard_map/key_back_stage/pallas_call | solution.py:490
  40.3 0.1 collective-permute-start.9
  40.4 0.5 %collective-permute-start.10 = (f32[1,128]{1,0:T(1,128)S(1)}, f32[1,128]{1,0:T(1,128)S(1)}, u32[]{:S(2)}, u32[]{:S(2)}) collective-permute-start(f32[1,128]{1,0:T(1,128)S(1)} %get-tuple-element.41.refs_7_), channel_id=1, source_target_pairs={{0,1},{1,0},{2,3},{3,2},{4,5},{5,4},{6,7},{7,6},{8,9},{9,8},{10,11... | collective-permute-start | bytes 1544 | tf_op jit(solution)/shard_map/ppermute | solution.py:658
  40.9 1.1 %kept_stage.1.refs_5_ = f32[128,1792]{1,0:T(8,128)S(1)} custom-call(s32[1]{0:T(128)} %bitcast.refs_0_.rank_ref, s32[1,128]{1,0:T(1,128)S(1)} %bitcast.13, f32[128,3584]{1,0:T(8,128)S(1)} %get-tuple-element.33.refs_5_.part_ref, bf16[2,3584,512]{2,1,0:T(8,128)(2,1)S(1)} %bitcast.5, bf16[128,512]{1,0:T(8,128)(2,1)S(1)} %get-tuple-element.39.back_ref), custom_call_target="tpu_custom_call" | custom-call | flops 2000000000 | bytes 4000000 | tf_op jit(solution)/shard_map/kept_stage/pallas_call | solution.py:515
  42.0 0.0 collective-permute-done.6.other_ref
  42.0 0.9 %merge.1 = bf16[128,1792]{1,0:T(8,128)(2,1)} custom-call(f32[128,1792]{1,0:T(8,128)S(1)} %get-tuple-element.29.kept_ref, bf16[128,1792]{1,0:T(8,128)(2,1)S(1)} %collective-permute-done.6.other_ref), custom_call_target="tpu_custom_call" | custom-call | flops 500000000 | bytes 1000000 | tf_op jit(solution)/shard_map/merge/pallas_call | solution.py:449
  42.9 0.0 collective-permute-done.10.refs_8_
  42.9 0.0 collective-permute-done.9.refs_6_
  42.9 1.2 %finish.1 = bf16[128,1792]{1,0:T(8,128)(2,1)} custom-call(s32[1]{0:T(128)} %bitcast.refs_0_.rank_ref, s32[1,128]{1,0:T(1,128)S(1)} %bitcast.14, f32[2,3584]{1,0:T(2,128)S(1)} %copy-done.4, f32[1,128]{1,0:T(1,128)S(1)} %get-tuple-element.32.refs_3_, bf16[128,1792]{1,0:T(8,128)(2,1)S(1)} %copy-done.3, f32[128,1792]{1,0:T(8,128)S(1)} %kept_stage.1.refs_5_, ...), custom_call_target="tpu_custom_call" | custom-call | flops 1000000000 | bytes 2000000 | tf_op jit(solution)/shard_map/finish/pallas_call | solution.py:551
  (3 shorter events, 0.0 us)
Async XLA Ops:
  0.6 4.0 %collective-permute-start = (bf16[128,1792]{1,0:T(8,128)(2,1)}, bf16[128,1792]{1,0:T(8,128)(2,1)S(1)}, u32[]{:S(2)}, u32[]{:S(2)}) collective-permute-start(bf16[128,1792]{1,0:T(8,128)(2,1)} %refs_4_.5), channel_id=1, source_target_pairs={{0,1},{1,0},{2,3},{3,2},{4,5},{5,4},{6,7},{7,6},{8,9},{9,8},{10,11... | collective-permute-start | bytes 1376264 | tf_op jit(solution)/shard_map/ppermute | solution.py:588
  1.1 10.8 %collective-permute-start.1 = (bf16[128,1792]{1,0:T(8,128)(2,1)}, bf16[128,1792]{1,0:T(8,128)(2,1)S(1)}, u32[]{:S(2)}, u32[]{:S(2)}) collective-permute-start(bf16[128,1792]{1,0:T(8,128)(2,1)} %refs_6_.2), channel_id=1, source_target_pairs={{0,1},{1,0},{2,3},{3,2},{4,5},{5,4},{6,7},{7,6},{8,9},{9,8},{10,11... | collective-permute-start | bytes 1376264 | tf_op jit(solution)/shard_map/ppermute | solution.py:588
  1.2 3.4 %copy-start.1 = (f32[2,2,128]{2,1,0:T(2,128)S(1)}, f32[2,2,128]{2,1,0:T(2,128)}, u32[]{:S(2)}) copy-start(f32[2,2,128]{2,1,0:T(2,128)} %refs_2_.8) | copy-start | bytes 6148
  1.2 3.4 %copy-start.2 = (s32[128]{0:T(128)S(1)}, s32[128]{0:T(128)}, u32[]{:S(2)}) copy-start(s32[128]{0:T(128)} %param.17) | copy-start | bytes 1540
  1.2 3.4 %copy-start.3 = (bf16[128,1792]{1,0:T(8,128)(2,1)S(1)}, bf16[128,1792]{1,0:T(8,128)(2,1)}, u32[]{:S(2)}) copy-start(bf16[128,1792]{1,0:T(8,128)(2,1)} %refs_4_.5) | copy-start | bytes 1376260
  1.2 3.4 %copy-start.4 = (f32[2,3584]{1,0:T(2,128)S(1)}, f32[2,3584]{1,0:T(2,128)}, u32[]{:S(2)}) copy-start(f32[2,3584]{1,0:T(2,128)} %refs_2_.9) | copy-start | bytes 86020
  1.2 10.7 %slice-start.2 = ((s8[14680064]{0:T(1024)(128)(4,1)}), s8[4194304]{0:T(1024)(128)(4,1)S(1)}, s32[]{:S(2)}) async-start(s8[14680064]{0:T(1024)(128)(4,1)} %bitcast.6), calls=%async_computation.2 | async-start | bytes 8388608
  1.3 10.7 %slice-start.3 = ((s8[14680064]{0:T(1024)(128)(4,1)}), s8[4194304]{0:T(1024)(128)(4,1)S(1)}, s32[]{:S(2)}) async-start(s8[14680064]{0:T(1024)(128)(4,1)} %bitcast.6), calls=%async_computation.3 | async-start | bytes 8388608
  4.6 7.3 %slice-start.4 = ((s8[14680064]{0:T(1024)(128)(4,1)}), s8[4194304]{0:T(1024)(128)(4,1)S(1)}, s32[]{:S(2)}) async-start(s8[14680064]{0:T(1024)(128)(4,1)} %bitcast.6), calls=%async_computation.4 | async-start | bytes 8388608
  4.7 7.3 %slice-start.5 = ((s8[14680064]{0:T(1024)(128)(4,1)}), s8[2097152]{0:T(1024)(128)(4,1)S(1)}, s32[]{:S(2)}) async-start(s8[14680064]{0:T(1024)(128)(4,1)} %bitcast.6), calls=%async_computation.5 | async-start | bytes 4194304
  4.7 7.3 %copy-start = (bf16[128,1792]{1,0:T(8,128)(2,1)S(1)}, bf16[128,1792]{1,0:T(8,128)(2,1)}, u32[]{:S(2)}) copy-start(bf16[128,1792]{1,0:T(8,128)(2,1)} %refs_6_.2) | copy-start | bytes 1376260
  6.2 14.0 %collective-permute-start.2 = (bf16[128,512]{1,0:T(8,128)(2,1)S(1)}, bf16[128,512]{1,0:T(8,128)(2,1)S(1)}, u32[]{:S(2)}, u32[]{:S(2)}) collective-permute-start(bf16[128,512]{1,0:T(8,128)(2,1)S(1)} %get-tuple-element.26.refs_8_), channel_id=1, source_target_pairs={{0,4},{2,6},{4,0},{6,2},{1,5},{3,7},{5,1},{7,3},{8,12},{10,14},{12... | collective-permute-start | bytes 393224 | tf_op jit(solution)/shard_map/ppermute | solution.py:609
  10.3 9.9 %collective-permute-start.3 = (bf16[128,512]{1,0:T(8,128)(2,1)S(1)}, bf16[128,512]{1,0:T(8,128)(2,1)S(1)}, u32[]{:S(2)}, u32[]{:S(2)}) collective-permute-start(bf16[128,512]{1,0:T(8,128)(2,1)S(1)} %get-tuple-element.26.refs_8_), channel_id=1, source_target_pairs={{0,2},{2,0},{4,6},{6,4},{1,3},{3,1},{5,7},{7,5},{8,10},{10,8},{12,... | collective-permute-start | bytes 393224 | tf_op jit(solution)/shard_map/ppermute | solution.py:609
  11.9 9.0 %collective-permute-start.4 = (bf16[128,512]{1,0:T(8,128)(2,1)S(1)}, bf16[128,512]{1,0:T(8,128)(2,1)S(1)}, u32[]{:S(2)}, u32[]{:S(2)}) collective-permute-start(bf16[128,512]{1,0:T(8,128)(2,1)S(1)} %get-tuple-element.26.refs_8_), channel_id=1, source_target_pairs={{0,6},{2,4},{4,2},{6,0},{1,7},{3,5},{5,3},{7,1},{8,14},{10,12},{12... | collective-permute-start | bytes 393224 | tf_op jit(solution)/shard_map/ppermute | solution.py:609
  12.0 8.9 %copy-start.5 = (s32[512]{0:T(512)S(1)}, s32[512]{0:T(512)}, u32[]{:S(2)}) copy-start(s32[512]{0:T(512)} %param.18) | copy-start | bytes 6148
  12.0 8.9 %copy-start.6 = (s32[4]{0:T(128)S(1)}, s32[4]{0:T(128)}, u32[]{:S(2)}) copy-start(s32[4]{0:T(128)} %refs_1_.1) | copy-start | bytes 52
  20.9 17.9 %slice-start = ((s8[7340032]{0:T(1024)(128)(4,1)}), s8[4194304]{0:T(1024)(128)(4,1)S(1)}, s32[]{:S(2)}) async-start(s8[7340032]{0:T(1024)(128)(4,1)} %bitcast.4), calls=%async_computation | async-start | bytes 8388608
  24.0 13.9 %collective-permute-start.5 = (bf16[128,512]{1,0:T(8,128)(2,1)S(1)}, bf16[128,512]{1,0:T(8,128)(2,1)S(1)}, u32[]{:S(2)}, u32[]{:S(2)}) collective-permute-start(bf16[128,512]{1,0:T(8,128)(2,1)S(1)} %get-tuple-element.31), channel_id=1, source_target_pairs={{4,0},{6,2},{0,4},{2,6},{5,1},{7,3},{1,5},{3,7},{12,8},{14,10},{8,... | collective-permute-start | bytes 393224 | tf_op jit(solution)/shard_map/ppermute | solution.py:626
  28.3 10.5 %collective-permute-start.7 = (bf16[128,512]{1,0:T(8,128)(2,1)S(1)}, bf16[128,512]{1,0:T(8,128)(2,1)S(1)}, u32[]{:S(2)}, u32[]{:S(2)}) collective-permute-start(bf16[128,512]{1,0:T(8,128)(2,1)S(1)} %get-tuple-element.37), channel_id=1, source_target_pairs={{2,0},{0,2},{6,4},{4,6},{3,1},{1,3},{7,5},{5,7},{10,8},{8,10},{14,... | collective-permute-start | bytes 393224 | tf_op jit(solution)/shard_map/ppermute | solution.py:626
  28.3 10.5 %collective-permute-start.8 = (bf16[128,512]{1,0:T(8,128)(2,1)S(1)}, bf16[128,512]{1,0:T(8,128)(2,1)S(1)}, u32[]{:S(2)}, u32[]{:S(2)}) collective-permute-start(bf16[128,512]{1,0:T(8,128)(2,1)S(1)} %get-tuple-element.38), channel_id=1, source_target_pairs={{6,0},{4,2},{2,4},{0,6},{7,1},{5,3},{3,5},{1,7},{14,8},{12,10},{10... | collective-permute-start | bytes 393224 | tf_op jit(solution)/shard_map/ppermute | solution.py:626
  29.8 9.0 %slice-start.1 = ((s8[7340032]{0:T(1024)(128)(4,1)}), s8[3145728]{0:T(1024)(128)(4,1)S(1)}, s32[]{:S(2)}) async-start(s8[7340032]{0:T(1024)(128)(4,1)} %bitcast.4), calls=%async_computation.1 | async-start | bytes 6291456
  37.9 4.1 %collective-permute-start.6 = (bf16[128,1792]{1,0:T(8,128)(2,1)S(1)}, bf16[128,1792]{1,0:T(8,128)(2,1)S(1)}, u32[]{:S(2)}, u32[]{:S(2)}) collective-permute-start(bf16[128,1792]{1,0:T(8,128)(2,1)S(1)} %tie.1), channel_id=1, source_target_pairs={{0,1},{1,0},{2,3},{3,2},{4,5},{5,4},{6,7},{7,6},{8,9},{9,8},{10,11... | collective-permute-start | bytes 1376264 | tf_op jit(solution)/shard_map/ppermute | solution.py:635
  40.3 2.6 %collective-permute-start.9 = (bf16[128,1792]{1,0:T(8,128)(2,1)S(1)}, bf16[128,1792]{1,0:T(8,128)(2,1)S(1)}, u32[]{:S(2)}, u32[]{:S(2)}) collective-permute-start(bf16[128,1792]{1,0:T(8,128)(2,1)S(1)} %get-tuple-element.40), channel_id=1, source_target_pairs={{0,1},{1,0},{2,3},{3,2},{4,5},{5,4},{6,7},{7,6},{8,9},{9,8},{10,11... | collective-permute-start | bytes 1376264 | tf_op jit(solution)/shard_map/ppermute | solution.py:659
  40.4 2.5 %collective-permute-start.10 = (f32[1,128]{1,0:T(1,128)S(1)}, f32[1,128]{1,0:T(1,128)S(1)}, u32[]{:S(2)}, u32[]{:S(2)}) collective-permute-start(f32[1,128]{1,0:T(1,128)S(1)} %get-tuple-element.41.refs_7_), channel_id=1, source_target_pairs={{0,1},{1,0},{2,3},{3,2},{4,5},{5,4},{6,7},{7,6},{8,9},{9,8},{10,11... | collective-permute-start | bytes 1544 | tf_op jit(solution)/shard_map/ppermute | solution.py:658

commit v9 on v8

--- a/solution.py
+++ b/solution.py
@@ -152,51 +152,101 @@
     return pltpu.VMEM((AHEAD, 2, pieces[0][1], weights.shape[2]), weights.dtype)
 
 
-def resident(weights):
-    return pltpu.VMEM(weights.shape, weights.dtype)
-
-
-def fetch_kernel(pieces, weight_ref, held_ref, sem_ref):
-    copies = copies_of(weight_ref, held_ref, sem_ref, pieces)
-    for pair in copies:
-        for copy in pair:
-            copy.start()
-    for pair in copies:
-        for copy in pair:
-            copy.wait()
-
-
-def fetch(weights):
-    pieces = chunks_of(weights.shape[1], 896)
+def gain_of(image, gain_ref, columns):
+    return jnp.where(image, gain_ref[1:2, columns], gain_ref[0:1, columns])
+
+
+def early_kernel(pieces, *refs):
+    rank_ref, weight_ref = refs[:2]
+    given_refs, (scaled_ref, squares_ref, total_ref, held_ref) = refs[2:5], refs[5:9]
+    own_held, sems, held_sems, given_sems = refs[9:13]
+    modality_ref, gain_ref, own_ref = refs[13:]
+    given = [
+        pltpu.make_async_copy(source, target, given_sems.at[index])
+        for index, (source, target) in enumerate(zip(given_refs, refs[13:]))
+    ]
+    for copy in given:
+        copy.start()
+    extent = own_ref.shape[1]
+    base = pl.multiple_of(rank_ref[0] * extent, HEAD_DIM)
+    away = pl.multiple_of((1 - rank_ref[0]) * extent, HEAD_DIM)
+    copies = copies_of(weight_ref, own_held, sems, pieces, base)
+    copies += copies_of(weight_ref, held_ref, held_sems, pieces, away)
+    for index in range(len(copies)):
+        begin(copies, index)
+    for copy in given:
+        copy.wait()
+    image = column(modality_ref[...]) > 0.0
+    rows = own_ref[...].astype(f32)
+    squares_ref[...] = row_of(jnp.sum(rows * rows, axis=1, keepdims=True))
+    scaled_ref[...] = (rows * gain_of(image, gain_ref, pl.ds(base, extent))).astype(bf16)
+    for index, (start, size) in enumerate(pieces):
+        arrive(copies, index)
+        part = slice(start, start + size)
+        product = both_experts(image, scaled_ref[:, part], own_held[:, part, :])
+        if index == 0:
+            total_ref[...] = product
+        else:
+            total_ref[...] += product
+    for index in range(len(pieces), len(copies)):
+        arrive(copies, index)
+
+
+def early_stage(rank, modality, norm_gain, own, weights):
+    _, depth, width = weights.shape
+    rows, extent = own.shape
+    pieces = chunks_of(extent, 896)
+    half_weights = (2, extent, width)
+    given = [modality, norm_gain, own]
     return pl.pallas_call(
-        functools.partial(fetch_kernel, pieces),
-        out_shape=resident(weights),
-        in_specs=[ANY],
-        out_specs=VMEM,
-        scratch_shapes=[pltpu.SemaphoreType.DMA((len(pieces), 2))],
-        compiler_params=params(1),
+        functools.partial(early_kernel, pieces),
+        out_shape=[
+            jax.ShapeDtypeStruct((rows, extent), bf16),
+            jax.ShapeDtypeStruct((1, rows), f32),
+            jax.ShapeDtypeStruct((rows, width), f32),
+            pltpu.VMEM(half_weights, bf16),
+        ],
+        in_specs=[SMEM] + [ANY] * 4,
+        out_specs=[VMEM] * 4,
+        scratch_shapes=[
+            pltpu.VMEM(half_weights, bf16),
+            pltpu.SemaphoreType.DMA((len(pieces), 2)),
+            pltpu.SemaphoreType.DMA((len(pieces), 2)),
+            pltpu.SemaphoreType.DMA((len(given),)),
+        ]
+        + [pltpu.VMEM(g.shape, g.dtype) for g in given],
+        compiler_params=params(8),
         cost_estimate=cost(0.2),
-        name="fetch",
-    )(streamed(weights))
-
-
-def key_kernel(count, *refs):
-    rank_ref, modality_ref, gain_ref, head_ref, weight_ref = refs[:5]
-    part_refs = refs[5 : 5 + count]
-    memory_ref, raw_ref, normed_ref, factor_ref = refs[5 + count :]
+        name="early_stage",
+    )(rank, streamed(weights), *(streamed(g) for g in given))
+
+
+def key_kernel(split, *refs):
+    rank_ref, modality_ref, gain_ref, head_ref, weight_ref, rows_ref = refs[:6]
+    memory_ref, raw_ref, scaled_ref, factor_ref = refs[-4:]
     image = column(modality_ref[...]) > 0.0
-    rows = in_order(rank_ref[0], part_refs).astype(f32)
-    factor = inverse_norm(rows)
-    scaling = jnp.where(image, gain_ref[1:2, :], gain_ref[0:1, :])
-    normed_ref[...] = (rows * factor * scaling).astype(bf16)
+    rows = rows_ref[...].astype(f32)
+    extent = rows.shape[1]
+    squares = jnp.sum(rows * rows, axis=1, keepdims=True)
+    if split:
+        own_ref, own_squares_ref, own_total_ref = refs[6:9]
+        squares += column(own_squares_ref[...])
+        columns = pl.ds(pl.multiple_of((1 - rank_ref[0]) * extent, HEAD_DIM), extent)
+    else:
+        columns = slice(0, extent)
+    scaled = (rows * gain_of(image, gain_ref, columns)).astype(bf16)
+    total = both_experts(image, scaled, weight_ref[...])
+    factor = lax.rsqrt(squares * (1.0 / scaled_ref.shape[1]) + epsilon)
     factor_ref[...] = row_of(factor)
-    for index, (start, size) in enumerate(chunks_of(normed_ref.shape[1], 1792)):
-        part = slice(start, start + size)
-        product = both_experts(image, normed_ref[:, part], weight_ref[:, part, :])
-        if index == 0:
-            raw_ref[...] = product
-        else:
-            raw_ref[...] += product
+    if split:
+        total += own_total_ref[...]
+        first = rank_ref[0] == 0
+        own = own_ref[...]
+        scaled_ref[:, :extent] = jnp.where(first, own, scaled)
+        scaled_ref[:, extent:] = jnp.where(first, scaled, own)
+    else:
+        scaled_ref[...] = scaled
+    raw_ref[...] = total * factor
     blocks = raw_ref.shape[1] // HEAD_DIM
     scaling = jnp.where(image, head_ref[1, 1:2, :], head_ref[0, 1:2, :])
     for b in range(blocks):
@@ -207,29 +257,31 @@
         memory_ref[:, part] = jnp.where(is_key, normed, raw).astype(bf16)
 
 
-def key_stage(rank, modality, norm_gain, head_gain, weights, parts):
-    _, depth, width = weights.shape
-    rows = parts[0].shape[0]
+def key_stage(rank, modality, norm_gain, head_gain, weights, part, early):
+    width = weights.shape[2]
+    rows = part.shape[0]
+    depth = norm_gain.shape[1]
     return pl.pallas_call(
-        functools.partial(key_kernel, len(parts)),
+        functools.partial(key_kernel, len(early) > 0),
         out_shape=[
             jax.ShapeDtypeStruct((rows, width), bf16),
             jax.ShapeDtypeStruct((rows, width), f32),
             jax.ShapeDtypeStruct((rows, depth), bf16),
             jax.ShapeDtypeStruct((1, rows), f32),
         ],
-        in_specs=[SMEM] + [VMEM] * (4 + len(parts)),
+        in_specs=[SMEM] + [VMEM] * (5 + len(early)),
         out_specs=[VMEM] * 4,
         compiler_params=params(8),
         cost_estimate=cost(10),
         name="key_stage",
-    )(rank, modality, norm_gain, head_gain, weights, *parts)
+    )(rank, modality, norm_gain, head_gain, weights, part, *early)
 
 
 def middle_kernel(count, pieces, *refs):
-    rank_ref, modality_ref, head_ref, normed_ref, output_ref, query_weight_ref = refs[:6]
-    part_refs = refs[6 : 6 + count]
-    query_ref, raw_ref, back_ref, slots, sems = refs[6 + count :]
+    rank_ref, modality_ref, head_ref, scaled_ref, factor_ref, output_ref = refs[:6]
+    query_weight_ref = refs[6]
+    part_refs = refs[7 : 7 + count]
+    query_ref, raw_ref, back_ref, slots, sems = refs[7 + count :]
     copies = copies_of(query_weight_ref, slots, sems, pieces, slots=AHEAD)
     begin_first(copies)
     image = column(modality_ref[...]) > 0.0
@@ -244,22 +296,24 @@
             arrive(copies, index)
             start, size = pieces[index]
             part = slice(start, start + size)
-            product = both_experts(image, normed_ref[:, part], slots[index % AHEAD])
+            product = both_experts(image, scaled_ref[:, part], slots[index % AHEAD])
             if index == 0:
                 raw_ref[...] = product
             else:
                 raw_ref[...] += product
             begin(copies, index + AHEAD)
         done = until
+    factor = column(factor_ref[...])
     scaling = jnp.where(image, head_ref[1, 0:1, :], head_ref[0, 0:1, :])
     for h in range(raw_ref.shape[1] // HEAD_DIM):
         part = slice(h * HEAD_DIM, (h + 1) * HEAD_DIM)
-        raw = raw_ref[:, part]
+        raw = raw_ref[:, part] * factor
+        raw_ref[:, part] = raw
         query_ref[:, part] = (raw * inverse_norm(raw) * scaling).astype(bf16)
 
 
-def middle_stage(rank, modality, head_gain, normed, output_weight, query_weight, parts):
-    rows = normed.shape[0]
+def middle_stage(rank, modality, head_gain, scaled, factor, output_weight, query_weight, parts):
+    rows = scaled.shape[0]
     width = query_weight.shape[2]
     pieces = chunks_of(query_weight.shape[1], 512)
     return pl.pallas_call(
@@ -269,7 +323,7 @@
             jax.ShapeDtypeStruct((rows, width), f32),
             jax.ShapeDtypeStruct((rows, width), bf16),
         ],
-        in_specs=[SMEM, VMEM, VMEM, VMEM, VMEM, ANY] + [VMEM] * len(parts),
+        in_specs=[SMEM, VMEM, VMEM, VMEM, VMEM, VMEM, ANY] + [VMEM] * len(parts),
         out_specs=[VMEM] * 3,
         scratch_shapes=[
             ring(query_weight, pieces),
@@ -278,7 +332,16 @@
         compiler_params=params(14),
         cost_estimate=cost(8),
         name="middle_stage",
-    )(rank, modality, head_gain, normed, output_weight, streamed(query_weight), *parts)
+    )(
+        rank,
+        modality,
+        head_gain,
+        scaled,
+        factor,
+        output_weight,
+        streamed(query_weight),
+        *parts,
+    )
 
 
 def attention_kernel(blocks, pairs, per_group, *refs):
@@ -441,22 +504,6 @@
     )(passed, arrived)
 
 
-def merge_kernel(kept_ref, other_ref, out_ref):
-    out_ref[...] = (kept_ref[...] + other_ref[...].astype(f32)).astype(bf16)
-
-
-def merge(kept, other):
-    return pl.pallas_call(
-        merge_kernel,
-        out_shape=jax.ShapeDtypeStruct(other.shape, bf16),
-        in_specs=[VMEM, VMEM],
-        out_specs=VMEM,
-        compiler_params=params(4),
-        cost_estimate=cost(0.5),
-        name="merge",
-    )(kept, other)
-
-
 def key_back_kernel(split, *refs):
     rank_ref, modality_ref, head_ref, raw_ref, inner_in_ref, part_ref, weight_ref = refs[:7]
     grad_refs = refs[7:-3]
@@ -527,32 +574,59 @@
     rank_ref, modality_ref, gain_ref, factor_ref, inputs_ref = refs[:5]
     back_refs = refs[5 : 5 + backs]
     inner_refs = refs[5 + backs : 5 + backs + inners]
-    out_ref = refs[-1]
+    rest = refs[5 + backs + inners :]
     width = inputs_ref.shape[1]
+    copies = []
+
+    def send(staged_ref, out_ref, sem, part):
+        copy = pltpu.make_async_copy(staged_ref.at[:, part], out_ref.at[:, part], sem)
+        copy.start()
+        copies.append(copy)
+
+    pieces = [slice(start, start + size) for start, size in chunks_of(width, 896)]
+    if len(rest) == 7:
+        kept_ref, other_ref, attention_ref, out_ref, staged, staged_attention, sems = rest
+        for index, part in enumerate(pieces):
+            whole = kept_ref[:, part] + other_ref[:, part].astype(f32)
+            staged_attention[:, part] = whole.astype(bf16)
+            send(staged_attention, attention_ref, sems.at[1, index], part)
+    else:
+        out_ref, staged, sems = rest
     image = column(modality_ref[...]) > 0.0
-    gain = gain_ref[...]
-    if gain.shape[1] != width:
-        gain = gain_ref[:, pl.ds(pl.multiple_of(rank_ref[0] * width, HEAD_DIM), width)]
-    scaling = jnp.where(image, gain[1:2, :], gain[0:1, :])
     factor = column(factor_ref[...])
-    back = back_refs[0][...].astype(f32)
-    for ref in back_refs[1:]:
-        back += ref[...].astype(f32)
     inner = inner_refs[0][...]
     for ref in inner_refs[1:]:
         inner += ref[...]
-    unit_rows = inputs_ref[...].astype(f32) * factor
-    inner_mean = column(inner) * (1.0 / total_width)
-    out_ref[...] = (factor * (scaling * back - unit_rows * inner_mean)).astype(bf16)
-
-
-def finish(rank, total_width, modality, gain, factor, inputs, backs, inners):
-    arrays = [modality, gain, factor, inputs, *backs, *inners]
+    inner_mean = factor * column(inner) * (1.0 / total_width)
+    gathered = gain_ref.shape[1] != width
+    for index, part in enumerate(pieces):
+        columns = part
+        if gathered:
+            first = pl.multiple_of(rank_ref[0] * width, HEAD_DIM) + part.start
+            columns = pl.ds(first, part.stop - part.start)
+        back = back_refs[0][:, part].astype(f32)
+        for ref in back_refs[1:]:
+            back += ref[:, part].astype(f32)
+        rows = inputs_ref[:, part].astype(f32)
+        result = factor * (gain_of(image, gain_ref, columns) * back - rows * inner_mean)
+        staged[:, part] = result.astype(bf16)
+        send(staged, out_ref, sems.at[0, index], part)
+    for copy in copies:
+        copy.wait()
+
+
+def finish(rank, total_width, modality, gain, factor, inputs, backs, inners, projected):
+    shape = jax.ShapeDtypeStruct(inputs.shape, bf16)
+    arrays = [modality, gain, factor, inputs, *backs, *inners, *projected]
+    count = 2 if projected else 1
+    pieces = len(chunks_of(inputs.shape[1], 896))
     return pl.pallas_call(
         functools.partial(finish_kernel, len(backs), len(inners), total_width),
-        out_shape=jax.ShapeDtypeStruct(inputs.shape, bf16),
+        out_shape=[shape] * count,
         in_specs=[SMEM] + [VMEM] * len(arrays),
-        out_specs=VMEM,
+        out_specs=[ANY] * count,
+        scratch_shapes=[pltpu.VMEM(inputs.shape, bf16)] * count
+        + [pltpu.SemaphoreType.DMA((count, pieces))],
         compiler_params=params(6),
         cost_estimate=cost(1),
         name="finish",
@@ -591,8 +665,14 @@
     def scatter_columns(part):
         return lax.psum_scatter(part, "tensor", scatter_dimension=1, tiled=True)
 
-    memory, key_raw, normed, row_factor = key_stage(
-        rank, modality, norm_gain, head_gain, fetch(key_weight), spread(inputs)
+    if split:
+        other = lax.ppermute(inputs, "tensor", swap)
+        *early, key_held = early_stage(rank, modality, norm_gain, inputs, key_weight)
+    else:
+        other = lax.all_gather(inputs, "tensor", axis=1, tiled=True)
+        early, key_held = [], key_weight
+    memory, key_raw, scaled, row_factor = key_stage(
+        rank, modality, norm_gain, head_gain, key_held, other, early
     )
     shared = tensor_count > KV_HEADS
     is_even = tensor_rank % 2 == 0
@@ -609,7 +689,14 @@
         memories.append(lax.ppermute(memory, "seq", seq_pairs(step, block_count)))
 
     query, query_raw, back_attended = middle_stage(
-        rank, modality, head_gain, normed, output_weight, query_weight, spread(cotangent)
+        rank,
+        modality,
+        head_gain,
+        scaled,
+        row_factor,
+        output_weight,
+        query_weight,
+        spread(cotangent),
     )
     attended, query_back, inner, own_grad, *grads = attention_stage(
         block_rank.astype(jnp.int32).reshape(1),
@@ -632,9 +719,10 @@
     )
     if split:
         passed = tie(projected[0], incoming[0])
-        attention_out = merge(projected[1], lax.ppermute(passed, "tensor", swap))
+        projected = [projected[1], lax.ppermute(passed, "tensor", swap)]
     else:
         attention_out = scatter_columns(projected[0])
+        projected = []
 
     if shared:
         total = own_grad + sum(grad.astype(f32) for grad in incoming)
@@ -664,8 +752,12 @@
         inners = [lax.psum(inner, "tensor")]
         backs = [scatter_columns(sent)]
         gain = lax.dynamic_slice_in_dim(norm_gain, tensor_rank * local_width, local_width, 1)
-    grad_input = finish(rank, full_width, modality, gain, row_factor, inputs, backs, inners)
-    return (attention_out, grad_input)
+    results = finish(
+        rank, full_width, modality, gain, row_factor, inputs, backs, inners, projected
+    )
+    if split:
+        attention_out = results[0]
+    return (attention_out, results[-1])
 
 
 def solution(mesh):

time: 44.3 us -> 44 us (level)
    pallas_call x3 -> x2, Pallas kernels: 5.75 us -> 5.16 us  [the longest x1 4.17 us: early_stage(): pl.pallas_call(functools.partial(early_kernel, pieces), out_shape=[jax.Sh...]
    ppermute x1 -> x2, starting transfers between devices: 0.01 us -> 0.52 us  [the longest x1 0.52 us: local(): other = lax.ppermute(inputs, 'tensor', swap)]
    ppermute x2 -> x1, starting transfers between devices: 0.6 us -> 0.08 us  [spread(): return [part, lax.ppermute(part, 'tensor', swap)]]
  transfers between devices with their start and end apart: 11 -> 11, of which waited for: 3 -> 4; matrix products, arithmetic and copies ran while one was open for 0% -> 0% of each run, Pallas kernels for 55% -> 54%
where the time goes in v9:
time: 44 us; the launch traced here: 43.9 us
  Pallas kernels  28.3 us (64%)
  starting transfers between devices  12.6 us (29%)
  waiting for transfers between devices  1.87 us (4%)
  between operations  1.04 us (2%)
    pallas_call x1, Pallas kernels, middle_stage(): pl.pallas_call(functools.partial(middle_kernel, len(parts), pieces), out_...  8.11 us
    pallas_call x1, Pallas kernels, turn_stage(): pl.pallas_call(functools.partial(turn_kernel, pieces, len(outs)), out_sha...  7.83 us
    ppermute x3, starting transfers between devices, local(): lax.ppermute(grad, 'seq', inverted(seq_pairs(step, block_count)))  5.83 us
    ppermute x3, starting transfers between devices, local(): memories.append(lax.ppermute(memory, 'seq', seq_pairs(step, block_count)))  5.66 us
    pallas_call x1, Pallas kernels, early_stage(): pl.pallas_call(functools.partial(early_kernel, pieces), out_shape=[jax.Sh...  4.17 us
    pallas_call x1, Pallas kernels, attention_stage(): pl.pallas_call(functools.partial(attention_kernel, blocks, pairs, per_gro...  3.06 us
    pallas_call x1, Pallas kernels, key_back_stage(): pl.pallas_call(functools.partial(key_back_kernel, split), out_shape=[jax....  1.49 us
    pallas_call x1, Pallas kernels, finish(): pl.pallas_call(functools.partial(finish_kernel, len(backs), len(inners),...  1.48 us
  transfers between devices with their start and end apart: 11, of which 4 were waited for; matrix products, arithmetic and copies ran while one was open for 0% of the time, Pallas kernels for 54%

profile of v9, /device:TPU:0, one launch (start us, length us, event | category | flops | bytes accessed | tf_op | source)
XLA Modules:
  0.0 43.9 jit_solution(2647356274953735029)
XLA Ops:
  0.6 0.0 copy-start.4
  0.6 0.0 copy-start.2
  0.7 0.0 copy-start.3
  0.7 0.5 %collective-permute-start = (bf16[128,1792]{1,0:T(8,128)(2,1)}, bf16[128,1792]{1,0:T(8,128)(2,1)S(1)}, u32[]{:S(2)}, u32[]{:S(2)}) collective-permute-start(bf16[128,1792]{1,0:T(8,128)(2,1)} %refs_4_.5), channel_id=1, source_target_pairs={{0,1},{1,0},{2,3},{3,2},{4,5},{5,4},{6,7},{7,6},{8,9},{9,8},{10,11... | collective-permute-start | bytes 1376264 | tf_op jit(solution)/shard_map/ppermute | solution.py:669
  1.2 0.1 collective-permute-start.1
  1.3 0.0 slice-start.2
  1.3 4.2 %early_stage.1 = (bf16[128,1792]{1,0:T(8,128)(2,1)S(1)}, f32[1,128]{1,0:T(1,128)S(1)}, f32[128,512]{1,0:T(8,128)S(1)}, bf16[2,1792,512]{2,1,0:T(8,128)(2,1)S(1)}) custom-call(s32[1]{0:T(128)} %bitcast.refs_0_.rank_ref, bf16[2,3584,512]{2,1,0:T(8,128)(2,1)} %weight_ref.1, s32[1,128]{1,0:T(1,128)} %bitcast.8, f32[2,3584]{1,0:T(2,128)} %refs_2_.9, ...), custom_call_target="tpu_custom_call" | custom-call | flops 200000000 | bytes 400000 | tf_op jit(solution)/shard_map/early_stage/pallas_call | solution.py:201
  5.4 0.0 collective-permute-done.refs_5_
  5.5 0.0 copy-done.4
  5.5 0.0 copy-done.2
  5.5 0.0 copy-done.3
  5.5 0.0 slice-start.3
  5.5 0.0 slice-start.4
  5.5 0.0 slice-start.5
  5.5 0.0 copy-start
  5.5 1.0 %key_stage.1 = (bf16[128,512]{1,0:T(8,128)(2,1)S(1)}, f32[128,512]{1,0:T(8,128)S(1)}, bf16[128,3584]{1,0:T(8,128)(2,1)S(1)}, f32[1,128]{1,0:T(1,128)S(1)}) custom-call(s32[1]{0:T(128)} %bitcast.refs_0_.rank_ref, s32[1,128]{1,0:T(1,128)S(1)} %bitcast.9, f32[2,3584]{1,0:T(2,128)S(1)} %copy-done.2, f32[2,2,128]{2,1,0:T(2,128)S(1)} %copy-done.3, ...), custom_call_target="tpu_custom_call" | custom-call | flops 10000000000 | bytes 20000000 | tf_op jit(solution)/shard_map/key_stage/pallas_call | solution.py:264
  6.5 4.1 %collective-permute-start.2 = (bf16[128,512]{1,0:T(8,128)(2,1)S(1)}, bf16[128,512]{1,0:T(8,128)(2,1)S(1)}, u32[]{:S(2)}, u32[]{:S(2)}) collective-permute-start(bf16[128,512]{1,0:T(8,128)(2,1)S(1)} %get-tuple-element.35.refs_8_), channel_id=1, source_target_pairs={{0,4},{2,6},{4,0},{6,2},{1,5},{3,7},{5,1},{7,3},{8,12},{10,14},{12... | collective-permute-start | bytes 393224 | tf_op jit(solution)/shard_map/ppermute | solution.py:689
  10.6 1.6 %collective-permute-start.3 = (bf16[128,512]{1,0:T(8,128)(2,1)S(1)}, bf16[128,512]{1,0:T(8,128)(2,1)S(1)}, u32[]{:S(2)}, u32[]{:S(2)}) collective-permute-start(bf16[128,512]{1,0:T(8,128)(2,1)S(1)} %get-tuple-element.35.refs_8_), channel_id=1, source_target_pairs={{0,2},{2,0},{4,6},{6,4},{1,3},{3,1},{5,7},{7,5},{8,10},{10,8},{12,... | collective-permute-start | bytes 393224 | tf_op jit(solution)/shard_map/ppermute | solution.py:689
  12.2 0.0 collective-permute-start.4
  12.2 0.0 collective-permute-done.1.refs_8_
  12.2 0.0 slice-done.2
  12.2 0.0 slice-done.3
  12.2 0.0 slice-done.4
  12.2 0.0 slice-done.5
  12.2 0.0 copy-done
  12.2 0.0 copy-start.5
  12.2 0.0 copy-start.6
  12.3 8.1 %middle_stage.1 = (bf16[128,1024]{1,0:T(8,128)(2,1)S(1)}, f32[128,1024]{1,0:T(8,128)S(1)}, bf16[128,1024]{1,0:T(8,128)(2,1)S(1)}) custom-call(s32[1]{0:T(128)} %bitcast.refs_0_.rank_ref, s32[1,128]{1,0:T(1,128)S(1)} %bitcast.10, f32[2,2,128]{2,1,0:T(2,128)S(1)} %copy-done.3, bf16[128,3584]{1,0:T(8,128)(2,1)S(1)} %get-tuple-element.31.refs_3_, ...), custom_call_target="tpu_custom_call" | custom-call | flops 8000000000 | bytes 16000000 | tf_op jit(solution)/shard_map/middle_stage/pallas_call | solution.py:319
  20.4 0.0 collective-permute-done.2.refs_9_
  20.4 0.0 collective-permute-done.3.refs_10_
  20.4 0.6 %collective-permute-done.4.refs_11_ = bf16[128,512]{1,0:T(8,128)(2,1)S(1)} collective-permute-done((bf16[128,512]{1,0:T(8,128)(2,1)S(1)}, bf16[128,512]{1,0:T(8,128)(2,1)S(1)}, u32[]{:S(2)}, u32[]{:S(2)}) %collective-permute-start.4) | collective-permute-done | bytes 131104 | tf_op jit(solution)/shard_map/ppermute | solution.py:689
  21.0 0.0 copy-done.5
  21.0 0.0 copy-done.6
  21.0 0.0 slice-start
  21.0 3.1 %attention_stage.1 = (bf16[128,1024]{1,0:T(8,128)(2,1)S(1)}, bf16[128,1024]{1,0:T(8,128)(2,1)S(1)}, f32[1,128]{1,0:T(1,128)S(1)}, f32[128,512]{1,0:T(8,128)S(1)}...) custom-call(s32[1]{0:T(128)} %bitcast.2.refs_0_, s32[4]{0:T(128)S(1)} %copy-done.6, ...), custom_call_target="tpu_custom_call" | custom-call | flops 4000000000 | bytes 8000000 | tf_op jit(solution)/shard_map/attention_stage/pallas_call | solution.py:417
  24.0 4.3 %collective-permute-start.5 = (bf16[128,512]{1,0:T(8,128)(2,1)S(1)}, bf16[128,512]{1,0:T(8,128)(2,1)S(1)}, u32[]{:S(2)}, u32[]{:S(2)}) collective-permute-start(bf16[128,512]{1,0:T(8,128)(2,1)S(1)} %get-tuple-element.42), channel_id=1, source_target_pairs={{4,0},{6,2},{0,4},{2,6},{5,1},{7,3},{1,5},{3,7},{12,8},{14,10},{8,... | collective-permute-start | bytes 393224 | tf_op jit(solution)/shard_map/ppermute | solution.py:713
  28.3 0.0 collective-permute-start.6
  28.3 1.5 %collective-permute-start.7 = (bf16[128,512]{1,0:T(8,128)(2,1)S(1)}, bf16[128,512]{1,0:T(8,128)(2,1)S(1)}, u32[]{:S(2)}, u32[]{:S(2)}) collective-permute-start(bf16[128,512]{1,0:T(8,128)(2,1)S(1)} %get-tuple-element.44), channel_id=1, source_target_pairs={{6,0},{4,2},{2,4},{0,6},{7,1},{5,3},{3,5},{1,7},{14,8},{12,10},{10... | collective-permute-start | bytes 393224 | tf_op jit(solution)/shard_map/ppermute | solution.py:713
  29.9 0.0 slice-start.1
  29.9 7.8 %turn_stage.1 = (bf16[128,1792]{1,0:T(8,128)(2,1)S(1)}, f32[128,1792]{1,0:T(8,128)S(1)}, f32[128,3584]{1,0:T(8,128)S(1)}) custom-call(s32[1]{0:T(128)} %bitcast.refs_0_.rank_ref, s32[1,128]{1,0:T(1,128)S(1)} %bitcast.12, bf16[2,1024,3584]{2,1,0:T(8,128)(2,1)S(1)} %bitcast.7, bf16[128,1024]{1,0:T(8,128)(2,1)S(1)} %get-tuple-element.36.refs_3_, ...), custom_call_target="tpu_custom_call" | custom-call | flops 10000000000 | bytes 20000000 | tf_op jit(solution)/shard_map/turn_stage/pallas_call | solution.py:475
  37.7 0.2 collective-permute-done.5.refs_8_.arrived_ref
  37.9 0.0 collective-permute-start.10
  37.9 0.9 %collective-permute-done.6.refs_9_ = bf16[128,512]{1,0:T(8,128)(2,1)S(1)} collective-permute-done((bf16[128,512]{1,0:T(8,128)(2,1)S(1)}, bf16[128,512]{1,0:T(8,128)(2,1)S(1)}, u32[]{:S(2)}, u32[]{:S(2)}) %collective-permute-start.6) | collective-permute-done | bytes 131104 | tf_op jit(solution)/shard_map/ppermute | solution.py:713
  38.8 0.0 collective-permute-done.7.refs_10_
  38.8 0.0 slice-done
  38.8 0.0 slice-done.1
  38.8 1.5 %key_back_stage.1 = (bf16[128,1792]{1,0:T(8,128)(2,1)S(1)}, bf16[128,512]{1,0:T(8,128)(2,1)S(1)}, f32[1,128]{1,0:T(1,128)S(1)}) custom-call(s32[1]{0:T(128)} %bitcast.refs_0_.rank_ref, s32[1,128]{1,0:T(1,128)S(1)} %bitcast.13, f32[2,2,128]{2,1,0:T(2,128)S(1)} %copy-done.3, f32[128,512]{1,0:T(8,128)S(1)} %get-tuple-element.39.refs_3_, ...), custom_call_target="tpu_custom_call" | custom-call | flops 2000000000 | bytes 4000000 | tf_op jit(solution)/shard_map/key_back_stage/pallas_call | solution.py:537
  40.3 0.0 copy-start.1
  40.4 0.1 collective-permute-start.8
  40.4 0.5 %collective-permute-start.9 = (f32[1,128]{1,0:T(1,128)S(1)}, f32[1,128]{1,0:T(1,128)S(1)}, u32[]{:S(2)}, u32[]{:S(2)}) collective-permute-start(f32[1,128]{1,0:T(1,128)S(1)} %get-tuple-element.47.refs_7_), channel_id=1, source_target_pairs={{0,1},{1,0},{2,3},{3,2},{4,5},{5,4},{6,7},{7,6},{8,9},{9,8},{10,11... | collective-permute-start | bytes 1544 | tf_op jit(solution)/shard_map/ppermute | solution.py:746
  40.9 1.1 %kept_stage.1.refs_5_ = f32[128,1792]{1,0:T(8,128)S(1)} custom-call(s32[1]{0:T(128)} %bitcast.refs_0_.rank_ref, s32[1,128]{1,0:T(1,128)S(1)} %bitcast.14, f32[128,3584]{1,0:T(8,128)S(1)} %get-tuple-element.38.refs_5_.part_ref, bf16[2,3584,512]{2,1,0:T(8,128)(2,1)S(1)} %bitcast.5, bf16[128,512]{1,0:T(8,128)(2,1)S(1)} %get-tuple-element.45.back_ref), custom_call_target="tpu_custom_call" | custom-call | flops 2000000000 | bytes 4000000 | tf_op jit(solution)/shard_map/kept_stage/pallas_call | solution.py:562
  42.1 0.2 collective-permute-done.9.refs_8_
  42.2 0.0 collective-permute-done.10.refs_10_
  42.2 0.0 collective-permute-done.8.refs_6_
  42.2 0.0 copy-done.1
  42.3 1.5 %finish.1 = (bf16[128,1792]{1,0:T(8,128)(2,1)}, bf16[128,1792]{1,0:T(8,128)(2,1)}) custom-call(s32[1]{0:T(128)} %bitcast.refs_0_.rank_ref, s32[1,128]{1,0:T(1,128)S(1)} %bitcast.15, f32[2,3584]{1,0:T(2,128)S(1)} %copy-done.2, f32[1,128]{1,0:T(1,128)S(1)} %get-tuple-element.30.refs_4_.refs_3_, bf16[128,1792]{1,0:T(8,128)(2,1)S(1)} %copy-done.1, ...), custom_call_target="tpu_custom_call" | custom-call | flops 1000000000 | bytes 2000000 | tf_op jit(solution)/shard_map/finish/pallas_call | solution.py:623
  (3 shorter events, 0.0 us)
Async XLA Ops:
  0.6 4.8 %copy-start.4 = (s32[128]{0:T(128)S(1)}, s32[128]{0:T(128)}, u32[]{:S(2)}) copy-start(s32[128]{0:T(128)} %param.17) | copy-start | bytes 1540
  0.6 4.8 %copy-start.2 = (f32[2,3584]{1,0:T(2,128)S(1)}, f32[2,3584]{1,0:T(2,128)}, u32[]{:S(2)}) copy-start(f32[2,3584]{1,0:T(2,128)} %refs_2_.9) | copy-start | bytes 86020
  0.7 4.8 %copy-start.3 = (f32[2,2,128]{2,1,0:T(2,128)S(1)}, f32[2,2,128]{2,1,0:T(2,128)}, u32[]{:S(2)}) copy-start(f32[2,2,128]{2,1,0:T(2,128)} %refs_2_.8) | copy-start | bytes 6148
  0.7 4.8 %collective-permute-start = (bf16[128,1792]{1,0:T(8,128)(2,1)}, bf16[128,1792]{1,0:T(8,128)(2,1)S(1)}, u32[]{:S(2)}, u32[]{:S(2)}) collective-permute-start(bf16[128,1792]{1,0:T(8,128)(2,1)} %refs_4_.5), channel_id=1, source_target_pairs={{0,1},{1,0},{2,3},{3,2},{4,5},{5,4},{6,7},{7,6},{8,9},{9,8},{10,11... | collective-permute-start | bytes 1376264 | tf_op jit(solution)/shard_map/ppermute | solution.py:669
  1.2 11.0 %collective-permute-start.1 = (bf16[128,1792]{1,0:T(8,128)(2,1)}, bf16[128,1792]{1,0:T(8,128)(2,1)S(1)}, u32[]{:S(2)}, u32[]{:S(2)}) collective-permute-start(bf16[128,1792]{1,0:T(8,128)(2,1)} %refs_7_.1), channel_id=1, source_target_pairs={{0,1},{1,0},{2,3},{3,2},{4,5},{5,4},{6,7},{7,6},{8,9},{9,8},{10,11... | collective-permute-start | bytes 1376264 | tf_op jit(solution)/shard_map/ppermute | solution.py:662
  1.3 10.9 %slice-start.2 = ((s8[14680064]{0:T(1024)(128)(4,1)}), s8[4194304]{0:T(1024)(128)(4,1)S(1)}, s32[]{:S(2)}) async-start(s8[14680064]{0:T(1024)(128)(4,1)} %bitcast.6), calls=%async_computation.2 | async-start | bytes 8388608
  5.5 6.7 %slice-start.3 = ((s8[14680064]{0:T(1024)(128)(4,1)}), s8[4194304]{0:T(1024)(128)(4,1)S(1)}, s32[]{:S(2)}) async-start(s8[14680064]{0:T(1024)(128)(4,1)} %bitcast.6), calls=%async_computation.3 | async-start | bytes 8388608
  5.5 6.7 %slice-start.4 = ((s8[14680064]{0:T(1024)(128)(4,1)}), s8[4194304]{0:T(1024)(128)(4,1)S(1)}, s32[]{:S(2)}) async-start(s8[14680064]{0:T(1024)(128)(4,1)} %bitcast.6), calls=%async_computation.4 | async-start | bytes 8388608
  5.5 6.7 %slice-start.5 = ((s8[14680064]{0:T(1024)(128)(4,1)}), s8[2097152]{0:T(1024)(128)(4,1)S(1)}, s32[]{:S(2)}) async-start(s8[14680064]{0:T(1024)(128)(4,1)} %bitcast.6), calls=%async_computation.5 | async-start | bytes 4194304
  5.5 6.7 %copy-start = (bf16[128,1792]{1,0:T(8,128)(2,1)S(1)}, bf16[128,1792]{1,0:T(8,128)(2,1)}, u32[]{:S(2)}) copy-start(bf16[128,1792]{1,0:T(8,128)(2,1)} %refs_7_.1) | copy-start | bytes 1376260
  6.5 13.9 %collective-permute-start.2 = (bf16[128,512]{1,0:T(8,128)(2,1)S(1)}, bf16[128,512]{1,0:T(8,128)(2,1)S(1)}, u32[]{:S(2)}, u32[]{:S(2)}) collective-permute-start(bf16[128,512]{1,0:T(8,128)(2,1)S(1)} %get-tuple-element.35.refs_8_), channel_id=1, source_target_pairs={{0,4},{2,6},{4,0},{6,2},{1,5},{3,7},{5,1},{7,3},{8,12},{10,14},{12... | collective-permute-start | bytes 393224 | tf_op jit(solution)/shard_map/ppermute | solution.py:689
  10.6 9.8 %collective-permute-start.3 = (bf16[128,512]{1,0:T(8,128)(2,1)S(1)}, bf16[128,512]{1,0:T(8,128)(2,1)S(1)}, u32[]{:S(2)}, u32[]{:S(2)}) collective-permute-start(bf16[128,512]{1,0:T(8,128)(2,1)S(1)} %get-tuple-element.35.refs_8_), channel_id=1, source_target_pairs={{0,2},{2,0},{4,6},{6,4},{1,3},{3,1},{5,7},{7,5},{8,10},{10,8},{12,... | collective-permute-start | bytes 393224 | tf_op jit(solution)/shard_map/ppermute | solution.py:689
  12.2 8.8 %collective-permute-start.4 = (bf16[128,512]{1,0:T(8,128)(2,1)S(1)}, bf16[128,512]{1,0:T(8,128)(2,1)S(1)}, u32[]{:S(2)}, u32[]{:S(2)}) collective-permute-start(bf16[128,512]{1,0:T(8,128)(2,1)S(1)} %get-tuple-element.35.refs_8_), channel_id=1, source_target_pairs={{0,6},{2,4},{4,2},{6,0},{1,7},{3,5},{5,3},{7,1},{8,14},{10,12},{12... | collective-permute-start | bytes 393224 | tf_op jit(solution)/shard_map/ppermute | solution.py:689
  12.2 8.7 %copy-start.5 = (s32[512]{0:T(512)S(1)}, s32[512]{0:T(512)}, u32[]{:S(2)}) copy-start(s32[512]{0:T(512)} %param.18) | copy-start | bytes 6148
  12.2 8.7 %copy-start.6 = (s32[4]{0:T(128)S(1)}, s32[4]{0:T(128)}, u32[]{:S(2)}) copy-start(s32[4]{0:T(128)} %refs_1_.3) | copy-start | bytes 52
  21.0 17.9 %slice-start = ((s8[7340032]{0:T(1024)(128)(4,1)}), s8[4194304]{0:T(1024)(128)(4,1)S(1)}, s32[]{:S(2)}) async-start(s8[7340032]{0:T(1024)(128)(4,1)} %bitcast.4), calls=%async_computation | async-start | bytes 8388608
  24.0 13.9 %collective-permute-start.5 = (bf16[128,512]{1,0:T(8,128)(2,1)S(1)}, bf16[128,512]{1,0:T(8,128)(2,1)S(1)}, u32[]{:S(2)}, u32[]{:S(2)}) collective-permute-start(bf16[128,512]{1,0:T(8,128)(2,1)S(1)} %get-tuple-element.42), channel_id=1, source_target_pairs={{4,0},{6,2},{0,4},{2,6},{5,1},{7,3},{1,5},{3,7},{12,8},{14,10},{8,... | collective-permute-start | bytes 393224 | tf_op jit(solution)/shard_map/ppermute | solution.py:713
  28.3 10.5 %collective-permute-start.6 = (bf16[128,512]{1,0:T(8,128)(2,1)S(1)}, bf16[128,512]{1,0:T(8,128)(2,1)S(1)}, u32[]{:S(2)}, u32[]{:S(2)}) collective-permute-start(bf16[128,512]{1,0:T(8,128)(2,1)S(1)} %get-tuple-element.43), channel_id=1, source_target_pairs={{2,0},{0,2},{6,4},{4,6},{3,1},{1,3},{7,5},{5,7},{10,8},{8,10},{14,... | collective-permute-start | bytes 393224 | tf_op jit(solution)/shard_map/ppermute | solution.py:713
  28.3 10.5 %collective-permute-start.7 = (bf16[128,512]{1,0:T(8,128)(2,1)S(1)}, bf16[128,512]{1,0:T(8,128)(2,1)S(1)}, u32[]{:S(2)}, u32[]{:S(2)}) collective-permute-start(bf16[128,512]{1,0:T(8,128)(2,1)S(1)} %get-tuple-element.44), channel_id=1, source_target_pairs={{6,0},{4,2},{2,4},{0,6},{7,1},{5,3},{3,5},{1,7},{14,8},{12,10},{10... | collective-permute-start | bytes 393224 | tf_op jit(solution)/shard_map/ppermute | solution.py:713
  29.9 9.0 %slice-start.1 = ((s8[7340032]{0:T(1024)(128)(4,1)}), s8[3145728]{0:T(1024)(128)(4,1)S(1)}, s32[]{:S(2)}) async-start(s8[7340032]{0:T(1024)(128)(4,1)} %bitcast.4), calls=%async_computation.1 | async-start | bytes 6291456
  37.9 4.3 %collective-permute-start.10 = (bf16[128,1792]{1,0:T(8,128)(2,1)S(1)}, bf16[128,1792]{1,0:T(8,128)(2,1)S(1)}, u32[]{:S(2)}, u32[]{:S(2)}) collective-permute-start(bf16[128,1792]{1,0:T(8,128)(2,1)S(1)} %tie.1), channel_id=1, source_target_pairs={{0,1},{1,0},{2,3},{3,2},{4,5},{5,4},{6,7},{7,6},{8,9},{9,8},{10,11... | collective-permute-start | bytes 1376264 | tf_op jit(solution)/shard_map/ppermute | solution.py:722
  40.3 1.9 %copy-start.1 = (bf16[128,1792]{1,0:T(8,128)(2,1)S(1)}, bf16[128,1792]{1,0:T(8,128)(2,1)}, u32[]{:S(2)}) copy-start(bf16[128,1792]{1,0:T(8,128)(2,1)} %refs_4_.5) | copy-start | bytes 1376260
  40.4 1.9 %collective-permute-start.8 = (bf16[128,1792]{1,0:T(8,128)(2,1)S(1)}, bf16[128,1792]{1,0:T(8,128)(2,1)S(1)}, u32[]{:S(2)}, u32[]{:S(2)}) collective-permute-start(bf16[128,1792]{1,0:T(8,128)(2,1)S(1)} %get-tuple-element.46), channel_id=1, source_target_pairs={{0,1},{1,0},{2,3},{3,2},{4,5},{5,4},{6,7},{7,6},{8,9},{9,8},{10,11... | collective-permute-start | bytes 1376264 | tf_op jit(solution)/shard_map/ppermute | solution.py:747
  40.4 1.8 %collective-permute-start.9 = (f32[1,128]{1,0:T(1,128)S(1)}, f32[1,128]{1,0:T(1,128)S(1)}, u32[]{:S(2)}, u32[]{:S(2)}) collective-permute-start(f32[1,128]{1,0:T(1,128)S(1)} %get-tuple-element.47.refs_7_), channel_id=1, source_target_pairs={{0,1},{1,0},{2,3},{3,2},{4,5},{5,4},{6,7},{7,6},{8,9},{9,8},{10,11... | collective-permute-start | bytes 1544 | tf_op jit(solution)/shard_map/ppermute | solution.py:746

commit v10 on v9

--- a/solution.py
+++ b/solution.py
@@ -172,7 +172,7 @@
     away = pl.multiple_of((1 - rank_ref[0]) * extent, HEAD_DIM)
     copies = copies_of(weight_ref, own_held, sems, pieces, base)
     copies += copies_of(weight_ref, held_ref, held_sems, pieces, away)
-    for index in range(len(copies)):
+    for index in range(len(pieces)):
         begin(copies, index)
     for copy in given:
         copy.wait()
@@ -180,6 +180,8 @@
     rows = own_ref[...].astype(f32)
     squares_ref[...] = row_of(jnp.sum(rows * rows, axis=1, keepdims=True))
     scaled_ref[...] = (rows * gain_of(image, gain_ref, pl.ds(base, extent))).astype(bf16)
+    for index in range(len(pieces), len(copies)):
+        begin(copies, index)
     for index, (start, size) in enumerate(pieces):
         arrive(copies, index)
         part = slice(start, start + size)

time: 44 us -> 44.4 us (level)
  no operation moved by 1% of the time
where the time goes in v10:
time: 44.4 us; the launch traced here: 44.3 us
  Pallas kernels  28.4 us (64%)
  starting transfers between devices  12.6 us (28%)
  waiting for transfers between devices  2.09 us (5%)
  between operations  1.04 us (2%)
    pallas_call x1, Pallas kernels, middle_stage(): pl.pallas_call(functools.partial(middle_kernel, len(parts), pieces), out_...  8.12 us
    pallas_call x1, Pallas kernels, turn_stage(): pl.pallas_call(functools.partial(turn_kernel, pieces, len(outs)), out_sha...  7.82 us
    ppermute x3, starting transfers between devices, local(): lax.ppermute(grad, 'seq', inverted(seq_pairs(step, block_count)))  5.82 us
    ppermute x3, starting transfers between devices, local(): memories.append(lax.ppermute(memory, 'seq', seq_pairs(step, block_count)))  5.66 us
    pallas_call x1, Pallas kernels, early_stage(): pl.pallas_call(functools.partial(early_kernel, pieces), out_shape=[jax.Sh...  4.35 us
    pallas_call x1, Pallas kernels, attention_stage(): pl.pallas_call(functools.partial(attention_kernel, blocks, pairs, per_gro...  3.06 us
    pallas_call x1, Pallas kernels, key_back_stage(): pl.pallas_call(functools.partial(key_back_kernel, split), out_shape=[jax....  1.49 us
    pallas_call x1, Pallas kernels, finish(): pl.pallas_call(functools.partial(finish_kernel, len(backs), len(inners),...  1.48 us
  transfers between devices with their start and end apart: 11, of which 4 were waited for; matrix products, arithmetic and copies ran while one was open for 0% of the time, Pallas kernels for 54%

profile of v10, /device:TPU:0, one launch (start us, length us, event | category | flops | bytes accessed | tf_op | source)
XLA Modules:
  0.0 44.3 jit_solution(1979401220468966411)
XLA Ops:
  0.6 0.0 copy-start.4
  0.6 0.0 copy-start.2
  0.7 0.0 copy-start.3
  0.7 0.5 %collective-permute-start = (bf16[128,1792]{1,0:T(8,128)(2,1)}, bf16[128,1792]{1,0:T(8,128)(2,1)S(1)}, u32[]{:S(2)}, u32[]{:S(2)}) collective-permute-start(bf16[128,1792]{1,0:T(8,128)(2,1)} %refs_4_.5), channel_id=1, source_target_pairs={{0,1},{1,0},{2,3},{3,2},{4,5},{5,4},{6,7},{7,6},{8,9},{9,8},{10,11... | collective-permute-start | bytes 1376264 | tf_op jit(solution)/shard_map/ppermute | solution.py:671
  1.2 0.1 collective-permute-start.1
  1.3 0.0 slice-start.2
  1.3 4.3 %early_stage.1 = (bf16[128,1792]{1,0:T(8,128)(2,1)S(1)}, f32[1,128]{1,0:T(1,128)S(1)}, f32[128,512]{1,0:T(8,128)S(1)}, bf16[2,1792,512]{2,1,0:T(8,128)(2,1)S(1)}) custom-call(s32[1]{0:T(128)} %bitcast.refs_0_.rank_ref, bf16[2,3584,512]{2,1,0:T(8,128)(2,1)} %weight_ref.1, s32[1,128]{1,0:T(1,128)} %bitcast.8, f32[2,3584]{1,0:T(2,128)} %refs_2_.9, ...), custom_call_target="tpu_custom_call" | custom-call | flops 200000000 | bytes 400000 | tf_op jit(solution)/shard_map/early_stage/pallas_call | solution.py:203
  5.6 0.0 collective-permute-done.refs_5_
  5.6 0.0 copy-done.4
  5.6 0.0 copy-done.2
  5.6 0.0 copy-done.3
  5.7 0.0 slice-start.3
  5.7 0.0 slice-start.4
  5.7 0.0 slice-start.5
  5.7 0.0 copy-start
  5.7 1.0 %key_stage.1 = (bf16[128,512]{1,0:T(8,128)(2,1)S(1)}, f32[128,512]{1,0:T(8,128)S(1)}, bf16[128,3584]{1,0:T(8,128)(2,1)S(1)}, f32[1,128]{1,0:T(1,128)S(1)}) custom-call(s32[1]{0:T(128)} %bitcast.refs_0_.rank_ref, s32[1,128]{1,0:T(1,128)S(1)} %bitcast.9, f32[2,3584]{1,0:T(2,128)S(1)} %copy-done.2, f32[2,2,128]{2,1,0:T(2,128)S(1)} %copy-done.3, ...), custom_call_target="tpu_custom_call" | custom-call | flops 10000000000 | bytes 20000000 | tf_op jit(solution)/shard_map/key_stage/pallas_call | solution.py:266
  6.7 4.1 %collective-permute-start.2 = (bf16[128,512]{1,0:T(8,128)(2,1)S(1)}, bf16[128,512]{1,0:T(8,128)(2,1)S(1)}, u32[]{:S(2)}, u32[]{:S(2)}) collective-permute-start(bf16[128,512]{1,0:T(8,128)(2,1)S(1)} %get-tuple-element.35.refs_8_), channel_id=1, source_target_pairs={{0,4},{2,6},{4,0},{6,2},{1,5},{3,7},{5,1},{7,3},{8,12},{10,14},{12... | collective-permute-start | bytes 393224 | tf_op jit(solution)/shard_map/ppermute | solution.py:691
  10.8 1.6 %collective-permute-start.3 = (bf16[128,512]{1,0:T(8,128)(2,1)S(1)}, bf16[128,512]{1,0:T(8,128)(2,1)S(1)}, u32[]{:S(2)}, u32[]{:S(2)}) collective-permute-start(bf16[128,512]{1,0:T(8,128)(2,1)S(1)} %get-tuple-element.35.refs_8_), channel_id=1, source_target_pairs={{0,2},{2,0},{4,6},{6,4},{1,3},{3,1},{5,7},{7,5},{8,10},{10,8},{12,... | collective-permute-start | bytes 393224 | tf_op jit(solution)/shard_map/ppermute | solution.py:691
  12.4 0.0 collective-permute-start.4
  12.4 0.0 collective-permute-done.1.refs_8_
  12.4 0.0 slice-done.2
  12.4 0.0 slice-done.3
  12.4 0.0 slice-done.4
  12.4 0.0 slice-done.5
  12.4 0.0 copy-done
  12.4 0.0 copy-start.5
  12.4 0.0 copy-start.6
  12.4 8.1 %middle_stage.1 = (bf16[128,1024]{1,0:T(8,128)(2,1)S(1)}, f32[128,1024]{1,0:T(8,128)S(1)}, bf16[128,1024]{1,0:T(8,128)(2,1)S(1)}) custom-call(s32[1]{0:T(128)} %bitcast.refs_0_.rank_ref, s32[1,128]{1,0:T(1,128)S(1)} %bitcast.10, f32[2,2,128]{2,1,0:T(2,128)S(1)} %copy-done.3, bf16[128,3584]{1,0:T(8,128)(2,1)S(1)} %get-tuple-element.31.refs_3_, ...), custom_call_target="tpu_custom_call" | custom-call | flops 8000000000 | bytes 16000000 | tf_op jit(solution)/shard_map/middle_stage/pallas_call | solution.py:321
  20.6 0.0 collective-permute-done.2.refs_9_
  20.6 0.0 collective-permute-done.3.refs_10_
  20.6 0.8 %collective-permute-done.4.refs_11_ = bf16[128,512]{1,0:T(8,128)(2,1)S(1)} collective-permute-done((bf16[128,512]{1,0:T(8,128)(2,1)S(1)}, bf16[128,512]{1,0:T(8,128)(2,1)S(1)}, u32[]{:S(2)}, u32[]{:S(2)}) %collective-permute-start.4) | collective-permute-done | bytes 131104 | tf_op jit(solution)/shard_map/ppermute | solution.py:691
  21.4 0.0 copy-done.5
  21.4 0.0 copy-done.6
  21.4 0.0 slice-start
  21.4 3.1 %attention_stage.1 = (bf16[128,1024]{1,0:T(8,128)(2,1)S(1)}, bf16[128,1024]{1,0:T(8,128)(2,1)S(1)}, f32[1,128]{1,0:T(1,128)S(1)}, f32[128,512]{1,0:T(8,128)S(1)}...) custom-call(s32[1]{0:T(128)} %bitcast.2.refs_0_, s32[4]{0:T(128)S(1)} %copy-done.6, ...), custom_call_target="tpu_custom_call" | custom-call | flops 4000000000 | bytes 8000000 | tf_op jit(solution)/shard_map/attention_stage/pallas_call | solution.py:419
  24.4 4.3 %collective-permute-start.5 = (bf16[128,512]{1,0:T(8,128)(2,1)S(1)}, bf16[128,512]{1,0:T(8,128)(2,1)S(1)}, u32[]{:S(2)}, u32[]{:S(2)}) collective-permute-start(bf16[128,512]{1,0:T(8,128)(2,1)S(1)} %get-tuple-element.42), channel_id=1, source_target_pairs={{4,0},{6,2},{0,4},{2,6},{5,1},{7,3},{1,5},{3,7},{12,8},{14,10},{8,... | collective-permute-start | bytes 393224 | tf_op jit(solution)/shard_map/ppermute | solution.py:715
  28.7 0.0 collective-permute-start.6
  28.7 1.5 %collective-permute-start.7 = (bf16[128,512]{1,0:T(8,128)(2,1)S(1)}, bf16[128,512]{1,0:T(8,128)(2,1)S(1)}, u32[]{:S(2)}, u32[]{:S(2)}) collective-permute-start(bf16[128,512]{1,0:T(8,128)(2,1)S(1)} %get-tuple-element.44), channel_id=1, source_target_pairs={{6,0},{4,2},{2,4},{0,6},{7,1},{5,3},{3,5},{1,7},{14,8},{12,10},{10... | collective-permute-start | bytes 393224 | tf_op jit(solution)/shard_map/ppermute | solution.py:715
  30.2 0.0 slice-start.1
  30.2 7.8 %turn_stage.1 = (bf16[128,1792]{1,0:T(8,128)(2,1)S(1)}, f32[128,1792]{1,0:T(8,128)S(1)}, f32[128,3584]{1,0:T(8,128)S(1)}) custom-call(s32[1]{0:T(128)} %bitcast.refs_0_.rank_ref, s32[1,128]{1,0:T(1,128)S(1)} %bitcast.12, bf16[2,1024,3584]{2,1,0:T(8,128)(2,1)S(1)} %bitcast.7, bf16[128,1024]{1,0:T(8,128)(2,1)S(1)} %get-tuple-element.36.refs_3_, ...), custom_call_target="tpu_custom_call" | custom-call | flops 10000000000 | bytes 20000000 | tf_op jit(solution)/shard_map/turn_stage/pallas_call | solution.py:477
  38.1 0.2 collective-permute-done.5.refs_8_.arrived_ref
  38.3 0.0 collective-permute-start.10
  38.3 0.9 %collective-permute-done.6.refs_9_ = bf16[128,512]{1,0:T(8,128)(2,1)S(1)} collective-permute-done((bf16[128,512]{1,0:T(8,128)(2,1)S(1)}, bf16[128,512]{1,0:T(8,128)(2,1)S(1)}, u32[]{:S(2)}, u32[]{:S(2)}) %collective-permute-start.6) | collective-permute-done | bytes 131104 | tf_op jit(solution)/shard_map/ppermute | solution.py:715
  39.2 0.0 collective-permute-done.7.refs_10_
  39.2 0.0 slice-done
  39.2 0.0 slice-done.1
  39.2 1.5 %key_back_stage.1 = (bf16[128,1792]{1,0:T(8,128)(2,1)S(1)}, bf16[128,512]{1,0:T(8,128)(2,1)S(1)}, f32[1,128]{1,0:T(1,128)S(1)}) custom-call(s32[1]{0:T(128)} %bitcast.refs_0_.rank_ref, s32[1,128]{1,0:T(1,128)S(1)} %bitcast.13, f32[2,2,128]{2,1,0:T(2,128)S(1)} %copy-done.3, f32[128,512]{1,0:T(8,128)S(1)} %get-tuple-element.39.refs_3_, ...), custom_call_target="tpu_custom_call" | custom-call | flops 2000000000 | bytes 4000000 | tf_op jit(solution)/shard_map/key_back_stage/pallas_call | solution.py:539
  40.7 0.0 copy-start.1
  40.7 0.1 collective-permute-start.8
  40.8 0.5 %collective-permute-start.9 = (f32[1,128]{1,0:T(1,128)S(1)}, f32[1,128]{1,0:T(1,128)S(1)}, u32[]{:S(2)}, u32[]{:S(2)}) collective-permute-start(f32[1,128]{1,0:T(1,128)S(1)} %get-tuple-element.47.refs_7_), channel_id=1, source_target_pairs={{0,1},{1,0},{2,3},{3,2},{4,5},{5,4},{6,7},{7,6},{8,9},{9,8},{10,11... | collective-permute-start | bytes 1544 | tf_op jit(solution)/shard_map/ppermute | solution.py:748
  41.3 1.1 %kept_stage.1.refs_5_ = f32[128,1792]{1,0:T(8,128)S(1)} custom-call(s32[1]{0:T(128)} %bitcast.refs_0_.rank_ref, s32[1,128]{1,0:T(1,128)S(1)} %bitcast.14, f32[128,3584]{1,0:T(8,128)S(1)} %get-tuple-element.38.refs_5_.part_ref, bf16[2,3584,512]{2,1,0:T(8,128)(2,1)S(1)} %bitcast.5, bf16[128,512]{1,0:T(8,128)(2,1)S(1)} %get-tuple-element.45.back_ref), custom_call_target="tpu_custom_call" | custom-call | flops 2000000000 | bytes 4000000 | tf_op jit(solution)/shard_map/kept_stage/pallas_call | solution.py:564
  42.5 0.2 collective-permute-done.9.refs_8_
  42.6 0.0 collective-permute-done.10.refs_10_
  42.6 0.0 collective-permute-done.8.refs_6_
  42.6 0.0 copy-done.1
  42.6 1.5 %finish.1 = (bf16[128,1792]{1,0:T(8,128)(2,1)}, bf16[128,1792]{1,0:T(8,128)(2,1)}) custom-call(s32[1]{0:T(128)} %bitcast.refs_0_.rank_ref, s32[1,128]{1,0:T(1,128)S(1)} %bitcast.15, f32[2,3584]{1,0:T(2,128)S(1)} %copy-done.2, f32[1,128]{1,0:T(1,128)S(1)} %get-tuple-element.30.refs_4_.refs_3_, bf16[128,1792]{1,0:T(8,128)(2,1)S(1)} %copy-done.1, ...), custom_call_target="tpu_custom_call" | custom-call | flops 1000000000 | bytes 2000000 | tf_op jit(solution)/shard_map/finish/pallas_call | solution.py:625
  (3 shorter events, 0.0 us)
Async XLA Ops:
  0.6 5.0 %copy-start.4 = (s32[128]{0:T(128)S(1)}, s32[128]{0:T(128)}, u32[]{:S(2)}) copy-start(s32[128]{0:T(128)} %param.17) | copy-start | bytes 1540
  0.6 5.0 %copy-start.2 = (f32[2,3584]{1,0:T(2,128)S(1)}, f32[2,3584]{1,0:T(2,128)}, u32[]{:S(2)}) copy-start(f32[2,3584]{1,0:T(2,128)} %refs_2_.9) | copy-start | bytes 86020
  0.7 5.0 %copy-start.3 = (f32[2,2,128]{2,1,0:T(2,128)S(1)}, f32[2,2,128]{2,1,0:T(2,128)}, u32[]{:S(2)}) copy-start(f32[2,2,128]{2,1,0:T(2,128)} %refs_2_.8) | copy-start | bytes 6148
  0.7 5.0 %collective-permute-start = (bf16[128,1792]{1,0:T(8,128)(2,1)}, bf16[128,1792]{1,0:T(8,128)(2,1)S(1)}, u32[]{:S(2)}, u32[]{:S(2)}) collective-permute-start(bf16[128,1792]{1,0:T(8,128)(2,1)} %refs_4_.5), channel_id=1, source_target_pairs={{0,1},{1,0},{2,3},{3,2},{4,5},{5,4},{6,7},{7,6},{8,9},{9,8},{10,11... | collective-permute-start | bytes 1376264 | tf_op jit(solution)/shard_map/ppermute | solution.py:671
  1.2 11.2 %collective-permute-start.1 = (bf16[128,1792]{1,0:T(8,128)(2,1)}, bf16[128,1792]{1,0:T(8,128)(2,1)S(1)}, u32[]{:S(2)}, u32[]{:S(2)}) collective-permute-start(bf16[128,1792]{1,0:T(8,128)(2,1)} %refs_7_.1), channel_id=1, source_target_pairs={{0,1},{1,0},{2,3},{3,2},{4,5},{5,4},{6,7},{7,6},{8,9},{9,8},{10,11... | collective-permute-start | bytes 1376264 | tf_op jit(solution)/shard_map/ppermute | solution.py:664
  1.3 11.1 %slice-start.2 = ((s8[14680064]{0:T(1024)(128)(4,1)}), s8[4194304]{0:T(1024)(128)(4,1)S(1)}, s32[]{:S(2)}) async-start(s8[14680064]{0:T(1024)(128)(4,1)} %bitcast.6), calls=%async_computation.2 | async-start | bytes 8388608
  5.7 6.7 %slice-start.3 = ((s8[14680064]{0:T(1024)(128)(4,1)}), s8[4194304]{0:T(1024)(128)(4,1)S(1)}, s32[]{:S(2)}) async-start(s8[14680064]{0:T(1024)(128)(4,1)} %bitcast.6), calls=%async_computation.3 | async-start | bytes 8388608
  5.7 6.7 %slice-start.4 = ((s8[14680064]{0:T(1024)(128)(4,1)}), s8[4194304]{0:T(1024)(128)(4,1)S(1)}, s32[]{:S(2)}) async-start(s8[14680064]{0:T(1024)(128)(4,1)} %bitcast.6), calls=%async_computation.4 | async-start | bytes 8388608
  5.7 6.7 %slice-start.5 = ((s8[14680064]{0:T(1024)(128)(4,1)}), s8[2097152]{0:T(1024)(128)(4,1)S(1)}, s32[]{:S(2)}) async-start(s8[14680064]{0:T(1024)(128)(4,1)} %bitcast.6), calls=%async_computation.5 | async-start | bytes 4194304
  5.7 6.7 %copy-start = (bf16[128,1792]{1,0:T(8,128)(2,1)S(1)}, bf16[128,1792]{1,0:T(8,128)(2,1)}, u32[]{:S(2)}) copy-start(bf16[128,1792]{1,0:T(8,128)(2,1)} %refs_7_.1) | copy-start | bytes 1376260
  6.7 13.9 %collective-permute-start.2 = (bf16[128,512]{1,0:T(8,128)(2,1)S(1)}, bf16[128,512]{1,0:T(8,128)(2,1)S(1)}, u32[]{:S(2)}, u32[]{:S(2)}) collective-permute-start(bf16[128,512]{1,0:T(8,128)(2,1)S(1)} %get-tuple-element.35.refs_8_), channel_id=1, source_target_pairs={{0,4},{2,6},{4,0},{6,2},{1,5},{3,7},{5,1},{7,3},{8,12},{10,14},{12... | collective-permute-start | bytes 393224 | tf_op jit(solution)/shard_map/ppermute | solution.py:691
  10.8 9.8 %collective-permute-start.3 = (bf16[128,512]{1,0:T(8,128)(2,1)S(1)}, bf16[128,512]{1,0:T(8,128)(2,1)S(1)}, u32[]{:S(2)}, u32[]{:S(2)}) collective-permute-start(bf16[128,512]{1,0:T(8,128)(2,1)S(1)} %get-tuple-element.35.refs_8_), channel_id=1, source_target_pairs={{0,2},{2,0},{4,6},{6,4},{1,3},{3,1},{5,7},{7,5},{8,10},{10,8},{12,... | collective-permute-start | bytes 393224 | tf_op jit(solution)/shard_map/ppermute | solution.py:691
  12.4 9.0 %collective-permute-start.4 = (bf16[128,512]{1,0:T(8,128)(2,1)S(1)}, bf16[128,512]{1,0:T(8,128)(2,1)S(1)}, u32[]{:S(2)}, u32[]{:S(2)}) collective-permute-start(bf16[128,512]{1,0:T(8,128)(2,1)S(1)} %get-tuple-element.35.refs_8_), channel_id=1, source_target_pairs={{0,6},{2,4},{4,2},{6,0},{1,7},{3,5},{5,3},{7,1},{8,14},{10,12},{12... | collective-permute-start | bytes 393224 | tf_op jit(solution)/shard_map/ppermute | solution.py:691
  12.4 8.9 %copy-start.5 = (s32[512]{0:T(512)S(1)}, s32[512]{0:T(512)}, u32[]{:S(2)}) copy-start(s32[512]{0:T(512)} %param.18) | copy-start | bytes 6148
  12.4 8.9 %copy-start.6 = (s32[4]{0:T(128)S(1)}, s32[4]{0:T(128)}, u32[]{:S(2)}) copy-start(s32[4]{0:T(128)} %refs_1_.3) | copy-start | bytes 52
  21.4 17.9 %slice-start = ((s8[7340032]{0:T(1024)(128)(4,1)}), s8[4194304]{0:T(1024)(128)(4,1)S(1)}, s32[]{:S(2)}) async-start(s8[7340032]{0:T(1024)(128)(4,1)} %bitcast.4), calls=%async_computation | async-start | bytes 8388608
  24.4 13.9 %collective-permute-start.5 = (bf16[128,512]{1,0:T(8,128)(2,1)S(1)}, bf16[128,512]{1,0:T(8,128)(2,1)S(1)}, u32[]{:S(2)}, u32[]{:S(2)}) collective-permute-start(bf16[128,512]{1,0:T(8,128)(2,1)S(1)} %get-tuple-element.42), channel_id=1, source_target_pairs={{4,0},{6,2},{0,4},{2,6},{5,1},{7,3},{1,5},{3,7},{12,8},{14,10},{8,... | collective-permute-start | bytes 393224 | tf_op jit(solution)/shard_map/ppermute | solution.py:715
  28.7 10.5 %collective-permute-start.6 = (bf16[128,512]{1,0:T(8,128)(2,1)S(1)}, bf16[128,512]{1,0:T(8,128)(2,1)S(1)}, u32[]{:S(2)}, u32[]{:S(2)}) collective-permute-start(bf16[128,512]{1,0:T(8,128)(2,1)S(1)} %get-tuple-element.43), channel_id=1, source_target_pairs={{2,0},{0,2},{6,4},{4,6},{3,1},{1,3},{7,5},{5,7},{10,8},{8,10},{14,... | collective-permute-start | bytes 393224 | tf_op jit(solution)/shard_map/ppermute | solution.py:715
  28.7 10.5 %collective-permute-start.7 = (bf16[128,512]{1,0:T(8,128)(2,1)S(1)}, bf16[128,512]{1,0:T(8,128)(2,1)S(1)}, u32[]{:S(2)}, u32[]{:S(2)}) collective-permute-start(bf16[128,512]{1,0:T(8,128)(2,1)S(1)} %get-tuple-element.44), channel_id=1, source_target_pairs={{6,0},{4,2},{2,4},{0,6},{7,1},{5,3},{3,5},{1,7},{14,8},{12,10},{10... | collective-permute-start | bytes 393224 | tf_op jit(solution)/shard_map/ppermute | solution.py:715
  30.2 9.0 %slice-start.1 = ((s8[7340032]{0:T(1024)(128)(4,1)}), s8[3145728]{0:T(1024)(128)(4,1)S(1)}, s32[]{:S(2)}) async-start(s8[7340032]{0:T(1024)(128)(4,1)} %bitcast.4), calls=%async_computation.1 | async-start | bytes 6291456
  38.3 4.3 %collective-permute-start.10 = (bf16[128,1792]{1,0:T(8,128)(2,1)S(1)}, bf16[128,1792]{1,0:T(8,128)(2,1)S(1)}, u32[]{:S(2)}, u32[]{:S(2)}) collective-permute-start(bf16[128,1792]{1,0:T(8,128)(2,1)S(1)} %tie.1), channel_id=1, source_target_pairs={{0,1},{1,0},{2,3},{3,2},{4,5},{5,4},{6,7},{7,6},{8,9},{9,8},{10,11... | collective-permute-start | bytes 1376264 | tf_op jit(solution)/shard_map/ppermute | solution.py:724
  40.7 1.9 %copy-start.1 = (bf16[128,1792]{1,0:T(8,128)(2,1)S(1)}, bf16[128,1792]{1,0:T(8,128)(2,1)}, u32[]{:S(2)}) copy-start(bf16[128,1792]{1,0:T(8,128)(2,1)} %refs_4_.5) | copy-start | bytes 1376260
  40.7 1.9 %collective-permute-start.8 = (bf16[128,1792]{1,0:T(8,128)(2,1)S(1)}, bf16[128,1792]{1,0:T(8,128)(2,1)S(1)}, u32[]{:S(2)}, u32[]{:S(2)}) collective-permute-start(bf16[128,1792]{1,0:T(8,128)(2,1)S(1)} %get-tuple-element.46), channel_id=1, source_target_pairs={{0,1},{1,0},{2,3},{3,2},{4,5},{5,4},{6,7},{7,6},{8,9},{9,8},{10,11... | collective-permute-start | bytes 1376264 | tf_op jit(solution)/shard_map/ppermute | solution.py:749
  40.8 1.8 %collective-permute-start.9 = (f32[1,128]{1,0:T(1,128)S(1)}, f32[1,128]{1,0:T(1,128)S(1)}, u32[]{:S(2)}, u32[]{:S(2)}) collective-permute-start(f32[1,128]{1,0:T(1,128)S(1)} %get-tuple-element.47.refs_7_), channel_id=1, source_target_pairs={{0,1},{1,0},{2,3},{3,2},{4,5},{5,4},{6,7},{7,6},{8,9},{9,8},{10,11... | collective-permute-start | bytes 1544 | tf_op jit(solution)/shard_map/ppermute | solution.py:748

commit v11 on v8

--- a/solution.py
+++ b/solution.py
@@ -178,6 +178,10 @@
         cost_estimate=cost(0.2),
         name="fetch",
     )(streamed(weights))
+
+
+def gain_of(image, gain_ref, columns):
+    return jnp.where(image, gain_ref[1:2, columns], gain_ref[0:1, columns])
 
 
 def key_kernel(count, *refs):
@@ -282,11 +286,10 @@
 
 
 def attention_kernel(blocks, pairs, per_group, *refs):
-    place_ref, order_ref, segments_ref, modality_ref, head_ref = refs[:5]
-    query_ref, raw_ref, back_ref = refs[5:8]
-    memory_refs = refs[8 : 8 + blocks]
-    attended_ref, query_back_ref, inner_ref = refs[8 + blocks : 11 + blocks]
-    grad_refs = refs[11 + blocks :]
+    place_ref, order_ref, segments_ref, query_ref, back_ref = refs[:5]
+    memory_refs = refs[5 : 5 + blocks]
+    attended_ref, upstream_ref = refs[5 + blocks : 7 + blocks]
+    grad_refs = refs[7 + blocks :]
     rows = query_ref.shape[0]
     scale = 1.0 / math.sqrt(HEAD_DIM)
     lines = [
@@ -295,9 +298,6 @@
     ]
     key_segments = jnp.concatenate(lines, axis=1).astype(f32)
     visible = key_segments <= column(lines[0])
-    image = column(modality_ref[...]) > 0.0
-    scaling = jnp.where(image, head_ref[1, 0:1, :], head_ref[0, 0:1, :])
-    inner = jnp.zeros((rows, 1), f32)
     for pair in range(pairs):
         columns = [
             slice(h * HEAD_DIM, (h + 1) * HEAD_DIM)
@@ -331,22 +331,17 @@
             grad_ref[:, values] = back_value[part].astype(grad_ref.dtype)
         for part, place in zip(parts, columns):
             attended_ref[:, place] = attended[part]
-            raw = raw_ref[:, place]
-            query_back = norm_back(raw, inverse_norm(raw), scaling, back_query[part]).astype(bf16)
-            query_back_ref[:, place] = query_back
-            inner += jnp.sum(query_back.astype(f32) * raw, axis=1, keepdims=True)
-    inner_ref[...] = row_of(inner)
-
-
-def attention_stage(place, order, segments, modality, head_gain, query, raw, back, memories):
+            upstream_ref[:, place] = back_query[part]
+
+
+def attention_stage(place, order, segments, query, back, memories):
     rows, width = query.shape
     blocks = len(memories)
     pairs = memories[0].shape[1] // (2 * HEAD_DIM)
     per_group = width // HEAD_DIM // pairs
     outs = [
         jax.ShapeDtypeStruct((rows, width), bf16),
-        jax.ShapeDtypeStruct((rows, width), bf16),
-        jax.ShapeDtypeStruct((1, rows), f32),
+        jax.ShapeDtypeStruct((rows, width), f32),
     ] + [
         jax.ShapeDtypeStruct((rows, pairs * 2 * HEAD_DIM), f32 if b == 0 else bf16)
         for b in range(blocks)
@@ -354,21 +349,31 @@
     return pl.pallas_call(
         functools.partial(attention_kernel, blocks, pairs, per_group),
         out_shape=outs,
-        in_specs=[SMEM, SMEM] + [VMEM] * (6 + blocks),
-        out_specs=[VMEM] * (3 + blocks),
+        in_specs=[SMEM, SMEM] + [VMEM] * (3 + blocks),
+        out_specs=[VMEM] * (2 + blocks),
         compiler_params=params(12),
         cost_estimate=cost(4),
         name="attention_stage",
-    )(place, order, segments, modality, head_gain, query, raw, back, *memories)
+    )(place, order, segments, query, back, *memories)
 
 
 def turn_kernel(pieces, outputs, *refs):
-    rank_ref, modality_ref, output_ref, attended_ref, back_ref, query_ref = refs[:6]
-    out_refs = refs[6 : 6 + outputs]
-    part_ref, slots, sems = refs[6 + outputs :]
+    rank_ref, modality_ref, head_ref, output_ref, attended_ref = refs[:5]
+    upstream_ref, raw_ref, query_ref = refs[5:8]
+    out_refs = refs[8 : 8 + outputs]
+    part_ref, inner_ref, back_ref, slots, sems = refs[8 + outputs :]
     copies = copies_of(query_ref, slots, sems, pieces, slots=AHEAD)
     begin_first(copies)
     image = column(modality_ref[...]) > 0.0
+    scaling = jnp.where(image, head_ref[1, 0:1, :], head_ref[0, 0:1, :])
+    inner = jnp.zeros((raw_ref.shape[0], 1), f32)
+    for start, size in chunks_of(raw_ref.shape[1], HEAD_DIM):
+        part = slice(start, start + size)
+        raw = raw_ref[:, part]
+        back = norm_back(raw, inverse_norm(raw), scaling, upstream_ref[:, part]).astype(bf16)
+        back_ref[:, part] = back
+        inner += jnp.sum(back.astype(f32) * raw, axis=1, keepdims=True)
+    inner_ref[...] = row_of(inner)
     attended = attended_ref[...]
     extent = output_ref.shape[2] // 2
 
@@ -397,7 +402,9 @@
         begin(copies, index + AHEAD)
 
 
-def turn_stage(rank, modality, output_weight, attended, query_back, query_weight, split):
+def turn_stage(
+    rank, modality, head_gain, output_weight, attended, upstream, raw, query_weight, split
+):
     depth = query_weight.shape[1]
     width = output_weight.shape[2]
     rows = attended.shape[0]
@@ -409,20 +416,22 @@
         ]
     else:
         outs = [jax.ShapeDtypeStruct((rows, width), bf16)]
-    *projected, part = pl.pallas_call(
+    *projected, part, inner = pl.pallas_call(
         functools.partial(turn_kernel, pieces, len(outs)),
-        out_shape=outs + [jax.ShapeDtypeStruct((rows, depth), f32)],
-        in_specs=[SMEM, VMEM, VMEM, VMEM, VMEM, ANY],
-        out_specs=[VMEM] * (len(outs) + 1),
+        out_shape=outs
+        + [jax.ShapeDtypeStruct((rows, depth), f32), jax.ShapeDtypeStruct((1, rows), f32)],
+        in_specs=[SMEM] + [VMEM] * 6 + [ANY],
+        out_specs=[VMEM] * (len(outs) + 2),
         scratch_shapes=[
+            pltpu.VMEM(attended.shape, bf16),
             ring(query_weight, pieces),
             pltpu.SemaphoreType.DMA((len(pieces), 2)),
         ],
         compiler_params=params(16),
         cost_estimate=cost(10),
         name="turn_stage",
-    )(rank, modality, output_weight, attended, query_back, streamed(query_weight))
-    return projected, part
+    )(rank, modality, head_gain, output_weight, attended, upstream, raw, streamed(query_weight))
+    return projected, part, inner
 
 
 def tie(passed, arrived):
@@ -439,22 +448,6 @@
         cost_estimate=cost(0.1),
         name="tie",
     )(passed, arrived)
-
-
-def merge_kernel(kept_ref, other_ref, out_ref):
-    out_ref[...] = (kept_ref[...] + other_ref[...].astype(f32)).astype(bf16)
-
-
-def merge(kept, other):
-    return pl.pallas_call(
-        merge_kernel,
-        out_shape=jax.ShapeDtypeStruct(other.shape, bf16),
-        in_specs=[VMEM, VMEM],
-        out_specs=VMEM,
-        compiler_params=params(4),
-        cost_estimate=cost(0.5),
-        name="merge",
-    )(kept, other)
 
 
 def key_back_kernel(split, *refs):
@@ -527,32 +520,59 @@
     rank_ref, modality_ref, gain_ref, factor_ref, inputs_ref = refs[:5]
     back_refs = refs[5 : 5 + backs]
     inner_refs = refs[5 + backs : 5 + backs + inners]
-    out_ref = refs[-1]
+    rest = refs[5 + backs + inners :]
     width = inputs_ref.shape[1]
+    copies = []
+
+    def send(staged_ref, out_ref, sem, part):
+        copy = pltpu.make_async_copy(staged_ref.at[:, part], out_ref.at[:, part], sem)
+        copy.start()
+        copies.append(copy)
+
+    pieces = [slice(start, start + size) for start, size in chunks_of(width, 896)]
+    if len(rest) == 7:
+        kept_ref, other_ref, attention_ref, out_ref, staged, staged_attention, sems = rest
+        for index, part in enumerate(pieces):
+            whole = kept_ref[:, part] + other_ref[:, part].astype(f32)
+            staged_attention[:, part] = whole.astype(bf16)
+            send(staged_attention, attention_ref, sems.at[1, index], part)
+    else:
+        out_ref, staged, sems = rest
     image = column(modality_ref[...]) > 0.0
-    gain = gain_ref[...]
-    if gain.shape[1] != width:
-        gain = gain_ref[:, pl.ds(pl.multiple_of(rank_ref[0] * width, HEAD_DIM), width)]
-    scaling = jnp.where(image, gain[1:2, :], gain[0:1, :])
     factor = column(factor_ref[...])
-    back = back_refs[0][...].astype(f32)
-    for ref in back_refs[1:]:
-        back += ref[...].astype(f32)
     inner = inner_refs[0][...]
     for ref in inner_refs[1:]:
         inner += ref[...]
-    unit_rows = inputs_ref[...].astype(f32) * factor
-    inner_mean = column(inner) * (1.0 / total_width)
-    out_ref[...] = (factor * (scaling * back - unit_rows * inner_mean)).astype(bf16)
-
-
-def finish(rank, total_width, modality, gain, factor, inputs, backs, inners):
-    arrays = [modality, gain, factor, inputs, *backs, *inners]
+    inner_mean = factor * column(inner) * (1.0 / total_width)
+    gathered = gain_ref.shape[1] != width
+    for index, part in enumerate(pieces):
+        columns = part
+        if gathered:
+            first = pl.multiple_of(rank_ref[0] * width, HEAD_DIM) + part.start
+            columns = pl.ds(first, part.stop - part.start)
+        back = back_refs[0][:, part].astype(f32)
+        for ref in back_refs[1:]:
+            back += ref[:, part].astype(f32)
+        rows = inputs_ref[:, part].astype(f32)
+        result = factor * (gain_of(image, gain_ref, columns) * back - rows * inner_mean)
+        staged[:, part] = result.astype(bf16)
+        send(staged, out_ref, sems.at[0, index], part)
+    for copy in copies:
+        copy.wait()
+
+
+def finish(rank, total_width, modality, gain, factor, inputs, backs, inners, projected):
+    shape = jax.ShapeDtypeStruct(inputs.shape, bf16)
+    arrays = [modality, gain, factor, inputs, *backs, *inners, *projected]
+    count = 2 if projected else 1
+    pieces = len(chunks_of(inputs.shape[1], 896))
     return pl.pallas_call(
         functools.partial(finish_kernel, len(backs), len(inners), total_width),
-        out_shape=jax.ShapeDtypeStruct(inputs.shape, bf16),
+        out_shape=[shape] * count,
         in_specs=[SMEM] + [VMEM] * len(arrays),
-        out_specs=VMEM,
+        out_specs=[ANY] * count,
+        scratch_shapes=[pltpu.VMEM(inputs.shape, bf16)] * count
+        + [pltpu.SemaphoreType.DMA((count, pieces))],
         compiler_params=params(6),
         cost_estimate=cost(1),
         name="finish",
@@ -611,14 +631,11 @@
     query, query_raw, back_attended = middle_stage(
         rank, modality, head_gain, normed, output_weight, query_weight, spread(cotangent)
     )
-    attended, query_back, inner, own_grad, *grads = attention_stage(
+    attended, upstream, own_grad, *grads = attention_stage(
         block_rank.astype(jnp.int32).reshape(1),
         block_order,
         segments,
-        modality,
-        head_gain,
         query,
-        query_raw,
         back_attended,
         memories,
     )
@@ -627,14 +644,23 @@
         for step, grad in zip(seq_steps(block_count), grads)
     ]
 
-    projected, gradient_part = turn_stage(
-        rank, modality, output_weight, attended, query_back, query_weight, split
+    projected, gradient_part, inner = turn_stage(
+        rank,
+        modality,
+        head_gain,
+        output_weight,
+        attended,
+        upstream,
+        query_raw,
+        query_weight,
+        split,
     )
     if split:
         passed = tie(projected[0], incoming[0])
-        attention_out = merge(projected[1], lax.ppermute(passed, "tensor", swap))
+        projected = [projected[1], lax.ppermute(passed, "tensor", swap)]
     else:
         attention_out = scatter_columns(projected[0])
+        projected = []
 
     if shared:
         total = own_grad + sum(grad.astype(f32) for grad in incoming)
@@ -664,8 +690,12 @@
         inners = [lax.psum(inner, "tensor")]
         backs = [scatter_columns(sent)]
         gain = lax.dynamic_slice_in_dim(norm_gain, tensor_rank * local_width, local_width, 1)
-    grad_input = finish(rank, full_width, modality, gain, row_factor, inputs, backs, inners)
-    return (attention_out, grad_input)
+    results = finish(
+        rank, full_width, modality, gain, row_factor, inputs, backs, inners, projected
+    )
+    if split:
+        attention_out = results[0]
+    return (attention_out, results[-1])
 
 
 def solution(mesh):

time: 44.3 us -> 43.8 us (0.989)
  waiting for transfers between devices: 1.81 us -> 1.15 us
    pallas_call x1 -> x0, Pallas kernels: 0.87 us -> none  [merge(): pl.pallas_call(merge_kernel, out_shape=jax.ShapeDtypeStruct(other.shape,...]
    ppermute x3, waiting for transfers between devices: 1.14 us -> 0.31 us  [local(): lax.ppermute(grad, 'seq', inverted(seq_pairs(step, block_count)))]
    pallas_call x1, Pallas kernels: 7.82 us -> 8.55 us  [turn_stage(): pl.pallas_call(functools.partial(turn_kernel, pieces, len(outs)), out_sha...]
  transfers between devices with their start and end apart: 11 -> 11, of which waited for: 3 -> 3; matrix products, arithmetic and copies ran while one was open for 0% -> 0% of each run, Pallas kernels for 55% -> 56%
where the time goes in v11:
time: 43.8 us; the launch traced here: 43.6 us
  Pallas kernels  28.6 us (65%)
  starting transfers between devices  12.7 us (29%)
  waiting for transfers between devices  1.15 us (3%)
  between operations  1.05 us (2%)
    pallas_call x1, Pallas kernels, turn_stage(): pl.pallas_call(functools.partial(turn_kernel, pieces, len(outs)), out_sha...  8.55 us
    pallas_call x1, Pallas kernels, middle_stage(): pl.pallas_call(functools.partial(middle_kernel, len(parts), pieces), out_...  8.23 us
    ppermute x3, starting transfers between devices, local(): lax.ppermute(grad, 'seq', inverted(seq_pairs(step, block_count)))  5.84 us
    ppermute x3, starting transfers between devices, local(): memories.append(lax.ppermute(memory, 'seq', seq_pairs(step, block_count)))  5.66 us
    pallas_call x1, Pallas kernels, fetch(): pl.pallas_call(functools.partial(fetch_kernel, pieces), out_shape=residen...  3.32 us
    pallas_call x1, Pallas kernels, attention_stage(): pl.pallas_call(functools.partial(attention_kernel, blocks, pairs, per_gro...  2.87 us
    pallas_call x1, Pallas kernels, key_stage(): pl.pallas_call(functools.partial(key_kernel, len(parts)), out_shape=[jax....  1.57 us
    pallas_call x1, Pallas kernels, key_back_stage(): pl.pallas_call(functools.partial(key_back_kernel, split), out_shape=[jax....  1.48 us
  transfers between devices with their start and end apart: 11, of which 3 were waited for; matrix products, arithmetic and copies ran while one was open for 0% of the time, Pallas kernels for 56%

profile of v11, /device:TPU:0, one launch (start us, length us, event | category | flops | bytes accessed | tf_op | source)
XLA Modules:
  0.0 43.6 jit_solution(15112149035441559413)
XLA Ops:
  0.6 0.5 %collective-permute-start = (bf16[128,1792]{1,0:T(8,128)(2,1)}, bf16[128,1792]{1,0:T(8,128)(2,1)S(1)}, u32[]{:S(2)}, u32[]{:S(2)}) collective-permute-start(bf16[128,1792]{1,0:T(8,128)(2,1)} %refs_4_.3), channel_id=1, source_target_pairs={{0,1},{1,0},{2,3},{3,2},{4,5},{5,4},{6,7},{7,6},{8,9},{9,8},{10,11... | collective-permute-start | bytes 1376264 | tf_op jit(solution)/shard_map/ppermute | solution.py:608
  1.1 0.1 collective-permute-start.1
  1.2 0.0 copy-start.1
  1.2 0.0 copy-start.2
  1.2 0.0 copy-start.3
  1.2 0.0 copy-start.4
  1.2 0.0 slice-start.2
  1.3 0.0 slice-start.3
  1.3 3.3 %fetch.1.refs_4_ = bf16[2,3584,512]{2,1,0:T(8,128)(2,1)S(1)} custom-call(bf16[2,3584,512]{2,1,0:T(8,128)(2,1)} %weight_ref.3), custom_call_target="tpu_custom_call" | custom-call | flops 200000000 | bytes 400000 | tf_op jit(solution)/shard_map/fetch/pallas_call | solution.py:171
  4.6 0.0 collective-permute-done.refs_6_
  4.6 0.0 copy-done.1
  4.6 0.0 copy-done.2
  4.6 0.0 copy-done.3
  4.6 0.0 copy-done.4
  4.6 0.0 slice-start.4
  4.7 0.0 slice-start.5
  4.7 0.0 copy-start
  4.7 1.6 %key_stage.1 = (bf16[128,512]{1,0:T(8,128)(2,1)S(1)}, f32[128,512]{1,0:T(8,128)S(1)}, bf16[128,3584]{1,0:T(8,128)(2,1)S(1)}, f32[1,128]{1,0:T(1,128)S(1)}) custom-call(s32[1]{0:T(128)} %bitcast.refs_0_.rank_ref, s32[1,128]{1,0:T(1,128)S(1)} %bitcast.8, f32[2,3584]{1,0:T(2,128)S(1)} %copy-done.4, f32[2,2,128]{2,1,0:T(2,128)S(1)} %copy-done.1, ...), custom_call_target="tpu_custom_call" | custom-call | flops 10000000000 | bytes 20000000 | tf_op jit(solution)/shard_map/key_stage/pallas_call | solution.py:217
  6.2 4.1 %collective-permute-start.2 = (bf16[128,512]{1,0:T(8,128)(2,1)S(1)}, bf16[128,512]{1,0:T(8,128)(2,1)S(1)}, u32[]{:S(2)}, u32[]{:S(2)}) collective-permute-start(bf16[128,512]{1,0:T(8,128)(2,1)S(1)} %get-tuple-element.26.refs_5_), channel_id=1, source_target_pairs={{0,4},{2,6},{4,0},{6,2},{1,5},{3,7},{5,1},{7,3},{8,12},{10,14},{12... | collective-permute-start | bytes 393224 | tf_op jit(solution)/shard_map/ppermute | solution.py:629
  10.3 1.6 %collective-permute-start.3 = (bf16[128,512]{1,0:T(8,128)(2,1)S(1)}, bf16[128,512]{1,0:T(8,128)(2,1)S(1)}, u32[]{:S(2)}, u32[]{:S(2)}) collective-permute-start(bf16[128,512]{1,0:T(8,128)(2,1)S(1)} %get-tuple-element.26.refs_5_), channel_id=1, source_target_pairs={{0,2},{2,0},{4,6},{6,4},{1,3},{3,1},{5,7},{7,5},{8,10},{10,8},{12,... | collective-permute-start | bytes 393224 | tf_op jit(solution)/shard_map/ppermute | solution.py:629
  11.9 0.0 collective-permute-start.4
  11.9 0.0 collective-permute-done.1.refs_7_
  11.9 0.0 slice-done.2
  11.9 0.0 slice-done.3
  11.9 0.0 slice-done.4
  11.9 0.0 slice-done.5
  11.9 0.0 copy-done
  12.0 0.0 copy-start.5
  12.0 0.0 copy-start.6
  12.0 8.2 %middle_stage.1 = (bf16[128,1024]{1,0:T(8,128)(2,1)S(1)}, f32[128,1024]{1,0:T(8,128)S(1)}, bf16[128,1024]{1,0:T(8,128)(2,1)S(1)}) custom-call(s32[1]{0:T(128)} %bitcast.refs_0_.rank_ref, s32[1,128]{1,0:T(1,128)S(1)} %bitcast.9, f32[2,2,128]{2,1,0:T(2,128)S(1)} %copy-done.1, bf16[128,3584]{1,0:T(8,128)(2,1)S(1)} %get-tuple-element.23.refs_3_, ...), custom_call_target="tpu_custom_call" | custom-call | flops 8000000000 | bytes 16000000 | tf_op jit(solution)/shard_map/middle_stage/pallas_call | solution.py:269
  20.2 0.0 collective-permute-done.2.refs_6_
  20.2 0.0 collective-permute-done.3.refs_7_
  20.3 0.6 %collective-permute-done.4.refs_8_ = bf16[128,512]{1,0:T(8,128)(2,1)S(1)} collective-permute-done((bf16[128,512]{1,0:T(8,128)(2,1)S(1)}, bf16[128,512]{1,0:T(8,128)(2,1)S(1)}, u32[]{:S(2)}, u32[]{:S(2)}) %collective-permute-start.4) | collective-permute-done | bytes 131104 | tf_op jit(solution)/shard_map/ppermute | solution.py:629
  20.9 0.0 copy-done.5
  20.9 0.0 copy-done.6
  20.9 0.0 slice-start
  20.9 2.9 %attention_stage.1 = (bf16[128,1024]{1,0:T(8,128)(2,1)S(1)}, f32[128,1024]{1,0:T(8,128)S(1)}, f32[128,512]{1,0:T(8,128)S(1)}, bf16[128,512]{1,0:T(8,128)(2,1)S(1...) custom-call(s32[1]{0:T(128)} %bitcast.2.refs_0_, s32[4]{0:T(128)S(1)} %copy-done.6, s32[4,128]{1,0:T(4,128)S(1)} %bitcast.14, ...), custom_call_target="tpu_custom_call" | custom-call | flops 4000000000 | bytes 8000000 | tf_op jit(solution)/shard_map/attention_stage/pallas_call | solution.py:349
  23.8 4.3 %collective-permute-start.5 = (bf16[128,512]{1,0:T(8,128)(2,1)S(1)}, bf16[128,512]{1,0:T(8,128)(2,1)S(1)}, u32[]{:S(2)}, u32[]{:S(2)}) collective-permute-start(bf16[128,512]{1,0:T(8,128)(2,1)S(1)} %get-tuple-element.34), channel_id=1, source_target_pairs={{4,0},{6,2},{0,4},{2,6},{5,1},{7,3},{1,5},{3,7},{12,8},{14,10},{8,... | collective-permute-start | bytes 393224 | tf_op jit(solution)/shard_map/ppermute | solution.py:643
  28.1 0.0 collective-permute-start.6
  28.1 1.5 %collective-permute-start.7 = (bf16[128,512]{1,0:T(8,128)(2,1)S(1)}, bf16[128,512]{1,0:T(8,128)(2,1)S(1)}, u32[]{:S(2)}, u32[]{:S(2)}) collective-permute-start(bf16[128,512]{1,0:T(8,128)(2,1)S(1)} %get-tuple-element.36), channel_id=1, source_target_pairs={{6,0},{4,2},{2,4},{0,6},{7,1},{5,3},{3,5},{1,7},{14,8},{12,10},{10... | collective-permute-start | bytes 393224 | tf_op jit(solution)/shard_map/ppermute | solution.py:643
  29.6 0.0 slice-start.1
  29.6 8.6 %turn_stage.1 = (bf16[128,1792]{1,0:T(8,128)(2,1)S(1)}, f32[128,1792]{1,0:T(8,128)S(1)}, f32[128,3584]{1,0:T(8,128)S(1)}, f32[1,128]{1,0:T(1,128)S(1)}) custom-call(s32[1]{0:T(128)} %bitcast.refs_0_.rank_ref, s32[1,128]{1,0:T(1,128)S(1)} %bitcast.10, f32[2,2,128]{2,1,0:T(2,128)S(1)} %copy-done.1, bf16[2,1024,3584]{2,1,0:T(8,128)(2,1)S(1)} %bitcast.7, ...), custom_call_target="tpu_custom_call" | custom-call | flops 10000000000 | bytes 20000000 | tf_op jit(solution)/shard_map/turn_stage/pallas_call | solution.py:419
  38.2 0.0 collective-permute-done.5.refs_8_.arrived_ref
  38.2 0.1 collective-permute-start.10
  38.3 0.3 collective-permute-done.6.refs_9_
  38.6 0.0 collective-permute-done.7.refs_10_
  38.6 0.0 slice-done
  38.6 0.0 slice-done.1
  38.6 1.5 %key_back_stage.1 = (bf16[128,1792]{1,0:T(8,128)(2,1)S(1)}, bf16[128,512]{1,0:T(8,128)(2,1)S(1)}, f32[1,128]{1,0:T(1,128)S(1)}) custom-call(s32[1]{0:T(128)} %bitcast.refs_0_.rank_ref, s32[1,128]{1,0:T(1,128)S(1)} %bitcast.11, f32[2,2,128]{2,1,0:T(2,128)S(1)} %copy-done.1, f32[128,512]{1,0:T(8,128)S(1)} %get-tuple-element.31.refs_3_, ...), custom_call_target="tpu_custom_call" | custom-call | flops 2000000000 | bytes 4000000 | tf_op jit(solution)/shard_map/key_back_stage/pallas_call | solution.py:483
  40.1 0.3 collective-permute-start.8
  40.4 0.3 collective-permute-start.9
  40.7 1.1 %kept_stage.1.refs_5_ = f32[128,1792]{1,0:T(8,128)S(1)} custom-call(s32[1]{0:T(128)} %bitcast.refs_0_.rank_ref, s32[1,128]{1,0:T(1,128)S(1)} %bitcast.12, f32[128,3584]{1,0:T(8,128)S(1)} %get-tuple-element.30.refs_5_.part_ref, bf16[2,3584,512]{2,1,0:T(8,128)(2,1)S(1)} %bitcast.5, bf16[128,512]{1,0:T(8,128)(2,1)S(1)} %get-tuple-element.37.back_ref), custom_call_target="tpu_custom_call" | custom-call | flops 2000000000 | bytes 4000000 | tf_op jit(solution)/shard_map/kept_stage/pallas_call | solution.py:508
  41.8 0.2 collective-permute-done.9.refs_8_
  42.0 0.0 collective-permute-done.10.refs_10_
  42.0 0.0 collective-permute-done.8.refs_6_
  42.0 1.5 %finish.1 = (bf16[128,1792]{1,0:T(8,128)(2,1)}, bf16[128,1792]{1,0:T(8,128)(2,1)}) custom-call(s32[1]{0:T(128)} %bitcast.refs_0_.rank_ref, s32[1,128]{1,0:T(1,128)S(1)} %bitcast.13, f32[2,3584]{1,0:T(2,128)S(1)} %copy-done.4, f32[1,128]{1,0:T(1,128)S(1)} %get-tuple-element.22.refs_3_, bf16[128,1792]{1,0:T(8,128)(2,1)S(1)} %copy-done.3, ...), custom_call_target="tpu_custom_call" | custom-call | flops 1000000000 | bytes 2000000 | tf_op jit(solution)/shard_map/finish/pallas_call | solution.py:569
  (3 shorter events, 0.0 us)
Async XLA Ops:
  0.6 4.0 %collective-permute-start = (bf16[128,1792]{1,0:T(8,128)(2,1)}, bf16[128,1792]{1,0:T(8,128)(2,1)S(1)}, u32[]{:S(2)}, u32[]{:S(2)}) collective-permute-start(bf16[128,1792]{1,0:T(8,128)(2,1)} %refs_4_.3), channel_id=1, source_target_pairs={{0,1},{1,0},{2,3},{3,2},{4,5},{5,4},{6,7},{7,6},{8,9},{9,8},{10,11... | collective-permute-start | bytes 1376264 | tf_op jit(solution)/shard_map/ppermute | solution.py:608
  1.1 10.8 %collective-permute-start.1 = (bf16[128,1792]{1,0:T(8,128)(2,1)}, bf16[128,1792]{1,0:T(8,128)(2,1)S(1)}, u32[]{:S(2)}, u32[]{:S(2)}) collective-permute-start(bf16[128,1792]{1,0:T(8,128)(2,1)} %refs_6_.2), channel_id=1, source_target_pairs={{0,1},{1,0},{2,3},{3,2},{4,5},{5,4},{6,7},{7,6},{8,9},{9,8},{10,11... | collective-permute-start | bytes 1376264 | tf_op jit(solution)/shard_map/ppermute | solution.py:608
  1.2 3.4 %copy-start.1 = (f32[2,2,128]{2,1,0:T(2,128)S(1)}, f32[2,2,128]{2,1,0:T(2,128)}, u32[]{:S(2)}) copy-start(f32[2,2,128]{2,1,0:T(2,128)} %refs_2_.8) | copy-start | bytes 6148
  1.2 3.4 %copy-start.2 = (s32[128]{0:T(128)S(1)}, s32[128]{0:T(128)}, u32[]{:S(2)}) copy-start(s32[128]{0:T(128)} %param.17) | copy-start | bytes 1540
  1.2 3.4 %copy-start.3 = (bf16[128,1792]{1,0:T(8,128)(2,1)S(1)}, bf16[128,1792]{1,0:T(8,128)(2,1)}, u32[]{:S(2)}) copy-start(bf16[128,1792]{1,0:T(8,128)(2,1)} %refs_4_.3) | copy-start | bytes 1376260
  1.2 3.4 %copy-start.4 = (f32[2,3584]{1,0:T(2,128)S(1)}, f32[2,3584]{1,0:T(2,128)}, u32[]{:S(2)}) copy-start(f32[2,3584]{1,0:T(2,128)} %refs_2_.9) | copy-start | bytes 86020
  1.2 10.7 %slice-start.2 = ((s8[14680064]{0:T(1024)(128)(4,1)}), s8[4194304]{0:T(1024)(128)(4,1)S(1)}, s32[]{:S(2)}) async-start(s8[14680064]{0:T(1024)(128)(4,1)} %bitcast.6), calls=%async_computation.2 | async-start | bytes 8388608
  1.3 10.7 %slice-start.3 = ((s8[14680064]{0:T(1024)(128)(4,1)}), s8[4194304]{0:T(1024)(128)(4,1)S(1)}, s32[]{:S(2)}) async-start(s8[14680064]{0:T(1024)(128)(4,1)} %bitcast.6), calls=%async_computation.3 | async-start | bytes 8388608
  4.6 7.3 %slice-start.4 = ((s8[14680064]{0:T(1024)(128)(4,1)}), s8[4194304]{0:T(1024)(128)(4,1)S(1)}, s32[]{:S(2)}) async-start(s8[14680064]{0:T(1024)(128)(4,1)} %bitcast.6), calls=%async_computation.4 | async-start | bytes 8388608
  4.7 7.3 %slice-start.5 = ((s8[14680064]{0:T(1024)(128)(4,1)}), s8[2097152]{0:T(1024)(128)(4,1)S(1)}, s32[]{:S(2)}) async-start(s8[14680064]{0:T(1024)(128)(4,1)} %bitcast.6), calls=%async_computation.5 | async-start | bytes 4194304
  4.7 7.3 %copy-start = (bf16[128,1792]{1,0:T(8,128)(2,1)S(1)}, bf16[128,1792]{1,0:T(8,128)(2,1)}, u32[]{:S(2)}) copy-start(bf16[128,1792]{1,0:T(8,128)(2,1)} %refs_6_.2) | copy-start | bytes 1376260
  6.2 14.0 %collective-permute-start.2 = (bf16[128,512]{1,0:T(8,128)(2,1)S(1)}, bf16[128,512]{1,0:T(8,128)(2,1)S(1)}, u32[]{:S(2)}, u32[]{:S(2)}) collective-permute-start(bf16[128,512]{1,0:T(8,128)(2,1)S(1)} %get-tuple-element.26.refs_5_), channel_id=1, source_target_pairs={{0,4},{2,6},{4,0},{6,2},{1,5},{3,7},{5,1},{7,3},{8,12},{10,14},{12... | collective-permute-start | bytes 393224 | tf_op jit(solution)/shard_map/ppermute | solution.py:629
  10.3 9.9 %collective-permute-start.3 = (bf16[128,512]{1,0:T(8,128)(2,1)S(1)}, bf16[128,512]{1,0:T(8,128)(2,1)S(1)}, u32[]{:S(2)}, u32[]{:S(2)}) collective-permute-start(bf16[128,512]{1,0:T(8,128)(2,1)S(1)} %get-tuple-element.26.refs_5_), channel_id=1, source_target_pairs={{0,2},{2,0},{4,6},{6,4},{1,3},{3,1},{5,7},{7,5},{8,10},{10,8},{12,... | collective-permute-start | bytes 393224 | tf_op jit(solution)/shard_map/ppermute | solution.py:629
  11.9 9.0 %collective-permute-start.4 = (bf16[128,512]{1,0:T(8,128)(2,1)S(1)}, bf16[128,512]{1,0:T(8,128)(2,1)S(1)}, u32[]{:S(2)}, u32[]{:S(2)}) collective-permute-start(bf16[128,512]{1,0:T(8,128)(2,1)S(1)} %get-tuple-element.26.refs_5_), channel_id=1, source_target_pairs={{0,6},{2,4},{4,2},{6,0},{1,7},{3,5},{5,3},{7,1},{8,14},{10,12},{12... | collective-permute-start | bytes 393224 | tf_op jit(solution)/shard_map/ppermute | solution.py:629
  12.0 8.9 %copy-start.5 = (s32[512]{0:T(512)S(1)}, s32[512]{0:T(512)}, u32[]{:S(2)}) copy-start(s32[512]{0:T(512)} %param.18) | copy-start | bytes 6148
  12.0 8.9 %copy-start.6 = (s32[4]{0:T(128)S(1)}, s32[4]{0:T(128)}, u32[]{:S(2)}) copy-start(s32[4]{0:T(128)} %refs_1_.1) | copy-start | bytes 52
  20.9 17.7 %slice-start = ((s8[7340032]{0:T(1024)(128)(4,1)}), s8[4194304]{0:T(1024)(128)(4,1)S(1)}, s32[]{:S(2)}) async-start(s8[7340032]{0:T(1024)(128)(4,1)} %bitcast.4), calls=%async_computation | async-start | bytes 8388608
  23.8 14.4 %collective-permute-start.5 = (bf16[128,512]{1,0:T(8,128)(2,1)S(1)}, bf16[128,512]{1,0:T(8,128)(2,1)S(1)}, u32[]{:S(2)}, u32[]{:S(2)}) collective-permute-start(bf16[128,512]{1,0:T(8,128)(2,1)S(1)} %get-tuple-element.34), channel_id=1, source_target_pairs={{4,0},{6,2},{0,4},{2,6},{5,1},{7,3},{1,5},{3,7},{12,8},{14,10},{8,... | collective-permute-start | bytes 393224 | tf_op jit(solution)/shard_map/ppermute | solution.py:643
  28.1 10.5 %collective-permute-start.6 = (bf16[128,512]{1,0:T(8,128)(2,1)S(1)}, bf16[128,512]{1,0:T(8,128)(2,1)S(1)}, u32[]{:S(2)}, u32[]{:S(2)}) collective-permute-start(bf16[128,512]{1,0:T(8,128)(2,1)S(1)} %get-tuple-element.35), channel_id=1, source_target_pairs={{2,0},{0,2},{6,4},{4,6},{3,1},{1,3},{7,5},{5,7},{10,8},{8,10},{14,... | collective-permute-start | bytes 393224 | tf_op jit(solution)/shard_map/ppermute | solution.py:643
  28.1 10.5 %collective-permute-start.7 = (bf16[128,512]{1,0:T(8,128)(2,1)S(1)}, bf16[128,512]{1,0:T(8,128)(2,1)S(1)}, u32[]{:S(2)}, u32[]{:S(2)}) collective-permute-start(bf16[128,512]{1,0:T(8,128)(2,1)S(1)} %get-tuple-element.36), channel_id=1, source_target_pairs={{6,0},{4,2},{2,4},{0,6},{7,1},{5,3},{3,5},{1,7},{14,8},{12,10},{10... | collective-permute-start | bytes 393224 | tf_op jit(solution)/shard_map/ppermute | solution.py:643
  29.6 9.0 %slice-start.1 = ((s8[7340032]{0:T(1024)(128)(4,1)}), s8[3145728]{0:T(1024)(128)(4,1)S(1)}, s32[]{:S(2)}) async-start(s8[7340032]{0:T(1024)(128)(4,1)} %bitcast.4), calls=%async_computation.1 | async-start | bytes 6291456
  38.2 3.8 %collective-permute-start.10 = (bf16[128,1792]{1,0:T(8,128)(2,1)S(1)}, bf16[128,1792]{1,0:T(8,128)(2,1)S(1)}, u32[]{:S(2)}, u32[]{:S(2)}) collective-permute-start(bf16[128,1792]{1,0:T(8,128)(2,1)S(1)} %tie.1), channel_id=1, source_target_pairs={{0,1},{1,0},{2,3},{3,2},{4,5},{5,4},{6,7},{7,6},{8,9},{9,8},{10,11... | collective-permute-start | bytes 1376264 | tf_op jit(solution)/shard_map/ppermute | solution.py:660
  40.1 1.9 %collective-permute-start.8 = (bf16[128,1792]{1,0:T(8,128)(2,1)S(1)}, bf16[128,1792]{1,0:T(8,128)(2,1)S(1)}, u32[]{:S(2)}, u32[]{:S(2)}) collective-permute-start(bf16[128,1792]{1,0:T(8,128)(2,1)S(1)} %get-tuple-element.38), channel_id=1, source_target_pairs={{0,1},{1,0},{2,3},{3,2},{4,5},{5,4},{6,7},{7,6},{8,9},{9,8},{10,11... | collective-permute-start | bytes 1376264 | tf_op jit(solution)/shard_map/ppermute | solution.py:685
  40.4 1.6 %collective-permute-start.9 = (f32[1,128]{1,0:T(1,128)S(1)}, f32[1,128]{1,0:T(1,128)S(1)}, u32[]{:S(2)}, u32[]{:S(2)}) collective-permute-start(f32[1,128]{1,0:T(1,128)S(1)} %get-tuple-element.39.refs_7_), channel_id=1, source_target_pairs={{0,1},{1,0},{2,3},{3,2},{4,5},{5,4},{6,7},{7,6},{8,9},{9,8},{10,11... | collective-permute-start | bytes 1544 | tf_op jit(solution)/shard_map/ppermute | solution.py:684

commit v12 on v11

--- a/solution.py
+++ b/solution.py
@@ -495,25 +495,45 @@
     )(rank, modality, head_gain, raw, inner, part, weights, *grads)
 
 
-def kept_kernel(rank_ref, modality_ref, part_ref, weight_ref, back_ref, out_ref):
+def kept_kernel(
+    rank_ref,
+    modality_ref,
+    part_ref,
+    weight_ref,
+    back_ref,
+    mine_ref,
+    other_ref,
+    out_ref,
+    attention_ref,
+    staged,
+    sem,
+):
+    staged[...] = (mine_ref[...] + other_ref[...].astype(f32)).astype(bf16)
+    copy = pltpu.make_async_copy(staged, attention_ref, sem)
+    copy.start()
     base = pl.multiple_of(rank_ref[0] * out_ref.shape[1], HEAD_DIM)
     image = column(modality_ref[...]) > 0.0
     for start, size in chunks_of(out_ref.shape[1], HEAD_DIM):
         place = pl.ds(base + start, size)
         product = both_back(image, back_ref[...], weight_ref[:, place, :])
         out_ref[:, start : start + size] = product + part_ref[:, place]
-
-
-def kept_stage(rank, modality, part, weights, back):
+    copy.wait()
+
+
+def kept_stage(rank, modality, part, weights, back, mine, other):
     return pl.pallas_call(
         kept_kernel,
-        out_shape=jax.ShapeDtypeStruct((back.shape[0], weights.shape[1] // 2), f32),
-        in_specs=[SMEM] + [VMEM] * 4,
-        out_specs=VMEM,
+        out_shape=[
+            jax.ShapeDtypeStruct((back.shape[0], weights.shape[1] // 2), f32),
+            jax.ShapeDtypeStruct(other.shape, bf16),
+        ],
+        in_specs=[SMEM] + [VMEM] * 6,
+        out_specs=[VMEM, ANY],
+        scratch_shapes=[pltpu.VMEM(other.shape, bf16), pltpu.SemaphoreType.DMA],
         compiler_params=params(6),
         cost_estimate=cost(2),
         name="kept_stage",
-    )(rank, modality, part, weights, back)
+    )(rank, modality, part, weights, back, mine, other)
 
 
 def finish_kernel(backs, inners, total_width, *refs):
@@ -530,14 +550,7 @@
         copies.append(copy)
 
     pieces = [slice(start, start + size) for start, size in chunks_of(width, 896)]
-    if len(rest) == 7:
-        kept_ref, other_ref, attention_ref, out_ref, staged, staged_attention, sems = rest
-        for index, part in enumerate(pieces):
-            whole = kept_ref[:, part] + other_ref[:, part].astype(f32)
-            staged_attention[:, part] = whole.astype(bf16)
-            send(staged_attention, attention_ref, sems.at[1, index], part)
-    else:
-        out_ref, staged, sems = rest
+    out_ref, staged, sems = rest
     image = column(modality_ref[...]) > 0.0
     factor = column(factor_ref[...])
     inner = inner_refs[0][...]
@@ -556,23 +569,20 @@
         rows = inputs_ref[:, part].astype(f32)
         result = factor * (gain_of(image, gain_ref, columns) * back - rows * inner_mean)
         staged[:, part] = result.astype(bf16)
-        send(staged, out_ref, sems.at[0, index], part)
+        send(staged, out_ref, sems.at[index], part)
     for copy in copies:
         copy.wait()
 
 
-def finish(rank, total_width, modality, gain, factor, inputs, backs, inners, projected):
-    shape = jax.ShapeDtypeStruct(inputs.shape, bf16)
-    arrays = [modality, gain, factor, inputs, *backs, *inners, *projected]
-    count = 2 if projected else 1
+def finish(rank, total_width, modality, gain, factor, inputs, backs, inners):
+    arrays = [modality, gain, factor, inputs, *backs, *inners]
     pieces = len(chunks_of(inputs.shape[1], 896))
     return pl.pallas_call(
         functools.partial(finish_kernel, len(backs), len(inners), total_width),
-        out_shape=[shape] * count,
+        out_shape=jax.ShapeDtypeStruct(inputs.shape, bf16),
         in_specs=[SMEM] + [VMEM] * len(arrays),
-        out_specs=[ANY] * count,
-        scratch_shapes=[pltpu.VMEM(inputs.shape, bf16)] * count
-        + [pltpu.SemaphoreType.DMA((count, pieces))],
+        out_specs=ANY,
+        scratch_shapes=[pltpu.VMEM(inputs.shape, bf16), pltpu.SemaphoreType.DMA((pieces,))],
         compiler_params=params(6),
         cost_estimate=cost(1),
         name="finish",
@@ -660,7 +670,6 @@
         projected = [projected[1], lax.ppermute(passed, "tensor", swap)]
     else:
         attention_out = scatter_columns(projected[0])
-        projected = []
 
     if shared:
         total = own_grad + sum(grad.astype(f32) for grad in incoming)
@@ -683,19 +692,17 @@
     if split:
         inners = [inner, lax.ppermute(inner, "tensor", swap)]
         other = lax.ppermute(sent, "tensor", swap)
-        kept = kept_stage(rank, modality, gradient_part, key_weight, slice_back)
+        kept, attention_out = kept_stage(
+            rank, modality, gradient_part, key_weight, slice_back, *projected
+        )
         backs = [kept, other]
         gain = norm_gain
     else:
         inners = [lax.psum(inner, "tensor")]
         backs = [scatter_columns(sent)]
         gain = lax.dynamic_slice_in_dim(norm_gain, tensor_rank * local_width, local_width, 1)
-    results = finish(
-        rank, full_width, modality, gain, row_factor, inputs, backs, inners, projected
-    )
-    if split:
-        attention_out = results[0]
-    return (attention_out, results[-1])
+    grad_input = finish(rank, full_width, modality, gain, row_factor, inputs, backs, inners)
+    return (attention_out, grad_input)
 
 
 def solution(mesh):

time: 43.8 us -> 44.3 us (1.011)
  Pallas kernels: 28.6 us -> 29.3 us
    pallas_call x1, Pallas kernels: 1.12 us -> 2.05 us  [kept_stage(): pl.pallas_call(kept_kernel, out_shape=[jax.ShapeDtypeStruct((back.shape[0...]
  transfers between devices with their start and end apart: 11 -> 11, of which waited for: 3 -> 2; matrix products, arithmetic and copies ran while one was open for 0% -> 0% of each run, Pallas kernels for 56% -> 57%
where the time goes in v12:
time: 44.3 us; the launch traced here: 44.1 us
  Pallas kernels  29.3 us (66%)
  starting transfers between devices  12.7 us (29%)
  between operations  1.06 us (2%)
  waiting for transfers between devices  0.97 us (2%)
    pallas_call x1, Pallas kernels, turn_stage(): pl.pallas_call(functools.partial(turn_kernel, pieces, len(outs)), out_sha...  8.55 us
    pallas_call x1, Pallas kernels, middle_stage(): pl.pallas_call(functools.partial(middle_kernel, len(parts), pieces), out_...  8.23 us
    ppermute x3, starting transfers between devices, local(): lax.ppermute(grad, 'seq', inverted(seq_pairs(step, block_count)))  5.84 us
    ppermute x3, starting transfers between devices, local(): memories.append(lax.ppermute(memory, 'seq', seq_pairs(step, block_count)))  5.66 us
    pallas_call x1, Pallas kernels, fetch(): pl.pallas_call(functools.partial(fetch_kernel, pieces), out_shape=residen...  3.32 us
    pallas_call x1, Pallas kernels, attention_stage(): pl.pallas_call(functools.partial(attention_kernel, blocks, pairs, per_gro...  2.87 us
    pallas_call x1, Pallas kernels, kept_stage(): pl.pallas_call(kept_kernel, out_shape=[jax.ShapeDtypeStruct((back.shape[0...  2.05 us
    pallas_call x1, Pallas kernels, key_stage(): pl.pallas_call(functools.partial(key_kernel, len(parts)), out_shape=[jax....  1.56 us
  transfers between devices with their start and end apart: 11, of which 2 were waited for; matrix products, arithmetic and copies ran while one was open for 0% of the time, Pallas kernels for 57%

profile of v12, /device:TPU:0, one launch (start us, length us, event | category | flops | bytes accessed | tf_op | source)
XLA Modules:
  0.0 44.1 jit_solution(7401982201760753700)
XLA Ops:
  0.6 0.5 %collective-permute-start = (bf16[128,1792]{1,0:T(8,128)(2,1)}, bf16[128,1792]{1,0:T(8,128)(2,1)S(1)}, u32[]{:S(2)}, u32[]{:S(2)}) collective-permute-start(bf16[128,1792]{1,0:T(8,128)(2,1)} %refs_4_.3), channel_id=1, source_target_pairs={{0,1},{1,0},{2,3},{3,2},{4,5},{5,4},{6,7},{7,6},{8,9},{9,8},{10,11... | collective-permute-start | bytes 1376264 | tf_op jit(solution)/shard_map/ppermute | solution.py:618
  1.1 0.1 collective-permute-start.1
  1.2 0.0 copy-start.1
  1.2 0.0 copy-start.2
  1.2 0.0 copy-start.3
  1.2 0.0 copy-start.4
  1.2 0.0 slice-start.2
  1.3 0.0 slice-start.3
  1.3 3.3 %fetch.1.refs_4_ = bf16[2,3584,512]{2,1,0:T(8,128)(2,1)S(1)} custom-call(bf16[2,3584,512]{2,1,0:T(8,128)(2,1)} %weight_ref.3), custom_call_target="tpu_custom_call" | custom-call | flops 200000000 | bytes 400000 | tf_op jit(solution)/shard_map/fetch/pallas_call | solution.py:171
  4.6 0.0 collective-permute-done.refs_6_
  4.6 0.0 copy-done.1
  4.6 0.0 copy-done.2
  4.6 0.0 copy-done.3
  4.6 0.0 copy-done.4
  4.6 0.0 slice-start.4
  4.7 0.0 slice-start.5
  4.7 0.0 copy-start
  4.7 1.6 %key_stage.1 = (bf16[128,512]{1,0:T(8,128)(2,1)S(1)}, f32[128,512]{1,0:T(8,128)S(1)}, bf16[128,3584]{1,0:T(8,128)(2,1)S(1)}, f32[1,128]{1,0:T(1,128)S(1)}) custom-call(s32[1]{0:T(128)} %bitcast.refs_0_.rank_ref, s32[1,128]{1,0:T(1,128)S(1)} %bitcast.8, f32[2,3584]{1,0:T(2,128)S(1)} %copy-done.4, f32[2,2,128]{2,1,0:T(2,128)S(1)} %copy-done.1, ...), custom_call_target="tpu_custom_call" | custom-call | flops 10000000000 | bytes 20000000 | tf_op jit(solution)/shard_map/key_stage/pallas_call | solution.py:217
  6.2 4.1 %collective-permute-start.2 = (bf16[128,512]{1,0:T(8,128)(2,1)S(1)}, bf16[128,512]{1,0:T(8,128)(2,1)S(1)}, u32[]{:S(2)}, u32[]{:S(2)}) collective-permute-start(bf16[128,512]{1,0:T(8,128)(2,1)S(1)} %get-tuple-element.27.refs_5_), channel_id=1, source_target_pairs={{0,4},{2,6},{4,0},{6,2},{1,5},{3,7},{5,1},{7,3},{8,12},{10,14},{12... | collective-permute-start | bytes 393224 | tf_op jit(solution)/shard_map/ppermute | solution.py:639
  10.3 1.6 %collective-permute-start.3 = (bf16[128,512]{1,0:T(8,128)(2,1)S(1)}, bf16[128,512]{1,0:T(8,128)(2,1)S(1)}, u32[]{:S(2)}, u32[]{:S(2)}) collective-permute-start(bf16[128,512]{1,0:T(8,128)(2,1)S(1)} %get-tuple-element.27.refs_5_), channel_id=1, source_target_pairs={{0,2},{2,0},{4,6},{6,4},{1,3},{3,1},{5,7},{7,5},{8,10},{10,8},{12,... | collective-permute-start | bytes 393224 | tf_op jit(solution)/shard_map/ppermute | solution.py:639
  11.9 0.0 collective-permute-start.4
  11.9 0.0 collective-permute-done.1.refs_7_
  11.9 0.0 slice-done.2
  11.9 0.0 slice-done.3
  11.9 0.0 slice-done.4
  11.9 0.0 slice-done.5
  11.9 0.0 copy-done
  12.0 0.0 copy-start.5
  12.0 0.0 copy-start.6
  12.0 8.2 %middle_stage.1 = (bf16[128,1024]{1,0:T(8,128)(2,1)S(1)}, f32[128,1024]{1,0:T(8,128)S(1)}, bf16[128,1024]{1,0:T(8,128)(2,1)S(1)}) custom-call(s32[1]{0:T(128)} %bitcast.refs_0_.rank_ref, s32[1,128]{1,0:T(1,128)S(1)} %bitcast.9, f32[2,2,128]{2,1,0:T(2,128)S(1)} %copy-done.1, bf16[128,3584]{1,0:T(8,128)(2,1)S(1)} %get-tuple-element.24.refs_3_, ...), custom_call_target="tpu_custom_call" | custom-call | flops 8000000000 | bytes 16000000 | tf_op jit(solution)/shard_map/middle_stage/pallas_call | solution.py:269
  20.2 0.0 collective-permute-done.2.refs_6_
  20.2 0.0 collective-permute-done.3.refs_7_
  20.2 0.6 %collective-permute-done.4.refs_8_ = bf16[128,512]{1,0:T(8,128)(2,1)S(1)} collective-permute-done((bf16[128,512]{1,0:T(8,128)(2,1)S(1)}, bf16[128,512]{1,0:T(8,128)(2,1)S(1)}, u32[]{:S(2)}, u32[]{:S(2)}) %collective-permute-start.4) | collective-permute-done | bytes 131104 | tf_op jit(solution)/shard_map/ppermute | solution.py:639
  20.9 0.0 copy-done.5
  20.9 0.0 copy-done.6
  20.9 0.0 slice-start
  20.9 2.9 %attention_stage.1 = (bf16[128,1024]{1,0:T(8,128)(2,1)S(1)}, f32[128,1024]{1,0:T(8,128)S(1)}, f32[128,512]{1,0:T(8,128)S(1)}, bf16[128,512]{1,0:T(8,128)(2,1)S(1...) custom-call(s32[1]{0:T(128)} %bitcast.2.refs_0_, s32[4]{0:T(128)S(1)} %copy-done.6, s32[4,128]{1,0:T(4,128)S(1)} %bitcast.14, ...), custom_call_target="tpu_custom_call" | custom-call | flops 4000000000 | bytes 8000000 | tf_op jit(solution)/shard_map/attention_stage/pallas_call | solution.py:349
  23.8 4.3 %collective-permute-start.5 = (bf16[128,512]{1,0:T(8,128)(2,1)S(1)}, bf16[128,512]{1,0:T(8,128)(2,1)S(1)}, u32[]{:S(2)}, u32[]{:S(2)}) collective-permute-start(bf16[128,512]{1,0:T(8,128)(2,1)S(1)} %get-tuple-element.35), channel_id=1, source_target_pairs={{4,0},{6,2},{0,4},{2,6},{5,1},{7,3},{1,5},{3,7},{12,8},{14,10},{8,... | collective-permute-start | bytes 393224 | tf_op jit(solution)/shard_map/ppermute | solution.py:653
  28.1 0.0 collective-permute-start.6
  28.1 1.5 %collective-permute-start.7 = (bf16[128,512]{1,0:T(8,128)(2,1)S(1)}, bf16[128,512]{1,0:T(8,128)(2,1)S(1)}, u32[]{:S(2)}, u32[]{:S(2)}) collective-permute-start(bf16[128,512]{1,0:T(8,128)(2,1)S(1)} %get-tuple-element.37), channel_id=1, source_target_pairs={{6,0},{4,2},{2,4},{0,6},{7,1},{5,3},{3,5},{1,7},{14,8},{12,10},{10... | collective-permute-start | bytes 393224 | tf_op jit(solution)/shard_map/ppermute | solution.py:653
  29.6 0.0 slice-start.1
  29.6 8.6 %turn_stage.1 = (bf16[128,1792]{1,0:T(8,128)(2,1)S(1)}, f32[128,1792]{1,0:T(8,128)S(1)}, f32[128,3584]{1,0:T(8,128)S(1)}, f32[1,128]{1,0:T(1,128)S(1)}) custom-call(s32[1]{0:T(128)} %bitcast.refs_0_.rank_ref, s32[1,128]{1,0:T(1,128)S(1)} %bitcast.10, f32[2,2,128]{2,1,0:T(2,128)S(1)} %copy-done.1, bf16[2,1024,3584]{2,1,0:T(8,128)(2,1)S(1)} %bitcast.7, ...), custom_call_target="tpu_custom_call" | custom-call | flops 10000000000 | bytes 20000000 | tf_op jit(solution)/shard_map/turn_stage/pallas_call | solution.py:419
  38.2 0.0 collective-permute-done.5.refs_8_.arrived_ref
  38.2 0.1 collective-permute-start.8
  38.3 0.3 collective-permute-done.6.refs_9_
  38.6 0.0 collective-permute-done.7.refs_10_
  38.6 0.0 slice-done
  38.6 0.0 slice-done.1
  38.6 1.5 %key_back_stage.1 = (bf16[128,1792]{1,0:T(8,128)(2,1)S(1)}, bf16[128,512]{1,0:T(8,128)(2,1)S(1)}, f32[1,128]{1,0:T(1,128)S(1)}) custom-call(s32[1]{0:T(128)} %bitcast.refs_0_.rank_ref, s32[1,128]{1,0:T(1,128)S(1)} %bitcast.11, f32[2,2,128]{2,1,0:T(2,128)S(1)} %copy-done.1, f32[128,512]{1,0:T(8,128)S(1)} %get-tuple-element.32.refs_3_, ...), custom_call_target="tpu_custom_call" | custom-call | flops 2000000000 | bytes 4000000 | tf_op jit(solution)/shard_map/key_back_stage/pallas_call | solution.py:483
  40.1 0.3 collective-permute-start.9
  40.4 0.3 collective-permute-start.10
  40.7 0.0 collective-permute-done.8.other_ref
  40.7 2.1 %kept_stage.1 = (f32[128,1792]{1,0:T(8,128)S(1)}, bf16[128,1792]{1,0:T(8,128)(2,1)}) custom-call(s32[1]{0:T(128)} %bitcast.refs_0_.rank_ref, s32[1,128]{1,0:T(1,128)S(1)} %bitcast.12, f32[128,3584]{1,0:T(8,128)S(1)} %get-tuple-element.31.refs_5_.part_ref, bf16[2,3584,512]{2,1,0:T(8,128)(2,1)S(1)} %bitcast.5, ...), custom_call_target="tpu_custom_call" | custom-call | flops 2000000000 | bytes 4000000 | tf_op jit(solution)/shard_map/kept_stage/pallas_call | solution.py:524
  42.7 0.0 collective-permute-done.10.refs_8_
  42.7 0.0 collective-permute-done.9.refs_6_
  42.7 1.2 %finish.1 = bf16[128,1792]{1,0:T(8,128)(2,1)} custom-call(s32[1]{0:T(128)} %bitcast.refs_0_.rank_ref, s32[1,128]{1,0:T(1,128)S(1)} %bitcast.13, f32[2,3584]{1,0:T(2,128)S(1)} %copy-done.4, f32[1,128]{1,0:T(1,128)S(1)} %get-tuple-element.42.refs_3_, bf16[128,1792]{1,0:T(8,128)(2,1)S(1)} %copy-done.3, f32[128,1792]{1,0:T(8,128)S(1)} %get-tuple-element.43.refs_5_, ...), custom_call_target="tpu_custom_call" | custom-call | flops 1000000000 | bytes 2000000 | tf_op jit(solution)/shard_map/finish/pallas_call | solution.py:580
  (3 shorter events, 0.0 us)
Async XLA Ops:
  0.6 4.0 %collective-permute-start = (bf16[128,1792]{1,0:T(8,128)(2,1)}, bf16[128,1792]{1,0:T(8,128)(2,1)S(1)}, u32[]{:S(2)}, u32[]{:S(2)}) collective-permute-start(bf16[128,1792]{1,0:T(8,128)(2,1)} %refs_4_.3), channel_id=1, source_target_pairs={{0,1},{1,0},{2,3},{3,2},{4,5},{5,4},{6,7},{7,6},{8,9},{9,8},{10,11... | collective-permute-start | bytes 1376264 | tf_op jit(solution)/shard_map/ppermute | solution.py:618
  1.1 10.8 %collective-permute-start.1 = (bf16[128,1792]{1,0:T(8,128)(2,1)}, bf16[128,1792]{1,0:T(8,128)(2,1)S(1)}, u32[]{:S(2)}, u32[]{:S(2)}) collective-permute-start(bf16[128,1792]{1,0:T(8,128)(2,1)} %refs_6_.2), channel_id=1, source_target_pairs={{0,1},{1,0},{2,3},{3,2},{4,5},{5,4},{6,7},{7,6},{8,9},{9,8},{10,11... | collective-permute-start | bytes 1376264 | tf_op jit(solution)/shard_map/ppermute | solution.py:618
  1.2 3.4 %copy-start.1 = (f32[2,2,128]{2,1,0:T(2,128)S(1)}, f32[2,2,128]{2,1,0:T(2,128)}, u32[]{:S(2)}) copy-start(f32[2,2,128]{2,1,0:T(2,128)} %refs_2_.8) | copy-start | bytes 6148
  1.2 3.4 %copy-start.2 = (s32[128]{0:T(128)S(1)}, s32[128]{0:T(128)}, u32[]{:S(2)}) copy-start(s32[128]{0:T(128)} %param.17) | copy-start | bytes 1540
  1.2 3.4 %copy-start.3 = (bf16[128,1792]{1,0:T(8,128)(2,1)S(1)}, bf16[128,1792]{1,0:T(8,128)(2,1)}, u32[]{:S(2)}) copy-start(bf16[128,1792]{1,0:T(8,128)(2,1)} %refs_4_.3) | copy-start | bytes 1376260
  1.2 3.4 %copy-start.4 = (f32[2,3584]{1,0:T(2,128)S(1)}, f32[2,3584]{1,0:T(2,128)}, u32[]{:S(2)}) copy-start(f32[2,3584]{1,0:T(2,128)} %refs_2_.9) | copy-start | bytes 86020
  1.2 10.7 %slice-start.2 = ((s8[14680064]{0:T(1024)(128)(4,1)}), s8[4194304]{0:T(1024)(128)(4,1)S(1)}, s32[]{:S(2)}) async-start(s8[14680064]{0:T(1024)(128)(4,1)} %bitcast.6), calls=%async_computation.2 | async-start | bytes 8388608
  1.3 10.7 %slice-start.3 = ((s8[14680064]{0:T(1024)(128)(4,1)}), s8[4194304]{0:T(1024)(128)(4,1)S(1)}, s32[]{:S(2)}) async-start(s8[14680064]{0:T(1024)(128)(4,1)} %bitcast.6), calls=%async_computation.3 | async-start | bytes 8388608
  4.6 7.3 %slice-start.4 = ((s8[14680064]{0:T(1024)(128)(4,1)}), s8[4194304]{0:T(1024)(128)(4,1)S(1)}, s32[]{:S(2)}) async-start(s8[14680064]{0:T(1024)(128)(4,1)} %bitcast.6), calls=%async_computation.4 | async-start | bytes 8388608
  4.7 7.3 %slice-start.5 = ((s8[14680064]{0:T(1024)(128)(4,1)}), s8[2097152]{0:T(1024)(128)(4,1)S(1)}, s32[]{:S(2)}) async-start(s8[14680064]{0:T(1024)(128)(4,1)} %bitcast.6), calls=%async_computation.5 | async-start | bytes 4194304
  4.7 7.3 %copy-start = (bf16[128,1792]{1,0:T(8,128)(2,1)S(1)}, bf16[128,1792]{1,0:T(8,128)(2,1)}, u32[]{:S(2)}) copy-start(bf16[128,1792]{1,0:T(8,128)(2,1)} %refs_6_.2) | copy-start | bytes 1376260
  6.2 14.0 %collective-permute-start.2 = (bf16[128,512]{1,0:T(8,128)(2,1)S(1)}, bf16[128,512]{1,0:T(8,128)(2,1)S(1)}, u32[]{:S(2)}, u32[]{:S(2)}) collective-permute-start(bf16[128,512]{1,0:T(8,128)(2,1)S(1)} %get-tuple-element.27.refs_5_), channel_id=1, source_target_pairs={{0,4},{2,6},{4,0},{6,2},{1,5},{3,7},{5,1},{7,3},{8,12},{10,14},{12... | collective-permute-start | bytes 393224 | tf_op jit(solution)/shard_map/ppermute | solution.py:639
  10.3 9.9 %collective-permute-start.3 = (bf16[128,512]{1,0:T(8,128)(2,1)S(1)}, bf16[128,512]{1,0:T(8,128)(2,1)S(1)}, u32[]{:S(2)}, u32[]{:S(2)}) collective-permute-start(bf16[128,512]{1,0:T(8,128)(2,1)S(1)} %get-tuple-element.27.refs_5_), channel_id=1, source_target_pairs={{0,2},{2,0},{4,6},{6,4},{1,3},{3,1},{5,7},{7,5},{8,10},{10,8},{12,... | collective-permute-start | bytes 393224 | tf_op jit(solution)/shard_map/ppermute | solution.py:639
  11.9 9.0 %collective-permute-start.4 = (bf16[128,512]{1,0:T(8,128)(2,1)S(1)}, bf16[128,512]{1,0:T(8,128)(2,1)S(1)}, u32[]{:S(2)}, u32[]{:S(2)}) collective-permute-start(bf16[128,512]{1,0:T(8,128)(2,1)S(1)} %get-tuple-element.27.refs_5_), channel_id=1, source_target_pairs={{0,6},{2,4},{4,2},{6,0},{1,7},{3,5},{5,3},{7,1},{8,14},{10,12},{12... | collective-permute-start | bytes 393224 | tf_op jit(solution)/shard_map/ppermute | solution.py:639
  12.0 8.9 %copy-start.5 = (s32[512]{0:T(512)S(1)}, s32[512]{0:T(512)}, u32[]{:S(2)}) copy-start(s32[512]{0:T(512)} %param.18) | copy-start | bytes 6148
  12.0 8.9 %copy-start.6 = (s32[4]{0:T(128)S(1)}, s32[4]{0:T(128)}, u32[]{:S(2)}) copy-start(s32[4]{0:T(128)} %refs_1_.1) | copy-start | bytes 52
  20.9 17.7 %slice-start = ((s8[7340032]{0:T(1024)(128)(4,1)}), s8[4194304]{0:T(1024)(128)(4,1)S(1)}, s32[]{:S(2)}) async-start(s8[7340032]{0:T(1024)(128)(4,1)} %bitcast.4), calls=%async_computation | async-start | bytes 8388608
  23.8 14.4 %collective-permute-start.5 = (bf16[128,512]{1,0:T(8,128)(2,1)S(1)}, bf16[128,512]{1,0:T(8,128)(2,1)S(1)}, u32[]{:S(2)}, u32[]{:S(2)}) collective-permute-start(bf16[128,512]{1,0:T(8,128)(2,1)S(1)} %get-tuple-element.35), channel_id=1, source_target_pairs={{4,0},{6,2},{0,4},{2,6},{5,1},{7,3},{1,5},{3,7},{12,8},{14,10},{8,... | collective-permute-start | bytes 393224 | tf_op jit(solution)/shard_map/ppermute | solution.py:653
  28.1 10.5 %collective-permute-start.6 = (bf16[128,512]{1,0:T(8,128)(2,1)S(1)}, bf16[128,512]{1,0:T(8,128)(2,1)S(1)}, u32[]{:S(2)}, u32[]{:S(2)}) collective-permute-start(bf16[128,512]{1,0:T(8,128)(2,1)S(1)} %get-tuple-element.36), channel_id=1, source_target_pairs={{2,0},{0,2},{6,4},{4,6},{3,1},{1,3},{7,5},{5,7},{10,8},{8,10},{14,... | collective-permute-start | bytes 393224 | tf_op jit(solution)/shard_map/ppermute | solution.py:653
  28.1 10.5 %collective-permute-start.7 = (bf16[128,512]{1,0:T(8,128)(2,1)S(1)}, bf16[128,512]{1,0:T(8,128)(2,1)S(1)}, u32[]{:S(2)}, u32[]{:S(2)}) collective-permute-start(bf16[128,512]{1,0:T(8,128)(2,1)S(1)} %get-tuple-element.37), channel_id=1, source_target_pairs={{6,0},{4,2},{2,4},{0,6},{7,1},{5,3},{3,5},{1,7},{14,8},{12,10},{10... | collective-permute-start | bytes 393224 | tf_op jit(solution)/shard_map/ppermute | solution.py:653
  29.6 9.0 %slice-start.1 = ((s8[7340032]{0:T(1024)(128)(4,1)}), s8[3145728]{0:T(1024)(128)(4,1)S(1)}, s32[]{:S(2)}) async-start(s8[7340032]{0:T(1024)(128)(4,1)} %bitcast.4), calls=%async_computation.1 | async-start | bytes 6291456
  38.2 2.5 %collective-permute-start.8 = (bf16[128,1792]{1,0:T(8,128)(2,1)S(1)}, bf16[128,1792]{1,0:T(8,128)(2,1)S(1)}, u32[]{:S(2)}, u32[]{:S(2)}) collective-permute-start(bf16[128,1792]{1,0:T(8,128)(2,1)S(1)} %tie.1), channel_id=1, source_target_pairs={{0,1},{1,0},{2,3},{3,2},{4,5},{5,4},{6,7},{7,6},{8,9},{9,8},{10,11... | collective-permute-start | bytes 1376264 | tf_op jit(solution)/shard_map/ppermute | solution.py:670
  40.1 2.7 %collective-permute-start.9 = (bf16[128,1792]{1,0:T(8,128)(2,1)S(1)}, bf16[128,1792]{1,0:T(8,128)(2,1)S(1)}, u32[]{:S(2)}, u32[]{:S(2)}) collective-permute-start(bf16[128,1792]{1,0:T(8,128)(2,1)S(1)} %get-tuple-element.44), channel_id=1, source_target_pairs={{0,1},{1,0},{2,3},{3,2},{4,5},{5,4},{6,7},{7,6},{8,9},{9,8},{10,11... | collective-permute-start | bytes 1376264 | tf_op jit(solution)/shard_map/ppermute | solution.py:694
  40.4 2.4 %collective-permute-start.10 = (f32[1,128]{1,0:T(1,128)S(1)}, f32[1,128]{1,0:T(1,128)S(1)}, u32[]{:S(2)}, u32[]{:S(2)}) collective-permute-start(f32[1,128]{1,0:T(1,128)S(1)} %get-tuple-element.45.refs_7_), channel_id=1, source_target_pairs={{0,1},{1,0},{2,3},{3,2},{4,5},{5,4},{6,7},{7,6},{8,9},{9,8},{10,11... | collective-permute-start | bytes 1544 | tf_op jit(solution)/shard_map/ppermute | solution.py:693

commit v13 on v11

--- a/solution.py
+++ b/solution.py
@@ -167,7 +167,7 @@
 
 
 def fetch(weights):
-    pieces = chunks_of(weights.shape[1], 896)
+    pieces = chunks_of(weights.shape[1], 448)
     return pl.pallas_call(
         functools.partial(fetch_kernel, pieces),
         out_shape=resident(weights),
@@ -225,7 +225,7 @@
         in_specs=[SMEM] + [VMEM] * (4 + len(parts)),
         out_specs=[VMEM] * 4,
         compiler_params=params(8),
-        cost_estimate=cost(10),
+        cost_estimate=cost(20),
         name="key_stage",
     )(rank, modality, norm_gain, head_gain, weights, *parts)
 

time: 43.8 us -> 43.9 us (level)
  no operation moved by 1% of the time
where the time goes in v13:
time: 43.9 us; the launch traced here: 43.7 us
  Pallas kernels  28.7 us (65%)
  starting transfers between devices  12.7 us (29%)
  waiting for transfers between devices  1.14 us (3%)
  between operations  1.05 us (2%)
    pallas_call x1, Pallas kernels, turn_stage(): pl.pallas_call(functools.partial(turn_kernel, pieces, len(outs)), out_sha...  8.55 us
    pallas_call x1, Pallas kernels, middle_stage(): pl.pallas_call(functools.partial(middle_kernel, len(parts), pieces), out_...  8.24 us
    ppermute x3, starting transfers between devices, local(): lax.ppermute(grad, 'seq', inverted(seq_pairs(step, block_count)))  5.84 us
    ppermute x3, starting transfers between devices, local(): memories.append(lax.ppermute(memory, 'seq', seq_pairs(step, block_count)))  5.66 us
    pallas_call x1, Pallas kernels, fetch(): pl.pallas_call(functools.partial(fetch_kernel, pieces), out_shape=residen...  3.45 us
    pallas_call x1, Pallas kernels, attention_stage(): pl.pallas_call(functools.partial(attention_kernel, blocks, pairs, per_gro...  2.87 us
    pallas_call x1, Pallas kernels, key_stage(): pl.pallas_call(functools.partial(key_kernel, len(parts)), out_shape=[jax....  1.57 us
    pallas_call x1, Pallas kernels, key_back_stage(): pl.pallas_call(functools.partial(key_back_kernel, split), out_shape=[jax....  1.48 us
  transfers between devices with their start and end apart: 11, of which 3 were waited for; matrix products, arithmetic and copies ran while one was open for 0% of the time, Pallas kernels for 56%

profile of v13, /device:TPU:0, one launch (start us, length us, event | category | flops | bytes accessed | tf_op | source)
XLA Modules:
  0.0 43.7 jit_solution(11952926255775577453)
XLA Ops:
  0.6 0.5 %collective-permute-start = (bf16[128,1792]{1,0:T(8,128)(2,1)}, bf16[128,1792]{1,0:T(8,128)(2,1)S(1)}, u32[]{:S(2)}, u32[]{:S(2)}) collective-permute-start(bf16[128,1792]{1,0:T(8,128)(2,1)} %refs_4_.3), channel_id=1, source_target_pairs={{0,1},{1,0},{2,3},{3,2},{4,5},{5,4},{6,7},{7,6},{8,9},{9,8},{10,11... | collective-permute-start | bytes 1376264 | tf_op jit(solution)/shard_map/ppermute | solution.py:608
  1.1 0.1 collective-permute-start.1
  1.2 0.0 copy-start.1
  1.2 0.0 copy-start.2
  1.2 0.0 copy-start.3
  1.2 0.0 copy-start.4
  1.2 0.0 slice-start.2
  1.3 3.4 %fetch.1.refs_4_ = bf16[2,3584,512]{2,1,0:T(8,128)(2,1)S(1)} custom-call(bf16[2,3584,512]{2,1,0:T(8,128)(2,1)} %weight_ref.3), custom_call_target="tpu_custom_call" | custom-call | flops 200000000 | bytes 400000 | tf_op jit(solution)/shard_map/fetch/pallas_call | solution.py:171
  4.7 0.0 collective-permute-done.refs_6_
  4.7 0.0 copy-done.1
  4.7 0.0 copy-done.2
  4.7 0.0 copy-done.3
  4.7 0.0 copy-done.4
  4.8 0.0 slice-start.3
  4.8 0.0 slice-start.4
  4.8 0.0 slice-start.5
  4.8 0.0 copy-start
  4.8 1.6 %key_stage.1 = (bf16[128,512]{1,0:T(8,128)(2,1)S(1)}, f32[128,512]{1,0:T(8,128)S(1)}, bf16[128,3584]{1,0:T(8,128)(2,1)S(1)}, f32[1,128]{1,0:T(1,128)S(1)}) custom-call(s32[1]{0:T(128)} %bitcast.refs_0_.rank_ref, s32[1,128]{1,0:T(1,128)S(1)} %bitcast.8, f32[2,3584]{1,0:T(2,128)S(1)} %copy-done.4, f32[2,2,128]{2,1,0:T(2,128)S(1)} %copy-done.1, ...), custom_call_target="tpu_custom_call" | custom-call | flops 20000000000 | bytes 40000000 | tf_op jit(solution)/shard_map/key_stage/pallas_call | solution.py:217
  6.4 4.1 %collective-permute-start.2 = (bf16[128,512]{1,0:T(8,128)(2,1)S(1)}, bf16[128,512]{1,0:T(8,128)(2,1)S(1)}, u32[]{:S(2)}, u32[]{:S(2)}) collective-permute-start(bf16[128,512]{1,0:T(8,128)(2,1)S(1)} %get-tuple-element.26.refs_5_), channel_id=1, source_target_pairs={{0,4},{2,6},{4,0},{6,2},{1,5},{3,7},{5,1},{7,3},{8,12},{10,14},{12... | collective-permute-start | bytes 393224 | tf_op jit(solution)/shard_map/ppermute | solution.py:629
  10.5 1.6 %collective-permute-start.3 = (bf16[128,512]{1,0:T(8,128)(2,1)S(1)}, bf16[128,512]{1,0:T(8,128)(2,1)S(1)}, u32[]{:S(2)}, u32[]{:S(2)}) collective-permute-start(bf16[128,512]{1,0:T(8,128)(2,1)S(1)} %get-tuple-element.26.refs_5_), channel_id=1, source_target_pairs={{0,2},{2,0},{4,6},{6,4},{1,3},{3,1},{5,7},{7,5},{8,10},{10,8},{12,... | collective-permute-start | bytes 393224 | tf_op jit(solution)/shard_map/ppermute | solution.py:629
  12.0 0.0 collective-permute-start.4
  12.0 0.0 collective-permute-done.1.refs_7_
  12.0 0.0 slice-done.2
  12.0 0.0 slice-done.3
  12.1 0.0 slice-done.4
  12.1 0.0 slice-done.5
  12.1 0.0 copy-done
  12.1 0.0 copy-start.5
  12.1 0.0 copy-start.6
  12.1 8.2 %middle_stage.1 = (bf16[128,1024]{1,0:T(8,128)(2,1)S(1)}, f32[128,1024]{1,0:T(8,128)S(1)}, bf16[128,1024]{1,0:T(8,128)(2,1)S(1)}) custom-call(s32[1]{0:T(128)} %bitcast.refs_0_.rank_ref, s32[1,128]{1,0:T(1,128)S(1)} %bitcast.9, f32[2,2,128]{2,1,0:T(2,128)S(1)} %copy-done.1, bf16[128,3584]{1,0:T(8,128)(2,1)S(1)} %get-tuple-element.23.refs_3_, ...), custom_call_target="tpu_custom_call" | custom-call | flops 8000000000 | bytes 16000000 | tf_op jit(solution)/shard_map/middle_stage/pallas_call | solution.py:269
  20.4 0.0 collective-permute-done.2.refs_6_
  20.4 0.0 collective-permute-done.3.refs_7_
  20.4 0.6 %collective-permute-done.4.refs_8_ = bf16[128,512]{1,0:T(8,128)(2,1)S(1)} collective-permute-done((bf16[128,512]{1,0:T(8,128)(2,1)S(1)}, bf16[128,512]{1,0:T(8,128)(2,1)S(1)}, u32[]{:S(2)}, u32[]{:S(2)}) %collective-permute-start.4) | collective-permute-done | bytes 131104 | tf_op jit(solution)/shard_map/ppermute | solution.py:629
  21.0 0.0 copy-done.5
  21.0 0.0 copy-done.6
  21.0 0.0 slice-start
  21.0 2.9 %attention_stage.1 = (bf16[128,1024]{1,0:T(8,128)(2,1)S(1)}, f32[128,1024]{1,0:T(8,128)S(1)}, f32[128,512]{1,0:T(8,128)S(1)}, bf16[128,512]{1,0:T(8,128)(2,1)S(1...) custom-call(s32[1]{0:T(128)} %bitcast.2.refs_0_, s32[4]{0:T(128)S(1)} %copy-done.6, s32[4,128]{1,0:T(4,128)S(1)} %bitcast.14, ...), custom_call_target="tpu_custom_call" | custom-call | flops 4000000000 | bytes 8000000 | tf_op jit(solution)/shard_map/attention_stage/pallas_call | solution.py:349
  23.9 4.3 %collective-permute-start.5 = (bf16[128,512]{1,0:T(8,128)(2,1)S(1)}, bf16[128,512]{1,0:T(8,128)(2,1)S(1)}, u32[]{:S(2)}, u32[]{:S(2)}) collective-permute-start(bf16[128,512]{1,0:T(8,128)(2,1)S(1)} %get-tuple-element.34), channel_id=1, source_target_pairs={{4,0},{6,2},{0,4},{2,6},{5,1},{7,3},{1,5},{3,7},{12,8},{14,10},{8,... | collective-permute-start | bytes 393224 | tf_op jit(solution)/shard_map/ppermute | solution.py:643
  28.2 0.0 collective-permute-start.6
  28.2 1.5 %collective-permute-start.7 = (bf16[128,512]{1,0:T(8,128)(2,1)S(1)}, bf16[128,512]{1,0:T(8,128)(2,1)S(1)}, u32[]{:S(2)}, u32[]{:S(2)}) collective-permute-start(bf16[128,512]{1,0:T(8,128)(2,1)S(1)} %get-tuple-element.36), channel_id=1, source_target_pairs={{6,0},{4,2},{2,4},{0,6},{7,1},{5,3},{3,5},{1,7},{14,8},{12,10},{10... | collective-permute-start | bytes 393224 | tf_op jit(solution)/shard_map/ppermute | solution.py:643
  29.8 0.0 slice-start.1
  29.8 8.6 %turn_stage.1 = (bf16[128,1792]{1,0:T(8,128)(2,1)S(1)}, f32[128,1792]{1,0:T(8,128)S(1)}, f32[128,3584]{1,0:T(8,128)S(1)}, f32[1,128]{1,0:T(1,128)S(1)}) custom-call(s32[1]{0:T(128)} %bitcast.refs_0_.rank_ref, s32[1,128]{1,0:T(1,128)S(1)} %bitcast.10, f32[2,2,128]{2,1,0:T(2,128)S(1)} %copy-done.1, bf16[2,1024,3584]{2,1,0:T(8,128)(2,1)S(1)} %bitcast.7, ...), custom_call_target="tpu_custom_call" | custom-call | flops 10000000000 | bytes 20000000 | tf_op jit(solution)/shard_map/turn_stage/pallas_call | solution.py:419
  38.3 0.0 collective-permute-done.5.refs_8_.arrived_ref
  38.3 0.1 collective-permute-start.10
  38.4 0.3 collective-permute-done.6.refs_9_
  38.7 0.0 collective-permute-done.7.refs_10_
  38.7 0.0 slice-done
  38.7 0.0 slice-done.1
  38.7 1.5 %key_back_stage.1 = (bf16[128,1792]{1,0:T(8,128)(2,1)S(1)}, bf16[128,512]{1,0:T(8,128)(2,1)S(1)}, f32[1,128]{1,0:T(1,128)S(1)}) custom-call(s32[1]{0:T(128)} %bitcast.refs_0_.rank_ref, s32[1,128]{1,0:T(1,128)S(1)} %bitcast.11, f32[2,2,128]{2,1,0:T(2,128)S(1)} %copy-done.1, f32[128,512]{1,0:T(8,128)S(1)} %get-tuple-element.31.refs_3_, ...), custom_call_target="tpu_custom_call" | custom-call | flops 2000000000 | bytes 4000000 | tf_op jit(solution)/shard_map/key_back_stage/pallas_call | solution.py:483
  40.2 0.3 collective-permute-start.8
  40.5 0.3 collective-permute-start.9
  40.8 1.1 %kept_stage.1.refs_5_ = f32[128,1792]{1,0:T(8,128)S(1)} custom-call(s32[1]{0:T(128)} %bitcast.refs_0_.rank_ref, s32[1,128]{1,0:T(1,128)S(1)} %bitcast.12, f32[128,3584]{1,0:T(8,128)S(1)} %get-tuple-element.30.refs_5_.part_ref, bf16[2,3584,512]{2,1,0:T(8,128)(2,1)S(1)} %bitcast.5, bf16[128,512]{1,0:T(8,128)(2,1)S(1)} %get-tuple-element.37.back_ref), custom_call_target="tpu_custom_call" | custom-call | flops 2000000000 | bytes 4000000 | tf_op jit(solution)/shard_map/kept_stage/pallas_call | solution.py:508
  41.9 0.2 collective-permute-done.9.refs_8_
  42.1 0.0 collective-permute-done.10.refs_10_
  42.1 0.0 collective-permute-done.8.refs_6_
  42.1 1.5 %finish.1 = (bf16[128,1792]{1,0:T(8,128)(2,1)}, bf16[128,1792]{1,0:T(8,128)(2,1)}) custom-call(s32[1]{0:T(128)} %bitcast.refs_0_.rank_ref, s32[1,128]{1,0:T(1,128)S(1)} %bitcast.13, f32[2,3584]{1,0:T(2,128)S(1)} %copy-done.4, f32[1,128]{1,0:T(1,128)S(1)} %get-tuple-element.22.refs_3_, bf16[128,1792]{1,0:T(8,128)(2,1)S(1)} %copy-done.3, ...), custom_call_target="tpu_custom_call" | custom-call | flops 1000000000 | bytes 2000000 | tf_op jit(solution)/shard_map/finish/pallas_call | solution.py:569
  (3 shorter events, 0.0 us)
Async XLA Ops:
  0.6 4.1 %collective-permute-start = (bf16[128,1792]{1,0:T(8,128)(2,1)}, bf16[128,1792]{1,0:T(8,128)(2,1)S(1)}, u32[]{:S(2)}, u32[]{:S(2)}) collective-permute-start(bf16[128,1792]{1,0:T(8,128)(2,1)} %refs_4_.3), channel_id=1, source_target_pairs={{0,1},{1,0},{2,3},{3,2},{4,5},{5,4},{6,7},{7,6},{8,9},{9,8},{10,11... | collective-permute-start | bytes 1376264 | tf_op jit(solution)/shard_map/ppermute | solution.py:608
  1.1 10.9 %collective-permute-start.1 = (bf16[128,1792]{1,0:T(8,128)(2,1)}, bf16[128,1792]{1,0:T(8,128)(2,1)S(1)}, u32[]{:S(2)}, u32[]{:S(2)}) collective-permute-start(bf16[128,1792]{1,0:T(8,128)(2,1)} %refs_6_.2), channel_id=1, source_target_pairs={{0,1},{1,0},{2,3},{3,2},{4,5},{5,4},{6,7},{7,6},{8,9},{9,8},{10,11... | collective-permute-start | bytes 1376264 | tf_op jit(solution)/shard_map/ppermute | solution.py:608
  1.2 3.5 %copy-start.1 = (f32[2,2,128]{2,1,0:T(2,128)S(1)}, f32[2,2,128]{2,1,0:T(2,128)}, u32[]{:S(2)}) copy-start(f32[2,2,128]{2,1,0:T(2,128)} %refs_2_.8) | copy-start | bytes 6148
  1.2 3.5 %copy-start.2 = (s32[128]{0:T(128)S(1)}, s32[128]{0:T(128)}, u32[]{:S(2)}) copy-start(s32[128]{0:T(128)} %param.17) | copy-start | bytes 1540
  1.2 3.5 %copy-start.3 = (bf16[128,1792]{1,0:T(8,128)(2,1)S(1)}, bf16[128,1792]{1,0:T(8,128)(2,1)}, u32[]{:S(2)}) copy-start(bf16[128,1792]{1,0:T(8,128)(2,1)} %refs_4_.3) | copy-start | bytes 1376260
  1.2 3.5 %copy-start.4 = (f32[2,3584]{1,0:T(2,128)S(1)}, f32[2,3584]{1,0:T(2,128)}, u32[]{:S(2)}) copy-start(f32[2,3584]{1,0:T(2,128)} %refs_2_.9) | copy-start | bytes 86020
  1.2 10.8 %slice-start.2 = ((s8[14680064]{0:T(1024)(128)(4,1)}), s8[4194304]{0:T(1024)(128)(4,1)S(1)}, s32[]{:S(2)}) async-start(s8[14680064]{0:T(1024)(128)(4,1)} %bitcast.6), calls=%async_computation.2 | async-start | bytes 8388608
  4.8 7.3 %slice-start.3 = ((s8[14680064]{0:T(1024)(128)(4,1)}), s8[4194304]{0:T(1024)(128)(4,1)S(1)}, s32[]{:S(2)}) async-start(s8[14680064]{0:T(1024)(128)(4,1)} %bitcast.6), calls=%async_computation.3 | async-start | bytes 8388608
  4.8 7.3 %slice-start.4 = ((s8[14680064]{0:T(1024)(128)(4,1)}), s8[4194304]{0:T(1024)(128)(4,1)S(1)}, s32[]{:S(2)}) async-start(s8[14680064]{0:T(1024)(128)(4,1)} %bitcast.6), calls=%async_computation.4 | async-start | bytes 8388608
  4.8 7.3 %slice-start.5 = ((s8[14680064]{0:T(1024)(128)(4,1)}), s8[2097152]{0:T(1024)(128)(4,1)S(1)}, s32[]{:S(2)}) async-start(s8[14680064]{0:T(1024)(128)(4,1)} %bitcast.6), calls=%async_computation.5 | async-start | bytes 4194304
  4.8 7.3 %copy-start = (bf16[128,1792]{1,0:T(8,128)(2,1)S(1)}, bf16[128,1792]{1,0:T(8,128)(2,1)}, u32[]{:S(2)}) copy-start(bf16[128,1792]{1,0:T(8,128)(2,1)} %refs_6_.2) | copy-start | bytes 1376260
  6.4 14.0 %collective-permute-start.2 = (bf16[128,512]{1,0:T(8,128)(2,1)S(1)}, bf16[128,512]{1,0:T(8,128)(2,1)S(1)}, u32[]{:S(2)}, u32[]{:S(2)}) collective-permute-start(bf16[128,512]{1,0:T(8,128)(2,1)S(1)} %get-tuple-element.26.refs_5_), channel_id=1, source_target_pairs={{0,4},{2,6},{4,0},{6,2},{1,5},{3,7},{5,1},{7,3},{8,12},{10,14},{12... | collective-permute-start | bytes 393224 | tf_op jit(solution)/shard_map/ppermute | solution.py:629
  10.5 9.9 %collective-permute-start.3 = (bf16[128,512]{1,0:T(8,128)(2,1)S(1)}, bf16[128,512]{1,0:T(8,128)(2,1)S(1)}, u32[]{:S(2)}, u32[]{:S(2)}) collective-permute-start(bf16[128,512]{1,0:T(8,128)(2,1)S(1)} %get-tuple-element.26.refs_5_), channel_id=1, source_target_pairs={{0,2},{2,0},{4,6},{6,4},{1,3},{3,1},{5,7},{7,5},{8,10},{10,8},{12,... | collective-permute-start | bytes 393224 | tf_op jit(solution)/shard_map/ppermute | solution.py:629
  12.0 9.0 %collective-permute-start.4 = (bf16[128,512]{1,0:T(8,128)(2,1)S(1)}, bf16[128,512]{1,0:T(8,128)(2,1)S(1)}, u32[]{:S(2)}, u32[]{:S(2)}) collective-permute-start(bf16[128,512]{1,0:T(8,128)(2,1)S(1)} %get-tuple-element.26.refs_5_), channel_id=1, source_target_pairs={{0,6},{2,4},{4,2},{6,0},{1,7},{3,5},{5,3},{7,1},{8,14},{10,12},{12... | collective-permute-start | bytes 393224 | tf_op jit(solution)/shard_map/ppermute | solution.py:629
  12.1 8.9 %copy-start.5 = (s32[512]{0:T(512)S(1)}, s32[512]{0:T(512)}, u32[]{:S(2)}) copy-start(s32[512]{0:T(512)} %param.18) | copy-start | bytes 6148
  12.1 8.9 %copy-start.6 = (s32[4]{0:T(128)S(1)}, s32[4]{0:T(128)}, u32[]{:S(2)}) copy-start(s32[4]{0:T(128)} %refs_1_.1) | copy-start | bytes 52
  21.0 17.7 %slice-start = ((s8[7340032]{0:T(1024)(128)(4,1)}), s8[4194304]{0:T(1024)(128)(4,1)S(1)}, s32[]{:S(2)}) async-start(s8[7340032]{0:T(1024)(128)(4,1)} %bitcast.4), calls=%async_computation | async-start | bytes 8388608
  23.9 14.4 %collective-permute-start.5 = (bf16[128,512]{1,0:T(8,128)(2,1)S(1)}, bf16[128,512]{1,0:T(8,128)(2,1)S(1)}, u32[]{:S(2)}, u32[]{:S(2)}) collective-permute-start(bf16[128,512]{1,0:T(8,128)(2,1)S(1)} %get-tuple-element.34), channel_id=1, source_target_pairs={{4,0},{6,2},{0,4},{2,6},{5,1},{7,3},{1,5},{3,7},{12,8},{14,10},{8,... | collective-permute-start | bytes 393224 | tf_op jit(solution)/shard_map/ppermute | solution.py:643
  28.2 10.5 %collective-permute-start.6 = (bf16[128,512]{1,0:T(8,128)(2,1)S(1)}, bf16[128,512]{1,0:T(8,128)(2,1)S(1)}, u32[]{:S(2)}, u32[]{:S(2)}) collective-permute-start(bf16[128,512]{1,0:T(8,128)(2,1)S(1)} %get-tuple-element.35), channel_id=1, source_target_pairs={{2,0},{0,2},{6,4},{4,6},{3,1},{1,3},{7,5},{5,7},{10,8},{8,10},{14,... | collective-permute-start | bytes 393224 | tf_op jit(solution)/shard_map/ppermute | solution.py:643
  28.2 10.5 %collective-permute-start.7 = (bf16[128,512]{1,0:T(8,128)(2,1)S(1)}, bf16[128,512]{1,0:T(8,128)(2,1)S(1)}, u32[]{:S(2)}, u32[]{:S(2)}) collective-permute-start(bf16[128,512]{1,0:T(8,128)(2,1)S(1)} %get-tuple-element.36), channel_id=1, source_target_pairs={{6,0},{4,2},{2,4},{0,6},{7,1},{5,3},{3,5},{1,7},{14,8},{12,10},{10... | collective-permute-start | bytes 393224 | tf_op jit(solution)/shard_map/ppermute | solution.py:643
  29.8 9.0 %slice-start.1 = ((s8[7340032]{0:T(1024)(128)(4,1)}), s8[3145728]{0:T(1024)(128)(4,1)S(1)}, s32[]{:S(2)}) async-start(s8[7340032]{0:T(1024)(128)(4,1)} %bitcast.4), calls=%async_computation.1 | async-start | bytes 6291456
  38.3 3.8 %collective-permute-start.10 = (bf16[128,1792]{1,0:T(8,128)(2,1)S(1)}, bf16[128,1792]{1,0:T(8,128)(2,1)S(1)}, u32[]{:S(2)}, u32[]{:S(2)}) collective-permute-start(bf16[128,1792]{1,0:T(8,128)(2,1)S(1)} %tie.1), channel_id=1, source_target_pairs={{0,1},{1,0},{2,3},{3,2},{4,5},{5,4},{6,7},{7,6},{8,9},{9,8},{10,11... | collective-permute-start | bytes 1376264 | tf_op jit(solution)/shard_map/ppermute | solution.py:660
  40.2 1.9 %collective-permute-start.8 = (bf16[128,1792]{1,0:T(8,128)(2,1)S(1)}, bf16[128,1792]{1,0:T(8,128)(2,1)S(1)}, u32[]{:S(2)}, u32[]{:S(2)}) collective-permute-start(bf16[128,1792]{1,0:T(8,128)(2,1)S(1)} %get-tuple-element.38), channel_id=1, source_target_pairs={{0,1},{1,0},{2,3},{3,2},{4,5},{5,4},{6,7},{7,6},{8,9},{9,8},{10,11... | collective-permute-start | bytes 1376264 | tf_op jit(solution)/shard_map/ppermute | solution.py:685
  40.5 1.6 %collective-permute-start.9 = (f32[1,128]{1,0:T(1,128)S(1)}, f32[1,128]{1,0:T(1,128)S(1)}, u32[]{:S(2)}, u32[]{:S(2)}) collective-permute-start(f32[1,128]{1,0:T(1,128)S(1)} %get-tuple-element.39.refs_7_), channel_id=1, source_target_pairs={{0,1},{1,0},{2,3},{3,2},{4,5},{5,4},{6,7},{7,6},{8,9},{9,8},{10,11... | collective-permute-start | bytes 1544 | tf_op jit(solution)/shard_map/ppermute | solution.py:684
